TPU v7x, 32 devices: a whole 2x2x4 slice. The times are simulated.
32 devices in a mesh: ctx: 8 (over y, x, core), head: 4 (over z).
Axes of the slice: x: 2, y: 2, z: 4, core: 2. Of those that a mesh axis runs over, the one named last changes fastest.
Arguments:
- features: bfloat16 [4096, 8192], P('ctx', 'head'), may hold values from -6 to 6
- gate_values: bfloat16 [4096, 8192], P('ctx', 'head'), may hold values from -6 to 6
- write_proj: bfloat16 [4096, 1024], P('ctx', 'head'), may hold values from -0.0234375 to 0.0234375
- read_proj: bfloat16 [4096, 1024], P('ctx', 'head'), may hold values from -6 to 6
- step_size: float32 [128, 4096], P('head', 'ctx'), may hold values from 0.25 to 2
- log_decay: float32 [128, 4096], P('head', 'ctx'), may hold values from -1 to 0
- starts: int32 [4096], P('ctx'), may hold values from 0 to 1
- skip_weight: float32 [128], P('head'), may hold values from 0.5 to 1.5
- norm_gain: float32 [8192], P('head'), may hold values from 0.1 to 1.9
- out_weight: bfloat16 [8192, 4096], P('head'), may hold values from -0.0625 to 0.0625
Outputs:
- mixed: bfloat16 [4096, 4096], P(('ctx', 'head'))
All inputs are finite; a program needn't handle non-finite values.
Results may differ from a plain program's by a relative error of at most 0.0061.
Values sent between devices are 32-bit elements; how exact they have to be, the bound alone decides.
No kernel may reach another device: no remote copies, remote signals or barrier semaphores. Data moves between devices by JAX's collectives and lax.ppermute only.
A program may use at most 128 MiB of HBM per device.

v0:
```python
import jax
import jax.numpy as jnp
from jax import lax
from jax.sharding import PartitionSpec as P

HEADS = 128
HEAD_DIM = 64
NSTATE = 128
GROUPS = 8
SPAN = 256


eps = 1e-05


def passed_along(value, axis, steps):
    count = lax.axis_size(axis)
    initial, last = (max(0, -steps), min(count, count - steps))
    return lax.ppermute(value, axis, [(source, source + steps) for source in range(initial, last)])


def body(
    features,
    gate_values,
    write_proj,
    read_proj,
    step_size,
    log_decay,
    starts,
    skip_weight,
    norm_gain,
    out_weight,
):
    tokens = features.shape[0]
    heads_dev = step_size.shape[0]
    groups_dev = write_proj.shape[1] // NSTATE
    per_group = HEADS // GROUPS
    blocks = tokens // SPAN
    feat_blocks = features.reshape(blocks, SPAN, heads_dev, HEAD_DIM)
    write_blocks = write_proj.reshape(blocks, SPAN, groups_dev, NSTATE)
    read_blocks = read_proj.reshape(blocks, SPAN, groups_dev, NSTATE)
    step_blocks = step_size.reshape(heads_dev, blocks, SPAN)
    running = jnp.cumsum(log_decay.reshape(heads_dev, blocks, SPAN), axis=2)
    seg_local = jnp.cumsum(starts.reshape(blocks, SPAN), axis=1)
    position = jnp.arange(SPAN)
    causal = position[:, None] >= position[None, :]
    together = (seg_local[:, :, None] == seg_local[:, None, :]) & causal[None]
    spread_log = running[:, :, :, None] - running[:, :, None, :]
    damping = jnp.where(together[None], jnp.exp(jnp.where(together[None], spread_log, 0.0)), 0.0)
    scores = jnp.einsum(
        "kign,kjgn->gkij", read_blocks, write_blocks, preferred_element_type=jnp.float32
    )
    weights = (
        (damping * step_blocks[:, :, None, :]).reshape(groups_dev, per_group, blocks, SPAN, SPAN)
        * scores[:, None]
    ).astype(jnp.bfloat16)
    weights = weights.reshape(heads_dev, blocks, SPAN, SPAN)
    intra_out = jnp.einsum(
        "hkij,kjhp->kihp", weights, feat_blocks, preferred_element_type=jnp.float32
    )
    tail_scale = (
        jnp.where(
            seg_local[None] == seg_local[None, :, -1:], jnp.exp(running[:, :, -1:] - running), 0.0
        )
        * step_blocks
    )
    scaled_in = (tail_scale.transpose(1, 2, 0)[..., None] * feat_blocks.astype(jnp.float32)).astype(
        jnp.bfloat16
    )
    block_states = jnp.einsum(
        "kjgep,kjgn->kgepn",
        scaled_in.reshape(blocks, SPAN, groups_dev, per_group, HEAD_DIM),
        write_blocks,
        preferred_element_type=jnp.float32,
    ).reshape(blocks, heads_dev, HEAD_DIM, NSTATE)
    keep_scale = jnp.where(seg_local[None, :, -1] == 0, jnp.exp(running[:, :, -1]), 0.0)
    total_mult = jnp.ones((heads_dev,), jnp.float32)
    total_state = jnp.zeros((heads_dev, HEAD_DIM, NSTATE), jnp.float32)
    entry_mult = []
    entry_state = []
    for block_id in range(blocks):
        entry_mult.append(total_mult)
        entry_state.append(total_state)
        total_state = keep_scale[:, block_id][:, None, None] * total_state + block_states[block_id]
        total_mult = total_mult * keep_scale[:, block_id]

    def relay_step(index, incoming):
        leaving = total_mult[:, None, None] * incoming + total_state
        return passed_along(leaving, "ctx", 1)

    incoming = lax.fori_loop(0, lax.axis_size("ctx") - 1, relay_step, jnp.zeros_like(total_state))
    carried = jnp.stack(
        [
            entry_mult[block_id][:, None, None] * incoming + entry_state[block_id]
            for block_id in range(blocks)
        ]
    )
    entry_read = carried.astype(jnp.bfloat16)
    carried_out = jnp.einsum(
        "kign,kgepn->kigep",
        read_blocks,
        entry_read.reshape(blocks, groups_dev, per_group, HEAD_DIM, NSTATE),
        preferred_element_type=jnp.float32,
    ).reshape(blocks, SPAN, heads_dev, HEAD_DIM)
    reach_scale = jnp.where(seg_local[None] == 0, jnp.exp(running), 0.0).transpose(1, 2, 0)
    mixed_out = (
        intra_out
        + reach_scale[..., None] * carried_out
        + skip_weight[None, None, :, None] * feat_blocks.astype(jnp.float32)
    )
    gated = mixed_out.reshape(tokens, heads_dev * HEAD_DIM) * jax.nn.silu(
        gate_values.astype(jnp.float32)
    )
    grouped = gated.reshape(tokens, groups_dev, per_group * HEAD_DIM)
    mean_square = jnp.mean(grouped * grouped, axis=-1, keepdims=True)
    normed = (
        (grouped * lax.rsqrt(mean_square + eps)).reshape(tokens, heads_dev * HEAD_DIM)
        * norm_gain[None, :]
    ).astype(jnp.bfloat16)
    summed = lax.psum_scatter(
        jnp.dot(normed, out_weight, preferred_element_type=jnp.float32),
        "head",
        scatter_dimension=0,
        tiled=True,
    )
    return summed.astype(jnp.bfloat16)


def solution(mesh):
    placed = (
        P("ctx", "head"),
        P("ctx", "head"),
        P("ctx", "head"),
        P("ctx", "head"),
        P("head", "ctx"),
        P("head", "ctx"),
        P("ctx"),
        P("head"),
        P("head"),
        P("head", None),
    )
    return jax.shard_map(
        body, mesh=mesh, in_specs=placed, out_specs=P(("ctx", "head"), None), check_vma=False
    )
```

profile of v0, /device:TPU:16, one launch (start us, length us, event | category | flops | bytes accessed | tf_op | source)
XLA Modules:
  0.0 368.4 jit_solution(18256229936106694381)
XLA Ops:
  6.5 1.4 reduce-window.14
  8.0 0.2 slice_reduce_fusion.1
  8.2 0.2 reduce-window.15
  8.6 0.9 reshape.207
  9.5 1.2 reduce-window.16
  11.3 0.6 slice_bitcast_fusion.1
  11.9 4.2 %copy.60 = f32[512,2048]{0,1:T(8,128)} copy(bf16[512,2048]{1,0:T(8,128)(2,1)} %param.12) | data formatting | bytes 6291456 | tf_op jit(solution)/shard_map/convert_element_type | solution.py:67
  16.0 5.3 %reshape.217 = bf16[2,256,32,64]{3,2,1,0:T(8,128)(2,1)} reshape(bf16[512,2048]{1,0:T(8,128)(2,1)S(1)} %copy-done.2) | data formatting | bytes 4194304 | tf_op jit(solution)/shard_map/reshape | solution.py:39
  21.4 0.6 copy.108
  22.1 0.7 select_bitcast_fusion
  22.9 5.9 %reshape.214 = f32[2,256,2,16,64]{1,0,4,3,2:T(2,128)} reshape(f32[512,2048]{0,1:T(8,128)} %copy.60) | data formatting | bytes 8388608 | tf_op jit(solution)/shard_map/convert_element_type | solution.py:67
  28.8 4.2 %multiply_convert_fusion.2 = bf16[2,256,2,16,64]{1,0,4,3,2:T(2,128)(2,1)S(1)} fusion(f32[2,256,2,16,64]{1,0,4,3,2:T(2,128)} %reshape.214, f32[2,256,2,16]{1,0,3,2:T(2,128)S(1)} %copy.59), kind=kLoop, calls=%fused_computation.16 | loop fusion | flops 2097152 | bytes 6356992 | tf_op jit(solution)/shard_map/convert_element_type | solution.py:67
  33.1 0.7 fusion.9
  33.8 0.2 fusion.23
  34.2 0.9 compare_and_fusion
  35.1 1.3 fusion.17
  36.3 5.8 %copy.56 = bf16[2,256,32,64]{1,3,2,0:T(8,128)(2,1)} copy(bf16[2,256,32,64]{3,2,1,0:T(8,128)(2,1)} %reshape.217) | data formatting | bytes 4194304 | tf_op jit(solution)/shard_map/reshape | solution.py:39
  42.2 0.9 bitcast_add_fusion.1
  43.2 101.2 %while.10 = (s32[]{:T(128)}, f32[32,64,128]{2,1,0:T(8,128)S(1)}, f32[32]{0:T(128)S(1)}, f32[32,64,128]{2,1,0:T(8,128)S(1)}, s32[]{:T(128)}) while((s32[]{:T(128)}, f32[32,64,128]{2,1,0:T(8,128)S(1)}, f32[32]{0:T(128)S(1)}, f32[32,64,128]{2,1,0:T(8,128)S(1)}, s32[]{:T(128)}) %tuple.24), condition=%wide.region_5.6_spmd, body=%wide.region_4.5_spmd.sunk | while | flops 524290 | bytes 7340261 | solution.py:91
  43.2 0.2 multiply_add_fusion.2
  43.4 1.8 collective-permute-start
  45.2 2.2 collective-permute-done
  47.4 0.2 multiply_add_fusion.2
  47.6 13.2 %collective-permute-start = (f32[32,64,128]{2,1,0:T(8,128)S(1)}, f32[32,64,128]{2,1,0:T(8,128)S(1)}, u32[]{:S(2)}, u32[]{:S(2)}) collective-permute-start(f32[32,64,128]{2,1,0:T(8,128)S(1)} %multiply_add_fusion.2), channel_id=1, source_target_pairs={{0,4},{4,8},{8,12},{12,16},{16,20},{20,24},{24,28},{1,5},{5,9},{9,... | collective-permute-start | bytes 3145736 | tf_op jit(solution)/shard_map/while/body/eval_jaxpr/ppermute | solution.py:19
  60.8 2.2 collective-permute-done
  63.0 0.2 multiply_add_fusion.2
  63.2 13.9 %collective-permute-start = (f32[32,64,128]{2,1,0:T(8,128)S(1)}, f32[32,64,128]{2,1,0:T(8,128)S(1)}, u32[]{:S(2)}, u32[]{:S(2)}) collective-permute-start(f32[32,64,128]{2,1,0:T(8,128)S(1)} %multiply_add_fusion.2), channel_id=1, source_target_pairs={{0,4},{4,8},{8,12},{12,16},{16,20},{20,24},{24,28},{1,5},{5,9},{9,... | collective-permute-start | bytes 3145736 | tf_op jit(solution)/shard_map/while/body/eval_jaxpr/ppermute | solution.py:19
  77.1 2.2 collective-permute-done
  79.5 13.9 %collective-permute-start = (f32[32,64,128]{2,1,0:T(8,128)S(1)}, f32[32,64,128]{2,1,0:T(8,128)S(1)}, u32[]{:S(2)}, u32[]{:S(2)}) collective-permute-start(f32[32,64,128]{2,1,0:T(8,128)S(1)} %multiply_add_fusion.2), channel_id=1, source_target_pairs={{0,4},{4,8},{8,12},{12,16},{16,20},{20,24},{24,28},{1,5},{5,9},{9,... | collective-permute-start | bytes 3145736 | tf_op jit(solution)/shard_map/while/body/eval_jaxpr/ppermute | solution.py:19
  93.4 2.2 collective-permute-done
  95.7 13.9 %collective-permute-start = (f32[32,64,128]{2,1,0:T(8,128)S(1)}, f32[32,64,128]{2,1,0:T(8,128)S(1)}, u32[]{:S(2)}, u32[]{:S(2)}) collective-permute-start(f32[32,64,128]{2,1,0:T(8,128)S(1)} %multiply_add_fusion.2), channel_id=1, source_target_pairs={{0,4},{4,8},{8,12},{12,16},{16,20},{20,24},{24,28},{1,5},{5,9},{9,... | collective-permute-start | bytes 3145736 | tf_op jit(solution)/shard_map/while/body/eval_jaxpr/ppermute | solution.py:19
  109.7 2.2 collective-permute-done
  112.0 13.9 %collective-permute-start = (f32[32,64,128]{2,1,0:T(8,128)S(1)}, f32[32,64,128]{2,1,0:T(8,128)S(1)}, u32[]{:S(2)}, u32[]{:S(2)}) collective-permute-start(f32[32,64,128]{2,1,0:T(8,128)S(1)} %multiply_add_fusion.2), channel_id=1, source_target_pairs={{0,4},{4,8},{8,12},{12,16},{16,20},{20,24},{24,28},{1,5},{5,9},{9,... | collective-permute-start | bytes 3145736 | tf_op jit(solution)/shard_map/while/body/eval_jaxpr/ppermute | solution.py:19
  126.0 2.2 collective-permute-done
  128.3 13.9 %collective-permute-start = (f32[32,64,128]{2,1,0:T(8,128)S(1)}, f32[32,64,128]{2,1,0:T(8,128)S(1)}, u32[]{:S(2)}, u32[]{:S(2)}) collective-permute-start(f32[32,64,128]{2,1,0:T(8,128)S(1)} %multiply_add_fusion.2), channel_id=1, source_target_pairs={{0,4},{4,8},{8,12},{12,16},{16,20},{20,24},{24,28},{1,5},{5,9},{9,... | collective-permute-start | bytes 3145736 | tf_op jit(solution)/shard_map/while/body/eval_jaxpr/ppermute | solution.py:19
  142.2 2.2 collective-permute-done
  144.4 1.6 fusion.24
  146.1 0.7 fusion.11
  146.9 7.7 %mul.124 = f32[2,16,2,256,256]{4,3,1,0,2:T(8,128)} broadcast(f32[2,2,256,256]{3,2,0,1:T(8,128)S(1)} %copy-done.3), dimensions={0,2,3,4} | broadcast | bytes 17825792 | tf_op jit(solution)/shard_map/mul | solution.py:54
  154.6 11.2 %fusion.8 = f32[2,256,32,64]{1,3,2,0:T(8,128)S(1)} fusion(bf16[2,256,32,64]{1,3,2,0:T(8,128)(2,1)S(1)} %copy-done.4, f32[2,256,32,64]{1,3,2,0:T(8,128)S(1)} %bitcast.87, f32[32,2,256,256]{3,2,0,1:T(8,128)} %bitcast.85, f32[32,2,256]{2,0,1:T(8,128)S(1)} %bitcast.95, f32[32,2,256]{2,0,1:T(8,128)S(1)} %copy_bitcast_fusion, ...), kind=kOutput, calls=%fused_computation.15 | convolution fusion | flops 567279616 | bytes 27590784 | tf_op jit(solution)/shard_map/hkij,kjhp->kihp/dot_general | solution.py:58
  165.9 3.3 copy.65
  169.2 2.4 copy.84
  171.6 2.9 copy.66
  174.5 3.7 %bitcast_reduce_fusion = f32[512,2]{0,1:T(2,128)S(1)} fusion(f32[512,2048]{0,1:T(8,128)} %bitcast.83, bf16[512,2048]{0,1:T(8,128)(2,1)S(1)} %copy.66), kind=kLoop, calls=%fused_computation.13 | loop fusion | flops 8387584 | bytes 6295552 | tf_op jit(solution)/shard_map/reduce_sum | solution.py:115
  178.2 1.5 fusion.7
  179.7 14.5 %fusion.25 = f32[512,4096]{1,0:T(8,128)} fusion(bf16[512,2048]{0,1:T(8,128)(2,1)S(1)} %fusion.7, bf16[2048,4096]{1,0:T(8,128)(2,1)} %param.21), kind=kOutput, calls=%fused_computation.55 | convolution fusion | flops 8589934592 | bytes 27262976 | tf_op jit(solution)/shard_map/dot_general | solution.py:121
  194.2 164.6 %reduce-scatter.2.cloned.1.call-done = f32[128,4096]{1,0:T(8,128)} async-done(((f32[512,4096]{1,0:T(8,128)}), f32[128,4096]{1,0:T(8,128)}) %reduce-scatter.2.cloned.1.call-update) | async-done | bytes 2097168 | tf_op jit(solution)/shard_map/reduce_scatter | solution.py:120
  358.8 2.7 convert_element_type.36
  (54 shorter events, 2.0 us)
Async XLA Ops:
  6.5 9.5 %copy-start.2 = (bf16[512,2048]{1,0:T(8,128)(2,1)S(1)}, bf16[512,2048]{1,0:T(8,128)(2,1)}, u32[]{:S(2)}) copy-start(bf16[512,2048]{1,0:T(8,128)(2,1)} %param.12) | copy-start | bytes 6291460
  6.5 352.3 %reduce-scatter.2.cloned.1.call-start = ((), (), s32[]{:S(2)}) async-start(), calls=%async_computation.1 | async-start | bytes 10485760 | tf_op jit(solution)/shard_map/reduce_scatter | solution.py:120
  16.0 5.4 %copy-start.7 = (f32[32,512]{1,0:T(8,128)S(1)}, f32[32,512]{1,0:T(8,128)}, u32[]{:S(2)}) copy-start(f32[32,512]{1,0:T(8,128)} %param.16) | copy-start | bytes 196612
  22.8 5.9 %copy-start.5 = (bf16[512,256]{1,0:T(8,128)(2,1)S(1)}, bf16[512,256]{1,0:T(8,128)(2,1)}, u32[]{:S(2)}) copy-start(bf16[512,256]{1,0:T(8,128)(2,1)} %param.14) | copy-start | bytes 786436
  33.1 1.0 copy-start.6
  34.1 8.1 %copy-start.1 = (f32[1,2,16,64,128]{4,3,2,1,0:T(8,128)}, f32[1,2,16,64,128]{4,3,2,1,0:T(8,128)S(1)}, u32[]{:S(2)}) copy-start(f32[1,2,16,64,128]{4,3,2,1,0:T(8,128)S(1)} %get-tuple-element.36) | copy-start | bytes 3145732
  43.4 4.0 %collective-permute-start = (f32[32,64,128]{2,1,0:T(8,128)S(1)}, f32[32,64,128]{2,1,0:T(8,128)S(1)}, u32[]{:S(2)}, u32[]{:S(2)}) collective-permute-start(f32[32,64,128]{2,1,0:T(8,128)S(1)} %multiply_add_fusion.2), channel_id=1, source_target_pairs={{0,4},{4,8},{8,12},{12,16},{16,20},{20,24},{24,28},{1,5},{5,9},{9,... | collective-permute-start | bytes 3145736 | tf_op jit(solution)/shard_map/while/body/eval_jaxpr/ppermute | solution.py:19
  47.6 15.4 %collective-permute-start = (f32[32,64,128]{2,1,0:T(8,128)S(1)}, f32[32,64,128]{2,1,0:T(8,128)S(1)}, u32[]{:S(2)}, u32[]{:S(2)}) collective-permute-start(f32[32,64,128]{2,1,0:T(8,128)S(1)} %multiply_add_fusion.2), channel_id=1, source_target_pairs={{0,4},{4,8},{8,12},{12,16},{16,20},{20,24},{24,28},{1,5},{5,9},{9,... | collective-permute-start | bytes 3145736 | tf_op jit(solution)/shard_map/while/body/eval_jaxpr/ppermute | solution.py:19
  63.2 16.1 %collective-permute-start = (f32[32,64,128]{2,1,0:T(8,128)S(1)}, f32[32,64,128]{2,1,0:T(8,128)S(1)}, u32[]{:S(2)}, u32[]{:S(2)}) collective-permute-start(f32[32,64,128]{2,1,0:T(8,128)S(1)} %multiply_add_fusion.2), channel_id=1, source_target_pairs={{0,4},{4,8},{8,12},{12,16},{16,20},{20,24},{24,28},{1,5},{5,9},{9,... | collective-permute-start | bytes 3145736 | tf_op jit(solution)/shard_map/while/body/eval_jaxpr/ppermute | solution.py:19
  79.5 16.1 %collective-permute-start = (f32[32,64,128]{2,1,0:T(8,128)S(1)}, f32[32,64,128]{2,1,0:T(8,128)S(1)}, u32[]{:S(2)}, u32[]{:S(2)}) collective-permute-start(f32[32,64,128]{2,1,0:T(8,128)S(1)} %multiply_add_fusion.2), channel_id=1, source_target_pairs={{0,4},{4,8},{8,12},{12,16},{16,20},{20,24},{24,28},{1,5},{5,9},{9,... | collective-permute-start | bytes 3145736 | tf_op jit(solution)/shard_map/while/body/eval_jaxpr/ppermute | solution.py:19
  95.7 16.1 %collective-permute-start = (f32[32,64,128]{2,1,0:T(8,128)S(1)}, f32[32,64,128]{2,1,0:T(8,128)S(1)}, u32[]{:S(2)}, u32[]{:S(2)}) collective-permute-start(f32[32,64,128]{2,1,0:T(8,128)S(1)} %multiply_add_fusion.2), channel_id=1, source_target_pairs={{0,4},{4,8},{8,12},{12,16},{16,20},{20,24},{24,28},{1,5},{5,9},{9,... | collective-permute-start | bytes 3145736 | tf_op jit(solution)/shard_map/while/body/eval_jaxpr/ppermute | solution.py:19
  112.0 16.1 %collective-permute-start = (f32[32,64,128]{2,1,0:T(8,128)S(1)}, f32[32,64,128]{2,1,0:T(8,128)S(1)}, u32[]{:S(2)}, u32[]{:S(2)}) collective-permute-start(f32[32,64,128]{2,1,0:T(8,128)S(1)} %multiply_add_fusion.2), channel_id=1, source_target_pairs={{0,4},{4,8},{8,12},{12,16},{16,20},{20,24},{24,28},{1,5},{5,9},{9,... | collective-permute-start | bytes 3145736 | tf_op jit(solution)/shard_map/while/body/eval_jaxpr/ppermute | solution.py:19
  128.3 16.1 %collective-permute-start = (f32[32,64,128]{2,1,0:T(8,128)S(1)}, f32[32,64,128]{2,1,0:T(8,128)S(1)}, u32[]{:S(2)}, u32[]{:S(2)}) collective-permute-start(f32[32,64,128]{2,1,0:T(8,128)S(1)} %multiply_add_fusion.2), channel_id=1, source_target_pairs={{0,4},{4,8},{8,12},{12,16},{16,20},{20,24},{24,28},{1,5},{5,9},{9,... | collective-permute-start | bytes 3145736 | tf_op jit(solution)/shard_map/while/body/eval_jaxpr/ppermute | solution.py:19
  144.4 2.4 copy-start.3
  146.8 7.8 %copy-start.4 = (bf16[2,256,32,64]{1,3,2,0:T(8,128)(2,1)S(1)}, bf16[2,256,32,64]{1,3,2,0:T(8,128)(2,1)}, u32[]{:S(2)}) copy-start(bf16[2,256,32,64]{1,3,2,0:T(8,128)(2,1)} %copy.56) | copy-start | bytes 6291460
  146.8 7.8 %copy-start.8 = (pred[2,256,256]{2,1,0:T(8,128)(4,1)S(1)}, pred[2,256,256]{2,1,0:T(8,128)(4,1)}, u32[]{:S(2)}) copy-start(pred[2,256,256]{2,1,0:T(8,128)(4,1)} %compare_and_fusion) | copy-start | bytes 393220
  146.8 7.8 %copy-start.9 = (f32[4,2,8,256]{3,2,0,1:T(8,128)S(1)}, f32[4,2,8,256]{3,2,0,1:T(8,128)}, u32[]{:S(2)}) copy-start(f32[4,2,8,256]{3,2,0,1:T(8,128)} %copy.108) | copy-start | bytes 196612
  146.8 7.8 %copy-start.10 = (f32[2,256,32]{1,2,0:T(8,128)S(1)}, f32[2,256,32]{1,2,0:T(8,128)}, u32[]{:S(2)}) copy-start(f32[2,256,32]{1,2,0:T(8,128)} %get-tuple-element.40) | copy-start | bytes 196612
  146.9 7.8 %copy-start.12 = (f32[32]{0:T(128)S(1)}, f32[32]{0:T(128)}, u32[]{:S(2)}) copy-start(f32[32]{0:T(128)} %param.19) | copy-start | bytes 388
  174.4 3.7 %copy-start = (f32[256,8,2,256]{3,1,2,0:T(8,128)S(1)}, f32[256,8,2,256]{3,1,2,0:T(8,128)}, u32[]{:S(2)}) copy-start(f32[256,8,2,256]{3,1,2,0:T(8,128)} %copy.84) | copy-start | bytes 12582916
  174.5 3.7 %copy-start.11 = (f32[2048]{0:T(1024)S(1)}, f32[2048]{0:T(1024)}, u32[]{:S(2)}) copy-start(f32[2048]{0:T(1024)} %param.20) | copy-start | bytes 24580
Sparse Core Ops, SparseCore 0:
  194.3 164.4 reduce-scatter.1
where the time goes:
time: 370 us; the launch traced here: 368 us
  waiting for transfers between devices  180 us (49%)
  starting transfers between devices  84.5 us (23%)
  local copies, waits for them, and re-layouts  41 us (11%)
  matrix products  28.4 us (8%)
  other arithmetic  20.6 us (6%)
  between operations  13.7 us (4%)
    reduce_scatter x1, waiting for transfers between devices, body(): lax.psum_scatter(jnp.dot(normed, out_weight, preferred_element_type=jnp.f...  165 us
    ppermute x7, starting transfers between devices, passed_along(): lax.ppermute(value, axis, [(source, source + steps) for source in range(i...  84.5 us
    ppermute x7, waiting for transfers between devices, passed_along(): lax.ppermute(value, axis, [(source, source + steps) for source in range(i...  15.4 us
    dot_general x1, matrix products, body(): jnp.dot(normed, out_weight, preferred_element_type=jnp.float32)  14.5 us
    dot_general x1, matrix products, body(): jnp.einsum('hkij,kjhp->kihp', weights, feat_blocks, preferred_element_typ...  11.2 us
    reshape x2, local copies, waits for them, and re-layouts, body(): feat_blocks = features.reshape(blocks, SPAN, heads_dev, HEAD_DIM)  11.2 us
    convert_element_type x2, local copies, waits for them, and re-layouts, body(): feat_blocks.astype(jnp.float32)  10.1 us
    mul x1, local copies, waits for them, and re-layouts, body(): (damping * step_blocks[:, :, None, :]).reshape(groups_dev, per_group, blo...  7.74 us
  transfers between devices with their start and end apart: 8, of which 8 were waited for; matrix products, arithmetic and copies ran while one was open for 0% of the time, Pallas kernels for 0%

commit v1 on v0

v1 whole, which is shorter than its diff:
```python
import jax
import jax.numpy as jnp
import numpy as np
from jax import lax
from jax.experimental import pallas as pl
from jax.experimental.pallas import tpu as pltpu
from jax.sharding import PartitionSpec as P

HEADS = 128
HEAD_DIM = 64
NSTATE = 128
GROUPS = 8
SPAN = 256
KROWS = 8
LOG2E = 1.4426950408889634
VMEM = 48 * 1024 * 1024

eps = 1e-05
F32 = jnp.float32
BF16 = jnp.bfloat16


def three_parts(value, axis):
    high = value.astype(BF16)
    rest = value - high.astype(F32)
    middle = rest.astype(BF16)
    low = (rest - middle.astype(F32)).astype(BF16)
    return jnp.concatenate([high, middle, low], axis=axis)


def head_spread(heads, channels):
    row = lax.broadcasted_iota(jnp.int32, (3 * heads, channels), 0)
    col = lax.broadcasted_iota(jnp.int32, (3 * heads, channels), 1)
    return jnp.where(lax.rem(row, heads) == lax.div(col, HEAD_DIM), 1.0, 0.0).astype(BF16)


def dot(a, b, contract=((1,), (0,))):
    return lax.dot_general(a, b, (contract, ((), ())), preferred_element_type=F32)


def states_kernel(me, feat, write, step, decay, starts, *refs, per_group, blocks, groups, pieces, width):
    msgs = refs[:pieces]
    pre_s, pre_k, vrow, segrow, cols, stack, run_s, run_k = refs[pieces:]
    group, block = pl.program_id(0), pl.program_id(1)
    upper = lax.broadcasted_iota(jnp.int32, (SPAN, SPAN), 0) <= lax.broadcasted_iota(
        jnp.int32, (SPAN, SPAN), 1
    )
    upper = jnp.where(upper, 1.0, 0.0).astype(BF16)
    begins = jnp.broadcast_to(starts[...].astype(F32), (16, SPAN)).astype(BF16)
    sums = dot(jnp.concatenate([three_parts(decay[...], 0), begins], axis=0), upper)
    cum = sums[:per_group] + sums[per_group : 2 * per_group] + sums[2 * per_group : 3 * per_group]
    seg = sums[3 * per_group : 3 * per_group + 8]
    dt = step[...]
    seg_row = seg[0:1]
    seg_last = seg_row[:, SPAN - 1 :]
    last = cum[:, SPAN - 1 :]
    tail = jnp.where(seg_row == seg_last, jnp.exp(last - cum), 0.0) * dt
    keep = jnp.where(seg_last == 0.0, jnp.exp(last), 0.0)
    spread = head_spread(per_group, feat.shape[1])
    tail_all = dot(three_parts(tail, 0), spread, ((0,), (0,)))
    scaled = (tail_all * feat[...].astype(F32)).astype(BF16)
    state = dot(write[...], scaled, ((0,), (0,)))
    keep_all = dot(three_parts(jnp.broadcast_to(keep, (per_group, 128)), 0), spread, ((0,), (0,)))
    keep_all = keep_all[:KROWS]

    reach = jnp.where(seg_row == 0.0, jnp.exp(cum), 0.0)
    vrow[...] = cum * LOG2E - jnp.log2(dt)
    segrow[...] = seg
    fill = jnp.zeros((128 - 2 * per_group - 8, SPAN), F32)
    cols[0] = jnp.concatenate([cum * LOG2E, reach, seg, fill], axis=0).T

    @pl.when(block == 0)
    def _():
        run_s[...] = state
        run_k[...] = keep_all

    @pl.when(block > 0)
    def _():
        run_s[...] = keep_all[0:1] * run_s[...] + state
        run_k[...] = keep_all * run_k[...]

    @pl.when(block < blocks - 1)
    def _():
        pre_s[0] = run_s[...]
        pre_k[0] = run_k[...]

    @pl.when(block == blocks - 1)
    def _():
        here = pieces // groups
        for index in range(here):
            part = slice(index * width, (index + 1) * width)
            stack[group * here + index, :NSTATE] = run_s[:, part]
            stack[group * here + index, NSTATE:] = run_k[:, part]

    @pl.when((block == blocks - 1) & (group == groups - 1))
    def _():
        for offset in range(pieces):
            msgs[offset][...] = stack[me[0] ^ offset]


def states_call(me, features, write_proj, step_size, log_decay, starts, pieces):
    tokens, channels = features.shape
    heads = step_size.shape[0]
    groups = write_proj.shape[1] // NSTATE
    blocks = tokens // SPAN
    per_group, gch = heads // groups, channels // groups
    width = channels // pieces
    last = blocks - 2

    def kernel(*refs):
        states_kernel(
            *refs, per_group=per_group, blocks=blocks, groups=groups, pieces=pieces, width=width
        )

    outs = pl.pallas_call(
        kernel,
        grid_spec=pltpu.PrefetchScalarGridSpec(
            num_scalar_prefetch=1,
            grid=(groups, blocks),
            in_specs=[
                pl.BlockSpec((SPAN, gch), lambda g, b, m: (b, g)),
                pl.BlockSpec((SPAN, NSTATE), lambda g, b, m: (b, g)),
                pl.BlockSpec((per_group, SPAN), lambda g, b, m: (g, b)),
                pl.BlockSpec((per_group, SPAN), lambda g, b, m: (g, b)),
                pl.BlockSpec((1, SPAN), lambda g, b, m: (0, b)),
            ],
            out_specs=[pl.BlockSpec((NSTATE + KROWS, width), lambda g, b, m: (0, 0))] * pieces
            + [
                pl.BlockSpec((1, NSTATE, gch), lambda g, b, m: (jnp.minimum(b, last), 0, g)),
                pl.BlockSpec((1, KROWS, gch), lambda g, b, m: (jnp.minimum(b, last), 0, g)),
                pl.BlockSpec((per_group, SPAN), lambda g, b, m: (g, b)),
                pl.BlockSpec((8, SPAN), lambda g, b, m: (0, b)),
                pl.BlockSpec((1, SPAN, 128), lambda g, b, m: (g, b, 0)),
            ],
            scratch_shapes=[
                pltpu.VMEM((pieces, NSTATE + KROWS, width), F32),
                pltpu.VMEM((NSTATE, gch), F32),
                pltpu.VMEM((KROWS, gch), F32),
            ],
        ),
        out_shape=[jax.ShapeDtypeStruct((NSTATE + KROWS, width), F32)] * pieces
        + [
            jax.ShapeDtypeStruct((blocks - 1, NSTATE, channels), F32),
            jax.ShapeDtypeStruct((blocks - 1, KROWS, channels), F32),
            jax.ShapeDtypeStruct((heads, tokens), F32),
            jax.ShapeDtypeStruct((8, tokens), F32),
            jax.ShapeDtypeStruct((groups, tokens, 128), F32),
        ],
        compiler_params=pltpu.CompilerParams(vmem_limit_bytes=VMEM),
        name="states",
    )(me, features, write_proj, step_size, log_decay, starts.reshape(1, tokens))
    return outs[:pieces], outs[pieces:]


def intra_kernel(feat, write, read, vrow, segrow, cols, skip, out, *, per_group):
    half = SPAN // 2
    x = feat[...]
    scores = dot(read[...], write[...], ((1,), (1,)))
    row = lax.broadcasted_iota(jnp.int32, (SPAN, SPAN), 0)
    col = lax.broadcasted_iota(jnp.int32, (SPAN, SPAN), 1)
    seg_i = cols[0, :, 2 * per_group : 2 * per_group + 1]
    together = (seg_i == segrow[0:1]) & (row >= col)
    scores = jnp.where(together, scores, 0.0)
    lane = lax.broadcasted_iota(jnp.int32, (SPAN, 2 * HEAD_DIM), 1)
    for pair in range(per_group // 2):
        part = slice(pair * 2 * HEAD_DIM, (pair + 1) * 2 * HEAD_DIM)
        xp = x[:, part]
        top = skip[:, part] * xp[:half].astype(F32)
        low = skip[:, part] * xp[half:].astype(F32)
        for which in range(2):
            head = 2 * pair + which
            mine = (lane >= HEAD_DIM) if which else (lane < HEAD_DIM)
            xh = jnp.where(mine, xp, jnp.zeros_like(xp))
            ci = cols[0, :, head : head + 1]
            vj = vrow[head : head + 1, :]
            w_top = jnp.exp2(jnp.minimum(ci[:half] - vj[:, :half], 1.0)) * scores[:half, :half]
            w_low = jnp.exp2(jnp.minimum(ci[half:] - vj, 1.0)) * scores[half:]
            top = top + dot(w_top.astype(BF16), xh[:half])
            low = low + dot(w_low.astype(BF16), xh)
        out[:half, part] = top
        out[half:, part] = low


def intra_call(group, features, write_proj, read_proj, vrow, segrow, cols, skip_row):
    tokens, channels = features.shape
    groups = write_proj.shape[1] // NSTATE
    per_group, gch = vrow.shape[0] // groups, channels // groups
    blocks = tokens // SPAN

    def kernel(*refs):
        intra_kernel(*refs, per_group=per_group)

    return pl.pallas_call(
        kernel,
        grid=(blocks,),
        in_specs=[
            pl.BlockSpec((SPAN, gch), lambda b: (b, group)),
            pl.BlockSpec((SPAN, NSTATE), lambda b: (b, group)),
            pl.BlockSpec((SPAN, NSTATE), lambda b: (b, group)),
            pl.BlockSpec((per_group, SPAN), lambda b: (group, b)),
            pl.BlockSpec((8, SPAN), lambda b: (0, b)),
            pl.BlockSpec((1, SPAN, 128), lambda b: (group, b, 0)),
            pl.BlockSpec((1, gch), lambda b: (0, group)),
        ],
        out_specs=pl.BlockSpec((SPAN, gch), lambda b: (b, 0)),
        out_shape=jax.ShapeDtypeStruct((tokens, gch), F32),
        compiler_params=pltpu.CompilerParams(vmem_limit_bytes=VMEM),
        cost_estimate=pl.CostEstimate(
            flops=8 * 10**9, bytes_accessed=tokens * gch * 6, transcendentals=0
        ),
        name="intra",
    )(features, write_proj, read_proj, vrow, segrow, cols, skip_row)


def prefix_kernel(me, *refs, pieces):
    ins, outs, stack = refs[:pieces], refs[pieces : 2 * pieces], refs[2 * pieces]
    for offset in range(pieces):
        stack[me[0] ^ offset] = ins[offset][...]
    entry = jnp.zeros(outs[0].shape, F32)
    for device in range(pieces):
        state, keep = stack[device, :NSTATE], stack[device, NSTATE : NSTATE + 1]
        stack[device, :NSTATE] = entry
        entry = keep * entry + state
    for offset in range(pieces):
        outs[offset][...] = stack[me[0] ^ offset, :NSTATE]


def prefix_call(me, parts):
    pieces, width = len(parts), parts[0].shape[1]

    def kernel(*refs):
        prefix_kernel(*refs, pieces=pieces)

    return pl.pallas_call(
        kernel,
        grid_spec=pltpu.PrefetchScalarGridSpec(
            num_scalar_prefetch=1,
            grid=(1,),
            in_specs=[pl.BlockSpec((NSTATE + KROWS, width), lambda i, m: (0, 0))] * pieces,
            out_specs=[pl.BlockSpec((NSTATE, width), lambda i, m: (0, 0))] * pieces,
            scratch_shapes=[pltpu.VMEM((pieces, NSTATE + KROWS, width), F32)],
        ),
        out_shape=[jax.ShapeDtypeStruct((NSTATE, width), F32)] * pieces,
        compiler_params=pltpu.CompilerParams(vmem_limit_bytes=VMEM),
        name="prefix",
    )(me, *parts)


def exchange(parts, axis):
    count = len(parts)
    return [parts[0]] + [
        lax.ppermute(parts[offset], axis, [(i, i ^ offset) for i in range(count)])
        for offset in range(1, count)
    ]


def relay(parts, axis):
    count = lax.axis_size(axis)
    total = parts[0][:NSTATE]
    keep = parts[0][NSTATE : NSTATE + 1]
    steps = [(i, i + 1) for i in range(count - 1)]

    def step(index, incoming):
        return lax.ppermute(keep * incoming + total, axis, steps)

    return [lax.fori_loop(0, count - 1, step, jnp.zeros_like(total))]


def normed_kernel(me, order, *refs, pieces, groups, rows, per_group):
    entries = refs[:pieces]
    pre_s, pre_k = refs[pieces : pieces + 2]
    inner = refs[pieces + 2 : pieces + 2 + groups]
    gate, read, cols, gain, out, held = refs[pieces + 2 + groups :]
    width = entries[0].shape[1]
    blocks = held.shape[0]

    @pl.when(pl.program_id(0) == 0)
    def _():
        for offset in range(pieces):
            piece = me[0] ^ offset
            entry = entries[offset][...]
            held[0, piece] = entry.astype(BF16)
            part = pl.ds(pl.multiple_of(piece * width, 128), width)
            for block in range(1, blocks):
                held[block, piece] = (
                    pre_k[block - 1, 0:1, part] * entry + pre_s[block - 1, :, part]
                ).astype(BF16)

    chunk = order[pl.program_id(0)]
    block = lax.div(chunk * rows, SPAN)
    gch = inner[0].shape[1]
    here = pieces // groups if pieces >= groups else 0
    spread = head_spread(per_group, gch)
    for group in range(groups):
        part = slice(group * gch, (group + 1) * gch)
        c_rows = read[:, group * NSTATE : (group + 1) * NSTATE]
        reach = dot(three_parts(cols[group, :, per_group : 2 * per_group], 1), spread)
        if here:
            carried = jnp.concatenate(
                [dot(c_rows, held[block, group * here + k]) for k in range(here)], axis=1
            )
        else:
            carried = dot(c_rows, held[block, 0, :, part])
        y = inner[group][...] + reach * carried
        g = gate[:, part].astype(F32)
        gated = y * (g / (1.0 + jnp.exp(-g)))
        mean_square = jnp.mean(gated * gated, axis=1, keepdims=True)
        out[0, :, part] = (gated * lax.rsqrt(mean_square + eps) * gain[:, part]).astype(BF16)


def normed_call(me, order, entries, pre_s, pre_k, inner, gate_values, read_proj, cols, gain):
    tokens, channels = gate_values.shape
    groups, pieces, width = len(inner), len(entries), entries[0].shape[1]
    count = order.shape[0]
    rows = tokens // count
    blocks = tokens // SPAN
    per_group = channels // groups // HEAD_DIM

    def kernel(*refs):
        normed_kernel(*refs, pieces=pieces, groups=groups, rows=rows, per_group=per_group)

    def whole(value):
        zeros = (0,) * value.ndim
        return pl.BlockSpec(value.shape, lambda j, m, o: zeros)

    def chunk(columns):
        return pl.BlockSpec((rows, columns), lambda j, m, o: (o[j], 0))

    return pl.pallas_call(
        kernel,
        grid_spec=pltpu.PrefetchScalarGridSpec(
            num_scalar_prefetch=2,
            grid=(count,),
            in_specs=[whole(e) for e in entries]
            + [whole(pre_s), whole(pre_k)]
            + [chunk(channels // groups)] * groups
            + [
                chunk(channels),
                chunk(groups * NSTATE),
                pl.BlockSpec((groups, rows, 128), lambda j, m, o: (0, o[j], 0)),
                whole(gain),
            ],
            out_specs=pl.BlockSpec((1, rows, channels), lambda j, m, o: (j, 0, 0)),
            scratch_shapes=[pltpu.VMEM((blocks, pieces, NSTATE, width), BF16)],
        ),
        out_shape=jax.ShapeDtypeStruct((count, rows, channels), BF16),
        compiler_params=pltpu.CompilerParams(vmem_limit_bytes=VMEM),
        name="normed",
    )(me, order, *entries, pre_s, pre_k, *inner, gate_values, read_proj, cols, gain)


def project_call(normed, out_weight, chunks, first, columns):
    _, rows, channels = normed.shape
    tile = min(512, columns)
    start = first // tile

    def kernel(a, w, out):
        out[...] = dot(a[...].reshape(chunks * rows, channels), w[...]).reshape(out.shape)

    return pl.pallas_call(
        kernel,
        grid=(columns // tile,),
        in_specs=[
            pl.BlockSpec((chunks, rows, channels), lambda j: (0, 0, 0)),
            pl.BlockSpec((channels, tile), lambda j: (0, start + j)),
        ],
        out_specs=pl.BlockSpec((chunks, rows, tile), lambda j: (0, 0, j)),
        out_shape=jax.ShapeDtypeStruct((chunks, rows, columns), F32),
        compiler_params=pltpu.CompilerParams(vmem_limit_bytes=VMEM),
        cost_estimate=pl.CostEstimate(
            flops=2 * chunks * rows * channels * columns,
            bytes_accessed=2 * channels * columns + 4 * chunks * rows * columns,
            transcendentals=0,
        ),
        name="project",
    )(normed, out_weight)


def line_tables(count):
    order, up, down = [], np.zeros((count, count), np.int32), np.zeros((count, count), np.int32)
    for me in range(count):
        def step(c):
            return count - c + me if c > me else (count + c - me if c < me else 10 * count)

        order.append(sorted(range(count), key=lambda c: (step(c), abs(c - me))))
        for s in range(1, count):
            if me < count - 1 and s > me:
                up[me, s] = order[me].index(count - s + me)
            if me > 0 and s > count - 1 - me:
                down[me, s] = order[me].index(s - count + me)
    return np.array(order, np.int32), up, down


def add_call(sel, mine, up, down, piece, final):
    count, rows, columns = mine.shape
    width = up.shape[1]
    tile = min(1024, width)
    tiles = width // tile
    moving = pl.BlockSpec((rows, tile), lambda j, s: (0, j))

    def own(place):
        return pl.BlockSpec((1, rows, tile), lambda j, s: (place(s), 0, piece * tiles + j))

    if final:
        def kernel(sel, a, c, d, out):
            out[...] = (a[0] + c[...] + d[...]).astype(BF16)

        return pl.pallas_call(
            kernel,
            grid_spec=pltpu.PrefetchScalarGridSpec(
                num_scalar_prefetch=1,
                grid=(tiles,),
                in_specs=[own(lambda s: count - 1), moving, moving],
                out_specs=moving,
            ),
            out_shape=jax.ShapeDtypeStruct((rows, width), BF16),
            name="last_sum",
        )(sel, mine, up, down)

    def kernel(sel, a, b, c, d, out_up, out_down):
        out_up[...] = a[0] + c[...]
        out_down[...] = b[0] + d[...]

    return pl.pallas_call(
        kernel,
        grid_spec=pltpu.PrefetchScalarGridSpec(
            num_scalar_prefetch=1,
            grid=(tiles,),
            in_specs=[own(lambda s: s[0]), own(lambda s: s[1]), moving, moving],
            out_specs=[moving, moving],
        ),
        out_shape=[jax.ShapeDtypeStruct((rows, width), F32)] * 2,
        cost_estimate=pl.CostEstimate(
            flops=10**10, bytes_accessed=24 * rows * width, transcendentals=0
        ),
        name="sum",
    )(sel, mine, mine, up, down)


def line_sum(first, mine, up_table, down_table, axis):
    count, me = lax.axis_size(axis), lax.axis_index(axis)
    ups, downs = jnp.asarray(up_table)[me], jnp.asarray(down_table)[me]
    pieces = len(first)
    up, down = [None] * pieces, [None] * pieces
    for s in range(1, count):
        sel = jnp.stack([ups[s], downs[s]])
        for p in range(pieces):
            if s == 1:
                to_up = to_down = first[p]
            else:
                to_up, to_down = add_call(sel, mine, up[p], down[p], p, False)
            up[p] = lax.ppermute(to_up, axis, [(i, i + 1) for i in range(count - 1) if s > i])
            down[p] = lax.ppermute(
                to_down, axis, [(i, i - 1) for i in range(1, count) if s > count - 1 - i]
            )
    sel = jnp.stack([ups[0], downs[0]])
    return jnp.concatenate(
        [add_call(sel, mine, up[p], down[p], p, True) for p in range(pieces)], axis=1
    )


def body(
    features,
    gate_values,
    write_proj,
    read_proj,
    step_size,
    log_decay,
    starts,
    skip_weight,
    norm_gain,
    out_weight,
):
    channels = features.shape[1]
    groups = write_proj.shape[1] // NSTATE
    count = lax.axis_size("ctx")
    direct = channels % (128 * count) == 0 and count & (count - 1) == 0 and count % groups == 0
    me = lax.axis_index("ctx").astype(jnp.int32).reshape(1) if direct else jnp.zeros((1,), jnp.int32)
    msgs, (pre_s, pre_k, vrow, segrow, cols) = states_call(
        me, features, write_proj, step_size, log_decay, starts, count if direct else groups
    )
    if direct:
        entries = exchange(prefix_call(me, exchange(msgs, "ctx")), "ctx")
    else:
        entries = [relay([m], "ctx")[0] for m in msgs]
    skip_row = jnp.repeat(skip_weight, HEAD_DIM).reshape(1, channels)
    inner = [
        intra_call(g, features, write_proj, read_proj, vrow, segrow, cols, skip_row)
        for g in range(groups)
    ]
    order, up_table, down_table = line_tables(lax.axis_size("head"))
    normed = normed_call(
        me,
        jnp.asarray(order)[lax.axis_index("head")],
        entries,
        pre_s,
        pre_k,
        inner,
        gate_values,
        read_proj,
        cols,
        norm_gain.reshape(1, channels),
    )
    wide = out_weight.shape[1]
    pieces = 4
    first = [
        project_call(normed, out_weight, 1, p * wide // pieces, wide // pieces)[0]
        for p in range(pieces)
    ]
    mine = project_call(normed, out_weight, order.shape[0], 0, wide)
    return line_sum(first, mine, up_table, down_table, "head")


def solution(mesh):
    placed = (
        P("ctx", "head"),
        P("ctx", "head"),
        P("ctx", "head"),
        P("ctx", "head"),
        P("head", "ctx"),
        P("head", "ctx"),
        P("ctx"),
        P("head"),
        P("head"),
        P("head", None),
    )
    return jax.shard_map(
        body, mesh=mesh, in_specs=placed, out_specs=P(("ctx", "head"), None), check_vma=False
    )
```

time: 370 us -> 226 us (0.61)
  waiting for transfers between devices: 180 us -> 39.3 us
  Pallas kernels: 0 us -> 80.4 us
  matrix products: 28.4 us -> 0 us
  local copies, waits for them, and re-layouts: 41 us -> 24.9 us
  starting transfers between devices: 84.5 us -> 71.3 us
  between operations: 13.7 us -> 0.5 us
  other arithmetic: 20.6 us -> 7.44 us
    reduce_scatter x1 -> x0, waiting for transfers between devices: 165 us -> none  [body(): lax.psum_scatter(jnp.dot(normed, out_weight, preferred_element_type=jnp.f...]
    pallas_call x0 -> x22, Pallas kernels: none -> 80.4 us  [the longest x12 37.1 us: add_call(): pl.pallas_call(kernel, grid_spec=pltpu.PrefetchScalarGridSpec(num_scalar_...]
    dot_general x5 -> x0, matrix products: 28.4 us -> none  [the longest x1 14.5 us: body(): jnp.dot(normed, out_weight, preferred_element_type=jnp.float32)]
    ppermute x7 -> x38, waiting for transfers between devices: 15.4 us -> 39.3 us  [the longest x12 27.7 us: line_sum(): lax.ppermute(to_down, axis, [(i, i - 1) for i in range(1, count) if s > c...]
    unnamed x30 -> x94, local copies, waits for them, and re-layouts: 5.4 us -> 20.8 us
    ppermute x7 -> x38, starting transfers between devices: 84.5 us -> 71.3 us  [the longest x12 40.8 us: line_sum(): lax.ppermute(to_down, axis, [(i, i - 1) for i in range(1, count) if s > c...]
    reshape x4 -> x0, local copies, waits for them, and re-layouts: 11.3 us -> none  [the longest x2 11.2 us: body(): feat_blocks = features.reshape(blocks, SPAN, heads_dev, HEAD_DIM)]
    convert_element_type x2 -> x0, local copies, waits for them, and re-layouts: 10.1 us -> none  [body(): feat_blocks.astype(jnp.float32)]
  transfers between devices with their start and end apart: 8 -> 38, of which waited for: 8 -> 13; matrix products, arithmetic and copies ran while one was open for 0% -> 4% of each run, Pallas kernels for 0% -> 28%
where the time goes in v1:
time: 226 us; the launch traced here: 224 us
  Pallas kernels  80.4 us (36%)
  starting transfers between devices  71.3 us (32%)
  waiting for transfers between devices  39.3 us (17%)
  local copies, waits for them, and re-layouts  24.9 us (11%)
  other arithmetic  7.44 us (3%)
    ppermute x12, starting transfers between devices, line_sum(): lax.ppermute(to_down, axis, [(i, i - 1) for i in range(1, count) if s > c...  40.8 us
    pallas_call x12, Pallas kernels, add_call(): pl.pallas_call(kernel, grid_spec=pltpu.PrefetchScalarGridSpec(num_scalar_...  37.1 us
    ppermute x12, waiting for transfers between devices, line_sum(): lax.ppermute(to_down, axis, [(i, i - 1) for i in range(1, count) if s > c...  27.7 us
    pallas_call x5, Pallas kernels, project_call(): pl.pallas_call(kernel, grid=(columns // tile,), in_specs=[pl.BlockSpec((c...  26.3 us
    unnamed x94, local copies, waits for them, and re-layouts  20.8 us
    ppermute x12, starting transfers between devices, line_sum(): lax.ppermute(to_up, axis, [(i, i + 1) for i in range(count - 1) if s > i])  16.2 us
    ppermute x14, starting transfers between devices, exchange(): lax.ppermute(parts[offset], axis, [(i, i ^ offset) for i in range(count)])  14.4 us
    ppermute x14, waiting for transfers between devices, exchange(): lax.ppermute(parts[offset], axis, [(i, i ^ offset) for i in range(count)])  11.6 us
  transfers between devices with their start and end apart: 38, of which 13 were waited for; matrix products, arithmetic and copies ran while one was open for 4% of the time, Pallas kernels for 28%

profile of v1, /device:TPU:16, one launch (start us, length us, event | category | flops | bytes accessed | tf_op | source)
XLA Modules:
  0.0 223.8 jit_solution(6568376588363959350)
XLA Ops:
  4.9 4.9 %states.1 = (f32[136,256]{1,0:T(8,128)S(1)}, f32[136,256]{1,0:T(8,128)}, f32[136,256]{1,0:T(8,128)}, f32[136,256]{1,0:T(8,128)}, f32[136,256]{1,0:T(8,128)}, /*i...) custom-call(s32[1]{0:T(128)} %bitcast.2.refs_0_, ...), custom_call_target="tpu_custom_call" | custom-call | tf_op jit(solution)/shard_map/states/pallas_call | solution.py:115
  22.3 2.3 %intra.3.refs_13_ = f32[512,1024]{1,0:T(8,128)S(1)} custom-call(bf16[512,2048]{1,0:T(8,128)(2,1)S(1)} %copy-done.3, bf16[512,256]{1,0:T(8,128)(2,1)S(1)} %copy-done.8, bf16[512,256]{1,0:T(8,128)(2,1)S(1)} %copy-done.9, f32[32,512]{1,0:T(8,128)S(1)} %copy-done.22, f32[8,512]{1,0:T(8,128)S(1)} %copy-done.24, f32[2,512,128]{2,1,0:T(8,128)S(1)} %copy-done.5, ...), custom_call_target="tpu_custom_call" | custom-call | flops 8000000000 | bytes 3145728 | tf_op jit(solution)/shard_map/intra/pallas_call | solution.py:193
  27.2 2.3 %intra.2.refs_12_ = f32[512,1024]{1,0:T(8,128)S(1)} custom-call(bf16[512,2048]{1,0:T(8,128)(2,1)S(1)} %copy-done.3, bf16[512,256]{1,0:T(8,128)(2,1)S(1)} %copy-done.8, bf16[512,256]{1,0:T(8,128)(2,1)S(1)} %copy-done.9, f32[32,512]{1,0:T(8,128)S(1)} %copy-done.22, f32[8,512]{1,0:T(8,128)S(1)} %copy-done.24, f32[2,512,128]{2,1,0:T(8,128)S(1)} %copy-done.5, ...), custom_call_target="tpu_custom_call" | custom-call | flops 8000000000 | bytes 3145728 | tf_op jit(solution)/shard_map/intra/pallas_call | solution.py:193
  30.8 2.4 %collective-permute-start.5 = (f32[136,256]{1,0:T(8,128)}, f32[136,256]{1,0:T(8,128)S(1)}, u32[]{:S(2)}, u32[]{:S(2)}) collective-permute-start(f32[136,256]{1,0:T(8,128)} %copy-done.20), channel_id=1, source_target_pairs={{0,24},{4,28},{8,16},{12,20},{16,8},{20,12},{24,0},{28,4},{1,25},{... | collective-permute-start | bytes 417800 | tf_op jit(solution)/shard_map/ppermute | solution.py:252
  34.9 3.5 %collective-permute-done.5.refs_7_ = f32[136,256]{1,0:T(8,128)S(1)} collective-permute-done((f32[136,256]{1,0:T(8,128)}, f32[136,256]{1,0:T(8,128)S(1)}, u32[]{:S(2)}, u32[]{:S(2)}) %collective-permute-start.5) | collective-permute-done | bytes 139296 | tf_op jit(solution)/shard_map/ppermute | solution.py:252
  38.4 2.2 collective-permute-done.6.refs_8_
  45.0 2.4 %collective-permute-start.12 = (f32[128,256]{1,0:T(8,128)S(1)}, f32[128,256]{1,0:T(8,128)S(1)}, u32[]{:S(2)}, u32[]{:S(2)}) collective-permute-start(f32[128,256]{1,0:T(8,128)S(1)} %get-tuple-element.56), channel_id=1, source_target_pairs={{0,24},{4,28},{8,16},{12,20},{16,8},{20,12},{24,0},{28,4},{1,25},{... | collective-permute-start | bytes 393224 | tf_op jit(solution)/shard_map/ppermute | solution.py:252
  49.9 5.5 %collective-permute-done.11.refs_7_ = f32[128,256]{1,0:T(8,128)S(1)} collective-permute-done((f32[128,256]{1,0:T(8,128)S(1)}, f32[128,256]{1,0:T(8,128)S(1)}, u32[]{:S(2)}, u32[]{:S(2)}) %collective-permute-start.11) | collective-permute-done | bytes 131104 | tf_op jit(solution)/shard_map/ppermute | solution.py:252
  55.4 1.9 collective-permute-start.9
  63.9 6.1 %normed.1.a = bf16[4,128,2048]{2,1,0:T(8,128)(2,1)S(1)} custom-call(s32[1]{0:T(128)} %bitcast.2.refs_0_, s32[4]{0:T(128)S(1)} %fusion.refs_1_, f32[128,256]{1,0:T(8,128)S(1)} %get-tuple-element.50.refs_2_, f32[128,256]{1,0:T(8,128)S(1)} %collective-permute-done.7.refs_3_, f32[128,256]{1,0:T(8,128)S(1)} %collective-permute-done.8.refs_4_, ...), custom_call_target="tpu_custom_call" | custom-call | tf_op jit(solution)/shard_map/normed/pallas_call | solution.py:329
  70.0 2.8 %project.6 = f32[1,128,1024]{2,1,0:T(8,128)S(1)} custom-call(bf16[4,128,2048]{2,1,0:T(8,128)(2,1)S(1)} %normed.1.a, bf16[2048,4096]{1,0:T(8,128)(2,1)} %w.9), custom_call_target="tpu_custom_call" | custom-call | flops 536870912 | bytes 4718592 | tf_op jit(solution)/shard_map/project/pallas_call | solution.py:360
  74.7 2.8 %project.7 = f32[1,128,1024]{2,1,0:T(8,128)S(1)} custom-call(bf16[4,128,2048]{2,1,0:T(8,128)(2,1)S(1)} %normed.1.a, bf16[2048,4096]{1,0:T(8,128)(2,1)} %w.9), custom_call_target="tpu_custom_call" | custom-call | flops 536870912 | bytes 4718592 | tf_op jit(solution)/shard_map/project/pallas_call | solution.py:360
  79.5 2.8 %project.8 = f32[1,128,1024]{2,1,0:T(8,128)S(1)} custom-call(bf16[4,128,2048]{2,1,0:T(8,128)(2,1)S(1)} %normed.1.a, bf16[2048,4096]{1,0:T(8,128)(2,1)} %w.9), custom_call_target="tpu_custom_call" | custom-call | flops 536870912 | bytes 4718592 | tf_op jit(solution)/shard_map/project/pallas_call | solution.py:360
  82.3 2.8 %project.9 = f32[1,128,1024]{2,1,0:T(8,128)S(1)} custom-call(bf16[4,128,2048]{2,1,0:T(8,128)(2,1)S(1)} %normed.1.a, bf16[2048,4096]{1,0:T(8,128)(2,1)} %w.9), custom_call_target="tpu_custom_call" | custom-call | flops 536870912 | bytes 4718592 | tf_op jit(solution)/shard_map/project/pallas_call | solution.py:360
  85.8 15.3 %project.5.a.b = f32[4,128,4096]{2,1,0:T(8,128)} custom-call(bf16[4,128,2048]{2,1,0:T(8,128)(2,1)S(1)} %normed.1.a, bf16[2048,4096]{1,0:T(8,128)(2,1)} %w.9), custom_call_target="tpu_custom_call" | custom-call | flops 8589934592 | bytes 25165824 | tf_op jit(solution)/shard_map/project/pallas_call | solution.py:360
  103.8 3.2 %sum.8 = (f32[128,1024]{1,0:T(8,128)}, f32[128,1024]{1,0:T(8,128)}) custom-call(s32[2]{0:T(128)} %pad_add_fusion.2.sel, f32[4,128,4096]{2,1,0:T(8,128)} %project.5.a.b, f32[4,128,4096]{2,1,0:T(8,128)} %project.5.a.b, f32[128,1024]{1,0:T(8,128)} %copy-done.45, f32[128,1024]{1,0:T(8,128)} %copy-done.46), custom_call_target="tpu_custom_call" | custom-call | flops 10000000000 | bytes 3145728 | tf_op jit(solution)/shard_map/sum/pallas_call | solution.py:424
  109.8 3.3 %sum.10 = (f32[128,1024]{1,0:T(8,128)}, f32[128,1024]{1,0:T(8,128)}) custom-call(s32[2]{0:T(128)} %pad_add_fusion.2.sel, f32[4,128,4096]{2,1,0:T(8,128)} %project.5.a.b, f32[4,128,4096]{2,1,0:T(8,128)} %project.5.a.b, f32[128,1024]{1,0:T(8,128)} %copy-done.44, f32[128,1024]{1,0:T(8,128)} %collective-permute-done.21.d), custom_call_target="tpu_custom_call" | custom-call | flops 10000000000 | bytes 3145728 | tf_op jit(solution)/shard_map/sum/pallas_call | solution.py:424
  113.2 5.3 %collective-permute-start.17 = (f32[128,1024]{1,0:T(8,128)S(1)}, f32[128,1024]{1,0:T(8,128)}, u32[]{:S(2)}, u32[]{:S(2)}) collective-permute-start(f32[128,1024]{1,0:T(8,128)S(1)} %copy-done.39), channel_id=1, source_target_pairs={{2,1},{3,2},{6,5},{7,6},{10,9},{11,10},{14,13},{15,14},{18,17},{19... | collective-permute-start | bytes 1572872 | tf_op jit(solution)/shard_map/ppermute | solution.py:453
  120.1 3.2 %sum.12 = (f32[128,1024]{1,0:T(8,128)}, f32[128,1024]{1,0:T(8,128)}) custom-call(s32[2]{0:T(128)} %pad_add_fusion.2.sel, f32[4,128,4096]{2,1,0:T(8,128)} %project.5.a.b, f32[4,128,4096]{2,1,0:T(8,128)} %project.5.a.b, f32[128,1024]{1,0:T(8,128)} %copy-done.43, f32[128,1024]{1,0:T(8,128)} %collective-permute-done.27.d), custom_call_target="tpu_custom_call" | custom-call | flops 10000000000 | bytes 3145728 | tf_op jit(solution)/shard_map/sum/pallas_call | solution.py:424
  123.3 4.6 %collective-permute-start.23 = (f32[128,1024]{1,0:T(8,128)S(1)}, f32[128,1024]{1,0:T(8,128)}, u32[]{:S(2)}, u32[]{:S(2)}) collective-permute-start(f32[128,1024]{1,0:T(8,128)S(1)} %copy-done.38), channel_id=1, source_target_pairs={{2,1},{3,2},{6,5},{7,6},{10,9},{11,10},{14,13},{15,14},{18,17},{19... | collective-permute-start | bytes 1572872 | tf_op jit(solution)/shard_map/ppermute | solution.py:453
  127.9 2.0 collective-permute-done.33.d
  131.3 3.2 %sum.14 = (f32[128,1024]{1,0:T(8,128)}, f32[128,1024]{1,0:T(8,128)}) custom-call(s32[2]{0:T(128)} %pad_add_fusion.2.sel, f32[4,128,4096]{2,1,0:T(8,128)} %project.5.a.b, f32[4,128,4096]{2,1,0:T(8,128)} %project.5.a.b, f32[128,1024]{1,0:T(8,128)} %copy-done.42, f32[128,1024]{1,0:T(8,128)} %collective-permute-done.33.d), custom_call_target="tpu_custom_call" | custom-call | flops 10000000000 | bytes 3145728 | tf_op jit(solution)/shard_map/sum/pallas_call | solution.py:424
  134.6 4.5 %collective-permute-start.29 = (f32[128,1024]{1,0:T(8,128)S(1)}, f32[128,1024]{1,0:T(8,128)}, u32[]{:S(2)}, u32[]{:S(2)}) collective-permute-start(f32[128,1024]{1,0:T(8,128)S(1)} %copy-done.37), channel_id=1, source_target_pairs={{2,1},{3,2},{6,5},{7,6},{10,9},{11,10},{14,13},{15,14},{18,17},{19... | collective-permute-start | bytes 1572872 | tf_op jit(solution)/shard_map/ppermute | solution.py:453
  139.1 2.0 collective-permute-done.17.d
  142.5 3.2 %sum.9 = (f32[128,1024]{1,0:T(8,128)}, f32[128,1024]{1,0:T(8,128)}) custom-call(s32[2]{0:T(128)} %pad_add_fusion.1.sel, f32[4,128,4096]{2,1,0:T(8,128)} %project.5.a.b, f32[4,128,4096]{2,1,0:T(8,128)} %project.5.a.b, f32[128,1024]{1,0:T(8,128)} %collective-permute-done.16.c, f32[128,1024]{1,0:T(8,128)} %collective-permute-done.17.d), custom_call_target="tpu_custom_call" | custom-call | flops 10000000000 | bytes 3145728 | tf_op jit(solution)/shard_map/sum/pallas_call | solution.py:424
  145.8 4.6 %collective-permute-start.35 = (f32[128,1024]{1,0:T(8,128)S(1)}, f32[128,1024]{1,0:T(8,128)}, u32[]{:S(2)}, u32[]{:S(2)}) collective-permute-start(f32[128,1024]{1,0:T(8,128)S(1)} %copy-done.35), channel_id=1, source_target_pairs={{2,1},{3,2},{6,5},{7,6},{10,9},{11,10},{14,13},{15,14},{18,17},{19... | collective-permute-start | bytes 1572872 | tf_op jit(solution)/shard_map/ppermute | solution.py:453
  150.4 2.0 collective-permute-done.23.d
  152.4 2.0 collective-permute-start.18
  154.4 3.2 %sum.11 = (f32[128,1024]{1,0:T(8,128)}, f32[128,1024]{1,0:T(8,128)}) custom-call(s32[2]{0:T(128)} %pad_add_fusion.1.sel, f32[4,128,4096]{2,1,0:T(8,128)} %project.5.a.b, f32[4,128,4096]{2,1,0:T(8,128)} %project.5.a.b, f32[128,1024]{1,0:T(8,128)} %copy-done.41, f32[128,1024]{1,0:T(8,128)} %collective-permute-done.23.d), custom_call_target="tpu_custom_call" | custom-call | flops 10000000000 | bytes 3145728 | tf_op jit(solution)/shard_map/sum/pallas_call | solution.py:424
  157.6 3.9 %collective-permute-start.19 = (f32[128,1024]{1,0:T(8,128)S(1)}, f32[128,1024]{1,0:T(8,128)S(1)}, u32[]{:S(2)}, u32[]{:S(2)}) collective-permute-start(f32[128,1024]{1,0:T(8,128)S(1)} %copy-done.36), channel_id=1, source_target_pairs={{1,0},{2,1},{3,2},{5,4},{6,5},{7,6},{9,8},{10,9},{11,10},{13,12},{... | collective-permute-start | bytes 1572872 | tf_op jit(solution)/shard_map/ppermute | solution.py:453
  161.5 2.0 collective-permute-done.29.d
  163.6 1.9 collective-permute-start.24
  165.5 3.2 %sum.13 = (f32[128,1024]{1,0:T(8,128)}, f32[128,1024]{1,0:T(8,128)}) custom-call(s32[2]{0:T(128)} %pad_add_fusion.1.sel, f32[4,128,4096]{2,1,0:T(8,128)} %project.5.a.b, f32[4,128,4096]{2,1,0:T(8,128)} %project.5.a.b, f32[128,1024]{1,0:T(8,128)} %copy-done.40, f32[128,1024]{1,0:T(8,128)} %collective-permute-done.29.d), custom_call_target="tpu_custom_call" | custom-call | flops 10000000000 | bytes 3145728 | tf_op jit(solution)/shard_map/sum/pallas_call | solution.py:424
  168.7 3.9 %collective-permute-start.25 = (f32[128,1024]{1,0:T(8,128)}, f32[128,1024]{1,0:T(8,128)S(1)}, u32[]{:S(2)}, u32[]{:S(2)}) collective-permute-start(f32[128,1024]{1,0:T(8,128)} %get-tuple-element.70), channel_id=1, source_target_pairs={{1,0},{2,1},{3,2},{5,4},{6,5},{7,6},{9,8},{10,9},{11,10},{13,12},{... | collective-permute-start | bytes 1572872 | tf_op jit(solution)/shard_map/ppermute | solution.py:453
  172.7 2.2 collective-permute-done.35.d
  174.8 1.9 collective-permute-start.30
  176.7 3.2 %sum.15 = (f32[128,1024]{1,0:T(8,128)}, f32[128,1024]{1,0:T(8,128)}) custom-call(s32[2]{0:T(128)} %pad_add_fusion.1.sel, f32[4,128,4096]{2,1,0:T(8,128)} %project.5.a.b, f32[4,128,4096]{2,1,0:T(8,128)} %project.5.a.b, f32[128,1024]{1,0:T(8,128)} %collective-permute-done.34.c, f32[128,1024]{1,0:T(8,128)} %collective-permute-done.35.d), custom_call_target="tpu_custom_call" | custom-call | flops 10000000000 | bytes 3145728 | tf_op jit(solution)/shard_map/sum/pallas_call | solution.py:424
  179.9 3.9 %collective-permute-start.31 = (f32[128,1024]{1,0:T(8,128)}, f32[128,1024]{1,0:T(8,128)}, u32[]{:S(2)}, u32[]{:S(2)}) collective-permute-start(f32[128,1024]{1,0:T(8,128)} %get-tuple-element.74), channel_id=1, source_target_pairs={{1,0},{2,1},{3,2},{5,4},{6,5},{7,6},{9,8},{10,9},{11,10},{13,12},{... | collective-permute-start | bytes 1572872 | tf_op jit(solution)/shard_map/ppermute | solution.py:453
  183.9 2.1 collective-permute-done.19.d
  186.0 1.9 collective-permute-start.36
  187.9 5.0 %collective-permute-start.37 = (f32[128,1024]{1,0:T(8,128)}, f32[128,1024]{1,0:T(8,128)}, u32[]{:S(2)}, u32[]{:S(2)}) collective-permute-start(f32[128,1024]{1,0:T(8,128)} %get-tuple-element.78), channel_id=1, source_target_pairs={{1,0},{2,1},{3,2},{5,4},{6,5},{7,6},{9,8},{10,9},{11,10},{13,12},{... | collective-permute-start | bytes 1572872 | tf_op jit(solution)/shard_map/ppermute | solution.py:453
  194.7 2.8 %last_sum.4 = bf16[128,1024]{1,0:T(8,128)(2,1)} custom-call(s32[2]{0:T(128)} %pad_add_fusion.sel, f32[4,128,4096]{2,1,0:T(8,128)} %project.5.a.b, f32[128,1024]{1,0:T(8,128)} %copy-done.28, f32[128,1024]{1,0:T(8,128)} %copy-done.29), custom_call_target="tpu_custom_call" | custom-call | tf_op jit(solution)/shard_map/last_sum/pallas_call | solution.py:408
  198.3 2.8 %last_sum.5 = bf16[128,1024]{1,0:T(8,128)(2,1)} custom-call(s32[2]{0:T(128)} %pad_add_fusion.sel, f32[4,128,4096]{2,1,0:T(8,128)} %project.5.a.b, f32[128,1024]{1,0:T(8,128)} %copy-done.30, f32[128,1024]{1,0:T(8,128)} %copy-done.32), custom_call_target="tpu_custom_call" | custom-call | tf_op jit(solution)/shard_map/last_sum/pallas_call | solution.py:408
  201.0 7.5 %collective-permute-done.31.d = f32[128,1024]{1,0:T(8,128)} collective-permute-done((f32[128,1024]{1,0:T(8,128)}, f32[128,1024]{1,0:T(8,128)}, u32[]{:S(2)}, u32[]{:S(2)}) %collective-permute-start.31) | collective-permute-done | bytes 524320 | tf_op jit(solution)/shard_map/ppermute | solution.py:453
  208.5 2.8 %last_sum.6 = bf16[128,1024]{1,0:T(8,128)(2,1)} custom-call(s32[2]{0:T(128)} %pad_add_fusion.sel, f32[4,128,4096]{2,1,0:T(8,128)} %project.5.a.b, f32[128,1024]{1,0:T(8,128)} %copy-done.31, f32[128,1024]{1,0:T(8,128)} %collective-permute-done.31.d), custom_call_target="tpu_custom_call" | custom-call | tf_op jit(solution)/shard_map/last_sum/pallas_call | solution.py:408
  211.4 7.6 %collective-permute-done.37.d = f32[128,1024]{1,0:T(8,128)} collective-permute-done((f32[128,1024]{1,0:T(8,128)}, f32[128,1024]{1,0:T(8,128)}, u32[]{:S(2)}, u32[]{:S(2)}) %collective-permute-start.37) | collective-permute-done | bytes 524320 | tf_op jit(solution)/shard_map/ppermute | solution.py:453
  219.0 2.8 %last_sum.7 = bf16[128,1024]{1,0:T(8,128)(2,1)} custom-call(s32[2]{0:T(128)} %pad_add_fusion.sel, f32[4,128,4096]{2,1,0:T(8,128)} %project.5.a.b, f32[128,1024]{1,0:T(8,128)} %copy-done.33, f32[128,1024]{1,0:T(8,128)} %collective-permute-done.37.d), custom_call_target="tpu_custom_call" | custom-call | tf_op jit(solution)/shard_map/last_sum/pallas_call | solution.py:408
  221.8 2.0 pad_maximum_fusion
  (154 shorter events, 53.6 us)
Async XLA Ops:
  0.0 17.3 %copy-start.34 = (f32[32]{0:T(128)S(1)}, f32[32]{0:T(128)}, u32[]{:S(2)}) copy-start(f32[32]{0:T(128)} %param.20) | copy-start | bytes 388
  4.9 13.8 %copy-start.3 = (bf16[512,2048]{1,0:T(8,128)(2,1)S(1)}, bf16[512,2048]{1,0:T(8,128)(2,1)}, u32[]{:S(2)}) copy-start(bf16[512,2048]{1,0:T(8,128)(2,1)} %refs_0_.3) | copy-start | bytes 6291460
  4.9 13.8 %copy-start.8 = (bf16[512,256]{1,0:T(8,128)(2,1)S(1)}, bf16[512,256]{1,0:T(8,128)(2,1)}, u32[]{:S(2)}) copy-start(bf16[512,256]{1,0:T(8,128)(2,1)} %refs_1_.5) | copy-start | bytes 786436
  13.8 17.0 %collective-permute-start = (f32[136,256]{1,0:T(8,128)}, f32[136,256]{1,0:T(8,128)}, u32[]{:S(2)}, u32[]{:S(2)}) collective-permute-start(f32[136,256]{1,0:T(8,128)} %get-tuple-element.43), channel_id=1, source_target_pairs={{0,4},{4,0},{8,12},{12,8},{16,20},{20,16},{24,28},{28,24},{1,5},{5... | collective-permute-start | bytes 417800 | tf_op jit(solution)/shard_map/ppermute | solution.py:252
  13.8 19.5 %collective-permute-start.1 = (f32[136,256]{1,0:T(8,128)}, f32[136,256]{1,0:T(8,128)}, u32[]{:S(2)}, u32[]{:S(2)}) collective-permute-start(f32[136,256]{1,0:T(8,128)} %get-tuple-element.44), channel_id=1, source_target_pairs={{0,8},{4,12},{8,0},{12,4},{16,24},{20,28},{24,16},{28,20},{1,9},{5... | collective-permute-start | bytes 417800 | tf_op jit(solution)/shard_map/ppermute | solution.py:252
  15.3 19.6 %collective-permute-start.2 = (f32[136,256]{1,0:T(8,128)}, f32[136,256]{1,0:T(8,128)}, u32[]{:S(2)}, u32[]{:S(2)}) collective-permute-start(f32[136,256]{1,0:T(8,128)} %get-tuple-element.45), channel_id=1, source_target_pairs={{0,12},{4,8},{8,4},{12,0},{16,28},{20,24},{24,20},{28,16},{1,13},{... | collective-permute-start | bytes 417800 | tf_op jit(solution)/shard_map/ppermute | solution.py:252
  15.7 19.3 %collective-permute-start.3 = (f32[136,256]{1,0:T(8,128)}, f32[136,256]{1,0:T(8,128)}, u32[]{:S(2)}, u32[]{:S(2)}) collective-permute-start(f32[136,256]{1,0:T(8,128)} %get-tuple-element.46), channel_id=1, source_target_pairs={{0,16},{4,20},{8,24},{12,28},{16,0},{20,4},{24,8},{28,12},{1,17},{... | collective-permute-start | bytes 417800 | tf_op jit(solution)/shard_map/ppermute | solution.py:252
  17.2 17.7 %collective-permute-start.4 = (f32[136,256]{1,0:T(8,128)}, f32[136,256]{1,0:T(8,128)}, u32[]{:S(2)}, u32[]{:S(2)}) collective-permute-start(f32[136,256]{1,0:T(8,128)} %get-tuple-element.47), channel_id=1, source_target_pairs={{0,20},{4,16},{8,28},{12,24},{16,4},{20,0},{24,12},{28,8},{1,21},{... | collective-permute-start | bytes 417800 | tf_op jit(solution)/shard_map/ppermute | solution.py:252
  27.2 33.8 %copy-start.15 = (f32[2048]{0:T(1024)S(1)}, f32[2048]{0:T(1024)}, u32[]{:S(2)}) copy-start(f32[2048]{0:T(1024)} %param.21) | copy-start | bytes 24580
  30.8 7.6 %collective-permute-start.5 = (f32[136,256]{1,0:T(8,128)}, f32[136,256]{1,0:T(8,128)S(1)}, u32[]{:S(2)}, u32[]{:S(2)}) collective-permute-start(f32[136,256]{1,0:T(8,128)} %copy-done.20), channel_id=1, source_target_pairs={{0,24},{4,28},{8,16},{12,20},{16,8},{20,12},{24,0},{28,4},{1,25},{... | collective-permute-start | bytes 417800 | tf_op jit(solution)/shard_map/ppermute | solution.py:252
  33.3 7.3 %collective-permute-start.6 = (f32[136,256]{1,0:T(8,128)}, f32[136,256]{1,0:T(8,128)S(1)}, u32[]{:S(2)}, u32[]{:S(2)}) collective-permute-start(f32[136,256]{1,0:T(8,128)} %copy-done.19), channel_id=1, source_target_pairs={{0,28},{4,24},{8,20},{12,16},{16,12},{20,8},{24,4},{28,0},{1,29},{... | collective-permute-start | bytes 417800 | tf_op jit(solution)/shard_map/ppermute | solution.py:252
  42.0 6.4 %collective-permute-start.10 = (f32[128,256]{1,0:T(8,128)S(1)}, f32[128,256]{1,0:T(8,128)S(1)}, u32[]{:S(2)}, u32[]{:S(2)}) collective-permute-start(f32[128,256]{1,0:T(8,128)S(1)} %get-tuple-element.54), channel_id=1, source_target_pairs={{0,16},{4,20},{8,24},{12,28},{16,0},{20,4},{24,8},{28,12},{1,17},{... | collective-permute-start | bytes 393224 | tf_op jit(solution)/shard_map/ppermute | solution.py:252
  43.6 11.8 %collective-permute-start.11 = (f32[128,256]{1,0:T(8,128)S(1)}, f32[128,256]{1,0:T(8,128)S(1)}, u32[]{:S(2)}, u32[]{:S(2)}) collective-permute-start(f32[128,256]{1,0:T(8,128)S(1)} %get-tuple-element.55), channel_id=1, source_target_pairs={{0,20},{4,16},{8,28},{12,24},{16,4},{20,0},{24,12},{28,8},{1,21},{... | collective-permute-start | bytes 393224 | tf_op jit(solution)/shard_map/ppermute | solution.py:252
  45.0 16.0 %collective-permute-start.12 = (f32[128,256]{1,0:T(8,128)S(1)}, f32[128,256]{1,0:T(8,128)S(1)}, u32[]{:S(2)}, u32[]{:S(2)}) collective-permute-start(f32[128,256]{1,0:T(8,128)S(1)} %get-tuple-element.56), channel_id=1, source_target_pairs={{0,24},{4,28},{8,16},{12,20},{16,8},{20,12},{24,0},{28,4},{1,25},{... | collective-permute-start | bytes 393224 | tf_op jit(solution)/shard_map/ppermute | solution.py:252
  47.4 13.6 %collective-permute-start.13 = (f32[128,256]{1,0:T(8,128)S(1)}, f32[128,256]{1,0:T(8,128)S(1)}, u32[]{:S(2)}, u32[]{:S(2)}) collective-permute-start(f32[128,256]{1,0:T(8,128)S(1)} %get-tuple-element.57), channel_id=1, source_target_pairs={{0,28},{4,24},{8,20},{12,16},{16,12},{20,8},{24,4},{28,0},{1,29},{... | collective-permute-start | bytes 393224 | tf_op jit(solution)/shard_map/ppermute | solution.py:252
  47.8 13.2 %collective-permute-start.7 = (f32[128,256]{1,0:T(8,128)S(1)}, f32[128,256]{1,0:T(8,128)S(1)}, u32[]{:S(2)}, u32[]{:S(2)}) collective-permute-start(f32[128,256]{1,0:T(8,128)S(1)} %get-tuple-element.51), channel_id=1, source_target_pairs={{0,4},{4,0},{8,12},{12,8},{16,20},{20,16},{24,28},{28,24},{1,5},{5... | collective-permute-start | bytes 393224 | tf_op jit(solution)/shard_map/ppermute | solution.py:252
  48.4 12.6 %collective-permute-start.8 = (f32[128,256]{1,0:T(8,128)S(1)}, f32[128,256]{1,0:T(8,128)S(1)}, u32[]{:S(2)}, u32[]{:S(2)}) collective-permute-start(f32[128,256]{1,0:T(8,128)S(1)} %get-tuple-element.52), channel_id=1, source_target_pairs={{0,8},{4,12},{8,0},{12,4},{16,24},{20,28},{24,16},{28,20},{1,9},{5... | collective-permute-start | bytes 393224 | tf_op jit(solution)/shard_map/ppermute | solution.py:252
  55.4 5.6 %collective-permute-start.9 = (f32[128,256]{1,0:T(8,128)S(1)}, f32[128,256]{1,0:T(8,128)S(1)}, u32[]{:S(2)}, u32[]{:S(2)}) collective-permute-start(f32[128,256]{1,0:T(8,128)S(1)} %get-tuple-element.53), channel_id=1, source_target_pairs={{0,12},{4,8},{8,4},{12,0},{16,28},{20,24},{24,20},{28,16},{1,13},{... | collective-permute-start | bytes 393224 | tf_op jit(solution)/shard_map/ppermute | solution.py:252
  72.7 28.3 %collective-permute-start.14 = (f32[128,1024]{1,0:T(8,128)S(1)}, f32[128,1024]{1,0:T(8,128)S(1)}, u32[]{:S(2)}, u32[]{:S(2)}) collective-permute-start(f32[128,1024]{1,0:T(8,128)S(1)} %bitcast.21), channel_id=1, source_target_pairs={{0,1},{4,5},{8,9},{12,13},{16,17},{20,21},{24,25},{28,29}} | collective-permute-start | bytes 1572872 | tf_op jit(solution)/shard_map/ppermute | solution.py:452
  73.4 28.9 %collective-permute-start.15 = (f32[128,1024]{1,0:T(8,128)S(1)}, f32[128,1024]{1,0:T(8,128)S(1)}, u32[]{:S(2)}, u32[]{:S(2)}) collective-permute-start(f32[128,1024]{1,0:T(8,128)S(1)} %bitcast.22), channel_id=1, source_target_pairs={{3,2},{7,6},{11,10},{15,14},{19,18},{23,22},{27,26},{31,30}} | collective-permute-start | bytes 1572872 | tf_op jit(solution)/shard_map/ppermute | solution.py:453
  77.5 29.6 %collective-permute-start.20 = (f32[128,1024]{1,0:T(8,128)S(1)}, f32[128,1024]{1,0:T(8,128)S(1)}, u32[]{:S(2)}, u32[]{:S(2)}) collective-permute-start(f32[128,1024]{1,0:T(8,128)S(1)} %bitcast.19), channel_id=1, source_target_pairs={{0,1},{4,5},{8,9},{12,13},{16,17},{20,21},{24,25},{28,29}} | collective-permute-start | bytes 1572872 | tf_op jit(solution)/shard_map/ppermute | solution.py:452
  78.2 30.2 %collective-permute-start.21 = (f32[128,1024]{1,0:T(8,128)S(1)}, f32[128,1024]{1,0:T(8,128)}, u32[]{:S(2)}, u32[]{:S(2)}) collective-permute-start(f32[128,1024]{1,0:T(8,128)S(1)} %bitcast.20), channel_id=1, source_target_pairs={{3,2},{7,6},{11,10},{15,14},{19,18},{23,22},{27,26},{31,30}} | collective-permute-start | bytes 1572872 | tf_op jit(solution)/shard_map/ppermute | solution.py:453
  85.1 28.1 %collective-permute-start.26 = (f32[128,1024]{1,0:T(8,128)S(1)}, f32[128,1024]{1,0:T(8,128)S(1)}, u32[]{:S(2)}, u32[]{:S(2)}) collective-permute-start(f32[128,1024]{1,0:T(8,128)S(1)} %bitcast.17), channel_id=1, source_target_pairs={{0,1},{4,5},{8,9},{12,13},{16,17},{20,21},{24,25},{28,29}} | collective-permute-start | bytes 1572872 | tf_op jit(solution)/shard_map/ppermute | solution.py:452
  101.1 17.6 %collective-permute-start.27 = (f32[128,1024]{1,0:T(8,128)S(1)}, f32[128,1024]{1,0:T(8,128)}, u32[]{:S(2)}, u32[]{:S(2)}) collective-permute-start(f32[128,1024]{1,0:T(8,128)S(1)} %bitcast.18), channel_id=1, source_target_pairs={{3,2},{7,6},{11,10},{15,14},{19,18},{23,22},{27,26},{31,30}} | collective-permute-start | bytes 1572872 | tf_op jit(solution)/shard_map/ppermute | solution.py:453
  103.2 20.2 %collective-permute-start.32 = (f32[128,1024]{1,0:T(8,128)S(1)}, f32[128,1024]{1,0:T(8,128)S(1)}, u32[]{:S(2)}, u32[]{:S(2)}) collective-permute-start(f32[128,1024]{1,0:T(8,128)S(1)} %bitcast.15), channel_id=1, source_target_pairs={{0,1},{4,5},{8,9},{12,13},{16,17},{20,21},{24,25},{28,29}} | collective-permute-start | bytes 1572872 | tf_op jit(solution)/shard_map/ppermute | solution.py:452
  107.1 22.8 %collective-permute-start.33 = (f32[128,1024]{1,0:T(8,128)S(1)}, f32[128,1024]{1,0:T(8,128)}, u32[]{:S(2)}, u32[]{:S(2)}) collective-permute-start(f32[128,1024]{1,0:T(8,128)S(1)} %bitcast.16), channel_id=1, source_target_pairs={{3,2},{7,6},{11,10},{15,14},{19,18},{23,22},{27,26},{31,30}} | collective-permute-start | bytes 1572872 | tf_op jit(solution)/shard_map/ppermute | solution.py:453
  108.4 26.1 %collective-permute-start.16 = (f32[128,1024]{1,0:T(8,128)}, f32[128,1024]{1,0:T(8,128)}, u32[]{:S(2)}, u32[]{:S(2)}) collective-permute-start(f32[128,1024]{1,0:T(8,128)} %get-tuple-element.63), channel_id=1, source_target_pairs={{0,1},{1,2},{4,5},{5,6},{8,9},{9,10},{12,13},{13,14},{16,17},{17,1... | collective-permute-start | bytes 1572872 | tf_op jit(solution)/shard_map/ppermute | solution.py:452
  113.2 28.0 %collective-permute-start.17 = (f32[128,1024]{1,0:T(8,128)S(1)}, f32[128,1024]{1,0:T(8,128)}, u32[]{:S(2)}, u32[]{:S(2)}) collective-permute-start(f32[128,1024]{1,0:T(8,128)S(1)} %copy-done.39), channel_id=1, source_target_pairs={{2,1},{3,2},{6,5},{7,6},{10,9},{11,10},{14,13},{15,14},{18,17},{19... | collective-permute-start | bytes 1572872 | tf_op jit(solution)/shard_map/ppermute | solution.py:453
  118.6 27.1 %collective-permute-start.22 = (f32[128,1024]{1,0:T(8,128)}, f32[128,1024]{1,0:T(8,128)S(1)}, u32[]{:S(2)}, u32[]{:S(2)}) collective-permute-start(f32[128,1024]{1,0:T(8,128)} %get-tuple-element.67), channel_id=1, source_target_pairs={{0,1},{1,2},{4,5},{5,6},{8,9},{9,10},{12,13},{13,14},{16,17},{17,1... | collective-permute-start | bytes 1572872 | tf_op jit(solution)/shard_map/ppermute | solution.py:452
  123.3 29.0 %collective-permute-start.23 = (f32[128,1024]{1,0:T(8,128)S(1)}, f32[128,1024]{1,0:T(8,128)}, u32[]{:S(2)}, u32[]{:S(2)}) collective-permute-start(f32[128,1024]{1,0:T(8,128)S(1)} %copy-done.38), channel_id=1, source_target_pairs={{2,1},{3,2},{6,5},{7,6},{10,9},{11,10},{14,13},{15,14},{18,17},{19... | collective-permute-start | bytes 1572872 | tf_op jit(solution)/shard_map/ppermute | solution.py:453
  129.9 27.7 %collective-permute-start.28 = (f32[128,1024]{1,0:T(8,128)}, f32[128,1024]{1,0:T(8,128)S(1)}, u32[]{:S(2)}, u32[]{:S(2)}) collective-permute-start(f32[128,1024]{1,0:T(8,128)} %get-tuple-element.71), channel_id=1, source_target_pairs={{0,1},{1,2},{4,5},{5,6},{8,9},{9,10},{12,13},{13,14},{16,17},{17,1... | collective-permute-start | bytes 1572872 | tf_op jit(solution)/shard_map/ppermute | solution.py:452
  134.6 29.0 %collective-permute-start.29 = (f32[128,1024]{1,0:T(8,128)S(1)}, f32[128,1024]{1,0:T(8,128)}, u32[]{:S(2)}, u32[]{:S(2)}) collective-permute-start(f32[128,1024]{1,0:T(8,128)S(1)} %copy-done.37), channel_id=1, source_target_pairs={{2,1},{3,2},{6,5},{7,6},{10,9},{11,10},{14,13},{15,14},{18,17},{19... | collective-permute-start | bytes 1572872 | tf_op jit(solution)/shard_map/ppermute | solution.py:453
  141.1 27.6 %collective-permute-start.34 = (f32[128,1024]{1,0:T(8,128)}, f32[128,1024]{1,0:T(8,128)}, u32[]{:S(2)}, u32[]{:S(2)}) collective-permute-start(f32[128,1024]{1,0:T(8,128)} %get-tuple-element.75), channel_id=1, source_target_pairs={{0,1},{1,2},{4,5},{5,6},{8,9},{9,10},{12,13},{13,14},{16,17},{17,1... | collective-permute-start | bytes 1572872 | tf_op jit(solution)/shard_map/ppermute | solution.py:452
  145.8 29.0 %collective-permute-start.35 = (f32[128,1024]{1,0:T(8,128)S(1)}, f32[128,1024]{1,0:T(8,128)}, u32[]{:S(2)}, u32[]{:S(2)}) collective-permute-start(f32[128,1024]{1,0:T(8,128)S(1)} %copy-done.35), channel_id=1, source_target_pairs={{2,1},{3,2},{6,5},{7,6},{10,9},{11,10},{14,13},{15,14},{18,17},{19... | collective-permute-start | bytes 1572872 | tf_op jit(solution)/shard_map/ppermute | solution.py:453
  152.4 27.6 %collective-permute-start.18 = (f32[128,1024]{1,0:T(8,128)}, f32[128,1024]{1,0:T(8,128)S(1)}, u32[]{:S(2)}, u32[]{:S(2)}) collective-permute-start(f32[128,1024]{1,0:T(8,128)} %get-tuple-element.65), channel_id=1, source_target_pairs={{0,1},{1,2},{2,3},{4,5},{5,6},{6,7},{8,9},{9,10},{10,11},{12,13},{... | collective-permute-start | bytes 1572872 | tf_op jit(solution)/shard_map/ppermute | solution.py:452
  157.6 28.3 %collective-permute-start.19 = (f32[128,1024]{1,0:T(8,128)S(1)}, f32[128,1024]{1,0:T(8,128)S(1)}, u32[]{:S(2)}, u32[]{:S(2)}) collective-permute-start(f32[128,1024]{1,0:T(8,128)S(1)} %copy-done.36), channel_id=1, source_target_pairs={{1,0},{2,1},{3,2},{5,4},{6,5},{7,6},{9,8},{10,9},{11,10},{13,12},{... | collective-permute-start | bytes 1572872 | tf_op jit(solution)/shard_map/ppermute | solution.py:453
  163.6 24.3 %collective-permute-start.24 = (f32[128,1024]{1,0:T(8,128)}, f32[128,1024]{1,0:T(8,128)S(1)}, u32[]{:S(2)}, u32[]{:S(2)}) collective-permute-start(f32[128,1024]{1,0:T(8,128)} %get-tuple-element.69), channel_id=1, source_target_pairs={{0,1},{1,2},{2,3},{4,5},{5,6},{6,7},{8,9},{9,10},{10,11},{12,13},{... | collective-permute-start | bytes 1572872 | tf_op jit(solution)/shard_map/ppermute | solution.py:452
  168.7 28.7 %collective-permute-start.25 = (f32[128,1024]{1,0:T(8,128)}, f32[128,1024]{1,0:T(8,128)S(1)}, u32[]{:S(2)}, u32[]{:S(2)}) collective-permute-start(f32[128,1024]{1,0:T(8,128)} %get-tuple-element.70), channel_id=1, source_target_pairs={{1,0},{2,1},{3,2},{5,4},{6,5},{7,6},{9,8},{10,9},{11,10},{13,12},{... | collective-permute-start | bytes 1572872 | tf_op jit(solution)/shard_map/ppermute | solution.py:453
  174.8 26.2 %collective-permute-start.30 = (f32[128,1024]{1,0:T(8,128)}, f32[128,1024]{1,0:T(8,128)S(1)}, u32[]{:S(2)}, u32[]{:S(2)}) collective-permute-start(f32[128,1024]{1,0:T(8,128)} %get-tuple-element.73), channel_id=1, source_target_pairs={{0,1},{1,2},{2,3},{4,5},{5,6},{6,7},{8,9},{9,10},{10,11},{12,13},{... | collective-permute-start | bytes 1572872 | tf_op jit(solution)/shard_map/ppermute | solution.py:452
  179.9 14.7 %copy-start.28 = (f32[128,1024]{1,0:T(8,128)}, f32[128,1024]{1,0:T(8,128)S(1)}, u32[]{:S(2)}) copy-start(f32[128,1024]{1,0:T(8,128)S(1)} %collective-permute-done.18.c) | copy-start | bytes 1572868
  179.9 28.6 %collective-permute-start.31 = (f32[128,1024]{1,0:T(8,128)}, f32[128,1024]{1,0:T(8,128)}, u32[]{:S(2)}, u32[]{:S(2)}) collective-permute-start(f32[128,1024]{1,0:T(8,128)} %get-tuple-element.74), channel_id=1, source_target_pairs={{1,0},{2,1},{3,2},{5,4},{6,5},{7,6},{9,8},{10,9},{11,10},{13,12},{... | collective-permute-start | bytes 1572872 | tf_op jit(solution)/shard_map/ppermute | solution.py:453
  186.0 8.7 %copy-start.29 = (f32[128,1024]{1,0:T(8,128)}, f32[128,1024]{1,0:T(8,128)S(1)}, u32[]{:S(2)}) copy-start(f32[128,1024]{1,0:T(8,128)S(1)} %collective-permute-done.19.d) | copy-start | bytes 1572868
  186.0 25.4 %collective-permute-start.36 = (f32[128,1024]{1,0:T(8,128)}, f32[128,1024]{1,0:T(8,128)S(1)}, u32[]{:S(2)}, u32[]{:S(2)}) collective-permute-start(f32[128,1024]{1,0:T(8,128)} %get-tuple-element.77), channel_id=1, source_target_pairs={{0,1},{1,2},{2,3},{4,5},{5,6},{6,7},{8,9},{9,10},{10,11},{12,13},{... | collective-permute-start | bytes 1572872 | tf_op jit(solution)/shard_map/ppermute | solution.py:452
  187.9 9.6 %copy-start.30 = (f32[128,1024]{1,0:T(8,128)}, f32[128,1024]{1,0:T(8,128)S(1)}, u32[]{:S(2)}) copy-start(f32[128,1024]{1,0:T(8,128)S(1)} %collective-permute-done.24.c) | copy-start | bytes 1572868
  187.9 31.1 %collective-permute-start.37 = (f32[128,1024]{1,0:T(8,128)}, f32[128,1024]{1,0:T(8,128)}, u32[]{:S(2)}, u32[]{:S(2)}) collective-permute-start(f32[128,1024]{1,0:T(8,128)} %get-tuple-element.78), channel_id=1, source_target_pairs={{1,0},{2,1},{3,2},{5,4},{6,5},{7,6},{9,8},{10,9},{11,10},{13,12},{... | collective-permute-start | bytes 1572872 | tf_op jit(solution)/shard_map/ppermute | solution.py:453
  211.3 10.5 %copy-start.25 = (bf16[128,1024]{1,0:T(8,128)(2,1)S(1)}, bf16[128,1024]{1,0:T(8,128)(2,1)}, u32[]{:S(2)}) copy-start(bf16[128,1024]{1,0:T(8,128)(2,1)} %last_sum.4) | copy-start | bytes 786436
  211.3 10.5 %copy-start.26 = (bf16[128,1024]{1,0:T(8,128)(2,1)S(1)}, bf16[128,1024]{1,0:T(8,128)(2,1)}, u32[]{:S(2)}) copy-start(bf16[128,1024]{1,0:T(8,128)(2,1)} %last_sum.5) | copy-start | bytes 786436
  211.4 10.5 %copy-start.27 = (bf16[128,1024]{1,0:T(8,128)(2,1)S(1)}, bf16[128,1024]{1,0:T(8,128)(2,1)}, u32[]{:S(2)}) copy-start(bf16[128,1024]{1,0:T(8,128)(2,1)} %last_sum.6) | copy-start | bytes 786436
  (37 other events, 89.1 us)

commit v2 on v0

v2 whole, which is shorter than its diff:
```python
import jax
import jax.numpy as jnp
import numpy as np
from jax import lax
from jax.experimental import pallas as pl
from jax.experimental.pallas import tpu as pltpu
from jax.sharding import PartitionSpec as P

HEADS = 128
HEAD_DIM = 64
NSTATE = 128
GROUPS = 8
SPAN = 256
KROWS = 8
LOG2E = 1.4426950408889634
MIB = 1024 * 1024

eps = 1e-05
F32 = jnp.float32
BF16 = jnp.bfloat16


def three_parts(value, axis):
    high = value.astype(BF16)
    rest = value - high.astype(F32)
    middle = rest.astype(BF16)
    low = (rest - middle.astype(F32)).astype(BF16)
    return jnp.concatenate([high, middle, low], axis=axis)


def head_spread(heads, channels):
    row = lax.broadcasted_iota(jnp.int32, (3 * heads, channels), 0)
    col = lax.broadcasted_iota(jnp.int32, (3 * heads, channels), 1)
    return jnp.where(lax.rem(row, heads) == lax.div(col, HEAD_DIM), 1.0, 0.0).astype(BF16)


def dot(a, b, contract=((1,), (0,))):
    return lax.dot_general(a, b, (contract, ((), ())), preferred_element_type=F32)


def block_sums(decay, starts):
    heads = decay.shape[0]
    row = lax.broadcasted_iota(jnp.int32, (SPAN, SPAN), 0)
    col = lax.broadcasted_iota(jnp.int32, (SPAN, SPAN), 1)
    upper = jnp.where(row <= col, 1.0, 0.0).astype(BF16)
    begins = jnp.broadcast_to(starts.astype(F32), (16, SPAN)).astype(BF16)
    sums = dot(jnp.concatenate([three_parts(decay, 0), begins], axis=0), upper)
    cum = sums[:heads] + sums[heads : 2 * heads] + sums[2 * heads : 3 * heads]
    return cum, sums[3 * heads : 3 * heads + 8]


def position(direct):
    if not direct:
        return 0, 0
    me = lax.axis_index("ctx").astype(jnp.int32)
    return lax.rem(me, 2), lax.div(me, 2)


def params(mib):
    return pltpu.CompilerParams(vmem_limit_bytes=mib * MIB)


def states_call(direct, features, write_proj, step_size, log_decay, starts, pieces):
    tokens, channels = features.shape
    heads = step_size.shape[0]
    groups = write_proj.shape[1] // NSTATE
    blocks = tokens // SPAN
    per_group, gch = heads // groups, channels // groups
    width = channels // (2 * pieces)

    def kernel(
        feat_hbm, write_hbm, step_hbm, decay_hbm, starts_hbm, mine, other, pre,
        feat, write, step, decay, starts, total, sems, small_sems,
    ):
        small = [
            pltpu.make_async_copy(src, dst, small_sems.at[k])
            for k, (src, dst) in enumerate(
                [(decay_hbm, decay), (starts_hbm, starts), (step_hbm, step), (write_hbm, write)]
            )
        ]
        for copy in small:
            copy.start()
        copies = []
        for group in range(groups):
            for block in range(blocks):
                copy = pltpu.make_async_copy(
                    feat_hbm.at[pl.ds(block * SPAN, SPAN), pl.ds(group * gch, gch)],
                    feat.at[block, group],
                    sems.at[block, group],
                )
                copy.start()
                copies.append(copy)
        for copy in small[:3]:
            copy.wait()
        spread = head_spread(per_group, gch)
        scales = []
        for block in range(blocks):
            span = slice(block * SPAN, (block + 1) * SPAN)
            cum, seg = block_sums(decay[:, span], starts[:, span])
            seg_last, last = seg[0:1, SPAN - 1 :], cum[:, SPAN - 1 :]
            tail = jnp.where(seg[0:1] == seg_last, jnp.exp(last - cum), 0.0) * step[:, span]
            keep = jnp.where(seg_last == 0.0, jnp.exp(last), 0.0)
            scales.append((tail, jnp.broadcast_to(keep, (heads, 128))))
        small[3].wait()
        for group in range(groups):
            rows = slice(group * per_group, (group + 1) * per_group)
            part = slice(group * gch, (group + 1) * gch)
            for block in range(blocks):
                span = slice(block * SPAN, (block + 1) * SPAN)
                tail, keep = scales[block]
                tail = dot(three_parts(tail[rows], 0), spread, ((0,), (0,)))
                keep = dot(three_parts(keep[rows], 0), spread, ((0,), (0,)))[:KROWS]
                copies[group * blocks + block].wait()
                scaled = (tail * feat[block, group].astype(F32)).astype(BF16)
                state = dot(
                    write[span, group * NSTATE : (group + 1) * NSTATE], scaled, ((0,), (0,))
                )
                if block > 0:
                    state = keep[0:1] * total[:NSTATE, part] + state
                    keep = keep * total[NSTATE:, part]
                total[:NSTATE, part] = state
                total[NSTATE:, part] = keep
                if block < blocks - 1:
                    pre[block, :NSTATE, part] = state
                    pre[block, NSTATE:, part] = keep
        core, _ = position(direct)
        for piece in range(pieces):
            here = (core * pieces + piece) * width
            there = ((1 - core) * pieces + piece) * width
            mine[piece] = total[:, pl.ds(pl.multiple_of(here, 128), width)]
            other[piece] = total[:, pl.ds(pl.multiple_of(there, 128), width)]

    half = jax.ShapeDtypeStruct((pieces, NSTATE + KROWS, width), F32)
    vmem = pl.BlockSpec(memory_space=pltpu.VMEM)
    return pl.pallas_call(
        kernel,
        in_specs=[pl.BlockSpec(memory_space=pltpu.HBM)] * 5,
        out_specs=[vmem] * 3,
        scratch_shapes=[
            pltpu.VMEM((blocks, groups, SPAN, gch), BF16),
            pltpu.VMEM(write_proj.shape, BF16),
            pltpu.VMEM(step_size.shape, F32),
            pltpu.VMEM(log_decay.shape, F32),
            pltpu.VMEM((1, tokens), jnp.int32),
            pltpu.VMEM((NSTATE + KROWS, channels), F32),
            pltpu.SemaphoreType.DMA((blocks, groups)),
            pltpu.SemaphoreType.DMA((4,)),
        ],
        out_shape=[half, half, jax.ShapeDtypeStruct((blocks - 1, NSTATE + KROWS, channels), F32)],
        compiler_params=params(60),
        name="states",
    )(features, write_proj, step_size, log_decay, starts.reshape(1, tokens))


def intra_call(group, features, write_proj, read_proj, step_size, log_decay, starts, skip_weight, after):
    tokens, channels = features.shape
    heads = step_size.shape[0]
    groups = write_proj.shape[1] // NSTATE
    per_group, gch = heads // groups, channels // groups
    blocks = tokens // SPAN
    half = SPAN // 2

    def kernel(feat, write, read, step, decay, starts, skip, after, out, reach):
        cum, seg = block_sums(decay[...], starts[...])
        cum_log2 = cum * LOG2E
        vrow = cum_log2 - jnp.log2(step[...])
        far = jnp.where(seg[0:1] == 0.0, jnp.exp(cum), 0.0)
        fill = jnp.zeros((128 - 2 * per_group - 8, SPAN), F32)
        cols = jnp.concatenate([far, cum_log2, seg, fill], axis=0).T
        reach[...] = cols
        x = feat[...]
        scores = dot(read[...], write[...], ((1,), (1,)))
        row = lax.broadcasted_iota(jnp.int32, (SPAN, SPAN), 0)
        col = lax.broadcasted_iota(jnp.int32, (SPAN, SPAN), 1)
        together = (cols[:, 2 * per_group : 2 * per_group + 1] == seg[0:1]) & (row >= col)
        scores = jnp.where(together, scores, 0.0)
        own = jnp.broadcast_to(skip[:, group * per_group : (group + 1) * per_group], (8, per_group))
        skip_row = dot(three_parts(own, 1), head_spread(per_group, gch))[0:1]
        lane = lax.broadcasted_iota(jnp.int32, (SPAN, 2 * HEAD_DIM), 1)
        for pair in range(per_group // 2):
            part = slice(pair * 2 * HEAD_DIM, (pair + 1) * 2 * HEAD_DIM)
            xp = x[:, part]
            top = skip_row[:, part] * xp[:half].astype(F32)
            low = skip_row[:, part] * xp[half:].astype(F32)
            for which in range(2):
                head = 2 * pair + which
                mine = (lane >= HEAD_DIM) if which else (lane < HEAD_DIM)
                xh = jnp.where(mine, xp, jnp.zeros_like(xp))
                ci = cols[:, per_group + head : per_group + head + 1]
                vj = vrow[head : head + 1, :]
                w_top = jnp.exp2(jnp.minimum(ci[:half] - vj[:, :half], 1.0)) * scores[:half, :half]
                w_low = jnp.exp2(jnp.minimum(ci[half:] - vj, 1.0)) * scores[half:]
                top = top + dot(w_top.astype(BF16), xh[:half])
                low = low + dot(w_low.astype(BF16), xh)
            out[:half, part] = top
            out[half:, part] = low

    return pl.pallas_call(
        kernel,
        grid=(blocks,),
        in_specs=[
            pl.BlockSpec((SPAN, gch), lambda b: (b, group)),
            pl.BlockSpec((SPAN, NSTATE), lambda b: (b, group)),
            pl.BlockSpec((SPAN, NSTATE), lambda b: (b, group)),
            pl.BlockSpec((per_group, SPAN), lambda b: (group, b)),
            pl.BlockSpec((per_group, SPAN), lambda b: (group, b)),
            pl.BlockSpec((1, SPAN), lambda b: (0, b)),
            pl.BlockSpec((1, heads), lambda b: (0, 0)),
            pl.BlockSpec(memory_space=pl.ANY),
        ],
        out_specs=[
            pl.BlockSpec((SPAN, gch), lambda b: (b, 0)),
            pl.BlockSpec((SPAN, 128), lambda b: (b, 0)),
        ],
        out_shape=[
            jax.ShapeDtypeStruct((tokens, gch), F32),
            jax.ShapeDtypeStruct((tokens, 128), F32),
        ],
        compiler_params=params(12),
        cost_estimate=pl.CostEstimate(flops=10**9, bytes_accessed=10**6, transcendentals=0),
        name="intra",
    )(
        features,
        write_proj,
        read_proj,
        step_size,
        log_decay,
        starts.reshape(1, tokens),
        skip_weight.reshape(1, heads),
        after,
    )


def chip_call(mine, theirs):
    pieces, rows, width = mine.shape

    def kernel(mine, theirs, *outs):
        core, chip = position(True)
        first_core = core == 0
        for offset in range(pieces):
            piece = chip ^ offset
            a, b = mine[piece], theirs[piece]
            first, second = jnp.where(first_core, a, b), jnp.where(first_core, b, a)
            keep = second[NSTATE:]
            outs[offset][:NSTATE] = keep[0:1] * first[:NSTATE] + second[:NSTATE]
            outs[offset][NSTATE:] = keep * first[NSTATE:]

    vmem = pl.BlockSpec(memory_space=pltpu.VMEM)
    return pl.pallas_call(
        kernel,
        in_specs=[vmem, vmem],
        out_specs=[vmem] * pieces,
        out_shape=[jax.ShapeDtypeStruct((rows, width), F32)] * pieces,
        compiler_params=params(6),
        name="chip_states",
    )(mine, theirs)


def prefix_call(parts, after):
    pieces, (rows, width) = len(parts), parts[0].shape

    def kernel(*refs):
        _, chip_here = position(True)
        ins, outs, stack = refs[:pieces], refs[pieces + 1 : 2 * pieces + 1], refs[2 * pieces + 1]
        for offset in range(pieces):
            stack[chip_here ^ offset] = ins[offset][...]
        entry = jnp.zeros((NSTATE, width), F32)
        for chip in range(pieces):
            state, keep = stack[chip, :NSTATE], stack[chip, NSTATE : NSTATE + 1]
            stack[chip, :NSTATE] = entry
            entry = keep * entry + state
        for offset in range(pieces):
            outs[offset][...] = stack[chip_here ^ offset, :NSTATE]

    vmem = pl.BlockSpec(memory_space=pltpu.VMEM)
    return pl.pallas_call(
        kernel,
        in_specs=[vmem] * pieces + [pl.BlockSpec(memory_space=pl.ANY)],
        out_specs=[vmem] * pieces,
        scratch_shapes=[pltpu.VMEM((pieces, rows, width), F32)],
        out_shape=[jax.ShapeDtypeStruct((NSTATE, width), F32)] * pieces,
        compiler_params=params(4),
        name="prefix",
    )(*parts, after)


def fold_call(theirs, pre, tokens):
    channels = pre.shape[2]
    blocks = tokens // SPAN
    parts, _, width = theirs[0].shape if theirs else (1, 0, channels // 2)

    def kernel(*refs):
        their_refs, (pre, out) = refs[:-2], refs[-2:]
        core, _ = position(bool(theirs))
        for side in range(2):
            for index in range(parts):
                piece = (core if side == 0 else 1 - core) * parts + index
                part = pl.ds(pl.multiple_of(piece * width, 128), width)
                state = jnp.zeros((NSTATE, width), F32)
                keep = jnp.ones((KROWS, width), F32)
                if theirs:
                    before = their_refs[side][index]
                    state = jnp.where(core == 0, state, before[:NSTATE])
                    keep = jnp.where(core == 0, keep, before[NSTATE:])
                out[0, :NSTATE, part] = state
                out[0, NSTATE:, part] = keep
                for block in range(1, blocks):
                    mult = pre[block - 1, NSTATE:, part]
                    out[block, :NSTATE, part] = mult[0:1] * state + pre[block - 1, :NSTATE, part]
                    out[block, NSTATE:, part] = mult * keep

    vmem = pl.BlockSpec(memory_space=pltpu.VMEM)
    return pl.pallas_call(
        kernel,
        in_specs=[vmem] * (len(theirs) + 1),
        out_specs=vmem,
        out_shape=jax.ShapeDtypeStruct((blocks, NSTATE + KROWS, channels), F32),
        compiler_params=params(8),
        name="fold",
    )(*theirs, pre)


def exchange(parts, axis):
    count = lax.axis_size(axis)
    return [parts[0]] + [
        lax.ppermute(parts[k], axis, [(i, i ^ (2 * k)) for i in range(count)])
        for k in range(1, len(parts))
    ]


def over(value, axis):
    return lax.ppermute(value, axis, [(i, i ^ 1) for i in range(lax.axis_size(axis))])


def chain(total, axis):
    count = lax.axis_size(axis)
    state, keep = total[:, :NSTATE], total[:, NSTATE : NSTATE + 1]
    steps = [(i, i + 1) for i in range(count - 1)]

    def step(index, incoming):
        return lax.ppermute(keep * incoming + state, axis, steps)

    return lax.fori_loop(0, count - 1, step, jnp.zeros_like(state))


def chunk_normed(blk, held, inner, reach, gate, read, gain):
    groups = len(inner)
    gch = inner[0].shape[1]
    per_group = gch // HEAD_DIM
    pieces, width = held.shape[1], held.shape[3]
    here = pieces // groups
    spread = head_spread(per_group, gch)
    result = []
    for group in range(groups):
        part = slice(group * gch, (group + 1) * gch)
        c_rows = read[:, group * NSTATE : (group + 1) * NSTATE]
        far = dot(three_parts(reach[group][:, :per_group], 1), spread)
        carried = [dot(c_rows, held[blk, group * here + k]) for k in range(here)]
        y = inner[group][...] + far * (jnp.concatenate(carried, axis=1) if here > 1 else carried[0])
        g = gate[:, part].astype(F32)
        gated = y * (g / (1.0 + jnp.exp(-g)))
        mean_square = jnp.mean(gated * gated, axis=1, keepdims=True)
        result.append((gated * lax.rsqrt(mean_square + eps) * gain[:, part]).astype(BF16))
    return result


def hold_entries(scal, entries, fold, held, blk, slot):
    parts = len(entries) // 2
    width = held.shape[-1]
    for k, ref in enumerate(entries):
        half = scal[0] if k < parts else 1 - scal[0]
        piece = half * parts + (scal[1] ^ (k % parts))
        part = pl.ds(pl.multiple_of(piece * width, 128), width)
        entry = ref[...].reshape(NSTATE, width)
        held[slot, piece] = (
            fold[blk, NSTATE : NSTATE + 1, part] * entry + fold[blk, :NSTATE, part]
        ).astype(BF16)


def first_call(scal, entries, fold, inner, reach, gate, read, gain, out_weight, rows, columns, early):
    tokens, channels = gate.shape
    groups, pieces, width = len(inner), len(entries), entries[0].shape[-1]
    tile = min(512, columns)
    total = early * columns

    def kernel(scal, *refs):
        entries, refs = refs[:pieces], refs[pieces:]
        inner, reach, refs = refs[:groups], refs[groups : 2 * groups], refs[2 * groups :]
        fold, gate_hbm, read, gain, w_hbm, out, *firsts, weight, gate, held, sems, gate_sem = refs
        gate_copy = pltpu.make_async_copy(
            gate_hbm.at[pl.ds(pl.multiple_of(scal[2] * rows, rows), rows)], gate, gate_sem
        )
        gate_copy.start()
        copies = []
        for t in range(total // tile):
            cut = pl.ds(t * tile, tile)
            copy = pltpu.make_async_copy(w_hbm.at[:, cut], weight.at[:, cut], sems.at[t])
            copy.start()
            copies.append(copy)
        hold_entries(scal, entries, fold, held, 0, 0)
        gate_copy.wait()
        normed = jnp.concatenate(chunk_normed(0, held, inner, reach, gate, read, gain), axis=1)
        out[0] = normed
        for t in range(total // tile):
            cut = slice(t * tile, (t + 1) * tile)
            copies[t].wait()
            at = t * tile % columns
            firsts[t * tile // columns][0, :, at : at + tile] = dot(normed, weight[:, cut])

    def whole(value):
        zeros = (0,) * value.ndim
        return pl.BlockSpec(value.shape, lambda j, s: zeros)

    def chunk(size):
        return pl.BlockSpec((rows, size), lambda j, s: (s[2], 0))

    return pl.pallas_call(
        kernel,
        grid_spec=pltpu.PrefetchScalarGridSpec(
            num_scalar_prefetch=1,
            grid=(1,),
            in_specs=[whole(v) for v in entries]
            + [chunk(channels // groups)] * groups
            + [chunk(128)] * groups
            + [
                pl.BlockSpec(
                    (1, NSTATE + KROWS, channels), lambda j, s: (lax.div(s[2] * rows, SPAN), 0, 0)
                ),
                pl.BlockSpec(memory_space=pltpu.HBM),
                chunk(groups * NSTATE),
                whole(gain),
                pl.BlockSpec(memory_space=pltpu.HBM),
            ],
            out_specs=[
                pl.BlockSpec((1, rows, channels), lambda j, s: (0, 0, 0)),
            ]
            + [pl.BlockSpec((1, rows, columns), lambda j, s: (0, 0, 0))] * early,
            scratch_shapes=[
                pltpu.VMEM((channels, total), BF16),
                pltpu.VMEM((rows, channels), BF16),
                pltpu.VMEM((1, pieces, NSTATE, width), BF16),
                pltpu.SemaphoreType.DMA((total // tile,)),
                pltpu.SemaphoreType.DMA(()),
            ],
        ),
        out_shape=[
            jax.ShapeDtypeStruct((1, rows, channels), BF16),
        ]
        + [jax.ShapeDtypeStruct((1, rows, columns), F32)] * early,
        compiler_params=params(34),
        name="first",
    )(scal, *entries, *inner, *reach, fold, gate, read, gain, out_weight)


def rest_call(scal, entries, fold, inner, reach, gate, read, gain, rows):
    tokens, channels = gate.shape
    groups, pieces, width = len(inner), len(entries), entries[0].shape[-1]
    count, blocks = tokens // rows, tokens // SPAN
    gch = channels // groups

    def kernel(scal, *refs):
        entries, refs = refs[:pieces], refs[pieces:]
        inner, reach, refs = refs[:groups], refs[groups : 2 * groups], refs[2 * groups :]
        fold, gate_hbm, read, gain, out, gate, held, sems = refs
        step = pl.program_id(0)

        def gate_copy(k):
            first_row = pl.multiple_of(scal[3 + k] * rows, rows)
            return pltpu.make_async_copy(gate_hbm.at[pl.ds(first_row, rows)], gate.at[k], sems.at[k])

        @pl.when(step == 0)
        def _():
            for k in range(count - 1):
                gate_copy(k).start()
            for block in range(blocks):
                hold_entries(scal, entries, fold, held, block, block)

        gate_copy(step).wait()
        blk = lax.div(scal[3 + step] * rows, SPAN)
        now = chunk_normed(blk, held, inner, reach, gate.at[step], read, gain)
        for group, part in enumerate(now):
            out[0, :, group * gch : (group + 1) * gch] = part

    def whole(value):
        zeros = (0,) * value.ndim
        return pl.BlockSpec(value.shape, lambda j, s: zeros)

    def chunk(size):
        return pl.BlockSpec((rows, size), lambda j, s: (s[3 + j], 0))

    return pl.pallas_call(
        kernel,
        grid_spec=pltpu.PrefetchScalarGridSpec(
            num_scalar_prefetch=1,
            grid=(count - 1,),
            in_specs=[whole(v) for v in entries]
            + [chunk(gch)] * groups
            + [chunk(128)] * groups
            + [whole(fold), pl.BlockSpec(memory_space=pltpu.HBM)]
            + [chunk(groups * NSTATE), whole(gain)],
            out_specs=pl.BlockSpec((1, rows, channels), lambda j, s: (j, 0, 0)),
            scratch_shapes=[
                pltpu.VMEM((count - 1, rows, channels), BF16),
                pltpu.VMEM((blocks, pieces, NSTATE, width), BF16),
                pltpu.SemaphoreType.DMA((count - 1,)),
            ],
        ),
        out_shape=jax.ShapeDtypeStruct((count - 1, rows, channels), BF16),
        compiler_params=params(14),
        cost_estimate=pl.CostEstimate(flops=10**9, bytes_accessed=10**6, transcendentals=0),
        name="rest",
    )(scal, *entries, *inner, *reach, fold, gate, read, gain)


def project_call(parts, out_weight, start, columns):
    chunks, rows, channels = sum(p.shape[0] for p in parts), *parts[0].shape[1:]
    tile = min(512, columns)
    tiles = columns // tile

    def kernel(*refs):
        w_hbm, out, weight, sems = refs[len(parts) :]
        copies = []
        for t in range(tiles):
            copy = pltpu.make_async_copy(
                w_hbm.at[:, pl.ds(start + t * tile, tile)], weight.at[t], sems.at[t]
            )
            copy.start()
            copies.append(copy)
        for t in range(tiles):
            copies[t].wait()
            at = 0
            for part in refs[: len(parts)]:
                size = part.shape[0]
                product = dot(part[...].reshape(size * rows, channels), weight[t])
                out[at : at + size, :, t * tile : (t + 1) * tile] = product.reshape(size, rows, tile)
                at += size

    vmem = pl.BlockSpec(memory_space=pltpu.VMEM)
    return pl.pallas_call(
        kernel,
        in_specs=[vmem] * len(parts) + [pl.BlockSpec(memory_space=pltpu.HBM)],
        out_specs=vmem,
        out_shape=jax.ShapeDtypeStruct((chunks, rows, columns), F32),
        scratch_shapes=[
            pltpu.VMEM((tiles, channels, tile), BF16),
            pltpu.SemaphoreType.DMA((tiles,)),
        ],
        compiler_params=params(14),
        cost_estimate=pl.CostEstimate(
            flops=2 * chunks * rows * channels * columns,
            bytes_accessed=2 * channels * columns + 4 * chunks * rows * columns,
            transcendentals=0,
        ),
        name="project",
    )(*parts, out_weight)


def line_tables(count):
    order, up, down = [], np.zeros((count, count), np.int32), np.zeros((count, count), np.int32)
    for me in range(count):
        def step(c):
            return count - c + me if c > me else (count + c - me if c < me else 10 * count)

        order.append(sorted(range(count), key=lambda c: (step(c), abs(c - me))))
        for s in range(1, count):
            if me < count - 1 and s > me:
                up[me, s] = order[me].index(count - s + me)
            if me > 0 and s > count - 1 - me:
                down[me, s] = order[me].index(s - count + me)
    return np.concatenate([np.array(order, np.int32), up, down], axis=1)


def sum_call(scal, mine, up, down, step):
    count, rows, width = mine.shape
    tile = min(1024, width)
    moving = pl.BlockSpec((1, rows, tile), lambda j, s: (0, 0, j))
    at_up, at_down = 2 + count + step, 2 + 2 * count + step

    def kernel(scal, a, b, c, d, out_up, out_down):
        out_up[...] = a[...] + c[...]
        out_down[...] = b[...] + d[...]

    return pl.pallas_call(
        kernel,
        grid_spec=pltpu.PrefetchScalarGridSpec(
            num_scalar_prefetch=1,
            grid=(width // tile,),
            in_specs=[
                pl.BlockSpec((1, rows, tile), lambda j, s: (s[at_up], 0, j)),
                pl.BlockSpec((1, rows, tile), lambda j, s: (s[at_down], 0, j)),
                moving,
                moving,
            ],
            out_specs=[moving, moving],
        ),
        out_shape=[jax.ShapeDtypeStruct(up.shape, F32)] * 2,
        cost_estimate=pl.CostEstimate(
            flops=10**10, bytes_accessed=24 * rows * width, transcendentals=0
        ),
        compiler_params=params(8),
        name="sum",
    )(scal, mine, mine, up, down)


def last_call(so_far, mine, up, down, first, wide):
    count, rows, width = mine.shape
    tile = min(512, width)
    moving = pl.BlockSpec((1, rows, tile), lambda j: (0, 0, j))

    def kernel(a, c, d, *refs):
        refs[-1][...] = (a[0] + c[0] + d[0]).astype(BF16)

    more = [] if so_far is None else [so_far]
    return pl.pallas_call(
        kernel,
        grid=(width // tile,),
        in_specs=[pl.BlockSpec((1, rows, tile), lambda j: (count - 1, 0, j)), moving, moving]
        + [pl.BlockSpec(memory_space=pl.ANY)] * len(more),
        out_specs=pl.BlockSpec((rows, tile), lambda j: (0, first // tile + j)),
        out_shape=jax.ShapeDtypeStruct((rows, wide), BF16),
        input_output_aliases={3: 0} if more else {},
        compiler_params=params(4),
        name="last_sum",
    )(mine, up, down, *more)


def send(to_up, to_down, step, axis):
    count = lax.axis_size(axis)
    return (
        lax.ppermute(to_up, axis, [(i, i + 1) for i in range(count - 1) if step > i]),
        lax.ppermute(to_down, axis, [(i, i - 1) for i in range(1, count) if step > count - 1 - i]),
    )


def body(
    features,
    gate_values,
    write_proj,
    read_proj,
    step_size,
    log_decay,
    starts,
    skip_weight,
    norm_gain,
    out_weight,
):
    tokens, channels = features.shape
    groups = write_proj.shape[1] // NSTATE
    count = lax.axis_size("ctx")
    chips = count // 2
    direct = channels % (128 * count) == 0 and chips & (chips - 1) == 0 and count % groups == 0
    me = lax.axis_index("ctx").astype(jnp.int32)
    place = jnp.stack([me % 2, me // 2]) if direct else jnp.zeros((2,), jnp.int32)
    line = lax.axis_size("head")
    scal = jnp.concatenate([place, jnp.asarray(line_tables(line))[lax.axis_index("head")]])
    rows = tokens // line

    features, scal = lax.optimization_barrier((features, scal))
    mine, other, pre = states_call(
        direct, features, write_proj, step_size, log_decay, starts, chips if direct else 1
    )
    def intra(group, after):
        return intra_call(
            group, features, write_proj, read_proj, step_size, log_decay, starts, skip_weight, after
        )

    if direct:
        theirs = over(other, "ctx")
        totals = chip_call(mine, theirs)
        rest_theirs = lax.ppermute(mine, "ctx", [(i, i + 1) for i in range(0, count, 2)])
        moved = exchange(totals, "ctx")
        local = [intra(0, totals[0])]
        entries = prefix_call(moved, local[0][1])
        own = exchange(entries, "ctx")
        local += [intra(g, entries[0]) for g in range(1, groups)]
        fold = fold_call([theirs, rest_theirs], pre, tokens)
        own, local, fold = lax.optimization_barrier((own, local, fold))
        entries = own + [over(e, "ctx") for e in own]
    else:
        entries = [chain(mine, "ctx"), chain(other, "ctx")]
        local = [intra(g, mine) for g in range(groups)]
        fold = fold_call([], pre, tokens)
    inner, reach = zip(*local)
    rest = (inner, reach, gate_values, read_proj, norm_gain.reshape(1, channels))
    wide = out_weight.shape[1]
    pieces = 4
    cut = wide // pieces
    early = pieces
    normed, *firsts = first_call(scal, entries, fold, *rest, out_weight, rows, cut, early)
    moving = [send(f, f, 1, "head") for f in firsts]
    others = rest_call(scal, entries, fold, *rest, rows)
    mine = [project_call([normed, others], out_weight, p * cut, cut) for p in range(pieces)]
    for s in range(2, line):
        for p in range(pieces):
            moving[p] = send(*sum_call(scal, mine[p], *moving[p], s), s, "head")
    result = None
    for p in range(pieces):
        result = last_call(result, mine[p], *moving[p], p * cut, wide)
    return result


def solution(mesh):
    placed = (
        P("ctx", "head"),
        P("ctx", "head"),
        P("ctx", "head"),
        P("ctx", "head"),
        P("head", "ctx"),
        P("head", "ctx"),
        P("ctx"),
        P("head"),
        P("head"),
        P("head", None),
    )
    return jax.shard_map(
        body, mesh=mesh, in_specs=placed, out_specs=P(("ctx", "head"), None), check_vma=False
    )
```

time: 370 us -> 183 us (0.49)
  waiting for transfers between devices: 180 us -> 55.9 us
  Pallas kernels: 0 us -> 43.9 us
  local copies, waits for them, and re-layouts: 41 us -> 3.55 us
  matrix products: 28.4 us -> 0 us
  other arithmetic: 20.6 us -> 0.08 us
  between operations: 13.7 us -> 0.61 us
  starting transfers between devices: 84.5 us -> 78.3 us
    reduce_scatter x1 -> x0, waiting for transfers between devices: 165 us -> none  [body(): lax.psum_scatter(jnp.dot(normed, out_weight, preferred_element_type=jnp.f...]
    pallas_call x0 -> x24, Pallas kernels: none -> 43.9 us  [the longest x4 12.8 us: project_call(): pl.pallas_call(kernel, in_specs=[vmem] * len(parts) + [pl.BlockSpec(memor...]
    ppermute x7 -> x36, waiting for transfers between devices: 15.4 us -> 55.9 us  [the longest x12 50.6 us: send(): lax.ppermute(to_down, axis, [(i, i - 1) for i in range(1, count) if step...]
    dot_general x5 -> x0, matrix products: 28.4 us -> none  [the longest x1 14.5 us: body(): jnp.dot(normed, out_weight, preferred_element_type=jnp.float32)]
    reshape x4 -> x0, local copies, waits for them, and re-layouts: 11.3 us -> none  [the longest x2 11.2 us: body(): feat_blocks = features.reshape(blocks, SPAN, heads_dev, HEAD_DIM)]
    convert_element_type x2 -> x0, local copies, waits for them, and re-layouts: 10.1 us -> none  [body(): feat_blocks.astype(jnp.float32)]
    mul x3 -> x0, local copies, waits for them, and re-layouts: 8.42 us -> none  [the longest x1 7.74 us: body(): (damping * step_blocks[:, :, None, :]).reshape(groups_dev, per_group, blo...]
    convert_element_type x3 -> x0, other arithmetic: 8.39 us -> none  [the longest x1 4.23 us: body(): (tail_scale.transpose(1, 2, 0)[..., None] * feat_blocks.astype(jnp.float3...]
  transfers between devices with their start and end apart: 8 -> 36, of which waited for: 8 -> 18; matrix products, arithmetic and copies ran while one was open for 0% -> 0% of each run, Pallas kernels for 0% -> 17%
where the time goes in v2:
time: 183 us; the launch traced here: 182 us
  starting transfers between devices  78.3 us (43%)
  waiting for transfers between devices  55.9 us (31%)
  Pallas kernels  43.9 us (24%)
  local copies, waits for them, and re-layouts  3.55 us (2%)
    ppermute x12, starting transfers between devices, send(): lax.ppermute(to_down, axis, [(i, i - 1) for i in range(1, count) if step...  52.1 us
    ppermute x12, waiting for transfers between devices, send(): lax.ppermute(to_down, axis, [(i, i - 1) for i in range(1, count) if step...  50.6 us
    ppermute x12, starting transfers between devices, send(): lax.ppermute(to_up, axis, [(i, i + 1) for i in range(count - 1) if step >...  15.5 us
    pallas_call x4, Pallas kernels, project_call(): pl.pallas_call(kernel, in_specs=[vmem] * len(parts) + [pl.BlockSpec(memor...  12.8 us
    pallas_call x1, Pallas kernels, first_call(): pl.pallas_call(kernel, grid_spec=pltpu.PrefetchScalarGridSpec(num_scalar_...  7.38 us
    ppermute x6, starting transfers between devices, exchange(): lax.ppermute(parts[k], axis, [(i, i ^ 2 * k) for i in range(count)])  7.11 us
    pallas_call x2, Pallas kernels, intra_call(): pl.pallas_call(kernel, grid=(blocks,), in_specs=[pl.BlockSpec((SPAN, gch)...  5.62 us
    pallas_call x1, Pallas kernels, states_call(): pl.pallas_call(kernel, in_specs=[pl.BlockSpec(memory_space=pltpu.HBM)] *...  5.4 us
  transfers between devices with their start and end apart: 36, of which 18 were waited for; matrix products, arithmetic and copies ran while one was open for 0% of the time, Pallas kernels for 17%

profile of v2, /device:TPU:16, one launch (start us, length us, event | category | flops | bytes accessed | tf_op | source)
XLA Modules:
  0.0 182.3 jit_solution(5085028970105022497)
XLA Ops:
  1.0 5.4 %states.1 = (f32[4,136,256]{2,1,0:T(8,128)}, f32[4,136,256]{2,1,0:T(8,128)}, f32[1,136,2048]{2,1,0:T(8,128)}) custom-call(bf16[512,2048]{1,0:T(8,128)(2,1)} %feat.1, bf16[512,256]{1,0:T(8,128)(2,1)} %write.3, f32[32,512]{1,0:T(8,128)} %step.3, f32[32,512]{1,0:T(8,128)} %decay.3, s32[1,512]{1,0:T(1,128)} %bitcast.11), custom_call_target="tpu_custom_call" | custom-call | tf_op jit(solution)/shard_map/states/pallas_call | solution.py:135
  6.5 2.4 %collective-permute-start.7 = (f32[4,136,256]{2,1,0:T(8,128)}, f32[4,136,256]{2,1,0:T(8,128)S(1)}, u32[]{:S(2)}, u32[]{:S(2)}) collective-permute-start(f32[4,136,256]{2,1,0:T(8,128)} %get-tuple-element.54.mine), channel_id=1, source_target_pairs={{0,4},{8,12},{16,20},{24,28},{1,5},{9,13},{17,21},{25,29},{2,6},{1... | collective-permute-start | bytes 1671176 | tf_op jit(solution)/shard_map/ppermute | solution.py:670
  8.9 1.0 copy-done.4
  10.0 1.6 collective-permute-start.1
  11.6 1.5 collective-permute-start.2
  14.6 2.8 %intra.2 = (f32[512,1024]{1,0:T(8,128)S(1)}, f32[512,128]{1,0:T(8,128)S(1)}) custom-call(bf16[512,2048]{1,0:T(8,128)(2,1)S(1)} %copy-done.1, bf16[512,256]{1,0:T(8,128)(2,1)S(1)} %copy-done.5, bf16[512,256]{1,0:T(8,128)(2,1)S(1)} %copy-done.3, f32[32,512]{1,0:T(8,128)S(1)} %copy-done.7, f32[32,512]{1,0:T(8,128)S(1)} %copy-done.8, s32[1,512]{1,0:T(1,128)S(1)} %bitcast.12, ...), custom_call_target="tpu_custom_call" | custom-call | flops 1000000000 | bytes 1000000 | tf_op jit(solution)/shard_map/intra/pallas_call | solution.py:198
  17.5 2.3 %collective-permute-done.2.refs_2_ = f32[136,256]{1,0:T(8,128)S(1)} collective-permute-done((f32[136,256]{1,0:T(8,128)S(1)}, f32[136,256]{1,0:T(8,128)S(1)}, u32[]{:S(2)}, u32[]{:S(2)}) %collective-permute-start.2) | collective-permute-done | bytes 139296 | tf_op jit(solution)/shard_map/ppermute | solution.py:326
  19.9 1.3 collective-permute-start.4
  22.0 1.4 collective-permute-start.6
  24.4 2.8 %intra.3 = (f32[512,1024]{1,0:T(8,128)S(1)}, f32[512,128]{1,0:T(8,128)S(1)}) custom-call(bf16[512,2048]{1,0:T(8,128)(2,1)S(1)} %copy-done.1, bf16[512,256]{1,0:T(8,128)(2,1)S(1)} %copy-done.6, bf16[512,256]{1,0:T(8,128)(2,1)S(1)} %copy-done.3, f32[32,512]{1,0:T(8,128)S(1)} %copy-done.7, f32[32,512]{1,0:T(8,128)S(1)} %copy-done.8, s32[1,512]{1,0:T(1,128)S(1)} %bitcast.13, ...), custom_call_target="tpu_custom_call" | custom-call | flops 1000000000 | bytes 1000000 | tf_op jit(solution)/shard_map/intra/pallas_call | solution.py:198
  30.2 7.4 %first.1 = (bf16[1,128,2048]{2,1,0:T(8,128)(2,1)S(1)}, f32[1,128,1024]{2,1,0:T(8,128)S(1)}, f32[1,128,1024]{2,1,0:T(8,128)S(1)}, f32[1,128,1024]{2,1,0:T(8,128)S(1)}, f32[1,128,1024]{2,1,0:T(8,128)S(1)}) custom-call(s32[14]{0:T(128)S(1)} %pad_add_fusion.scal, f32[128,256]{1,0:T(8,128)S(1)} %get-tuple-element.69.after.refs_0_, ...), custom_call_target="tpu_custom_call" | custom-call | tf_op jit(solution)/shard_map/first/pallas_call | solution.py:417
  37.5 1.6 collective-permute-start.13
  39.8 1.3 collective-permute-start.31
  41.8 1.7 collective-permute-start.25
  43.6 3.4 %rest.1.refs_1_ = bf16[3,128,2048]{2,1,0:T(8,128)(2,1)S(1)} custom-call(s32[14]{0:T(128)S(1)} %pad_add_fusion.scal, f32[128,256]{1,0:T(8,128)S(1)} %get-tuple-element.69.after.refs_0_, f32[128,256]{1,0:T(8,128)S(1)} %collective-permute-done.4.refs_1_, f32[128,256]{1,0:T(8,128)S(1)} %collective-permute-done.5.refs_2_, ...), custom_call_target="tpu_custom_call" | custom-call | flops 1000000000 | bytes 1000000 | tf_op jit(solution)/shard_map/rest/pallas_call | solution.py:491
  47.0 3.2 %project.7.a.b = f32[4,128,1024]{2,1,0:T(8,128)S(1)} custom-call(bf16[1,128,2048]{2,1,0:T(8,128)(2,1)S(1)} %get-tuple-element.78.refs_0_, bf16[3,128,2048]{2,1,0:T(8,128)(2,1)S(1)} %rest.1.refs_1_, bf16[2048,4096]{1,0:T(8,128)(2,1)S(1)} %bitcast.8), custom_call_target="tpu_custom_call" | custom-call | flops 2147483648 | bytes 6291456 | tf_op jit(solution)/shard_map/project/pallas_call | solution.py:539
  50.2 3.2 %project.6.a.b = f32[4,128,1024]{2,1,0:T(8,128)S(1)} custom-call(bf16[1,128,2048]{2,1,0:T(8,128)(2,1)S(1)} %get-tuple-element.78.refs_0_, bf16[3,128,2048]{2,1,0:T(8,128)(2,1)S(1)} %rest.1.refs_1_, bf16[2048,4096]{1,0:T(8,128)(2,1)S(1)} %bitcast.8), custom_call_target="tpu_custom_call" | custom-call | flops 2147483648 | bytes 6291456 | tf_op jit(solution)/shard_map/project/pallas_call | solution.py:539
  53.4 3.2 %project.5.a.b = f32[4,128,1024]{2,1,0:T(8,128)S(1)} custom-call(bf16[1,128,2048]{2,1,0:T(8,128)(2,1)S(1)} %get-tuple-element.78.refs_0_, bf16[3,128,2048]{2,1,0:T(8,128)(2,1)S(1)} %rest.1.refs_1_, bf16[2048,4096]{1,0:T(8,128)(2,1)S(1)} %bitcast.8), custom_call_target="tpu_custom_call" | custom-call | flops 2147483648 | bytes 6291456 | tf_op jit(solution)/shard_map/project/pallas_call | solution.py:539
  56.6 3.2 %project.4.a.b = f32[4,128,1024]{2,1,0:T(8,128)S(1)} custom-call(bf16[1,128,2048]{2,1,0:T(8,128)(2,1)S(1)} %get-tuple-element.78.refs_0_, bf16[3,128,2048]{2,1,0:T(8,128)(2,1)S(1)} %rest.1.refs_1_, bf16[2048,4096]{1,0:T(8,128)(2,1)S(1)} %bitcast.8), custom_call_target="tpu_custom_call" | custom-call | flops 2147483648 | bytes 6291456 | tf_op jit(solution)/shard_map/project/pallas_call | solution.py:539
  59.8 5.8 %collective-permute-done.31.d = f32[1,128,1024]{2,1,0:T(8,128)S(1)} collective-permute-done((f32[1,128,1024]{2,1,0:T(8,128)S(1)}, f32[1,128,1024]{2,1,0:T(8,128)S(1)}, u32[]{:S(2)}, u32[]{:S(2)}) %collective-permute-start.31) | collective-permute-done | bytes 524320 | tf_op jit(solution)/shard_map/ppermute | solution.py:631
  66.4 1.3 collective-permute-start.19
  68.3 8.6 %collective-permute-done.25.d = f32[1,128,1024]{2,1,0:T(8,128)S(1)} collective-permute-done((f32[1,128,1024]{2,1,0:T(8,128)S(1)}, f32[1,128,1024]{2,1,0:T(8,128)S(1)}, u32[]{:S(2)}, u32[]{:S(2)}) %collective-permute-start.25) | collective-permute-done | bytes 524320 | tf_op jit(solution)/shard_map/ppermute | solution.py:631
  77.6 1.3 collective-permute-start.32
  79.6 8.0 %collective-permute-done.19.d = f32[1,128,1024]{2,1,0:T(8,128)S(1)} collective-permute-done((f32[1,128,1024]{2,1,0:T(8,128)S(1)}, f32[1,128,1024]{2,1,0:T(8,128)S(1)}, u32[]{:S(2)}, u32[]{:S(2)}) %collective-permute-start.19) | collective-permute-done | bytes 524320 | tf_op jit(solution)/shard_map/ppermute | solution.py:631
  87.6 1.9 %collective-permute-start.33 = (f32[1,128,1024]{2,1,0:T(8,128)S(1)}, f32[1,128,1024]{2,1,0:T(8,128)S(1)}, u32[]{:S(2)}, u32[]{:S(2)}) collective-permute-start(f32[1,128,1024]{2,1,0:T(8,128)S(1)} %get-tuple-element.96), channel_id=1, source_target_pairs={{2,1},{3,2},{6,5},{7,6},{10,9},{11,10},{14,13},{15,14},{18,17},{19... | collective-permute-start | bytes 1572872 | tf_op jit(solution)/shard_map/ppermute | solution.py:631
  89.5 1.3 collective-permute-start.26
  91.5 4.6 %collective-permute-start.27 = (f32[1,128,1024]{2,1,0:T(8,128)S(1)}, f32[1,128,1024]{2,1,0:T(8,128)S(1)}, u32[]{:S(2)}, u32[]{:S(2)}) collective-permute-start(f32[1,128,1024]{2,1,0:T(8,128)S(1)} %get-tuple-element.91), channel_id=1, source_target_pairs={{2,1},{3,2},{6,5},{7,6},{10,9},{11,10},{14,13},{15,14},{18,17},{19... | collective-permute-start | bytes 1572872 | tf_op jit(solution)/shard_map/ppermute | solution.py:631
  96.0 1.3 collective-permute-start.20
  98.0 4.6 %collective-permute-start.21 = (f32[1,128,1024]{2,1,0:T(8,128)S(1)}, f32[1,128,1024]{2,1,0:T(8,128)S(1)}, u32[]{:S(2)}, u32[]{:S(2)}) collective-permute-start(f32[1,128,1024]{2,1,0:T(8,128)S(1)} %get-tuple-element.86), channel_id=1, source_target_pairs={{2,1},{3,2},{6,5},{7,6},{10,9},{11,10},{14,13},{15,14},{18,17},{19... | collective-permute-start | bytes 1572872 | tf_op jit(solution)/shard_map/ppermute | solution.py:631
  102.6 1.7 collective-permute-done.33.d
  104.3 1.3 collective-permute-start.14
  106.3 7.4 %collective-permute-start.15 = (f32[1,128,1024]{2,1,0:T(8,128)S(1)}, f32[1,128,1024]{2,1,0:T(8,128)S(1)}, u32[]{:S(2)}, u32[]{:S(2)}) collective-permute-start(f32[1,128,1024]{2,1,0:T(8,128)S(1)} %get-tuple-element.81), channel_id=1, source_target_pairs={{2,1},{3,2},{6,5},{7,6},{10,9},{11,10},{14,13},{15,14},{18,17},{19... | collective-permute-start | bytes 1572872 | tf_op jit(solution)/shard_map/ppermute | solution.py:631
  113.7 1.8 %collective-permute-done.27.d = f32[1,128,1024]{2,1,0:T(8,128)S(1)} collective-permute-done((f32[1,128,1024]{2,1,0:T(8,128)S(1)}, f32[1,128,1024]{2,1,0:T(8,128)S(1)}, u32[]{:S(2)}, u32[]{:S(2)}) %collective-permute-start.27) | collective-permute-done | bytes 524320 | tf_op jit(solution)/shard_map/ppermute | solution.py:631
  115.5 1.9 %collective-permute-start.34 = (f32[1,128,1024]{2,1,0:T(8,128)S(1)}, f32[1,128,1024]{2,1,0:T(8,128)S(1)}, u32[]{:S(2)}, u32[]{:S(2)}) collective-permute-start(f32[1,128,1024]{2,1,0:T(8,128)S(1)} %get-tuple-element.97), channel_id=1, source_target_pairs={{0,1},{1,2},{2,3},{4,5},{5,6},{6,7},{8,9},{9,10},{10,11},{12,13},{... | collective-permute-start | bytes 1572872 | tf_op jit(solution)/shard_map/ppermute | solution.py:630
  118.2 6.8 %collective-permute-start.35 = (f32[1,128,1024]{2,1,0:T(8,128)S(1)}, f32[1,128,1024]{2,1,0:T(8,128)S(1)}, u32[]{:S(2)}, u32[]{:S(2)}) collective-permute-start(f32[1,128,1024]{2,1,0:T(8,128)S(1)} %get-tuple-element.98), channel_id=1, source_target_pairs={{1,0},{2,1},{3,2},{5,4},{6,5},{7,6},{9,8},{10,9},{11,10},{13,12},{... | collective-permute-start | bytes 1572872 | tf_op jit(solution)/shard_map/ppermute | solution.py:631
  124.9 1.8 %collective-permute-done.21.d = f32[1,128,1024]{2,1,0:T(8,128)S(1)} collective-permute-done((f32[1,128,1024]{2,1,0:T(8,128)S(1)}, f32[1,128,1024]{2,1,0:T(8,128)S(1)}, u32[]{:S(2)}, u32[]{:S(2)}) %collective-permute-start.21) | collective-permute-done | bytes 524320 | tf_op jit(solution)/shard_map/ppermute | solution.py:631
  126.8 1.9 %collective-permute-start.28 = (f32[1,128,1024]{2,1,0:T(8,128)S(1)}, f32[1,128,1024]{2,1,0:T(8,128)S(1)}, u32[]{:S(2)}, u32[]{:S(2)}) collective-permute-start(f32[1,128,1024]{2,1,0:T(8,128)S(1)} %get-tuple-element.92), channel_id=1, source_target_pairs={{0,1},{1,2},{2,3},{4,5},{5,6},{6,7},{8,9},{9,10},{10,11},{12,13},{... | collective-permute-start | bytes 1572872 | tf_op jit(solution)/shard_map/ppermute | solution.py:630
  129.4 6.8 %collective-permute-start.29 = (f32[1,128,1024]{2,1,0:T(8,128)S(1)}, f32[1,128,1024]{2,1,0:T(8,128)S(1)}, u32[]{:S(2)}, u32[]{:S(2)}) collective-permute-start(f32[1,128,1024]{2,1,0:T(8,128)S(1)} %get-tuple-element.93), channel_id=1, source_target_pairs={{1,0},{2,1},{3,2},{5,4},{6,5},{7,6},{9,8},{10,9},{11,10},{13,12},{... | collective-permute-start | bytes 1572872 | tf_op jit(solution)/shard_map/ppermute | solution.py:631
  136.2 1.8 %collective-permute-done.15.d = f32[1,128,1024]{2,1,0:T(8,128)S(1)} collective-permute-done((f32[1,128,1024]{2,1,0:T(8,128)S(1)}, f32[1,128,1024]{2,1,0:T(8,128)S(1)}, u32[]{:S(2)}, u32[]{:S(2)}) %collective-permute-start.15) | collective-permute-done | bytes 524320 | tf_op jit(solution)/shard_map/ppermute | solution.py:631
  138.0 1.9 %collective-permute-start.22 = (f32[1,128,1024]{2,1,0:T(8,128)S(1)}, f32[1,128,1024]{2,1,0:T(8,128)S(1)}, u32[]{:S(2)}, u32[]{:S(2)}) collective-permute-start(f32[1,128,1024]{2,1,0:T(8,128)S(1)} %get-tuple-element.87), channel_id=1, source_target_pairs={{0,1},{1,2},{2,3},{4,5},{5,6},{6,7},{8,9},{9,10},{10,11},{12,13},{... | collective-permute-start | bytes 1572872 | tf_op jit(solution)/shard_map/ppermute | solution.py:630
  140.6 6.8 %collective-permute-start.23 = (f32[1,128,1024]{2,1,0:T(8,128)S(1)}, f32[1,128,1024]{2,1,0:T(8,128)S(1)}, u32[]{:S(2)}, u32[]{:S(2)}) collective-permute-start(f32[1,128,1024]{2,1,0:T(8,128)S(1)} %get-tuple-element.88), channel_id=1, source_target_pairs={{1,0},{2,1},{3,2},{5,4},{6,5},{7,6},{9,8},{10,9},{11,10},{13,12},{... | collective-permute-start | bytes 1572872 | tf_op jit(solution)/shard_map/ppermute | solution.py:631
  147.4 1.8 %collective-permute-done.35.d = f32[1,128,1024]{2,1,0:T(8,128)S(1)} collective-permute-done((f32[1,128,1024]{2,1,0:T(8,128)S(1)}, f32[1,128,1024]{2,1,0:T(8,128)S(1)}, u32[]{:S(2)}, u32[]{:S(2)}) %collective-permute-start.35) | collective-permute-done | bytes 524320 | tf_op jit(solution)/shard_map/ppermute | solution.py:631
  149.2 1.9 %collective-permute-start.16 = (f32[1,128,1024]{2,1,0:T(8,128)S(1)}, f32[1,128,1024]{2,1,0:T(8,128)S(1)}, u32[]{:S(2)}, u32[]{:S(2)}) collective-permute-start(f32[1,128,1024]{2,1,0:T(8,128)S(1)} %get-tuple-element.82), channel_id=1, source_target_pairs={{0,1},{1,2},{2,3},{4,5},{5,6},{6,7},{8,9},{9,10},{10,11},{12,13},{... | collective-permute-start | bytes 1572872 | tf_op jit(solution)/shard_map/ppermute | solution.py:630
  151.2 7.4 %collective-permute-start.17 = (f32[1,128,1024]{2,1,0:T(8,128)S(1)}, f32[1,128,1024]{2,1,0:T(8,128)S(1)}, u32[]{:S(2)}, u32[]{:S(2)}) collective-permute-start(f32[1,128,1024]{2,1,0:T(8,128)S(1)} %get-tuple-element.83), channel_id=1, source_target_pairs={{1,0},{2,1},{3,2},{5,4},{6,5},{7,6},{9,8},{10,9},{11,10},{13,12},{... | collective-permute-start | bytes 1572872 | tf_op jit(solution)/shard_map/ppermute | solution.py:631
  159.5 1.0 collective-permute-done.29.d
  161.4 1.1 collective-permute-done.22.c
  162.4 9.3 %collective-permute-done.23.d = f32[1,128,1024]{2,1,0:T(8,128)S(1)} collective-permute-done((f32[1,128,1024]{2,1,0:T(8,128)S(1)}, f32[1,128,1024]{2,1,0:T(8,128)S(1)}, u32[]{:S(2)}, u32[]{:S(2)}) %collective-permute-start.23) | collective-permute-done | bytes 524320 | tf_op jit(solution)/shard_map/ppermute | solution.py:631
  172.6 8.8 %collective-permute-done.17.d = f32[1,128,1024]{2,1,0:T(8,128)S(1)} collective-permute-done((f32[1,128,1024]{2,1,0:T(8,128)S(1)}, f32[1,128,1024]{2,1,0:T(8,128)S(1)}, u32[]{:S(2)}, u32[]{:S(2)}) %collective-permute-start.17) | collective-permute-done | bytes 524320 | tf_op jit(solution)/shard_map/ppermute | solution.py:631
  (83 shorter events, 19.1 us)
Async XLA Ops:
  0.0 13.6 %copy-start.1 = (bf16[512,2048]{1,0:T(8,128)(2,1)S(1)}, bf16[512,2048]{1,0:T(8,128)(2,1)}, u32[]{:S(2)}) copy-start(bf16[512,2048]{1,0:T(8,128)(2,1)} %feat.1) | copy-start | bytes 6291460
  0.0 13.6 %copy-start.8 = (f32[32,512]{1,0:T(8,128)S(1)}, f32[32,512]{1,0:T(8,128)}, u32[]{:S(2)}) copy-start(f32[32,512]{1,0:T(8,128)} %decay.3) | copy-start | bytes 196612
  0.0 13.6 %copy-start.7 = (f32[32,512]{1,0:T(8,128)S(1)}, f32[32,512]{1,0:T(8,128)}, u32[]{:S(2)}) copy-start(f32[32,512]{1,0:T(8,128)} %step.3) | copy-start | bytes 196612
  0.0 13.6 %copy-start.10 = (s32[512]{0:T(512)S(1)}, s32[512]{0:T(512)}, u32[]{:S(2)}) copy-start(s32[512]{0:T(512)} %param.17) | copy-start | bytes 6148
  0.0 13.6 %copy-start.3 = (bf16[512,256]{1,0:T(8,128)(2,1)S(1)}, bf16[512,256]{1,0:T(8,128)(2,1)}, u32[]{:S(2)}) copy-start(bf16[512,256]{1,0:T(8,128)(2,1)} %refs_14_.3) | copy-start | bytes 786436
  0.0 13.6 %copy-start.11 = (f32[32]{0:T(128)S(1)}, f32[32]{0:T(128)}, u32[]{:S(2)}) copy-start(f32[32]{0:T(128)} %param.18) | copy-start | bytes 388
  6.4 2.5 %collective-permute-start = (f32[4,136,256]{2,1,0:T(8,128)}, f32[4,136,256]{2,1,0:T(8,128)S(1)}, u32[]{:S(2)}, u32[]{:S(2)}) collective-permute-start(f32[4,136,256]{2,1,0:T(8,128)} %get-tuple-element.55), channel_id=1, source_target_pairs={{0,4},{4,0},{8,12},{12,8},{16,20},{20,16},{24,28},{28,24},{1,5},{5... | collective-permute-start | bytes 1671176 | tf_op jit(solution)/shard_map/ppermute | solution.py:332
  6.5 17.0 %collective-permute-start.7 = (f32[4,136,256]{2,1,0:T(8,128)}, f32[4,136,256]{2,1,0:T(8,128)S(1)}, u32[]{:S(2)}, u32[]{:S(2)}) collective-permute-start(f32[4,136,256]{2,1,0:T(8,128)} %get-tuple-element.54.mine), channel_id=1, source_target_pairs={{0,4},{8,12},{16,20},{24,28},{1,5},{9,13},{17,21},{25,29},{2,6},{1... | collective-permute-start | bytes 1671176 | tf_op jit(solution)/shard_map/ppermute | solution.py:670
  10.0 7.4 %collective-permute-start.1 = (f32[136,256]{1,0:T(8,128)S(1)}, f32[136,256]{1,0:T(8,128)S(1)}, u32[]{:S(2)}, u32[]{:S(2)}) collective-permute-start(f32[136,256]{1,0:T(8,128)S(1)} %get-tuple-element.57), channel_id=1, source_target_pairs={{0,8},{4,12},{8,0},{12,4},{16,24},{20,28},{24,16},{28,20},{1,9},{5... | collective-permute-start | bytes 417800 | tf_op jit(solution)/shard_map/ppermute | solution.py:326
  11.6 8.1 %collective-permute-start.2 = (f32[136,256]{1,0:T(8,128)S(1)}, f32[136,256]{1,0:T(8,128)S(1)}, u32[]{:S(2)}, u32[]{:S(2)}) collective-permute-start(f32[136,256]{1,0:T(8,128)S(1)} %get-tuple-element.58), channel_id=1, source_target_pairs={{0,16},{4,20},{8,24},{12,28},{16,0},{20,4},{24,8},{28,12},{1,17},{... | collective-permute-start | bytes 417800 | tf_op jit(solution)/shard_map/ppermute | solution.py:326
  13.1 6.6 %collective-permute-start.3 = (f32[136,256]{1,0:T(8,128)S(1)}, f32[136,256]{1,0:T(8,128)S(1)}, u32[]{:S(2)}, u32[]{:S(2)}) collective-permute-start(f32[136,256]{1,0:T(8,128)S(1)} %get-tuple-element.59), channel_id=1, source_target_pairs={{0,24},{4,28},{8,16},{12,20},{16,8},{20,12},{24,0},{28,4},{1,25},{... | collective-permute-start | bytes 417800 | tf_op jit(solution)/shard_map/ppermute | solution.py:326
  14.6 8.8 %copy-start.2 = (f32[1,136,2048]{2,1,0:T(8,128)S(1)}, f32[1,136,2048]{2,1,0:T(8,128)}, u32[]{:S(2)}) copy-start(f32[1,136,2048]{2,1,0:T(8,128)} %get-tuple-element.68.refs_2_) | copy-start | bytes 3342340
  19.9 7.3 %collective-permute-start.4 = (f32[128,256]{1,0:T(8,128)S(1)}, f32[128,256]{1,0:T(8,128)S(1)}, u32[]{:S(2)}, u32[]{:S(2)}) collective-permute-start(f32[128,256]{1,0:T(8,128)S(1)} %get-tuple-element.62), channel_id=1, source_target_pairs={{0,8},{4,12},{8,0},{12,4},{16,24},{20,28},{24,16},{28,20},{1,9},{5... | collective-permute-start | bytes 393224 | tf_op jit(solution)/shard_map/ppermute | solution.py:326
  21.2 6.9 %collective-permute-start.5 = (f32[128,256]{1,0:T(8,128)S(1)}, f32[128,256]{1,0:T(8,128)S(1)}, u32[]{:S(2)}, u32[]{:S(2)}) collective-permute-start(f32[128,256]{1,0:T(8,128)S(1)} %get-tuple-element.63), channel_id=1, source_target_pairs={{0,16},{4,20},{8,24},{12,28},{16,0},{20,4},{24,8},{28,12},{1,17},{... | collective-permute-start | bytes 393224 | tf_op jit(solution)/shard_map/ppermute | solution.py:326
  22.0 6.1 %collective-permute-start.6 = (f32[128,256]{1,0:T(8,128)S(1)}, f32[128,256]{1,0:T(8,128)S(1)}, u32[]{:S(2)}, u32[]{:S(2)}) collective-permute-start(f32[128,256]{1,0:T(8,128)S(1)} %get-tuple-element.64), channel_id=1, source_target_pairs={{0,24},{4,28},{8,16},{12,20},{16,8},{20,12},{24,0},{28,4},{1,25},{... | collective-permute-start | bytes 393224 | tf_op jit(solution)/shard_map/ppermute | solution.py:326
  23.7 6.4 %copy-start = (bf16[512,2048]{1,0:T(8,128)(2,1)S(1)}, bf16[512,2048]{1,0:T(8,128)(2,1)}, u32[]{:S(2)}) copy-start(bf16[512,2048]{1,0:T(8,128)(2,1)} %refs_13_.3) | copy-start | bytes 6291460
  23.7 6.4 %copy-start.9 = (f32[2048]{0:T(1024)S(1)}, f32[2048]{0:T(1024)}, u32[]{:S(2)}) copy-start(f32[2048]{0:T(1024)} %param.19) | copy-start | bytes 24580
  28.1 1.3 collective-permute-start.8
  28.1 1.5 collective-permute-start.9
  28.6 1.3 collective-permute-start.10
  28.6 1.5 collective-permute-start.11
  30.1 16.8 %slice-start = ((s8[16777216]{0:T(1024)(128)(4,1)}), s8[4194304]{0:T(1024)(128)(4,1)S(1)}, s32[]{:S(2)}) async-start(s8[16777216]{0:T(1024)(128)(4,1)} %bitcast.7), calls=%async_computation | async-start | bytes 8388608
  30.1 16.9 %slice-start.1 = ((s8[16777216]{0:T(1024)(128)(4,1)}), s8[4194304]{0:T(1024)(128)(4,1)S(1)}, s32[]{:S(2)}) async-start(s8[16777216]{0:T(1024)(128)(4,1)} %bitcast.7), calls=%async_computation.1 | async-start | bytes 8388608
  30.1 16.9 %slice-start.2 = ((s8[16777216]{0:T(1024)(128)(4,1)}), s8[4194304]{0:T(1024)(128)(4,1)S(1)}, s32[]{:S(2)}) async-start(s8[16777216]{0:T(1024)(128)(4,1)} %bitcast.7), calls=%async_computation.2 | async-start | bytes 8388608
  37.5 53.9 %collective-permute-start.13 = (f32[1,128,1024]{2,1,0:T(8,128)S(1)}, f32[1,128,1024]{2,1,0:T(8,128)S(1)}, u32[]{:S(2)}, u32[]{:S(2)}) collective-permute-start(f32[1,128,1024]{2,1,0:T(8,128)S(1)} %get-tuple-element.79), channel_id=1, source_target_pairs={{3,2},{7,6},{11,10},{15,14},{19,18},{23,22},{27,26},{31,30}} | collective-permute-start | bytes 1572872 | tf_op jit(solution)/shard_map/ppermute | solution.py:631
  39.1 56.9 %collective-permute-start.12 = (f32[1,128,1024]{2,1,0:T(8,128)S(1)}, f32[1,128,1024]{2,1,0:T(8,128)S(1)}, u32[]{:S(2)}, u32[]{:S(2)}) collective-permute-start(f32[1,128,1024]{2,1,0:T(8,128)S(1)} %get-tuple-element.79), channel_id=1, source_target_pairs={{0,1},{4,5},{8,9},{12,13},{16,17},{20,21},{24,25},{28,29}} | collective-permute-start | bytes 1572872 | tf_op jit(solution)/shard_map/ppermute | solution.py:630
  39.8 25.9 %collective-permute-start.31 = (f32[1,128,1024]{2,1,0:T(8,128)S(1)}, f32[1,128,1024]{2,1,0:T(8,128)S(1)}, u32[]{:S(2)}, u32[]{:S(2)}) collective-permute-start(f32[1,128,1024]{2,1,0:T(8,128)S(1)} %get-tuple-element.94), channel_id=1, source_target_pairs={{3,2},{7,6},{11,10},{15,14},{19,18},{23,22},{27,26},{31,30}} | collective-permute-start | bytes 1572872 | tf_op jit(solution)/shard_map/ppermute | solution.py:631
  41.1 25.3 %collective-permute-start.30 = (f32[1,128,1024]{2,1,0:T(8,128)S(1)}, f32[1,128,1024]{2,1,0:T(8,128)S(1)}, u32[]{:S(2)}, u32[]{:S(2)}) collective-permute-start(f32[1,128,1024]{2,1,0:T(8,128)S(1)} %get-tuple-element.94), channel_id=1, source_target_pairs={{0,1},{4,5},{8,9},{12,13},{16,17},{20,21},{24,25},{28,29}} | collective-permute-start | bytes 1572872 | tf_op jit(solution)/shard_map/ppermute | solution.py:630
  41.8 35.1 %collective-permute-start.25 = (f32[1,128,1024]{2,1,0:T(8,128)S(1)}, f32[1,128,1024]{2,1,0:T(8,128)S(1)}, u32[]{:S(2)}, u32[]{:S(2)}) collective-permute-start(f32[1,128,1024]{2,1,0:T(8,128)S(1)} %get-tuple-element.89), channel_id=1, source_target_pairs={{3,2},{7,6},{11,10},{15,14},{19,18},{23,22},{27,26},{31,30}} | collective-permute-start | bytes 1572872 | tf_op jit(solution)/shard_map/ppermute | solution.py:631
  65.7 11.9 %collective-permute-start.24 = (f32[1,128,1024]{2,1,0:T(8,128)S(1)}, f32[1,128,1024]{2,1,0:T(8,128)S(1)}, u32[]{:S(2)}, u32[]{:S(2)}) collective-permute-start(f32[1,128,1024]{2,1,0:T(8,128)S(1)} %get-tuple-element.89), channel_id=1, source_target_pairs={{0,1},{4,5},{8,9},{12,13},{16,17},{20,21},{24,25},{28,29}} | collective-permute-start | bytes 1572872 | tf_op jit(solution)/shard_map/ppermute | solution.py:630
  66.4 21.2 %collective-permute-start.19 = (f32[1,128,1024]{2,1,0:T(8,128)S(1)}, f32[1,128,1024]{2,1,0:T(8,128)S(1)}, u32[]{:S(2)}, u32[]{:S(2)}) collective-permute-start(f32[1,128,1024]{2,1,0:T(8,128)S(1)} %get-tuple-element.84), channel_id=1, source_target_pairs={{3,2},{7,6},{11,10},{15,14},{19,18},{23,22},{27,26},{31,30}} | collective-permute-start | bytes 1572872 | tf_op jit(solution)/shard_map/ppermute | solution.py:631
  76.9 12.6 %collective-permute-start.18 = (f32[1,128,1024]{2,1,0:T(8,128)S(1)}, f32[1,128,1024]{2,1,0:T(8,128)S(1)}, u32[]{:S(2)}, u32[]{:S(2)}) collective-permute-start(f32[1,128,1024]{2,1,0:T(8,128)S(1)} %get-tuple-element.84), channel_id=1, source_target_pairs={{0,1},{4,5},{8,9},{12,13},{16,17},{20,21},{24,25},{28,29}} | collective-permute-start | bytes 1572872 | tf_op jit(solution)/shard_map/ppermute | solution.py:630
  77.6 20.4 %collective-permute-start.32 = (f32[1,128,1024]{2,1,0:T(8,128)S(1)}, f32[1,128,1024]{2,1,0:T(8,128)S(1)}, u32[]{:S(2)}, u32[]{:S(2)}) collective-permute-start(f32[1,128,1024]{2,1,0:T(8,128)S(1)} %get-tuple-element.95), channel_id=1, source_target_pairs={{0,1},{1,2},{4,5},{5,6},{8,9},{9,10},{12,13},{13,14},{16,17},{17,1... | collective-permute-start | bytes 1572872 | tf_op jit(solution)/shard_map/ppermute | solution.py:630
  87.6 16.7 %collective-permute-start.33 = (f32[1,128,1024]{2,1,0:T(8,128)S(1)}, f32[1,128,1024]{2,1,0:T(8,128)S(1)}, u32[]{:S(2)}, u32[]{:S(2)}) collective-permute-start(f32[1,128,1024]{2,1,0:T(8,128)S(1)} %get-tuple-element.96), channel_id=1, source_target_pairs={{2,1},{3,2},{6,5},{7,6},{10,9},{11,10},{14,13},{15,14},{18,17},{19... | collective-permute-start | bytes 1572872 | tf_op jit(solution)/shard_map/ppermute | solution.py:631
  89.5 16.8 %collective-permute-start.26 = (f32[1,128,1024]{2,1,0:T(8,128)S(1)}, f32[1,128,1024]{2,1,0:T(8,128)S(1)}, u32[]{:S(2)}, u32[]{:S(2)}) collective-permute-start(f32[1,128,1024]{2,1,0:T(8,128)S(1)} %get-tuple-element.90), channel_id=1, source_target_pairs={{0,1},{1,2},{4,5},{5,6},{8,9},{9,10},{12,13},{13,14},{16,17},{17,1... | collective-permute-start | bytes 1572872 | tf_op jit(solution)/shard_map/ppermute | solution.py:630
  91.5 24.1 %collective-permute-start.27 = (f32[1,128,1024]{2,1,0:T(8,128)S(1)}, f32[1,128,1024]{2,1,0:T(8,128)S(1)}, u32[]{:S(2)}, u32[]{:S(2)}) collective-permute-start(f32[1,128,1024]{2,1,0:T(8,128)S(1)} %get-tuple-element.91), channel_id=1, source_target_pairs={{2,1},{3,2},{6,5},{7,6},{10,9},{11,10},{14,13},{15,14},{18,17},{19... | collective-permute-start | bytes 1572872 | tf_op jit(solution)/shard_map/ppermute | solution.py:631
  96.0 22.1 %collective-permute-start.20 = (f32[1,128,1024]{2,1,0:T(8,128)S(1)}, f32[1,128,1024]{2,1,0:T(8,128)S(1)}, u32[]{:S(2)}, u32[]{:S(2)}) collective-permute-start(f32[1,128,1024]{2,1,0:T(8,128)S(1)} %get-tuple-element.85), channel_id=1, source_target_pairs={{0,1},{1,2},{4,5},{5,6},{8,9},{9,10},{12,13},{13,14},{16,17},{17,1... | collective-permute-start | bytes 1572872 | tf_op jit(solution)/shard_map/ppermute | solution.py:630
  98.0 28.7 %collective-permute-start.21 = (f32[1,128,1024]{2,1,0:T(8,128)S(1)}, f32[1,128,1024]{2,1,0:T(8,128)S(1)}, u32[]{:S(2)}, u32[]{:S(2)}) collective-permute-start(f32[1,128,1024]{2,1,0:T(8,128)S(1)} %get-tuple-element.86), channel_id=1, source_target_pairs={{2,1},{3,2},{6,5},{7,6},{10,9},{11,10},{14,13},{15,14},{18,17},{19... | collective-permute-start | bytes 1572872 | tf_op jit(solution)/shard_map/ppermute | solution.py:631
  104.3 25.1 %collective-permute-start.14 = (f32[1,128,1024]{2,1,0:T(8,128)S(1)}, f32[1,128,1024]{2,1,0:T(8,128)S(1)}, u32[]{:S(2)}, u32[]{:S(2)}) collective-permute-start(f32[1,128,1024]{2,1,0:T(8,128)S(1)} %get-tuple-element.80), channel_id=1, source_target_pairs={{0,1},{1,2},{4,5},{5,6},{8,9},{9,10},{12,13},{13,14},{16,17},{17,1... | collective-permute-start | bytes 1572872 | tf_op jit(solution)/shard_map/ppermute | solution.py:630
  106.3 31.7 %collective-permute-start.15 = (f32[1,128,1024]{2,1,0:T(8,128)S(1)}, f32[1,128,1024]{2,1,0:T(8,128)S(1)}, u32[]{:S(2)}, u32[]{:S(2)}) collective-permute-start(f32[1,128,1024]{2,1,0:T(8,128)S(1)} %get-tuple-element.81), channel_id=1, source_target_pairs={{2,1},{3,2},{6,5},{7,6},{10,9},{11,10},{14,13},{15,14},{18,17},{19... | collective-permute-start | bytes 1572872 | tf_op jit(solution)/shard_map/ppermute | solution.py:631
  115.5 25.0 %collective-permute-start.34 = (f32[1,128,1024]{2,1,0:T(8,128)S(1)}, f32[1,128,1024]{2,1,0:T(8,128)S(1)}, u32[]{:S(2)}, u32[]{:S(2)}) collective-permute-start(f32[1,128,1024]{2,1,0:T(8,128)S(1)} %get-tuple-element.97), channel_id=1, source_target_pairs={{0,1},{1,2},{2,3},{4,5},{5,6},{6,7},{8,9},{9,10},{10,11},{12,13},{... | collective-permute-start | bytes 1572872 | tf_op jit(solution)/shard_map/ppermute | solution.py:630
  118.2 31.1 %collective-permute-start.35 = (f32[1,128,1024]{2,1,0:T(8,128)S(1)}, f32[1,128,1024]{2,1,0:T(8,128)S(1)}, u32[]{:S(2)}, u32[]{:S(2)}) collective-permute-start(f32[1,128,1024]{2,1,0:T(8,128)S(1)} %get-tuple-element.98), channel_id=1, source_target_pairs={{1,0},{2,1},{3,2},{5,4},{6,5},{7,6},{9,8},{10,9},{11,10},{13,12},{... | collective-permute-start | bytes 1572872 | tf_op jit(solution)/shard_map/ppermute | solution.py:631
  126.8 24.4 %collective-permute-start.28 = (f32[1,128,1024]{2,1,0:T(8,128)S(1)}, f32[1,128,1024]{2,1,0:T(8,128)S(1)}, u32[]{:S(2)}, u32[]{:S(2)}) collective-permute-start(f32[1,128,1024]{2,1,0:T(8,128)S(1)} %get-tuple-element.92), channel_id=1, source_target_pairs={{0,1},{1,2},{2,3},{4,5},{5,6},{6,7},{8,9},{9,10},{10,11},{12,13},{... | collective-permute-start | bytes 1572872 | tf_op jit(solution)/shard_map/ppermute | solution.py:630
  129.4 31.1 %collective-permute-start.29 = (f32[1,128,1024]{2,1,0:T(8,128)S(1)}, f32[1,128,1024]{2,1,0:T(8,128)S(1)}, u32[]{:S(2)}, u32[]{:S(2)}) collective-permute-start(f32[1,128,1024]{2,1,0:T(8,128)S(1)} %get-tuple-element.93), channel_id=1, source_target_pairs={{1,0},{2,1},{3,2},{5,4},{6,5},{7,6},{9,8},{10,9},{11,10},{13,12},{... | collective-permute-start | bytes 1572872 | tf_op jit(solution)/shard_map/ppermute | solution.py:631
  138.0 24.4 %collective-permute-start.22 = (f32[1,128,1024]{2,1,0:T(8,128)S(1)}, f32[1,128,1024]{2,1,0:T(8,128)S(1)}, u32[]{:S(2)}, u32[]{:S(2)}) collective-permute-start(f32[1,128,1024]{2,1,0:T(8,128)S(1)} %get-tuple-element.87), channel_id=1, source_target_pairs={{0,1},{1,2},{2,3},{4,5},{5,6},{6,7},{8,9},{9,10},{10,11},{12,13},{... | collective-permute-start | bytes 1572872 | tf_op jit(solution)/shard_map/ppermute | solution.py:630
  140.6 31.1 %collective-permute-start.23 = (f32[1,128,1024]{2,1,0:T(8,128)S(1)}, f32[1,128,1024]{2,1,0:T(8,128)S(1)}, u32[]{:S(2)}, u32[]{:S(2)}) collective-permute-start(f32[1,128,1024]{2,1,0:T(8,128)S(1)} %get-tuple-element.88), channel_id=1, source_target_pairs={{1,0},{2,1},{3,2},{5,4},{6,5},{7,6},{9,8},{10,9},{11,10},{13,12},{... | collective-permute-start | bytes 1572872 | tf_op jit(solution)/shard_map/ppermute | solution.py:631
  149.2 23.4 %collective-permute-start.16 = (f32[1,128,1024]{2,1,0:T(8,128)S(1)}, f32[1,128,1024]{2,1,0:T(8,128)S(1)}, u32[]{:S(2)}, u32[]{:S(2)}) collective-permute-start(f32[1,128,1024]{2,1,0:T(8,128)S(1)} %get-tuple-element.82), channel_id=1, source_target_pairs={{0,1},{1,2},{2,3},{4,5},{5,6},{6,7},{8,9},{9,10},{10,11},{12,13},{... | collective-permute-start | bytes 1572872 | tf_op jit(solution)/shard_map/ppermute | solution.py:630
  151.2 30.3 %collective-permute-start.17 = (f32[1,128,1024]{2,1,0:T(8,128)S(1)}, f32[1,128,1024]{2,1,0:T(8,128)S(1)}, u32[]{:S(2)}, u32[]{:S(2)}) collective-permute-start(f32[1,128,1024]{2,1,0:T(8,128)S(1)} %get-tuple-element.83), channel_id=1, source_target_pairs={{1,0},{2,1},{3,2},{5,4},{6,5},{7,6},{9,8},{10,9},{11,10},{13,12},{... | collective-permute-start | bytes 1572872 | tf_op jit(solution)/shard_map/ppermute | solution.py:631
  (4 other events, 8.2 us)

commit v3 on v2

v3 whole, which is shorter than its diff:
```python
import jax
import jax.numpy as jnp
import numpy as np
from jax import lax
from jax.experimental import pallas as pl
from jax.experimental.pallas import tpu as pltpu
from jax.sharding import PartitionSpec as P

HEADS = 128
HEAD_DIM = 64
NSTATE = 128
GROUPS = 8
SPAN = 256
KROWS = 8
LOG2E = 1.4426950408889634
MIB = 1024 * 1024

eps = 1e-05
F32 = jnp.float32
BF16 = jnp.bfloat16


def three_parts(value, axis):
    high = value.astype(BF16)
    rest = value - high.astype(F32)
    middle = rest.astype(BF16)
    low = (rest - middle.astype(F32)).astype(BF16)
    return jnp.concatenate([high, middle, low], axis=axis)


def head_spread(heads, channels):
    row = lax.broadcasted_iota(jnp.int32, (3 * heads, channels), 0)
    col = lax.broadcasted_iota(jnp.int32, (3 * heads, channels), 1)
    return jnp.where(lax.rem(row, heads) == lax.div(col, HEAD_DIM), 1.0, 0.0).astype(BF16)


def dot(a, b, contract=((1,), (0,))):
    return lax.dot_general(a, b, (contract, ((), ())), preferred_element_type=F32)


def block_sums(decay, starts):
    heads = decay.shape[0]
    row = lax.broadcasted_iota(jnp.int32, (SPAN, SPAN), 0)
    col = lax.broadcasted_iota(jnp.int32, (SPAN, SPAN), 1)
    upper = jnp.where(row <= col, 1.0, 0.0).astype(BF16)
    begins = jnp.broadcast_to(starts.astype(F32), (16, SPAN)).astype(BF16)
    sums = dot(jnp.concatenate([three_parts(decay, 0), begins], axis=0), upper)
    cum = sums[:heads] + sums[heads : 2 * heads] + sums[2 * heads : 3 * heads]
    return cum, sums[3 * heads : 3 * heads + 8]


def position(direct):
    if not direct:
        return 0, 0
    me = lax.axis_index("ctx").astype(jnp.int32)
    return lax.rem(me, 2), lax.div(me, 2)


def cut(start, size, step=128):
    return pl.ds(start if isinstance(start, int) else pl.multiple_of(start, step), size)


def params(mib):
    return pltpu.CompilerParams(vmem_limit_bytes=mib * MIB)


def states_call(side, direct, features, write_proj, step_size, log_decay, starts, pieces, after):
    tokens, channels = features.shape
    groups = write_proj.shape[1] // NSTATE
    blocks = tokens // SPAN
    parts = max(1, groups // 2)
    heads, size = step_size.shape[0] // 2, channels // 2
    per_part, gch = heads // parts, size // parts
    width = size // pieces

    def kernel(
        feat_hbm, write_hbm, step_hbm, decay_hbm, starts_hbm, after, out, pre,
        feat, write, step, decay, starts, total, sems, write_sems, small_sems,
    ):
        core, _ = position(direct)
        half = core if side == 0 else 1 - core
        rows = cut(half * heads, heads, 8)
        small = [
            pltpu.make_async_copy(src, dst, small_sems.at[k])
            for k, (src, dst) in enumerate(
                [(decay_hbm.at[rows], decay), (starts_hbm, starts), (step_hbm.at[rows], step)]
            )
        ]
        for copy in small:
            copy.start()
        copies = []
        for part in range(parts):
            group = half * parts + part if groups > 1 else 0
            copy = pltpu.make_async_copy(
                write_hbm.at[:, cut(group * NSTATE, NSTATE)], write.at[part], write_sems.at[part]
            )
            copy.start()
            copies.append(copy)
            for block in range(blocks):
                copy = pltpu.make_async_copy(
                    feat_hbm.at[
                        pl.ds(block * SPAN, SPAN), cut(half * size + part * gch, gch)
                    ],
                    feat.at[part, block],
                    sems.at[part, block],
                )
                copy.start()
                copies.append(copy)
        spread = head_spread(per_part, gch)
        for copy in small:
            copy.wait()
        scales = []
        for block in range(blocks):
            span = slice(block * SPAN, (block + 1) * SPAN)
            cum, seg = block_sums(decay[:, span], starts[:, span])
            seg_last, last = seg[0:1, SPAN - 1 :], cum[:, SPAN - 1 :]
            tail = jnp.where(seg[0:1] == seg_last, jnp.exp(last - cum), 0.0) * step[:, span]
            keep = jnp.where(seg_last == 0.0, jnp.exp(last), 0.0)
            scales.append((tail, jnp.broadcast_to(keep, (heads, 128))))
        for part in range(parts):
            rows = slice(part * per_part, (part + 1) * per_part)
            lanes = slice(part * gch, (part + 1) * gch)
            copies.pop(0).wait()
            for block in range(blocks):
                tail, keep = scales[block]
                tail = dot(three_parts(tail[rows], 0), spread, ((0,), (0,)))
                keep = dot(three_parts(keep[rows], 0), spread, ((0,), (0,)))[:KROWS]
                copies.pop(0).wait()
                scaled = (tail * feat[part, block].astype(F32)).astype(BF16)
                state = dot(write[part, block * SPAN : (block + 1) * SPAN], scaled, ((0,), (0,)))
                if block > 0:
                    state = keep[0:1] * total[:NSTATE, lanes] + state
                    keep = keep * total[NSTATE:, lanes]
                total[:NSTATE, lanes] = state
                total[NSTATE:, lanes] = keep
                if block < blocks - 1:
                    pre[block, :NSTATE, lanes] = state
                    pre[block, NSTATE:, lanes] = keep
        for piece in range(pieces):
            out[piece] = total[:, piece * width : (piece + 1) * width]

    vmem = pl.BlockSpec(memory_space=pltpu.VMEM)
    return pl.pallas_call(
        kernel,
        in_specs=[pl.BlockSpec(memory_space=pltpu.HBM)] * 5 + [pl.BlockSpec(memory_space=pl.ANY)],
        out_specs=[vmem] * 2,
        scratch_shapes=[
            pltpu.VMEM((parts, blocks, SPAN, gch), BF16),
            pltpu.VMEM((parts, tokens, NSTATE), BF16),
            pltpu.VMEM((heads, tokens), F32),
            pltpu.VMEM((heads, tokens), F32),
            pltpu.VMEM((1, tokens), jnp.int32),
            pltpu.VMEM((NSTATE + KROWS, size), F32),
            pltpu.SemaphoreType.DMA((parts, blocks)),
            pltpu.SemaphoreType.DMA((parts,)),
            pltpu.SemaphoreType.DMA((3,)),
        ],
        out_shape=[
            jax.ShapeDtypeStruct((pieces, NSTATE + KROWS, width), F32),
            jax.ShapeDtypeStruct((blocks - 1, NSTATE + KROWS, size), F32),
        ],
        compiler_params=params(60 if side else 44),
        cost_estimate=pl.CostEstimate(flops=10**8, bytes_accessed=10**6, transcendentals=0),
        name="states",
    )(features, write_proj, step_size, log_decay, starts.reshape(1, tokens), after)


def intra_call(scal, side, features, write_proj, read_proj, step_size, log_decay, starts, skip_weight, after):
    tokens, channels = features.shape
    heads = step_size.shape[0]
    groups = write_proj.shape[1] // NSTATE
    per_group, gch = heads // groups, channels // groups
    blocks = tokens // SPAN
    half = SPAN // 2

    def group(s):
        return s[0] ^ side if groups > 1 else 0

    def kernel(scal, feat, write, read, step, decay, starts, skip, after, out, reach):
        cum, seg = block_sums(decay[...], starts[...])
        cum_log2 = cum * LOG2E
        vrow = cum_log2 - jnp.log2(step[...])
        far = jnp.where(seg[0:1] == 0.0, jnp.exp(cum), 0.0)
        fill = jnp.zeros((128 - 2 * per_group - 8, SPAN), F32)
        cols = jnp.concatenate([far, cum_log2, seg, fill], axis=0).T
        reach[...] = cols
        x = feat[...]
        scores = dot(read[...], write[...], ((1,), (1,)))
        row = lax.broadcasted_iota(jnp.int32, (SPAN, SPAN), 0)
        col = lax.broadcasted_iota(jnp.int32, (SPAN, SPAN), 1)
        together = (cols[:, 2 * per_group : 2 * per_group + 1] == seg[0:1]) & (row >= col)
        scores = jnp.where(together, scores, 0.0)
        own = skip[:, :per_group]
        for other in range(1, groups):
            theirs = skip[:, other * per_group : (other + 1) * per_group]
            own = jnp.where(group(scal) == other, theirs, own)
        own = jnp.broadcast_to(own, (8, per_group))
        skip_row = dot(three_parts(own, 1), head_spread(per_group, gch))[0:1]
        lane = lax.broadcasted_iota(jnp.int32, (SPAN, 2 * HEAD_DIM), 1)
        for pair in range(per_group // 2):
            part = slice(pair * 2 * HEAD_DIM, (pair + 1) * 2 * HEAD_DIM)
            xp = x[:, part]
            top = skip_row[:, part] * xp[:half].astype(F32)
            low = skip_row[:, part] * xp[half:].astype(F32)
            for which in range(2):
                head = 2 * pair + which
                mine = (lane >= HEAD_DIM) if which else (lane < HEAD_DIM)
                xh = jnp.where(mine, xp, jnp.zeros_like(xp))
                ci = cols[:, per_group + head : per_group + head + 1]
                vj = vrow[head : head + 1, :]
                w_top = jnp.exp2(jnp.minimum(ci[:half] - vj[:, :half], 1.0)) * scores[:half, :half]
                w_low = jnp.exp2(jnp.minimum(ci[half:] - vj, 1.0)) * scores[half:]
                top = top + dot(w_top.astype(BF16), xh[:half])
                low = low + dot(w_low.astype(BF16), xh)
            out[:half, part] = top
            out[half:, part] = low

    return pl.pallas_call(
        kernel,
        grid_spec=pltpu.PrefetchScalarGridSpec(
            num_scalar_prefetch=1,
            grid=(blocks,),
            in_specs=[
                pl.BlockSpec((SPAN, gch), lambda b, s: (b, group(s))),
                pl.BlockSpec((SPAN, NSTATE), lambda b, s: (b, group(s))),
                pl.BlockSpec((SPAN, NSTATE), lambda b, s: (b, group(s))),
                pl.BlockSpec((per_group, SPAN), lambda b, s: (group(s), b)),
                pl.BlockSpec((per_group, SPAN), lambda b, s: (group(s), b)),
                pl.BlockSpec((1, SPAN), lambda b, s: (0, b)),
                pl.BlockSpec((1, heads), lambda b, s: (0, 0)),
                pl.BlockSpec(memory_space=pl.ANY),
            ],
            out_specs=[
                pl.BlockSpec((SPAN, gch), lambda b, s: (b, 0)),
                pl.BlockSpec((SPAN, 128), lambda b, s: (b, 0)),
            ],
        ),
        out_shape=[
            jax.ShapeDtypeStruct((tokens, gch), F32),
            jax.ShapeDtypeStruct((tokens, 128), F32),
        ],
        compiler_params=params(12),
        cost_estimate=pl.CostEstimate(flops=10**9, bytes_accessed=10**6, transcendentals=0),
        name="intra",
    )(
        scal,
        features,
        write_proj,
        read_proj,
        step_size,
        log_decay,
        starts.reshape(1, tokens),
        skip_weight.reshape(1, heads),
        after,
    )


def chip_call(mine, theirs):
    pieces, rows, width = mine.shape

    def kernel(mine, theirs, *outs):
        core, chip = position(True)
        first_core = core == 0
        for offset in range(pieces):
            piece = chip ^ offset
            a, b = mine[piece], theirs[piece]
            first, second = jnp.where(first_core, a, b), jnp.where(first_core, b, a)
            keep = second[NSTATE:]
            outs[offset][:NSTATE] = keep[0:1] * first[:NSTATE] + second[:NSTATE]
            outs[offset][NSTATE:] = keep * first[NSTATE:]

    vmem = pl.BlockSpec(memory_space=pltpu.VMEM)
    return pl.pallas_call(
        kernel,
        in_specs=[vmem, vmem],
        out_specs=[vmem] * pieces,
        out_shape=[jax.ShapeDtypeStruct((rows, width), F32)] * pieces,
        compiler_params=params(6),
        name="chip_states",
    )(mine, theirs)


def prefix_call(parts, after):
    pieces, (rows, width) = len(parts), parts[0].shape

    def kernel(*refs):
        _, chip_here = position(True)
        ins, outs, stack = refs[:pieces], refs[pieces + 1 : 2 * pieces + 1], refs[2 * pieces + 1]
        for offset in range(pieces):
            stack[chip_here ^ offset] = ins[offset][...]
        entry = jnp.zeros((NSTATE, width), F32)
        for chip in range(pieces):
            state, keep = stack[chip, :NSTATE], stack[chip, NSTATE : NSTATE + 1]
            stack[chip, :NSTATE] = entry
            entry = keep * entry + state
        for offset in range(pieces):
            outs[offset][...] = stack[chip_here ^ offset, :NSTATE]

    vmem = pl.BlockSpec(memory_space=pltpu.VMEM)
    return pl.pallas_call(
        kernel,
        in_specs=[vmem] * pieces + [pl.BlockSpec(memory_space=pl.ANY)],
        out_specs=[vmem] * pieces,
        scratch_shapes=[pltpu.VMEM((pieces, rows, width), F32)],
        out_shape=[jax.ShapeDtypeStruct((NSTATE, width), F32)] * pieces,
        compiler_params=params(4),
        name="prefix",
    )(*parts, after)


def fold_call(theirs, pre, tokens, at=()):
    size = pre.shape[2]
    blocks = tokens // SPAN

    def kernel(*refs):
        pre, out = refs[-2:]
        state, keep = jnp.zeros((NSTATE, size), F32), jnp.ones((KROWS, size), F32)
        if theirs:
            core, _ = position(True)
            before = refs[0]
            before = jnp.concatenate(
                [before[(*at, p)] for p in range(theirs[0].shape[-3])], axis=1
            )
            state = jnp.where(core == 0, state, before[:NSTATE])
            keep = jnp.where(core == 0, keep, before[NSTATE:])
        out[0, :NSTATE] = state
        out[0, NSTATE:] = keep
        for block in range(1, blocks):
            here = pre[block - 1]
            out[block, :NSTATE] = here[NSTATE : NSTATE + 1] * state + here[:NSTATE]
            out[block, NSTATE:] = here[NSTATE:] * keep

    vmem = pl.BlockSpec(memory_space=pltpu.VMEM)
    return pl.pallas_call(
        kernel,
        in_specs=[vmem] * (len(theirs) + 1),
        out_specs=vmem,
        out_shape=jax.ShapeDtypeStruct((blocks, NSTATE + KROWS, size), F32),
        compiler_params=params(8),
        name="fold",
    )(*theirs, pre)


def pack_call(entries, mine):
    pieces, rows, width = mine.shape

    def kernel(*refs):
        mine, out = refs[-2:]
        for piece in range(pieces):
            out[0, piece, :NSTATE] = refs[piece][...]
            out[0, piece, NSTATE:] = jnp.zeros((rows - NSTATE, width), F32)
            out[1, piece] = mine[piece]

    vmem = pl.BlockSpec(memory_space=pltpu.VMEM)
    return pl.pallas_call(
        kernel,
        in_specs=[vmem] * (pieces + 1),
        out_specs=vmem,
        out_shape=jax.ShapeDtypeStruct((2, *mine.shape), F32),
        compiler_params=params(6),
        name="pack",
    )(*entries, mine)


def exchange(parts, axis):
    count = lax.axis_size(axis)
    return [parts[0]] + [
        lax.ppermute(parts[k], axis, [(i, i ^ (2 * k)) for i in range(count)])
        for k in range(1, len(parts))
    ]


def over(value, axis):
    return lax.ppermute(value, axis, [(i, i ^ 1) for i in range(lax.axis_size(axis))])


def chain(total, axis):
    count = lax.axis_size(axis)
    state, keep = total[:, :NSTATE], total[:, NSTATE : NSTATE + 1]
    steps = [(i, i + 1) for i in range(count - 1)]

    def step(index, incoming):
        return lax.ppermute(keep * incoming + state, axis, steps)

    return lax.fori_loop(0, count - 1, step, jnp.zeros_like(state))


def hold_entries(chip, entries, fold, held):
    pieces, _, width = held.shape
    for offset in range(pieces):
        piece = chip ^ offset
        part = cut(piece * width, width)
        entry = entries[0, offset, :NSTATE]
        held[piece] = (fold[NSTATE : NSTATE + 1, part] * entry + fold[:NSTATE, part]).astype(BF16)


def group_normed(held, c_rows, inner, reach, gate, gain):
    gch = inner.shape[1]
    per_group = gch // HEAD_DIM
    far = dot(three_parts(reach[:, :per_group], 1), head_spread(per_group, gch))
    carried = [dot(c_rows, piece) for piece in held]
    y = inner + far * (jnp.concatenate(carried, axis=1) if len(carried) > 1 else carried[0])
    g = gate.astype(F32)
    gated = y * (g / (1.0 + jnp.exp(-g)))
    mean_square = jnp.mean(gated * gated, axis=1, keepdims=True)
    return (gated * lax.rsqrt(mean_square + eps) * gain).astype(BF16)


def first_call(scal, sides, entries, fold, inner, reach, gate, read, gain, out_weight, rows, columns, early, before):
    tokens, channels = gate.shape
    gch = inner.shape[1]
    groups = channels // gch
    parts, width = entries[0].shape[1], entries[0].shape[3]
    wide = early * columns
    tile = min(512, columns)
    last = groups == 1 or bool(before)

    def group(s):
        return s[0] ^ sides[0] if groups > 1 else 0

    def kernel(scal, *refs):
        entry_refs, refs = refs[: len(sides)], refs[len(sides) :]
        folds, refs = refs[: len(sides)], refs[len(sides) :]
        inner, reach, read, gain, gate_hbm, w_hbm = refs[:6]
        earlier, refs = refs[6 : 6 + len(before)], refs[6 + len(before) :]
        out, *firsts, weight, gate, held, sems, gate_sem = refs
        lanes = cut(group(scal) * gch, gch)
        gate_copy = pltpu.make_async_copy(
            gate_hbm.at[cut(scal[2] * rows, rows, rows), lanes], gate, gate_sem
        )
        gate_copy.start()
        copies = []
        for t in range(wide // tile):
            copy = pltpu.make_async_copy(
                w_hbm.at[cut(group(scal) * gch, gch), pl.ds(t * tile, tile)], weight.at[t], sems.at[t]
            )
            copy.start()
            copies.append(copy)
        for k in range(len(sides)):
            hold_entries(scal[1], entry_refs[k], folds[k].at[0], held.at[k])
        gate_copy.wait()
        pieces = [held[k, p] for k in range(len(sides)) for p in range(parts)]
        normed = group_normed(pieces, read[...], inner[...], reach[...], gate[...], gain[...])
        if last:
            out[0, :, lanes] = normed
            if before:
                out[0, :, cut((1 - group(scal)) * gch, gch)] = earlier[0][...]
        else:
            out[...] = normed
        for t in range(wide // tile):
            copies[t].wait()
            product = dot(normed, weight[t])
            here = slice(t * tile, (t + 1) * tile)
            if not last:
                firsts[0][:, here] = product
                continue
            if before:
                product = product + earlier[1][:, here]
            at = t * tile % columns
            firsts[t * tile // columns][0, :, at : at + tile] = product

    def whole(value):
        zeros = (0,) * value.ndim
        return pl.BlockSpec(value.shape, lambda j, s: zeros)

    def chunk(size):
        return pl.BlockSpec((rows, size), lambda j, s: (s[2], 0))

    if last:
        shapes = [((1, rows, channels), BF16)] + [((1, rows, columns), F32)] * (wide // columns)
    else:
        shapes = [((rows, gch), BF16), ((rows, wide), F32)]
    return pl.pallas_call(
        kernel,
        grid_spec=pltpu.PrefetchScalarGridSpec(
            num_scalar_prefetch=1,
            grid=(1,),
            in_specs=[whole(v) for v in entries]
            + [pl.BlockSpec((1, *f.shape[1:]), lambda j, s: (lax.div(s[2] * rows, SPAN), 0, 0)) for f in fold]
            + [
                chunk(gch),
                chunk(128),
                pl.BlockSpec((rows, NSTATE), lambda j, s: (s[2], group(s))),
                pl.BlockSpec((1, gch), lambda j, s: (0, group(s))),
                pl.BlockSpec(memory_space=pltpu.HBM),
                pl.BlockSpec(memory_space=pltpu.HBM),
            ]
            + [whole(v) for v in before],
            out_specs=[
                pl.BlockSpec(shape, lambda j, s, zeros=(0,) * len(shape): zeros) for shape, _ in shapes
            ],
            scratch_shapes=[
                pltpu.VMEM((wide // tile, gch, tile), BF16),
                pltpu.VMEM((rows, gch), BF16),
                pltpu.VMEM((len(sides), parts, NSTATE, width), BF16),
                pltpu.SemaphoreType.DMA((wide // tile,)),
                pltpu.SemaphoreType.DMA(()),
            ],
        ),
        out_shape=[jax.ShapeDtypeStruct(shape, kind) for shape, kind in shapes],
        compiler_params=params(40),
        name="first",
    )(scal, *entries, *fold, inner, reach, read, gain, gate, out_weight, *before)


def rest_call(scal, entries, fold, inner, reach, gate, read, gain, rows):
    tokens, channels = gate.shape
    groups, parts, width = len(inner), entries[0].shape[1], entries[0].shape[3]
    count, blocks = tokens // rows, tokens // SPAN
    gch = channels // groups

    def kernel(scal, *refs):
        entry_refs, refs = refs[:2], refs[2:]
        inner, reach, refs = refs[:groups], refs[groups : 2 * groups], refs[2 * groups :]
        folds, refs = refs[:2], refs[2:]
        gate_hbm, read, gain, out, gate, held, sems = refs
        step = pl.program_id(0)

        def gate_copy(k):
            first_row = pl.multiple_of(scal[3 + k] * rows, rows)
            return pltpu.make_async_copy(gate_hbm.at[pl.ds(first_row, rows)], gate.at[k], sems.at[k])

        @pl.when(step == 0)
        def _():
            for k in range(count - 1):
                gate_copy(k).start()
            for block in range(blocks):
                for side in range(2):
                    hold_entries(scal[1], entry_refs[side], folds[side].at[block], held.at[block, side])

        gate_copy(step).wait()
        blk = lax.div(scal[3 + step] * rows, SPAN)
        for k in range(groups):
            group = scal[0] ^ k if groups > 1 else 0
            sides = [k] if groups > 1 else [0, 1]
            pieces = [held[blk, side, p] for side in sides for p in range(parts)]
            lanes = cut(group * gch, gch)
            c_rows = read[:, cut(group * NSTATE, NSTATE)]
            out[0, :, lanes] = group_normed(
                pieces, c_rows, inner[k][...], reach[k][...], gate[step, :, lanes], gain[:, lanes]
            )

    def whole(value):
        zeros = (0,) * value.ndim
        return pl.BlockSpec(value.shape, lambda j, s: zeros)

    def chunk(size):
        return pl.BlockSpec((rows, size), lambda j, s: (s[3 + j], 0))

    return pl.pallas_call(
        kernel,
        grid_spec=pltpu.PrefetchScalarGridSpec(
            num_scalar_prefetch=1,
            grid=(count - 1,),
            in_specs=[whole(v) for v in entries]
            + [chunk(gch)] * groups
            + [chunk(128)] * groups
            + [whole(f) for f in fold]
            + [pl.BlockSpec(memory_space=pltpu.HBM)]
            + [chunk(groups * NSTATE), whole(gain)],
            out_specs=pl.BlockSpec((1, rows, channels), lambda j, s: (j, 0, 0)),
            scratch_shapes=[
                pltpu.VMEM((count - 1, rows, channels), BF16),
                pltpu.VMEM((blocks, 2, parts, NSTATE, width), BF16),
                pltpu.SemaphoreType.DMA((count - 1,)),
            ],
        ),
        out_shape=jax.ShapeDtypeStruct((count - 1, rows, channels), BF16),
        compiler_params=params(14),
        cost_estimate=pl.CostEstimate(flops=10**9, bytes_accessed=10**6, transcendentals=0),
        name="rest",
    )(scal, *entries, *inner, *reach, *fold, gate, read, gain)


def project_call(parts, out_weight, start, columns, pieces=1):
    chunks, rows, channels = sum(p.shape[0] for p in parts), *parts[0].shape[1:]
    width = columns // pieces
    tile = min(512, width)
    tiles = columns // tile

    def kernel(*refs):
        w_hbm, *outs, weight, sems = refs[len(parts) :]
        copies = []
        for t in range(tiles):
            copy = pltpu.make_async_copy(
                w_hbm.at[:, pl.ds(start + t * tile, tile)], weight.at[t], sems.at[t]
            )
            copy.start()
            copies.append(copy)
        for t in range(tiles):
            copies[t].wait()
            at = 0
            for part in refs[: len(parts)]:
                size = part.shape[0]
                product = dot(part[...].reshape(size * rows, channels), weight[t])
                out, column = outs[t * tile // width], t * tile % width
                out[at : at + size, :, column : column + tile] = product.reshape(size, rows, tile)
                at += size

    vmem = pl.BlockSpec(memory_space=pltpu.VMEM)
    return pl.pallas_call(
        kernel,
        in_specs=[vmem] * len(parts) + [pl.BlockSpec(memory_space=pltpu.HBM)],
        out_specs=[vmem] * pieces,
        out_shape=[jax.ShapeDtypeStruct((chunks, rows, width), F32)] * pieces,
        scratch_shapes=[
            pltpu.VMEM((tiles, channels, tile), BF16),
            pltpu.SemaphoreType.DMA((tiles,)),
        ],
        compiler_params=params(40),
        cost_estimate=pl.CostEstimate(
            flops=2 * chunks * rows * channels * columns,
            bytes_accessed=2 * channels * columns + 4 * chunks * rows * columns,
            transcendentals=0,
        ),
        name="project",
    )(*parts, out_weight)


def line_tables(count):
    order, up, down = [], np.zeros((count, count), np.int32), np.zeros((count, count), np.int32)
    for me in range(count):
        def step(c):
            return count - c + me if c > me else (count + c - me if c < me else 10 * count)

        order.append(sorted(range(count), key=lambda c: (step(c), abs(c - me))))
        for s in range(1, count):
            if me < count - 1 and s > me:
                up[me, s] = order[me].index(count - s + me)
            if me > 0 and s > count - 1 - me:
                down[me, s] = order[me].index(s - count + me)
    return np.concatenate([np.array(order, np.int32), up, down], axis=1)


def sum_call(scal, mine, up, down, step):
    count, rows, width = mine.shape
    tile = min(1024, width)
    moving = pl.BlockSpec((1, rows, tile), lambda j, s: (0, 0, j))
    at_up, at_down = 2 + count + step, 2 + 2 * count + step

    def kernel(scal, a, b, c, d, out_up, out_down):
        out_up[...] = a[...] + c[...]
        out_down[...] = b[...] + d[...]

    return pl.pallas_call(
        kernel,
        grid_spec=pltpu.PrefetchScalarGridSpec(
            num_scalar_prefetch=1,
            grid=(width // tile,),
            in_specs=[
                pl.BlockSpec((1, rows, tile), lambda j, s: (s[at_up], 0, j)),
                pl.BlockSpec((1, rows, tile), lambda j, s: (s[at_down], 0, j)),
                moving,
                moving,
            ],
            out_specs=[moving, moving],
        ),
        out_shape=[jax.ShapeDtypeStruct(up.shape, F32)] * 2,
        cost_estimate=pl.CostEstimate(
            flops=10**10, bytes_accessed=24 * rows * width, transcendentals=0
        ),
        compiler_params=params(8),
        name="sum",
    )(scal, mine, mine, up, down)


def last_call(so_far, mine, up, down, first, wide):
    count, rows, width = mine.shape
    tile = min(512, width)
    moving = pl.BlockSpec((1, rows, tile), lambda j: (0, 0, j))

    def kernel(a, c, d, *refs):
        refs[-1][...] = (a[0] + c[0] + d[0]).astype(BF16)

    more = [] if so_far is None else [so_far]
    return pl.pallas_call(
        kernel,
        grid=(width // tile,),
        in_specs=[pl.BlockSpec((1, rows, tile), lambda j: (count - 1, 0, j)), moving, moving]
        + [pl.BlockSpec(memory_space=pl.ANY)] * len(more),
        out_specs=pl.BlockSpec((rows, tile), lambda j: (0, first // tile + j)),
        out_shape=jax.ShapeDtypeStruct((rows, wide), BF16),
        input_output_aliases={3: 0} if more else {},
        compiler_params=params(4),
        name="last_sum",
    )(mine, up, down, *more)


def send(to_up, to_down, step, axis):
    count = lax.axis_size(axis)
    return (
        lax.ppermute(to_up, axis, [(i, i + 1) for i in range(count - 1) if step > i]),
        lax.ppermute(to_down, axis, [(i, i - 1) for i in range(1, count) if step > count - 1 - i]),
    )


def body(
    features,
    gate_values,
    write_proj,
    read_proj,
    step_size,
    log_decay,
    starts,
    skip_weight,
    norm_gain,
    out_weight,
):
    tokens, channels = features.shape
    groups = write_proj.shape[1] // NSTATE
    count = lax.axis_size("ctx")
    chips = count // 2
    direct = channels % (128 * count) == 0 and chips & (chips - 1) == 0 and groups == 2
    me = lax.axis_index("ctx").astype(jnp.int32)
    place = jnp.stack([me % 2, me // 2]) if direct else jnp.zeros((2,), jnp.int32)
    line = lax.axis_size("head")
    table = jnp.asarray(line_tables(line))

    def scalars(table):
        return jnp.concatenate([place, table[lax.axis_index("head")]])

    rows = tokens // line

    inputs = (features, write_proj, step_size, log_decay, starts)
    chunks = chips if direct else 1
    other, pre_other = states_call(1, direct, *inputs, chunks, starts)
    mine, pre_mine = states_call(0, direct, *inputs, chunks, other)

    def intra(side, after):
        return intra_call(
            scal, side, features, write_proj, read_proj, step_size, log_decay, starts, skip_weight, after
        )

    if direct:
        theirs = over(other, "ctx")
        totals = chip_call(mine, theirs)
        totals, table = lax.optimization_barrier((totals, table))
        scal = scalars(table)
        moved = exchange(totals, "ctx")
        local = [intra(0, totals[0])]
        entries = prefix_call(moved, local[0][1])
        own = exchange(entries, "ctx")
        local += [intra(g, entries[0]) for g in range(1, groups)]
        fold = [fold_call([theirs], pre_mine, tokens)]
        own, mine, local, fold = lax.optimization_barrier((own, mine, local, fold))
        packed = pack_call(own, mine)
        entries = [packed, over(packed, "ctx")]
        fold.append(fold_call([entries[1]], pre_other, tokens, (1,)))
    else:
        scal = scalars(table)
        entries = [chain(mine, "ctx")[None], chain(other, "ctx")[None]]
        local = [intra(g, mine) for g in range(groups)]
        fold = [fold_call([], pre, tokens) for pre in (pre_mine, pre_other)]
    inner, reach = zip(*local)
    gain = norm_gain.reshape(1, channels)
    wide = out_weight.shape[1]
    pieces = 4
    size = wide // pieces
    early = 2
    firsts = []
    for sides in [[0], [1]] if groups > 1 else [[0, 1]]:
        at = sides[0]
        firsts = first_call(
            scal, sides, [entries[k] for k in sides], [fold[k] for k in sides], inner[at], reach[at], gate_values, read_proj,
            gain, out_weight, rows, size, early, firsts,
        )
    normed, *firsts = firsts
    moving = [send(f, f, 1, "head") for f in firsts]
    late, moving[0] = lax.optimization_barrier((normed, moving[0]))
    firsts = project_call([late], out_weight, early * size, wide - early * size, pieces - early)
    moving += [send(f, f, 1, "head") for f in firsts]
    inner, firsts = lax.optimization_barrier((inner, firsts))
    others = rest_call(scal, entries, fold, inner, reach, gate_values, read_proj, gain, rows)
    mine = [project_call([normed, others], out_weight, p * size, size)[0] for p in range(pieces)]
    sums = None
    for s in range(2, line):
        for p in range(pieces):
            if sums is not None:
                mine[p], sums = lax.optimization_barrier((mine[p], sums))
            sums = sum_call(scal, mine[p], *moving[p], s)
            moving[p] = send(*sums, s, "head")
    result = None
    for p in range(pieces):
        result = last_call(result, mine[p], *moving[p], p * size, wide)
    return result


def solution(mesh):
    placed = (
        P("ctx", "head"),
        P("ctx", "head"),
        P("ctx", "head"),
        P("ctx", "head"),
        P("head", "ctx"),
        P("head", "ctx"),
        P("ctx"),
        P("head"),
        P("head"),
        P("head", None),
    )
    return jax.shard_map(
        body, mesh=mesh, in_specs=placed, out_specs=P(("ctx", "head"), None), check_vma=False
    )
```

time: 183 us -> 178 us (0.973); the launches traced: 182 us -> 175 us
  starting transfers between devices: 78.3 us -> 67.5 us
  Pallas kernels: 43.9 us -> 51.8 us
  waiting for transfers between devices: 55.9 us -> 53.6 us
    ppermute x12, waiting for transfers between devices: 50.6 us -> 35 us  [send(): lax.ppermute(to_down, axis, [(i, i - 1) for i in range(1, count) if step...]
    ppermute x12, waiting for transfers between devices: 1.1 us -> 14.3 us  [send(): lax.ppermute(to_up, axis, [(i, i + 1) for i in range(count - 1) if step >...]
    pallas_call x4 -> x5, Pallas kernels: 12.8 us -> 20.8 us  [project_call(): pl.pallas_call(kernel, in_specs=[vmem] * len(parts) + [pl.BlockSpec(memor...]
    ppermute x12, starting transfers between devices: 52.1 us -> 44.4 us  [send(): lax.ppermute(to_down, axis, [(i, i - 1) for i in range(1, count) if step...]
    ppermute x1 -> x0, starting transfers between devices: 2.42 us -> none  [body(): lax.ppermute(mine, 'ctx', [(i, i + 1) for i in range(0, count, 2)])]
    pallas_call x2 -> x3, Pallas kernels: 5.62 us -> 7.02 us  [the longest x2 6.95 us: intra_call(): pl.pallas_call(kernel, grid_spec=pltpu.PrefetchScalarGridSpec(num_scalar_...]
    pallas_call x1 -> x2, Pallas kernels: 7.38 us -> 6.29 us  [first_call(): pl.pallas_call(kernel, grid_spec=pltpu.PrefetchScalarGridSpec(num_scalar_...]
    pallas_call x1 -> x2, Pallas kernels: 5.4 us -> 4.97 us  [states_call(): pl.pallas_call(kernel, in_specs=[pl.BlockSpec(memory_space=pltpu.HBM)] *...]
  transfers between devices with their start and end apart: 36 -> 32, of which waited for: 18 -> 15; matrix products, arithmetic and copies ran while one was open for 0% -> 0% of each run, Pallas kernels for 17% -> 25%
where the time goes in v3:
time: 178 us; the launch traced here: 175 us
  starting transfers between devices  67.5 us (38%)
  waiting for transfers between devices  53.6 us (30%)
  Pallas kernels  51.8 us (29%)
  local copies, waits for them, and re-layouts  1.81 us (1%)
    ppermute x12, starting transfers between devices, send(): lax.ppermute(to_down, axis, [(i, i - 1) for i in range(1, count) if step...  44.4 us
    ppermute x12, waiting for transfers between devices, send(): lax.ppermute(to_down, axis, [(i, i - 1) for i in range(1, count) if step...  35 us
    pallas_call x5, Pallas kernels, project_call(): pl.pallas_call(kernel, in_specs=[vmem] * len(parts) + [pl.BlockSpec(memor...  20.8 us
    ppermute x12, starting transfers between devices, send(): lax.ppermute(to_up, axis, [(i, i + 1) for i in range(count - 1) if step >...  15.8 us
    ppermute x12, waiting for transfers between devices, send(): lax.ppermute(to_up, axis, [(i, i + 1) for i in range(count - 1) if step >...  14.3 us
    ppermute x6, starting transfers between devices, exchange(): lax.ppermute(parts[k], axis, [(i, i ^ 2 * k) for i in range(count)])  7.11 us
    pallas_call x2, Pallas kernels, intra_call(): pl.pallas_call(kernel, grid_spec=pltpu.PrefetchScalarGridSpec(num_scalar_...  6.95 us
    pallas_call x2, Pallas kernels, first_call(): pl.pallas_call(kernel, grid_spec=pltpu.PrefetchScalarGridSpec(num_scalar_...  6.29 us
  transfers between devices with their start and end apart: 32, of which 15 were waited for; matrix products, arithmetic and copies ran while one was open for 0% of the time, Pallas kernels for 25%

profile of v3, /device:TPU:16, one launch (start us, length us, event | category | flops | bytes accessed | tf_op | source)
XLA Modules:
  0.0 175.4 jit_solution(6465070832316842658)
XLA Ops:
  0.0 3.3 %states.2 = (f32[4,136,256]{2,1,0:T(8,128)}, f32[1,136,1024]{2,1,0:T(8,128)}) custom-call(bf16[512,2048]{1,0:T(8,128)(2,1)} %feat.3, bf16[512,256]{1,0:T(8,128)(2,1)} %write.3, f32[32,512]{1,0:T(8,128)} %step.3, f32[32,512]{1,0:T(8,128)} %decay.3, s32[1,512]{1,0:T(1,128)} %bitcast.10, s32[512]{0:T(512)} %after.1), custom_call_target="tpu_custom_call" | custom-call | flops 100000000 | bytes 1000000 | tf_op jit(solution)/shard_map/states/pallas_call | solution.py:143
  4.6 1.6 states.3
  6.4 1.6 collective-permute-start.1
  7.9 1.5 collective-permute-start.2
  10.7 3.5 %intra.2 = (f32[512,1024]{1,0:T(8,128)S(1)}, f32[512,128]{1,0:T(8,128)S(1)}) custom-call(s32[14]{0:T(128)S(1)} %pad_add_fusion.scal, bf16[512,2048]{1,0:T(8,128)(2,1)S(1)} %copy-done.1, bf16[512,256]{1,0:T(8,128)(2,1)S(1)} %copy-done.3, bf16[512,256]{1,0:T(8,128)(2,1)S(1)} %copy-done.2, f32[32,512]{1,0:T(8,128)S(1)} %copy-done.6, f32[32,512]{1,0:T(8,128)S(1)} %copy-done.7, ...), custom_call_target="tpu_custom_call" | custom-call | flops 1000000000 | bytes 1000000 | tf_op jit(solution)/shard_map/intra/pallas_call | solution.py:218
  14.2 2.5 %collective-permute-done.2.refs_2_ = f32[136,256]{1,0:T(8,128)S(1)} collective-permute-done((f32[136,256]{1,0:T(8,128)S(1)}, f32[136,256]{1,0:T(8,128)S(1)}, u32[]{:S(2)}, u32[]{:S(2)}) %collective-permute-start.2) | collective-permute-done | bytes 139296 | tf_op jit(solution)/shard_map/ppermute | solution.py:368
  16.8 1.3 collective-permute-start.4
  18.9 1.4 collective-permute-start.6
  20.5 3.5 %intra.3 = (f32[512,1024]{1,0:T(8,128)S(1)}, f32[512,128]{1,0:T(8,128)S(1)}) custom-call(s32[14]{0:T(128)S(1)} %pad_add_fusion.scal, bf16[512,2048]{1,0:T(8,128)(2,1)S(1)} %copy-done.1, bf16[512,256]{1,0:T(8,128)(2,1)S(1)} %copy-done.3, bf16[512,256]{1,0:T(8,128)(2,1)S(1)} %copy-done.2, f32[32,512]{1,0:T(8,128)S(1)} %copy-done.6, f32[32,512]{1,0:T(8,128)S(1)} %copy-done.7, ...), custom_call_target="tpu_custom_call" | custom-call | flops 1000000000 | bytes 1000000 | tf_op jit(solution)/shard_map/intra/pallas_call | solution.py:218
  24.0 1.7 collective-permute-done.5.refs_2_
  25.9 3.1 %first.2 = (bf16[128,1024]{1,0:T(8,128)(2,1)S(1)}, f32[128,2048]{1,0:T(8,128)S(1)}) custom-call(s32[14]{0:T(128)S(1)} %pad_add_fusion.scal, f32[2,4,136,256]{3,2,1,0:T(8,128)S(1)} %pack.1.refs_0_, f32[2,136,1024]{2,1,0:T(8,128)S(1)} %fold.2.refs_1_.refs_6_, f32[512,1024]{1,0:T(8,128)S(1)} %get-tuple-element.109.refs_2_, ...), custom_call_target="tpu_custom_call" | custom-call | tf_op jit(solution)/shard_map/first/pallas_call | solution.py:473
  29.2 3.1 %first.3 = (bf16[1,128,2048]{2,1,0:T(8,128)(2,1)S(1)}, f32[1,128,1024]{2,1,0:T(8,128)S(1)}, f32[1,128,1024]{2,1,0:T(8,128)S(1)}) custom-call(s32[14]{0:T(128)S(1)} %pad_add_fusion.scal, f32[2,4,136,256]{3,2,1,0:T(8,128)S(1)} %collective-permute-done.7.refs_0_.refs_1_, f32[2,136,1024]{2,1,0:T(8,128)S(1)} %fold.3.refs_1_.refs_7_, ...), custom_call_target="tpu_custom_call" | custom-call | tf_op jit(solution)/shard_map/first/pallas_call | solution.py:473
  33.1 1.3 collective-permute-start.9
  35.1 1.3 collective-permute-start.11
  36.4 13.3 %collective-permute-done.9.d = f32[1,128,1024]{2,1,0:T(8,128)S(1)} collective-permute-done((f32[1,128,1024]{2,1,0:T(8,128)S(1)}, f32[1,128,1024]{2,1,0:T(8,128)S(1)}, u32[]{:S(2)}, u32[]{:S(2)}) %collective-permute-start.9) | collective-permute-done | bytes 524320 | tf_op jit(solution)/shard_map/ppermute | solution.py:693
  49.7 4.0 %project.5 = (f32[1,128,1024]{2,1,0:T(8,128)S(1)}, f32[1,128,1024]{2,1,0:T(8,128)S(1)}) custom-call(bf16[1,128,2048]{2,1,0:T(8,128)(2,1)S(1)} %get-tuple-element.106.refs_0_, bf16[2048,4096]{1,0:T(8,128)(2,1)} %refs_2_.7), custom_call_target="tpu_custom_call" | custom-call | flops 1073741824 | bytes 9437184 | tf_op jit(solution)/shard_map/project/pallas_call | solution.py:601
  54.4 1.3 collective-permute-start.13
  56.6 3.5 %rest.1.refs_1_ = bf16[3,128,2048]{2,1,0:T(8,128)(2,1)S(1)} custom-call(s32[14]{0:T(128)S(1)} %pad_add_fusion.scal, f32[2,4,136,256]{3,2,1,0:T(8,128)S(1)} %pack.1.refs_0_, f32[2,4,136,256]{3,2,1,0:T(8,128)S(1)} %collective-permute-done.7.refs_0_.refs_1_, f32[512,1024]{1,0:T(8,128)S(1)} %get-tuple-element.109.refs_2_, ...), custom_call_target="tpu_custom_call" | custom-call | flops 1000000000 | bytes 1000000 | tf_op jit(solution)/shard_map/rest/pallas_call | solution.py:550
  60.1 4.2 %project.9.a.b = f32[4,128,1024]{2,1,0:T(8,128)S(1)} custom-call(bf16[1,128,2048]{2,1,0:T(8,128)(2,1)S(1)} %get-tuple-element.106.refs_0_, bf16[3,128,2048]{2,1,0:T(8,128)(2,1)S(1)} %rest.1.refs_1_, bf16[2048,4096]{1,0:T(8,128)(2,1)} %refs_2_.7), custom_call_target="tpu_custom_call" | custom-call | flops 2147483648 | bytes 6291456 | tf_op jit(solution)/shard_map/project/pallas_call | solution.py:601
  65.0 4.2 %project.8.a.b = f32[4,128,1024]{2,1,0:T(8,128)S(1)} custom-call(bf16[1,128,2048]{2,1,0:T(8,128)(2,1)S(1)} %get-tuple-element.106.refs_0_, bf16[3,128,2048]{2,1,0:T(8,128)(2,1)S(1)} %rest.1.refs_1_, bf16[2048,4096]{1,0:T(8,128)(2,1)} %refs_2_.7), custom_call_target="tpu_custom_call" | custom-call | flops 2147483648 | bytes 6291456 | tf_op jit(solution)/shard_map/project/pallas_call | solution.py:601
  69.2 1.3 collective-permute-start.15
  70.5 1.3 collective-permute-start.16
  72.5 4.2 %project.7.a.b = f32[4,128,1024]{2,1,0:T(8,128)S(1)} custom-call(bf16[1,128,2048]{2,1,0:T(8,128)(2,1)S(1)} %get-tuple-element.106.refs_0_, bf16[3,128,2048]{2,1,0:T(8,128)(2,1)S(1)} %rest.1.refs_1_, bf16[2048,4096]{1,0:T(8,128)(2,1)} %refs_2_.7), custom_call_target="tpu_custom_call" | custom-call | flops 2147483648 | bytes 6291456 | tf_op jit(solution)/shard_map/project/pallas_call | solution.py:601
  76.7 4.2 %project.6.a.b = f32[4,128,1024]{2,1,0:T(8,128)S(1)} custom-call(bf16[1,128,2048]{2,1,0:T(8,128)(2,1)S(1)} %get-tuple-element.106.refs_0_, bf16[3,128,2048]{2,1,0:T(8,128)(2,1)S(1)} %rest.1.refs_1_, bf16[2048,4096]{1,0:T(8,128)(2,1)} %refs_2_.7), custom_call_target="tpu_custom_call" | custom-call | flops 2147483648 | bytes 6291456 | tf_op jit(solution)/shard_map/project/pallas_call | solution.py:601
  80.9 4.5 %collective-permute-start.17 = (f32[1,128,1024]{2,1,0:T(8,128)S(1)}, f32[1,128,1024]{2,1,0:T(8,128)S(1)}, u32[]{:S(2)}, u32[]{:S(2)}) collective-permute-start(f32[1,128,1024]{2,1,0:T(8,128)S(1)} %get-tuple-element.114), channel_id=1, source_target_pairs={{2,1},{3,2},{6,5},{7,6},{10,9},{11,10},{14,13},{15,14},{18,17},{19... | collective-permute-start | bytes 1572872 | tf_op jit(solution)/shard_map/ppermute | solution.py:693
  85.4 1.3 collective-permute-start.18
  87.4 4.6 %collective-permute-start.19 = (f32[1,128,1024]{2,1,0:T(8,128)S(1)}, f32[1,128,1024]{2,1,0:T(8,128)S(1)}, u32[]{:S(2)}, u32[]{:S(2)}) collective-permute-start(f32[1,128,1024]{2,1,0:T(8,128)S(1)} %get-tuple-element.118), channel_id=1, source_target_pairs={{2,1},{3,2},{6,5},{7,6},{10,9},{11,10},{14,13},{15,14},{18,17},{19... | collective-permute-start | bytes 1572872 | tf_op jit(solution)/shard_map/ppermute | solution.py:693
  93.9 4.6 %collective-permute-start.21 = (f32[1,128,1024]{2,1,0:T(8,128)S(1)}, f32[1,128,1024]{2,1,0:T(8,128)S(1)}, u32[]{:S(2)}, u32[]{:S(2)}) collective-permute-start(f32[1,128,1024]{2,1,0:T(8,128)S(1)} %get-tuple-element.121), channel_id=1, source_target_pairs={{2,1},{3,2},{6,5},{7,6},{10,9},{11,10},{14,13},{15,14},{18,17},{19... | collective-permute-start | bytes 1572872 | tf_op jit(solution)/shard_map/ppermute | solution.py:693
  100.5 1.7 collective-permute-done.18.c
  102.2 5.3 %collective-permute-start.23 = (f32[1,128,1024]{2,1,0:T(8,128)S(1)}, f32[1,128,1024]{2,1,0:T(8,128)S(1)}, u32[]{:S(2)}, u32[]{:S(2)}) collective-permute-start(f32[1,128,1024]{2,1,0:T(8,128)S(1)} %get-tuple-element.124), channel_id=1, source_target_pairs={{2,1},{3,2},{6,5},{7,6},{10,9},{11,10},{14,13},{15,14},{18,17},{19... | collective-permute-start | bytes 1572872 | tf_op jit(solution)/shard_map/ppermute | solution.py:693
  107.5 1.5 collective-permute-done.19.d
  109.7 1.9 %collective-permute-start.28 = (f32[1,128,1024]{2,1,0:T(8,128)S(1)}, f32[1,128,1024]{2,1,0:T(8,128)S(1)}, u32[]{:S(2)}, u32[]{:S(2)}) collective-permute-start(f32[1,128,1024]{2,1,0:T(8,128)S(1)} %get-tuple-element.129), channel_id=1, source_target_pairs={{0,1},{1,2},{2,3},{4,5},{5,6},{6,7},{8,9},{9,10},{10,11},{12,13},{... | collective-permute-start | bytes 1572872 | tf_op jit(solution)/shard_map/ppermute | solution.py:692
  111.6 1.8 %collective-permute-done.20.c = f32[1,128,1024]{2,1,0:T(8,128)S(1)} collective-permute-done((f32[1,128,1024]{2,1,0:T(8,128)S(1)}, f32[1,128,1024]{2,1,0:T(8,128)S(1)}, u32[]{:S(2)}, u32[]{:S(2)}) %collective-permute-start.20) | collective-permute-done | bytes 524320 | tf_op jit(solution)/shard_map/ppermute | solution.py:692
  113.4 5.3 %collective-permute-start.29 = (f32[1,128,1024]{2,1,0:T(8,128)S(1)}, f32[1,128,1024]{2,1,0:T(8,128)S(1)}, u32[]{:S(2)}, u32[]{:S(2)}) collective-permute-start(f32[1,128,1024]{2,1,0:T(8,128)S(1)} %get-tuple-element.130), channel_id=1, source_target_pairs={{1,0},{2,1},{3,2},{5,4},{6,5},{7,6},{9,8},{10,9},{11,10},{13,12},{... | collective-permute-start | bytes 1572872 | tf_op jit(solution)/shard_map/ppermute | solution.py:693
  118.7 1.5 collective-permute-done.21.d
  120.2 1.9 %collective-permute-start.30 = (f32[1,128,1024]{2,1,0:T(8,128)S(1)}, f32[1,128,1024]{2,1,0:T(8,128)S(1)}, u32[]{:S(2)}, u32[]{:S(2)}) collective-permute-start(f32[1,128,1024]{2,1,0:T(8,128)S(1)} %get-tuple-element.126), channel_id=1, source_target_pairs={{0,1},{1,2},{2,3},{4,5},{5,6},{6,7},{8,9},{9,10},{10,11},{12,13},{... | collective-permute-start | bytes 1572872 | tf_op jit(solution)/shard_map/ppermute | solution.py:692
  122.8 1.8 %collective-permute-done.22.c = f32[1,128,1024]{2,1,0:T(8,128)S(1)} collective-permute-done((f32[1,128,1024]{2,1,0:T(8,128)S(1)}, f32[1,128,1024]{2,1,0:T(8,128)S(1)}, u32[]{:S(2)}, u32[]{:S(2)}) %collective-permute-start.22) | collective-permute-done | bytes 524320 | tf_op jit(solution)/shard_map/ppermute | solution.py:692
  124.7 5.3 %collective-permute-start.31 = (f32[1,128,1024]{2,1,0:T(8,128)S(1)}, f32[1,128,1024]{2,1,0:T(8,128)S(1)}, u32[]{:S(2)}, u32[]{:S(2)}) collective-permute-start(f32[1,128,1024]{2,1,0:T(8,128)S(1)} %get-tuple-element.127), channel_id=1, source_target_pairs={{1,0},{2,1},{3,2},{5,4},{6,5},{7,6},{9,8},{10,9},{11,10},{13,12},{... | collective-permute-start | bytes 1572872 | tf_op jit(solution)/shard_map/ppermute | solution.py:693
  130.0 1.5 collective-permute-done.23.d
  131.5 1.9 %collective-permute-start.26 = (f32[1,128,1024]{2,1,0:T(8,128)S(1)}, f32[1,128,1024]{2,1,0:T(8,128)S(1)}, u32[]{:S(2)}, u32[]{:S(2)}) collective-permute-start(f32[1,128,1024]{2,1,0:T(8,128)S(1)} %get-tuple-element.132), channel_id=1, source_target_pairs={{0,1},{1,2},{2,3},{4,5},{5,6},{6,7},{8,9},{9,10},{10,11},{12,13},{... | collective-permute-start | bytes 1572872 | tf_op jit(solution)/shard_map/ppermute | solution.py:692
  134.1 1.8 %collective-permute-done.28.c = f32[1,128,1024]{2,1,0:T(8,128)S(1)} collective-permute-done((f32[1,128,1024]{2,1,0:T(8,128)S(1)}, f32[1,128,1024]{2,1,0:T(8,128)S(1)}, u32[]{:S(2)}, u32[]{:S(2)}) %collective-permute-start.28) | collective-permute-done | bytes 524320 | tf_op jit(solution)/shard_map/ppermute | solution.py:692
  135.9 5.3 %collective-permute-start.27 = (f32[1,128,1024]{2,1,0:T(8,128)S(1)}, f32[1,128,1024]{2,1,0:T(8,128)S(1)}, u32[]{:S(2)}, u32[]{:S(2)}) collective-permute-start(f32[1,128,1024]{2,1,0:T(8,128)S(1)} %get-tuple-element.133), channel_id=1, source_target_pairs={{1,0},{2,1},{3,2},{5,4},{6,5},{7,6},{9,8},{10,9},{11,10},{13,12},{... | collective-permute-start | bytes 1572872 | tf_op jit(solution)/shard_map/ppermute | solution.py:693
  141.2 5.9 %collective-permute-done.30.c = f32[1,128,1024]{2,1,0:T(8,128)S(1)} collective-permute-done((f32[1,128,1024]{2,1,0:T(8,128)S(1)}, f32[1,128,1024]{2,1,0:T(8,128)S(1)}, u32[]{:S(2)}, u32[]{:S(2)}) %collective-permute-start.30) | collective-permute-done | bytes 524320 | tf_op jit(solution)/shard_map/ppermute | solution.py:692
  147.1 1.9 %collective-permute-start.24 = (f32[1,128,1024]{2,1,0:T(8,128)S(1)}, f32[1,128,1024]{2,1,0:T(8,128)S(1)}, u32[]{:S(2)}, u32[]{:S(2)}) collective-permute-start(f32[1,128,1024]{2,1,0:T(8,128)S(1)} %get-tuple-element.135), channel_id=1, source_target_pairs={{0,1},{1,2},{2,3},{4,5},{5,6},{6,7},{8,9},{9,10},{10,11},{12,13},{... | collective-permute-start | bytes 1572872 | tf_op jit(solution)/shard_map/ppermute | solution.py:692
  149.0 4.9 %collective-permute-done.31.d = f32[1,128,1024]{2,1,0:T(8,128)S(1)} collective-permute-done((f32[1,128,1024]{2,1,0:T(8,128)S(1)}, f32[1,128,1024]{2,1,0:T(8,128)S(1)}, u32[]{:S(2)}, u32[]{:S(2)}) %collective-permute-start.31) | collective-permute-done | bytes 524320 | tf_op jit(solution)/shard_map/ppermute | solution.py:693
  154.0 4.4 %collective-permute-start.25 = (f32[1,128,1024]{2,1,0:T(8,128)S(1)}, f32[1,128,1024]{2,1,0:T(8,128)S(1)}, u32[]{:S(2)}, u32[]{:S(2)}) collective-permute-start(f32[1,128,1024]{2,1,0:T(8,128)S(1)} %get-tuple-element.136), channel_id=1, source_target_pairs={{1,0},{2,1},{3,2},{5,4},{6,5},{7,6},{9,8},{10,9},{11,10},{13,12},{... | collective-permute-start | bytes 1572872 | tf_op jit(solution)/shard_map/ppermute | solution.py:693
  160.1 5.1 %collective-permute-done.27.d = f32[1,128,1024]{2,1,0:T(8,128)S(1)} collective-permute-done((f32[1,128,1024]{2,1,0:T(8,128)S(1)}, f32[1,128,1024]{2,1,0:T(8,128)S(1)}, u32[]{:S(2)}, u32[]{:S(2)}) %collective-permute-start.27) | collective-permute-done | bytes 524320 | tf_op jit(solution)/shard_map/ppermute | solution.py:693
  167.2 7.2 %collective-permute-done.25.d = f32[1,128,1024]{2,1,0:T(8,128)S(1)} collective-permute-done((f32[1,128,1024]{2,1,0:T(8,128)S(1)}, f32[1,128,1024]{2,1,0:T(8,128)S(1)}, u32[]{:S(2)}, u32[]{:S(2)}) %collective-permute-start.25) | collective-permute-done | bytes 524320 | tf_op jit(solution)/shard_map/ppermute | solution.py:693
  (69 shorter events, 19.4 us)
Async XLA Ops:
  0.0 3.5 %copy-start.1 = (bf16[512,2048]{1,0:T(8,128)(2,1)S(1)}, bf16[512,2048]{1,0:T(8,128)(2,1)}, u32[]{:S(2)}) copy-start(bf16[512,2048]{1,0:T(8,128)(2,1)} %feat.3) | copy-start | bytes 6291460
  0.0 3.5 %copy-start.3 = (bf16[512,256]{1,0:T(8,128)(2,1)S(1)}, bf16[512,256]{1,0:T(8,128)(2,1)}, u32[]{:S(2)}) copy-start(bf16[512,256]{1,0:T(8,128)(2,1)} %write.3) | copy-start | bytes 786436
  0.0 3.5 %copy-start.6 = (f32[32,512]{1,0:T(8,128)S(1)}, f32[32,512]{1,0:T(8,128)}, u32[]{:S(2)}) copy-start(f32[32,512]{1,0:T(8,128)} %step.3) | copy-start | bytes 196612
  0.0 3.5 %copy-start.7 = (f32[32,512]{1,0:T(8,128)S(1)}, f32[32,512]{1,0:T(8,128)}, u32[]{:S(2)}) copy-start(f32[32,512]{1,0:T(8,128)} %decay.3) | copy-start | bytes 196612
  0.0 3.5 %copy-start.9 = (s32[512]{0:T(512)S(1)}, s32[512]{0:T(512)}, u32[]{:S(2)}) copy-start(s32[512]{0:T(512)} %after.1) | copy-start | bytes 6148
  3.4 2.9 %collective-permute-start = (f32[4,136,256]{2,1,0:T(8,128)}, f32[4,136,256]{2,1,0:T(8,128)S(1)}, u32[]{:S(2)}, u32[]{:S(2)}) collective-permute-start(f32[4,136,256]{2,1,0:T(8,128)} %get-tuple-element.71.after), channel_id=1, source_target_pairs={{0,4},{4,0},{8,12},{12,8},{16,20},{20,16},{24,28},{28,24},{1,5},{5... | collective-permute-start | bytes 1671176 | tf_op jit(solution)/shard_map/ppermute | solution.py:374
  3.5 7.2 %copy-start.10 = (f32[32]{0:T(128)S(1)}, f32[32]{0:T(128)}, u32[]{:S(2)}) copy-start(f32[32]{0:T(128)} %param.18) | copy-start | bytes 388
  3.5 7.2 %copy-start.2 = (bf16[512,256]{1,0:T(8,128)(2,1)S(1)}, bf16[512,256]{1,0:T(8,128)(2,1)}, u32[]{:S(2)}) copy-start(bf16[512,256]{1,0:T(8,128)(2,1)} %refs_9_.1) | copy-start | bytes 786436
  3.6 1.1 copy-start.5
  6.4 7.8 %collective-permute-start.1 = (f32[136,256]{1,0:T(8,128)S(1)}, f32[136,256]{1,0:T(8,128)S(1)}, u32[]{:S(2)}, u32[]{:S(2)}) collective-permute-start(f32[136,256]{1,0:T(8,128)S(1)} %get-tuple-element.79), channel_id=1, source_target_pairs={{0,8},{4,12},{8,0},{12,4},{16,24},{20,28},{24,16},{28,20},{1,9},{5... | collective-permute-start | bytes 417800 | tf_op jit(solution)/shard_map/ppermute | solution.py:368
  7.9 8.7 %collective-permute-start.2 = (f32[136,256]{1,0:T(8,128)S(1)}, f32[136,256]{1,0:T(8,128)S(1)}, u32[]{:S(2)}, u32[]{:S(2)}) collective-permute-start(f32[136,256]{1,0:T(8,128)S(1)} %get-tuple-element.80), channel_id=1, source_target_pairs={{0,16},{4,20},{8,24},{12,28},{16,0},{20,4},{24,8},{28,12},{1,17},{... | collective-permute-start | bytes 417800 | tf_op jit(solution)/shard_map/ppermute | solution.py:368
  9.5 7.2 %collective-permute-start.3 = (f32[136,256]{1,0:T(8,128)S(1)}, f32[136,256]{1,0:T(8,128)S(1)}, u32[]{:S(2)}, u32[]{:S(2)}) collective-permute-start(f32[136,256]{1,0:T(8,128)S(1)} %get-tuple-element.81), channel_id=1, source_target_pairs={{0,24},{4,28},{8,16},{12,20},{16,8},{20,12},{24,0},{28,4},{1,25},{... | collective-permute-start | bytes 417800 | tf_op jit(solution)/shard_map/ppermute | solution.py:368
  16.8 7.2 %collective-permute-start.4 = (f32[128,256]{1,0:T(8,128)S(1)}, f32[128,256]{1,0:T(8,128)S(1)}, u32[]{:S(2)}, u32[]{:S(2)}) collective-permute-start(f32[128,256]{1,0:T(8,128)S(1)} %get-tuple-element.84), channel_id=1, source_target_pairs={{0,8},{4,12},{8,0},{12,4},{16,24},{20,28},{24,16},{28,20},{1,9},{5... | collective-permute-start | bytes 393224 | tf_op jit(solution)/shard_map/ppermute | solution.py:368
  18.1 7.6 %collective-permute-start.5 = (f32[128,256]{1,0:T(8,128)S(1)}, f32[128,256]{1,0:T(8,128)S(1)}, u32[]{:S(2)}, u32[]{:S(2)}) collective-permute-start(f32[128,256]{1,0:T(8,128)S(1)} %get-tuple-element.85), channel_id=1, source_target_pairs={{0,16},{4,20},{8,24},{12,28},{16,0},{20,4},{24,8},{28,12},{1,17},{... | collective-permute-start | bytes 393224 | tf_op jit(solution)/shard_map/ppermute | solution.py:368
  18.9 6.8 %collective-permute-start.6 = (f32[128,256]{1,0:T(8,128)S(1)}, f32[128,256]{1,0:T(8,128)S(1)}, u32[]{:S(2)}, u32[]{:S(2)}) collective-permute-start(f32[128,256]{1,0:T(8,128)S(1)} %get-tuple-element.86), channel_id=1, source_target_pairs={{0,24},{4,28},{8,16},{12,20},{16,8},{20,12},{24,0},{28,4},{1,25},{... | collective-permute-start | bytes 393224 | tf_op jit(solution)/shard_map/ppermute | solution.py:368
  20.5 5.4 %copy-start = (bf16[512,2048]{1,0:T(8,128)(2,1)S(1)}, bf16[512,2048]{1,0:T(8,128)(2,1)}, u32[]{:S(2)}) copy-start(bf16[512,2048]{1,0:T(8,128)(2,1)} %refs_8_.1) | copy-start | bytes 6291460
  20.5 5.4 %copy-start.8 = (f32[2048]{0:T(1024)S(1)}, f32[2048]{0:T(1024)}, u32[]{:S(2)}) copy-start(f32[2048]{0:T(1024)} %param.19) | copy-start | bytes 24580
  25.8 3.3 %collective-permute-start.7 = (f32[2,4,136,256]{3,2,1,0:T(8,128)S(1)}, f32[2,4,136,256]{3,2,1,0:T(8,128)S(1)}, u32[]{:S(2)}, u32[]{:S(2)}) collective-permute-start(f32[2,4,136,256]{3,2,1,0:T(8,128)S(1)} %pack.1.refs_0_), channel_id=1, source_target_pairs={{0,4},{4,0},{8,12},{12,8},{16,20},{20,16},{24,28},{28,24},{1,5},{5... | collective-permute-start | bytes 3342344 | tf_op jit(solution)/shard_map/ppermute | solution.py:374
  25.9 3.2 %copy-start.4 = (f32[1,136,1024]{2,1,0:T(8,128)S(1)}, f32[1,136,1024]{2,1,0:T(8,128)}, u32[]{:S(2)}) copy-start(f32[1,136,1024]{2,1,0:T(8,128)} %get-tuple-element.96.refs_1_) | copy-start | bytes 1671172
  32.4 4.0 %collective-permute-start.8 = (f32[1,128,1024]{2,1,0:T(8,128)S(1)}, f32[1,128,1024]{2,1,0:T(8,128)S(1)}, u32[]{:S(2)}, u32[]{:S(2)}) collective-permute-start(f32[1,128,1024]{2,1,0:T(8,128)S(1)} %get-tuple-element.105), channel_id=1, source_target_pairs={{0,1},{4,5},{8,9},{12,13},{16,17},{20,21},{24,25},{28,29}} | collective-permute-start | bytes 1572872 | tf_op jit(solution)/shard_map/ppermute | solution.py:692
  33.1 16.6 %collective-permute-start.9 = (f32[1,128,1024]{2,1,0:T(8,128)S(1)}, f32[1,128,1024]{2,1,0:T(8,128)S(1)}, u32[]{:S(2)}, u32[]{:S(2)}) collective-permute-start(f32[1,128,1024]{2,1,0:T(8,128)S(1)} %get-tuple-element.105), channel_id=1, source_target_pairs={{3,2},{7,6},{11,10},{15,14},{19,18},{23,22},{27,26},{31,30}} | collective-permute-start | bytes 1572872 | tf_op jit(solution)/shard_map/ppermute | solution.py:693
  34.4 34.8 %collective-permute-start.10 = (f32[1,128,1024]{2,1,0:T(8,128)S(1)}, f32[1,128,1024]{2,1,0:T(8,128)S(1)}, u32[]{:S(2)}, u32[]{:S(2)}) collective-permute-start(f32[1,128,1024]{2,1,0:T(8,128)S(1)} %get-tuple-element.116), channel_id=1, source_target_pairs={{0,1},{4,5},{8,9},{12,13},{16,17},{20,21},{24,25},{28,29}} | collective-permute-start | bytes 1572872 | tf_op jit(solution)/shard_map/ppermute | solution.py:692
  35.1 35.4 %collective-permute-start.11 = (f32[1,128,1024]{2,1,0:T(8,128)S(1)}, f32[1,128,1024]{2,1,0:T(8,128)S(1)}, u32[]{:S(2)}, u32[]{:S(2)}) collective-permute-start(f32[1,128,1024]{2,1,0:T(8,128)S(1)} %get-tuple-element.116), channel_id=1, source_target_pairs={{3,2},{7,6},{11,10},{15,14},{19,18},{23,22},{27,26},{31,30}} | collective-permute-start | bytes 1572872 | tf_op jit(solution)/shard_map/ppermute | solution.py:693
  53.7 27.2 %collective-permute-start.12 = (f32[1,128,1024]{2,1,0:T(8,128)S(1)}, f32[1,128,1024]{2,1,0:T(8,128)S(1)}, u32[]{:S(2)}, u32[]{:S(2)}) collective-permute-start(f32[1,128,1024]{2,1,0:T(8,128)S(1)} %get-tuple-element.107), channel_id=1, source_target_pairs={{0,1},{4,5},{8,9},{12,13},{16,17},{20,21},{24,25},{28,29}} | collective-permute-start | bytes 1572872 | tf_op jit(solution)/shard_map/ppermute | solution.py:692
  54.4 31.0 %collective-permute-start.13 = (f32[1,128,1024]{2,1,0:T(8,128)S(1)}, f32[1,128,1024]{2,1,0:T(8,128)S(1)}, u32[]{:S(2)}, u32[]{:S(2)}) collective-permute-start(f32[1,128,1024]{2,1,0:T(8,128)S(1)} %get-tuple-element.107), channel_id=1, source_target_pairs={{3,2},{7,6},{11,10},{15,14},{19,18},{23,22},{27,26},{31,30}} | collective-permute-start | bytes 1572872 | tf_op jit(solution)/shard_map/ppermute | solution.py:693
  55.7 31.7 %collective-permute-start.14 = (f32[1,128,1024]{2,1,0:T(8,128)S(1)}, f32[1,128,1024]{2,1,0:T(8,128)S(1)}, u32[]{:S(2)}, u32[]{:S(2)}) collective-permute-start(f32[1,128,1024]{2,1,0:T(8,128)S(1)} %get-tuple-element.108), channel_id=1, source_target_pairs={{0,1},{4,5},{8,9},{12,13},{16,17},{20,21},{24,25},{28,29}} | collective-permute-start | bytes 1572872 | tf_op jit(solution)/shard_map/ppermute | solution.py:692
  69.2 22.8 %collective-permute-start.15 = (f32[1,128,1024]{2,1,0:T(8,128)S(1)}, f32[1,128,1024]{2,1,0:T(8,128)S(1)}, u32[]{:S(2)}, u32[]{:S(2)}) collective-permute-start(f32[1,128,1024]{2,1,0:T(8,128)S(1)} %get-tuple-element.108), channel_id=1, source_target_pairs={{3,2},{7,6},{11,10},{15,14},{19,18},{23,22},{27,26},{31,30}} | collective-permute-start | bytes 1572872 | tf_op jit(solution)/shard_map/ppermute | solution.py:693
  70.5 23.4 %collective-permute-start.16 = (f32[1,128,1024]{2,1,0:T(8,128)S(1)}, f32[1,128,1024]{2,1,0:T(8,128)S(1)}, u32[]{:S(2)}, u32[]{:S(2)}) collective-permute-start(f32[1,128,1024]{2,1,0:T(8,128)S(1)} %get-tuple-element.113), channel_id=1, source_target_pairs={{0,1},{1,2},{4,5},{5,6},{8,9},{9,10},{12,13},{13,14},{16,17},{17,1... | collective-permute-start | bytes 1572872 | tf_op jit(solution)/shard_map/ppermute | solution.py:692
  80.9 17.6 %collective-permute-start.17 = (f32[1,128,1024]{2,1,0:T(8,128)S(1)}, f32[1,128,1024]{2,1,0:T(8,128)S(1)}, u32[]{:S(2)}, u32[]{:S(2)}) collective-permute-start(f32[1,128,1024]{2,1,0:T(8,128)S(1)} %get-tuple-element.114), channel_id=1, source_target_pairs={{2,1},{3,2},{6,5},{7,6},{10,9},{11,10},{14,13},{15,14},{18,17},{19... | collective-permute-start | bytes 1572872 | tf_op jit(solution)/shard_map/ppermute | solution.py:693
  85.4 16.8 %collective-permute-start.18 = (f32[1,128,1024]{2,1,0:T(8,128)S(1)}, f32[1,128,1024]{2,1,0:T(8,128)S(1)}, u32[]{:S(2)}, u32[]{:S(2)}) collective-permute-start(f32[1,128,1024]{2,1,0:T(8,128)S(1)} %get-tuple-element.117), channel_id=1, source_target_pairs={{0,1},{1,2},{4,5},{5,6},{8,9},{9,10},{12,13},{13,14},{16,17},{17,1... | collective-permute-start | bytes 1572872 | tf_op jit(solution)/shard_map/ppermute | solution.py:692
  87.4 21.6 %collective-permute-start.19 = (f32[1,128,1024]{2,1,0:T(8,128)S(1)}, f32[1,128,1024]{2,1,0:T(8,128)S(1)}, u32[]{:S(2)}, u32[]{:S(2)}) collective-permute-start(f32[1,128,1024]{2,1,0:T(8,128)S(1)} %get-tuple-element.118), channel_id=1, source_target_pairs={{2,1},{3,2},{6,5},{7,6},{10,9},{11,10},{14,13},{15,14},{18,17},{19... | collective-permute-start | bytes 1572872 | tf_op jit(solution)/shard_map/ppermute | solution.py:693
  92.0 21.5 %collective-permute-start.20 = (f32[1,128,1024]{2,1,0:T(8,128)S(1)}, f32[1,128,1024]{2,1,0:T(8,128)S(1)}, u32[]{:S(2)}, u32[]{:S(2)}) collective-permute-start(f32[1,128,1024]{2,1,0:T(8,128)S(1)} %get-tuple-element.120), channel_id=1, source_target_pairs={{0,1},{1,2},{4,5},{5,6},{8,9},{9,10},{12,13},{13,14},{16,17},{17,1... | collective-permute-start | bytes 1572872 | tf_op jit(solution)/shard_map/ppermute | solution.py:692
  93.9 26.3 %collective-permute-start.21 = (f32[1,128,1024]{2,1,0:T(8,128)S(1)}, f32[1,128,1024]{2,1,0:T(8,128)S(1)}, u32[]{:S(2)}, u32[]{:S(2)}) collective-permute-start(f32[1,128,1024]{2,1,0:T(8,128)S(1)} %get-tuple-element.121), channel_id=1, source_target_pairs={{2,1},{3,2},{6,5},{7,6},{10,9},{11,10},{14,13},{15,14},{18,17},{19... | collective-permute-start | bytes 1572872 | tf_op jit(solution)/shard_map/ppermute | solution.py:693
  98.5 26.2 %collective-permute-start.22 = (f32[1,128,1024]{2,1,0:T(8,128)S(1)}, f32[1,128,1024]{2,1,0:T(8,128)S(1)}, u32[]{:S(2)}, u32[]{:S(2)}) collective-permute-start(f32[1,128,1024]{2,1,0:T(8,128)S(1)} %get-tuple-element.123), channel_id=1, source_target_pairs={{0,1},{1,2},{4,5},{5,6},{8,9},{9,10},{12,13},{13,14},{16,17},{17,1... | collective-permute-start | bytes 1572872 | tf_op jit(solution)/shard_map/ppermute | solution.py:692
  102.2 29.3 %collective-permute-start.23 = (f32[1,128,1024]{2,1,0:T(8,128)S(1)}, f32[1,128,1024]{2,1,0:T(8,128)S(1)}, u32[]{:S(2)}, u32[]{:S(2)}) collective-permute-start(f32[1,128,1024]{2,1,0:T(8,128)S(1)} %get-tuple-element.124), channel_id=1, source_target_pairs={{2,1},{3,2},{6,5},{7,6},{10,9},{11,10},{14,13},{15,14},{18,17},{19... | collective-permute-start | bytes 1572872 | tf_op jit(solution)/shard_map/ppermute | solution.py:693
  109.7 26.2 %collective-permute-start.28 = (f32[1,128,1024]{2,1,0:T(8,128)S(1)}, f32[1,128,1024]{2,1,0:T(8,128)S(1)}, u32[]{:S(2)}, u32[]{:S(2)}) collective-permute-start(f32[1,128,1024]{2,1,0:T(8,128)S(1)} %get-tuple-element.129), channel_id=1, source_target_pairs={{0,1},{1,2},{2,3},{4,5},{5,6},{6,7},{8,9},{9,10},{10,11},{12,13},{... | collective-permute-start | bytes 1572872 | tf_op jit(solution)/shard_map/ppermute | solution.py:692
  113.4 45.8 %collective-permute-start.29 = (f32[1,128,1024]{2,1,0:T(8,128)S(1)}, f32[1,128,1024]{2,1,0:T(8,128)S(1)}, u32[]{:S(2)}, u32[]{:S(2)}) collective-permute-start(f32[1,128,1024]{2,1,0:T(8,128)S(1)} %get-tuple-element.130), channel_id=1, source_target_pairs={{1,0},{2,1},{3,2},{5,4},{6,5},{7,6},{9,8},{10,9},{11,10},{13,12},{... | collective-permute-start | bytes 1572872 | tf_op jit(solution)/shard_map/ppermute | solution.py:693
  120.2 26.9 %collective-permute-start.30 = (f32[1,128,1024]{2,1,0:T(8,128)S(1)}, f32[1,128,1024]{2,1,0:T(8,128)S(1)}, u32[]{:S(2)}, u32[]{:S(2)}) collective-permute-start(f32[1,128,1024]{2,1,0:T(8,128)S(1)} %get-tuple-element.126), channel_id=1, source_target_pairs={{0,1},{1,2},{2,3},{4,5},{5,6},{6,7},{8,9},{9,10},{10,11},{12,13},{... | collective-permute-start | bytes 1572872 | tf_op jit(solution)/shard_map/ppermute | solution.py:692
  124.7 29.3 %collective-permute-start.31 = (f32[1,128,1024]{2,1,0:T(8,128)S(1)}, f32[1,128,1024]{2,1,0:T(8,128)S(1)}, u32[]{:S(2)}, u32[]{:S(2)}) collective-permute-start(f32[1,128,1024]{2,1,0:T(8,128)S(1)} %get-tuple-element.127), channel_id=1, source_target_pairs={{1,0},{2,1},{3,2},{5,4},{6,5},{7,6},{9,8},{10,9},{11,10},{13,12},{... | collective-permute-start | bytes 1572872 | tf_op jit(solution)/shard_map/ppermute | solution.py:693
  131.5 28.6 %collective-permute-start.26 = (f32[1,128,1024]{2,1,0:T(8,128)S(1)}, f32[1,128,1024]{2,1,0:T(8,128)S(1)}, u32[]{:S(2)}, u32[]{:S(2)}) collective-permute-start(f32[1,128,1024]{2,1,0:T(8,128)S(1)} %get-tuple-element.132), channel_id=1, source_target_pairs={{0,1},{1,2},{2,3},{4,5},{5,6},{6,7},{8,9},{9,10},{10,11},{12,13},{... | collective-permute-start | bytes 1572872 | tf_op jit(solution)/shard_map/ppermute | solution.py:692
  135.9 29.3 %collective-permute-start.27 = (f32[1,128,1024]{2,1,0:T(8,128)S(1)}, f32[1,128,1024]{2,1,0:T(8,128)S(1)}, u32[]{:S(2)}, u32[]{:S(2)}) collective-permute-start(f32[1,128,1024]{2,1,0:T(8,128)S(1)} %get-tuple-element.133), channel_id=1, source_target_pairs={{1,0},{2,1},{3,2},{5,4},{6,5},{7,6},{9,8},{10,9},{11,10},{13,12},{... | collective-permute-start | bytes 1572872 | tf_op jit(solution)/shard_map/ppermute | solution.py:693
  147.1 20.1 %collective-permute-start.24 = (f32[1,128,1024]{2,1,0:T(8,128)S(1)}, f32[1,128,1024]{2,1,0:T(8,128)S(1)}, u32[]{:S(2)}, u32[]{:S(2)}) collective-permute-start(f32[1,128,1024]{2,1,0:T(8,128)S(1)} %get-tuple-element.135), channel_id=1, source_target_pairs={{0,1},{1,2},{2,3},{4,5},{5,6},{6,7},{8,9},{9,10},{10,11},{12,13},{... | collective-permute-start | bytes 1572872 | tf_op jit(solution)/shard_map/ppermute | solution.py:692
  154.0 20.5 %collective-permute-start.25 = (f32[1,128,1024]{2,1,0:T(8,128)S(1)}, f32[1,128,1024]{2,1,0:T(8,128)S(1)}, u32[]{:S(2)}, u32[]{:S(2)}) collective-permute-start(f32[1,128,1024]{2,1,0:T(8,128)S(1)} %get-tuple-element.136), channel_id=1, source_target_pairs={{1,0},{2,1},{3,2},{5,4},{6,5},{7,6},{9,8},{10,9},{11,10},{13,12},{... | collective-permute-start | bytes 1572872 | tf_op jit(solution)/shard_map/ppermute | solution.py:693

commit v4 on v3

--- a/solution.py
+++ b/solution.py
@@ -766,12 +766,14 @@
         )
     normed, *firsts = firsts
     moving = [send(f, f, 1, "head") for f in firsts]
-    late, moving[0] = lax.optimization_barrier((normed, moving[0]))
+    others = rest_call(scal, entries, fold, inner, reach, gate_values, read_proj, gain, rows)
+    mine = [project_call([normed, others], out_weight, p * size, size)[0] for p in range(2)]
+    late, mine, moving[0] = lax.optimization_barrier((normed, mine, moving[0]))
     firsts = project_call([late], out_weight, early * size, wide - early * size, pieces - early)
     moving += [send(f, f, 1, "head") for f in firsts]
-    inner, firsts = lax.optimization_barrier((inner, firsts))
-    others = rest_call(scal, entries, fold, inner, reach, gate_values, read_proj, gain, rows)
-    mine = [project_call([normed, others], out_weight, p * size, size)[0] for p in range(pieces)]
+    for p in range(2, pieces):
+        later, moving[p] = lax.optimization_barrier((others, moving[p]))
+        mine.append(project_call([normed, later], out_weight, p * size, size)[0])
     sums = None
     for s in range(2, line):
         for p in range(pieces):

time: 178 us -> 174 us (0.978); the launches traced: 175 us -> 174 us
  waiting for transfers between devices: 53.6 us -> 31.4 us
  starting transfers between devices: 67.5 us -> 87.9 us
    ppermute x12, starting transfers between devices: 44.4 us -> 65 us  [send(): lax.ppermute(to_down, axis, [(i, i - 1) for i in range(1, count) if step...]
    ppermute x12, waiting for transfers between devices: 14.3 us -> 0.89 us  [send(): lax.ppermute(to_up, axis, [(i, i + 1) for i in range(count - 1) if step >...]
    ppermute x12, waiting for transfers between devices: 35 us -> 26.3 us  [send(): lax.ppermute(to_down, axis, [(i, i - 1) for i in range(1, count) if step...]
  transfers between devices with their start and end apart: 32 -> 32, of which waited for: 15 -> 8; matrix products, arithmetic and copies ran while one was open for 0% -> 0% of each run, Pallas kernels for 25% -> 25%
where the time goes in v4:
time: 174 us
  starting transfers between devices  87.9 us (51%)
  Pallas kernels  51.8 us (30%)
  waiting for transfers between devices  31.4 us (18%)
  local copies, waits for them, and re-layouts  1.81 us (1%)
    ppermute x12, starting transfers between devices, send(): lax.ppermute(to_down, axis, [(i, i - 1) for i in range(1, count) if step...  65 us
    ppermute x12, waiting for transfers between devices, send(): lax.ppermute(to_down, axis, [(i, i - 1) for i in range(1, count) if step...  26.3 us
    pallas_call x5, Pallas kernels, project_call(): pl.pallas_call(kernel, in_specs=[vmem] * len(parts) + [pl.BlockSpec(memor...  20.8 us
    ppermute x12, starting transfers between devices, send(): lax.ppermute(to_up, axis, [(i, i + 1) for i in range(count - 1) if step >...  15.6 us
    ppermute x6, starting transfers between devices, exchange(): lax.ppermute(parts[k], axis, [(i, i ^ 2 * k) for i in range(count)])  7.11 us
    pallas_call x2, Pallas kernels, intra_call(): pl.pallas_call(kernel, grid_spec=pltpu.PrefetchScalarGridSpec(num_scalar_...  6.95 us
    pallas_call x2, Pallas kernels, first_call(): pl.pallas_call(kernel, grid_spec=pltpu.PrefetchScalarGridSpec(num_scalar_...  6.28 us
    pallas_call x8, Pallas kernels, sum_call(): pl.pallas_call(kernel, grid_spec=pltpu.PrefetchScalarGridSpec(num_scalar_...  5.29 us
  transfers between devices with their start and end apart: 32, of which 8 were waited for; matrix products, arithmetic and copies ran while one was open for 0% of the time, Pallas kernels for 25%

profile of v4, /device:TPU:16, one launch (start us, length us, event | category | flops | bytes accessed | tf_op | source)
XLA Modules:
  0.0 173.7 jit_solution(14239806179010897451)
XLA Ops:
  0.0 3.3 %states.2 = (f32[4,136,256]{2,1,0:T(8,128)}, f32[1,136,1024]{2,1,0:T(8,128)}) custom-call(bf16[512,2048]{1,0:T(8,128)(2,1)} %feat.3, bf16[512,256]{1,0:T(8,128)(2,1)} %write.3, f32[32,512]{1,0:T(8,128)} %step.3, f32[32,512]{1,0:T(8,128)} %decay.3, s32[1,512]{1,0:T(1,128)} %bitcast.10, s32[512]{0:T(512)} %after.1), custom_call_target="tpu_custom_call" | custom-call | flops 100000000 | bytes 1000000 | tf_op jit(solution)/shard_map/states/pallas_call | solution.py:143
  3.6 1.1 copy-done.5
  4.6 1.6 states.3
  6.4 1.6 collective-permute-start.1
  7.9 1.5 collective-permute-start.2
  10.7 3.5 %intra.2 = (f32[512,1024]{1,0:T(8,128)S(1)}, f32[512,128]{1,0:T(8,128)S(1)}) custom-call(s32[14]{0:T(128)S(1)} %pad_add_fusion.scal, bf16[512,2048]{1,0:T(8,128)(2,1)S(1)} %copy-done.1, bf16[512,256]{1,0:T(8,128)(2,1)S(1)} %copy-done.3, bf16[512,256]{1,0:T(8,128)(2,1)S(1)} %copy-done.2, f32[32,512]{1,0:T(8,128)S(1)} %copy-done.6, f32[32,512]{1,0:T(8,128)S(1)} %copy-done.7, ...), custom_call_target="tpu_custom_call" | custom-call | flops 1000000000 | bytes 1000000 | tf_op jit(solution)/shard_map/intra/pallas_call | solution.py:218
  14.2 2.5 %collective-permute-done.2.refs_2_ = f32[136,256]{1,0:T(8,128)S(1)} collective-permute-done((f32[136,256]{1,0:T(8,128)S(1)}, f32[136,256]{1,0:T(8,128)S(1)}, u32[]{:S(2)}, u32[]{:S(2)}) %collective-permute-start.2) | collective-permute-done | bytes 139296 | tf_op jit(solution)/shard_map/ppermute | solution.py:368
  16.8 1.3 collective-permute-start.4
  18.9 1.4 collective-permute-start.6
  20.5 3.5 %intra.3 = (f32[512,1024]{1,0:T(8,128)S(1)}, f32[512,128]{1,0:T(8,128)S(1)}) custom-call(s32[14]{0:T(128)S(1)} %pad_add_fusion.scal, bf16[512,2048]{1,0:T(8,128)(2,1)S(1)} %copy-done.1, bf16[512,256]{1,0:T(8,128)(2,1)S(1)} %copy-done.3, bf16[512,256]{1,0:T(8,128)(2,1)S(1)} %copy-done.2, f32[32,512]{1,0:T(8,128)S(1)} %copy-done.6, f32[32,512]{1,0:T(8,128)S(1)} %copy-done.7, ...), custom_call_target="tpu_custom_call" | custom-call | flops 1000000000 | bytes 1000000 | tf_op jit(solution)/shard_map/intra/pallas_call | solution.py:218
  24.0 1.7 collective-permute-done.5.refs_2_
  25.9 3.1 %first.2 = (bf16[128,1024]{1,0:T(8,128)(2,1)S(1)}, f32[128,2048]{1,0:T(8,128)S(1)}) custom-call(s32[14]{0:T(128)S(1)} %pad_add_fusion.scal, f32[2,4,136,256]{3,2,1,0:T(8,128)S(1)} %pack.1.refs_0_, f32[2,136,1024]{2,1,0:T(8,128)S(1)} %fold.2.refs_1_.refs_6_, f32[512,1024]{1,0:T(8,128)S(1)} %get-tuple-element.106.refs_2_, ...), custom_call_target="tpu_custom_call" | custom-call | tf_op jit(solution)/shard_map/first/pallas_call | solution.py:473
  29.2 3.1 %first.3 = (bf16[1,128,2048]{2,1,0:T(8,128)(2,1)S(1)}, f32[1,128,1024]{2,1,0:T(8,128)S(1)}, f32[1,128,1024]{2,1,0:T(8,128)S(1)}) custom-call(s32[14]{0:T(128)S(1)} %pad_add_fusion.scal, f32[2,4,136,256]{3,2,1,0:T(8,128)S(1)} %collective-permute-done.7.refs_0_.refs_1_, f32[2,136,1024]{2,1,0:T(8,128)S(1)} %fold.3.refs_1_.refs_7_, ...), custom_call_target="tpu_custom_call" | custom-call | tf_op jit(solution)/shard_map/first/pallas_call | solution.py:473
  33.0 1.3 collective-permute-start.9
  35.1 1.5 collective-permute-start.15
  36.5 3.5 %rest.1.refs_1_ = bf16[3,128,2048]{2,1,0:T(8,128)(2,1)S(1)} custom-call(s32[14]{0:T(128)S(1)} %pad_add_fusion.scal, f32[2,4,136,256]{3,2,1,0:T(8,128)S(1)} %pack.1.refs_0_, f32[2,4,136,256]{3,2,1,0:T(8,128)S(1)} %collective-permute-done.7.refs_0_.refs_1_, f32[512,1024]{1,0:T(8,128)S(1)} %get-tuple-element.106.refs_2_, ...), custom_call_target="tpu_custom_call" | custom-call | flops 1000000000 | bytes 1000000 | tf_op jit(solution)/shard_map/rest/pallas_call | solution.py:550
  40.1 4.2 %project.5.a.b = f32[4,128,1024]{2,1,0:T(8,128)S(1)} custom-call(bf16[1,128,2048]{2,1,0:T(8,128)(2,1)S(1)} %get-tuple-element.112.refs_0_, bf16[3,128,2048]{2,1,0:T(8,128)(2,1)S(1)} %rest.1.refs_1_, bf16[2048,4096]{1,0:T(8,128)(2,1)} %refs_2_.7), custom_call_target="tpu_custom_call" | custom-call | flops 2147483648 | bytes 6291456 | tf_op jit(solution)/shard_map/project/pallas_call | solution.py:601
  44.3 4.2 %project.6.a.b = f32[4,128,1024]{2,1,0:T(8,128)S(1)} custom-call(bf16[1,128,2048]{2,1,0:T(8,128)(2,1)S(1)} %get-tuple-element.112.refs_0_, bf16[3,128,2048]{2,1,0:T(8,128)(2,1)S(1)} %rest.1.refs_1_, bf16[2048,4096]{1,0:T(8,128)(2,1)} %refs_2_.7), custom_call_target="tpu_custom_call" | custom-call | flops 2147483648 | bytes 6291456 | tf_op jit(solution)/shard_map/project/pallas_call | solution.py:601
  48.5 1.2 collective-permute-done.9.d
  49.7 4.0 %project.7 = (f32[1,128,1024]{2,1,0:T(8,128)S(1)}, f32[1,128,1024]{2,1,0:T(8,128)S(1)}) custom-call(bf16[1,128,2048]{2,1,0:T(8,128)(2,1)S(1)} %get-tuple-element.112.refs_0_, bf16[2048,4096]{1,0:T(8,128)(2,1)} %refs_2_.7), custom_call_target="tpu_custom_call" | custom-call | flops 1073741824 | bytes 9437184 | tf_op jit(solution)/shard_map/project/pallas_call | solution.py:601
  54.4 1.3 collective-permute-start.11
  57.1 1.3 collective-permute-start.13
  58.4 2.5 %collective-permute-done.15.d = f32[1,128,1024]{2,1,0:T(8,128)S(1)} collective-permute-done((f32[1,128,1024]{2,1,0:T(8,128)S(1)}, f32[1,128,1024]{2,1,0:T(8,128)S(1)}, u32[]{:S(2)}, u32[]{:S(2)}) %collective-permute-start.15) | collective-permute-done | bytes 524320 | tf_op jit(solution)/shard_map/ppermute | solution.py:693
  60.9 1.3 collective-permute-start.16
  62.9 10.9 %collective-permute-start.17 = (f32[1,128,1024]{2,1,0:T(8,128)S(1)}, f32[1,128,1024]{2,1,0:T(8,128)S(1)}, u32[]{:S(2)}, u32[]{:S(2)}) collective-permute-start(f32[1,128,1024]{2,1,0:T(8,128)S(1)} %get-tuple-element.122), channel_id=1, source_target_pairs={{2,1},{3,2},{6,5},{7,6},{10,9},{11,10},{14,13},{15,14},{18,17},{19... | collective-permute-start | bytes 1572872 | tf_op jit(solution)/shard_map/ppermute | solution.py:693
  73.8 1.3 collective-permute-start.18
  75.1 4.2 %project.8.a.b = f32[4,128,1024]{2,1,0:T(8,128)S(1)} custom-call(bf16[1,128,2048]{2,1,0:T(8,128)(2,1)S(1)} %get-tuple-element.112.refs_0_, bf16[3,128,2048]{2,1,0:T(8,128)(2,1)S(1)} %rest.1.refs_1_, bf16[2048,4096]{1,0:T(8,128)(2,1)} %refs_2_.7), custom_call_target="tpu_custom_call" | custom-call | flops 2147483648 | bytes 6291456 | tf_op jit(solution)/shard_map/project/pallas_call | solution.py:601
  79.3 5.7 %collective-permute-start.19 = (f32[1,128,1024]{2,1,0:T(8,128)S(1)}, f32[1,128,1024]{2,1,0:T(8,128)S(1)}, u32[]{:S(2)}, u32[]{:S(2)}) collective-permute-start(f32[1,128,1024]{2,1,0:T(8,128)S(1)} %get-tuple-element.126), channel_id=1, source_target_pairs={{2,1},{3,2},{6,5},{7,6},{10,9},{11,10},{14,13},{15,14},{18,17},{19... | collective-permute-start | bytes 1572872 | tf_op jit(solution)/shard_map/ppermute | solution.py:693
  85.0 4.2 %project.9.a.b = f32[4,128,1024]{2,1,0:T(8,128)S(1)} custom-call(bf16[1,128,2048]{2,1,0:T(8,128)(2,1)S(1)} %get-tuple-element.112.refs_0_, bf16[3,128,2048]{2,1,0:T(8,128)(2,1)S(1)} %rest.1.refs_1_, bf16[2048,4096]{1,0:T(8,128)(2,1)} %refs_2_.7), custom_call_target="tpu_custom_call" | custom-call | flops 2147483648 | bytes 6291456 | tf_op jit(solution)/shard_map/project/pallas_call | solution.py:601
  89.9 1.3 collective-permute-start.20
  91.9 4.6 %collective-permute-start.21 = (f32[1,128,1024]{2,1,0:T(8,128)S(1)}, f32[1,128,1024]{2,1,0:T(8,128)S(1)}, u32[]{:S(2)}, u32[]{:S(2)}) collective-permute-start(f32[1,128,1024]{2,1,0:T(8,128)S(1)} %get-tuple-element.131), channel_id=1, source_target_pairs={{2,1},{3,2},{6,5},{7,6},{10,9},{11,10},{14,13},{15,14},{18,17},{19... | collective-permute-start | bytes 1572872 | tf_op jit(solution)/shard_map/ppermute | solution.py:693
  96.4 1.3 collective-permute-start.22
  98.4 9.1 %collective-permute-start.23 = (f32[1,128,1024]{2,1,0:T(8,128)S(1)}, f32[1,128,1024]{2,1,0:T(8,128)S(1)}, u32[]{:S(2)}, u32[]{:S(2)}) collective-permute-start(f32[1,128,1024]{2,1,0:T(8,128)S(1)} %get-tuple-element.136), channel_id=1, source_target_pairs={{2,1},{3,2},{6,5},{7,6},{10,9},{11,10},{14,13},{15,14},{18,17},{19... | collective-permute-start | bytes 1572872 | tf_op jit(solution)/shard_map/ppermute | solution.py:693
  108.2 1.9 %collective-permute-start.28 = (f32[1,128,1024]{2,1,0:T(8,128)S(1)}, f32[1,128,1024]{2,1,0:T(8,128)S(1)}, u32[]{:S(2)}, u32[]{:S(2)}) collective-permute-start(f32[1,128,1024]{2,1,0:T(8,128)S(1)} %get-tuple-element.141), channel_id=1, source_target_pairs={{0,1},{1,2},{2,3},{4,5},{5,6},{6,7},{8,9},{9,10},{10,11},{12,13},{... | collective-permute-start | bytes 1572872 | tf_op jit(solution)/shard_map/ppermute | solution.py:692
  110.1 8.6 %collective-permute-start.29 = (f32[1,128,1024]{2,1,0:T(8,128)S(1)}, f32[1,128,1024]{2,1,0:T(8,128)S(1)}, u32[]{:S(2)}, u32[]{:S(2)}) collective-permute-start(f32[1,128,1024]{2,1,0:T(8,128)S(1)} %get-tuple-element.142), channel_id=1, source_target_pairs={{1,0},{2,1},{3,2},{5,4},{6,5},{7,6},{9,8},{10,9},{11,10},{13,12},{... | collective-permute-start | bytes 1572872 | tf_op jit(solution)/shard_map/ppermute | solution.py:693
  118.7 1.9 %collective-permute-start.30 = (f32[1,128,1024]{2,1,0:T(8,128)S(1)}, f32[1,128,1024]{2,1,0:T(8,128)S(1)}, u32[]{:S(2)}, u32[]{:S(2)}) collective-permute-start(f32[1,128,1024]{2,1,0:T(8,128)S(1)} %get-tuple-element.138), channel_id=1, source_target_pairs={{0,1},{1,2},{2,3},{4,5},{5,6},{6,7},{8,9},{9,10},{10,11},{12,13},{... | collective-permute-start | bytes 1572872 | tf_op jit(solution)/shard_map/ppermute | solution.py:692
  121.4 8.6 %collective-permute-start.31 = (f32[1,128,1024]{2,1,0:T(8,128)S(1)}, f32[1,128,1024]{2,1,0:T(8,128)S(1)}, u32[]{:S(2)}, u32[]{:S(2)}) collective-permute-start(f32[1,128,1024]{2,1,0:T(8,128)S(1)} %get-tuple-element.139), channel_id=1, source_target_pairs={{1,0},{2,1},{3,2},{5,4},{6,5},{7,6},{9,8},{10,9},{11,10},{13,12},{... | collective-permute-start | bytes 1572872 | tf_op jit(solution)/shard_map/ppermute | solution.py:693
  130.0 1.9 %collective-permute-start.26 = (f32[1,128,1024]{2,1,0:T(8,128)S(1)}, f32[1,128,1024]{2,1,0:T(8,128)S(1)}, u32[]{:S(2)}, u32[]{:S(2)}) collective-permute-start(f32[1,128,1024]{2,1,0:T(8,128)S(1)} %get-tuple-element.144), channel_id=1, source_target_pairs={{0,1},{1,2},{2,3},{4,5},{5,6},{6,7},{8,9},{9,10},{10,11},{12,13},{... | collective-permute-start | bytes 1572872 | tf_op jit(solution)/shard_map/ppermute | solution.py:692
  132.6 8.6 %collective-permute-start.27 = (f32[1,128,1024]{2,1,0:T(8,128)S(1)}, f32[1,128,1024]{2,1,0:T(8,128)S(1)}, u32[]{:S(2)}, u32[]{:S(2)}) collective-permute-start(f32[1,128,1024]{2,1,0:T(8,128)S(1)} %get-tuple-element.145), channel_id=1, source_target_pairs={{1,0},{2,1},{3,2},{5,4},{6,5},{7,6},{9,8},{10,9},{11,10},{13,12},{... | collective-permute-start | bytes 1572872 | tf_op jit(solution)/shard_map/ppermute | solution.py:693
  141.2 1.9 %collective-permute-start.24 = (f32[1,128,1024]{2,1,0:T(8,128)S(1)}, f32[1,128,1024]{2,1,0:T(8,128)S(1)}, u32[]{:S(2)}, u32[]{:S(2)}) collective-permute-start(f32[1,128,1024]{2,1,0:T(8,128)S(1)} %get-tuple-element.147), channel_id=1, source_target_pairs={{0,1},{1,2},{2,3},{4,5},{5,6},{6,7},{8,9},{9,10},{10,11},{12,13},{... | collective-permute-start | bytes 1572872 | tf_op jit(solution)/shard_map/ppermute | solution.py:692
  143.1 7.6 %collective-permute-done.31.d = f32[1,128,1024]{2,1,0:T(8,128)S(1)} collective-permute-done((f32[1,128,1024]{2,1,0:T(8,128)S(1)}, f32[1,128,1024]{2,1,0:T(8,128)S(1)}, u32[]{:S(2)}, u32[]{:S(2)}) %collective-permute-start.31) | collective-permute-done | bytes 524320 | tf_op jit(solution)/shard_map/ppermute | solution.py:693
  150.8 3.6 %collective-permute-start.25 = (f32[1,128,1024]{2,1,0:T(8,128)S(1)}, f32[1,128,1024]{2,1,0:T(8,128)S(1)}, u32[]{:S(2)}, u32[]{:S(2)}) collective-permute-start(f32[1,128,1024]{2,1,0:T(8,128)S(1)} %get-tuple-element.148), channel_id=1, source_target_pairs={{1,0},{2,1},{3,2},{5,4},{6,5},{7,6},{9,8},{10,9},{11,10},{13,12},{... | collective-permute-start | bytes 1572872 | tf_op jit(solution)/shard_map/ppermute | solution.py:693
  154.4 0.9 last_sum.4.refs_0_
  155.3 0.9 last_sum.5.refs_0_
  156.2 5.9 %collective-permute-done.27.d = f32[1,128,1024]{2,1,0:T(8,128)S(1)} collective-permute-done((f32[1,128,1024]{2,1,0:T(8,128)S(1)}, f32[1,128,1024]{2,1,0:T(8,128)S(1)}, u32[]{:S(2)}, u32[]{:S(2)}) %collective-permute-start.27) | collective-permute-done | bytes 524320 | tf_op jit(solution)/shard_map/ppermute | solution.py:693
  162.0 0.9 last_sum.6.refs_0_
  163.8 9.1 %collective-permute-done.25.d = f32[1,128,1024]{2,1,0:T(8,128)S(1)} collective-permute-done((f32[1,128,1024]{2,1,0:T(8,128)S(1)}, f32[1,128,1024]{2,1,0:T(8,128)S(1)}, u32[]{:S(2)}, u32[]{:S(2)}) %collective-permute-start.25) | collective-permute-done | bytes 524320 | tf_op jit(solution)/shard_map/ppermute | solution.py:693
  172.8 0.9 last_sum.7
  (69 shorter events, 11.8 us)
Async XLA Ops:
  0.0 3.5 %copy-start.1 = (bf16[512,2048]{1,0:T(8,128)(2,1)S(1)}, bf16[512,2048]{1,0:T(8,128)(2,1)}, u32[]{:S(2)}) copy-start(bf16[512,2048]{1,0:T(8,128)(2,1)} %feat.3) | copy-start | bytes 6291460
  0.0 3.5 %copy-start.3 = (bf16[512,256]{1,0:T(8,128)(2,1)S(1)}, bf16[512,256]{1,0:T(8,128)(2,1)}, u32[]{:S(2)}) copy-start(bf16[512,256]{1,0:T(8,128)(2,1)} %write.3) | copy-start | bytes 786436
  0.0 3.5 %copy-start.6 = (f32[32,512]{1,0:T(8,128)S(1)}, f32[32,512]{1,0:T(8,128)}, u32[]{:S(2)}) copy-start(f32[32,512]{1,0:T(8,128)} %step.3) | copy-start | bytes 196612
  0.0 3.5 %copy-start.7 = (f32[32,512]{1,0:T(8,128)S(1)}, f32[32,512]{1,0:T(8,128)}, u32[]{:S(2)}) copy-start(f32[32,512]{1,0:T(8,128)} %decay.3) | copy-start | bytes 196612
  0.0 3.5 %copy-start.9 = (s32[512]{0:T(512)S(1)}, s32[512]{0:T(512)}, u32[]{:S(2)}) copy-start(s32[512]{0:T(512)} %after.1) | copy-start | bytes 6148
  3.4 2.9 %collective-permute-start = (f32[4,136,256]{2,1,0:T(8,128)}, f32[4,136,256]{2,1,0:T(8,128)S(1)}, u32[]{:S(2)}, u32[]{:S(2)}) collective-permute-start(f32[4,136,256]{2,1,0:T(8,128)} %get-tuple-element.77.after), channel_id=1, source_target_pairs={{0,4},{4,0},{8,12},{12,8},{16,20},{20,16},{24,28},{28,24},{1,5},{5... | collective-permute-start | bytes 1671176 | tf_op jit(solution)/shard_map/ppermute | solution.py:374
  3.5 7.2 %copy-start.10 = (f32[32]{0:T(128)S(1)}, f32[32]{0:T(128)}, u32[]{:S(2)}) copy-start(f32[32]{0:T(128)} %param.18) | copy-start | bytes 388
  3.5 7.2 %copy-start.2 = (bf16[512,256]{1,0:T(8,128)(2,1)S(1)}, bf16[512,256]{1,0:T(8,128)(2,1)}, u32[]{:S(2)}) copy-start(bf16[512,256]{1,0:T(8,128)(2,1)} %refs_9_.1) | copy-start | bytes 786436
  3.6 1.1 copy-start.5
  6.4 7.8 %collective-permute-start.1 = (f32[136,256]{1,0:T(8,128)S(1)}, f32[136,256]{1,0:T(8,128)S(1)}, u32[]{:S(2)}, u32[]{:S(2)}) collective-permute-start(f32[136,256]{1,0:T(8,128)S(1)} %get-tuple-element.85), channel_id=1, source_target_pairs={{0,8},{4,12},{8,0},{12,4},{16,24},{20,28},{24,16},{28,20},{1,9},{5... | collective-permute-start | bytes 417800 | tf_op jit(solution)/shard_map/ppermute | solution.py:368
  7.9 8.7 %collective-permute-start.2 = (f32[136,256]{1,0:T(8,128)S(1)}, f32[136,256]{1,0:T(8,128)S(1)}, u32[]{:S(2)}, u32[]{:S(2)}) collective-permute-start(f32[136,256]{1,0:T(8,128)S(1)} %get-tuple-element.86), channel_id=1, source_target_pairs={{0,16},{4,20},{8,24},{12,28},{16,0},{20,4},{24,8},{28,12},{1,17},{... | collective-permute-start | bytes 417800 | tf_op jit(solution)/shard_map/ppermute | solution.py:368
  9.5 7.2 %collective-permute-start.3 = (f32[136,256]{1,0:T(8,128)S(1)}, f32[136,256]{1,0:T(8,128)S(1)}, u32[]{:S(2)}, u32[]{:S(2)}) collective-permute-start(f32[136,256]{1,0:T(8,128)S(1)} %get-tuple-element.87), channel_id=1, source_target_pairs={{0,24},{4,28},{8,16},{12,20},{16,8},{20,12},{24,0},{28,4},{1,25},{... | collective-permute-start | bytes 417800 | tf_op jit(solution)/shard_map/ppermute | solution.py:368
  16.8 7.2 %collective-permute-start.4 = (f32[128,256]{1,0:T(8,128)S(1)}, f32[128,256]{1,0:T(8,128)S(1)}, u32[]{:S(2)}, u32[]{:S(2)}) collective-permute-start(f32[128,256]{1,0:T(8,128)S(1)} %get-tuple-element.90), channel_id=1, source_target_pairs={{0,8},{4,12},{8,0},{12,4},{16,24},{20,28},{24,16},{28,20},{1,9},{5... | collective-permute-start | bytes 393224 | tf_op jit(solution)/shard_map/ppermute | solution.py:368
  18.1 7.6 %collective-permute-start.5 = (f32[128,256]{1,0:T(8,128)S(1)}, f32[128,256]{1,0:T(8,128)S(1)}, u32[]{:S(2)}, u32[]{:S(2)}) collective-permute-start(f32[128,256]{1,0:T(8,128)S(1)} %get-tuple-element.91), channel_id=1, source_target_pairs={{0,16},{4,20},{8,24},{12,28},{16,0},{20,4},{24,8},{28,12},{1,17},{... | collective-permute-start | bytes 393224 | tf_op jit(solution)/shard_map/ppermute | solution.py:368
  18.9 6.8 %collective-permute-start.6 = (f32[128,256]{1,0:T(8,128)S(1)}, f32[128,256]{1,0:T(8,128)S(1)}, u32[]{:S(2)}, u32[]{:S(2)}) collective-permute-start(f32[128,256]{1,0:T(8,128)S(1)} %get-tuple-element.92), channel_id=1, source_target_pairs={{0,24},{4,28},{8,16},{12,20},{16,8},{20,12},{24,0},{28,4},{1,25},{... | collective-permute-start | bytes 393224 | tf_op jit(solution)/shard_map/ppermute | solution.py:368
  20.5 5.4 %copy-start = (bf16[512,2048]{1,0:T(8,128)(2,1)S(1)}, bf16[512,2048]{1,0:T(8,128)(2,1)}, u32[]{:S(2)}) copy-start(bf16[512,2048]{1,0:T(8,128)(2,1)} %refs_8_.1) | copy-start | bytes 6291460
  20.5 5.4 %copy-start.8 = (f32[2048]{0:T(1024)S(1)}, f32[2048]{0:T(1024)}, u32[]{:S(2)}) copy-start(f32[2048]{0:T(1024)} %param.19) | copy-start | bytes 24580
  25.8 3.3 %collective-permute-start.7 = (f32[2,4,136,256]{3,2,1,0:T(8,128)S(1)}, f32[2,4,136,256]{3,2,1,0:T(8,128)S(1)}, u32[]{:S(2)}, u32[]{:S(2)}) collective-permute-start(f32[2,4,136,256]{3,2,1,0:T(8,128)S(1)} %pack.1.refs_0_), channel_id=1, source_target_pairs={{0,4},{4,0},{8,12},{12,8},{16,20},{20,16},{24,28},{28,24},{1,5},{5... | collective-permute-start | bytes 3342344 | tf_op jit(solution)/shard_map/ppermute | solution.py:374
  25.9 3.2 %copy-start.4 = (f32[1,136,1024]{2,1,0:T(8,128)S(1)}, f32[1,136,1024]{2,1,0:T(8,128)}, u32[]{:S(2)}) copy-start(f32[1,136,1024]{2,1,0:T(8,128)} %get-tuple-element.102.refs_1_) | copy-start | bytes 1671172
  32.3 16.1 %collective-permute-start.8 = (f32[1,128,1024]{2,1,0:T(8,128)S(1)}, f32[1,128,1024]{2,1,0:T(8,128)S(1)}, u32[]{:S(2)}, u32[]{:S(2)}) collective-permute-start(f32[1,128,1024]{2,1,0:T(8,128)S(1)} %get-tuple-element.111), channel_id=1, source_target_pairs={{0,1},{4,5},{8,9},{12,13},{16,17},{20,21},{24,25},{28,29}} | collective-permute-start | bytes 1572872 | tf_op jit(solution)/shard_map/ppermute | solution.py:692
  33.0 16.6 %collective-permute-start.9 = (f32[1,128,1024]{2,1,0:T(8,128)S(1)}, f32[1,128,1024]{2,1,0:T(8,128)S(1)}, u32[]{:S(2)}, u32[]{:S(2)}) collective-permute-start(f32[1,128,1024]{2,1,0:T(8,128)S(1)} %get-tuple-element.111), channel_id=1, source_target_pairs={{3,2},{7,6},{11,10},{15,14},{19,18},{23,22},{27,26},{31,30}} | collective-permute-start | bytes 1572872 | tf_op jit(solution)/shard_map/ppermute | solution.py:693
  34.3 22.7 %collective-permute-start.14 = (f32[1,128,1024]{2,1,0:T(8,128)S(1)}, f32[1,128,1024]{2,1,0:T(8,128)S(1)}, u32[]{:S(2)}, u32[]{:S(2)}) collective-permute-start(f32[1,128,1024]{2,1,0:T(8,128)S(1)} %get-tuple-element.124), channel_id=1, source_target_pairs={{0,1},{4,5},{8,9},{12,13},{16,17},{20,21},{24,25},{28,29}} | collective-permute-start | bytes 1572872 | tf_op jit(solution)/shard_map/ppermute | solution.py:692
  35.1 25.9 %collective-permute-start.15 = (f32[1,128,1024]{2,1,0:T(8,128)S(1)}, f32[1,128,1024]{2,1,0:T(8,128)S(1)}, u32[]{:S(2)}, u32[]{:S(2)}) collective-permute-start(f32[1,128,1024]{2,1,0:T(8,128)S(1)} %get-tuple-element.124), channel_id=1, source_target_pairs={{3,2},{7,6},{11,10},{15,14},{19,18},{23,22},{27,26},{31,30}} | collective-permute-start | bytes 1572872 | tf_op jit(solution)/shard_map/ppermute | solution.py:693
  53.7 9.2 %collective-permute-start.10 = (f32[1,128,1024]{2,1,0:T(8,128)S(1)}, f32[1,128,1024]{2,1,0:T(8,128)S(1)}, u32[]{:S(2)}, u32[]{:S(2)}) collective-permute-start(f32[1,128,1024]{2,1,0:T(8,128)S(1)} %get-tuple-element.113), channel_id=1, source_target_pairs={{0,1},{4,5},{8,9},{12,13},{16,17},{20,21},{24,25},{28,29}} | collective-permute-start | bytes 1572872 | tf_op jit(solution)/shard_map/ppermute | solution.py:692
  54.4 19.4 %collective-permute-start.11 = (f32[1,128,1024]{2,1,0:T(8,128)S(1)}, f32[1,128,1024]{2,1,0:T(8,128)S(1)}, u32[]{:S(2)}, u32[]{:S(2)}) collective-permute-start(f32[1,128,1024]{2,1,0:T(8,128)S(1)} %get-tuple-element.113), channel_id=1, source_target_pairs={{3,2},{7,6},{11,10},{15,14},{19,18},{23,22},{27,26},{31,30}} | collective-permute-start | bytes 1572872 | tf_op jit(solution)/shard_map/ppermute | solution.py:693
  55.7 23.6 %collective-permute-start.12 = (f32[1,128,1024]{2,1,0:T(8,128)S(1)}, f32[1,128,1024]{2,1,0:T(8,128)S(1)}, u32[]{:S(2)}, u32[]{:S(2)}) collective-permute-start(f32[1,128,1024]{2,1,0:T(8,128)S(1)} %get-tuple-element.115), channel_id=1, source_target_pairs={{0,1},{4,5},{8,9},{12,13},{16,17},{20,21},{24,25},{28,29}} | collective-permute-start | bytes 1572872 | tf_op jit(solution)/shard_map/ppermute | solution.py:692
  57.1 27.9 %collective-permute-start.13 = (f32[1,128,1024]{2,1,0:T(8,128)S(1)}, f32[1,128,1024]{2,1,0:T(8,128)S(1)}, u32[]{:S(2)}, u32[]{:S(2)}) collective-permute-start(f32[1,128,1024]{2,1,0:T(8,128)S(1)} %get-tuple-element.115), channel_id=1, source_target_pairs={{3,2},{7,6},{11,10},{15,14},{19,18},{23,22},{27,26},{31,30}} | collective-permute-start | bytes 1572872 | tf_op jit(solution)/shard_map/ppermute | solution.py:693
  60.9 30.9 %collective-permute-start.16 = (f32[1,128,1024]{2,1,0:T(8,128)S(1)}, f32[1,128,1024]{2,1,0:T(8,128)S(1)}, u32[]{:S(2)}, u32[]{:S(2)}) collective-permute-start(f32[1,128,1024]{2,1,0:T(8,128)S(1)} %get-tuple-element.121), channel_id=1, source_target_pairs={{0,1},{1,2},{4,5},{5,6},{8,9},{9,10},{12,13},{13,14},{16,17},{17,1... | collective-permute-start | bytes 1572872 | tf_op jit(solution)/shard_map/ppermute | solution.py:692
  62.9 33.5 %collective-permute-start.17 = (f32[1,128,1024]{2,1,0:T(8,128)S(1)}, f32[1,128,1024]{2,1,0:T(8,128)S(1)}, u32[]{:S(2)}, u32[]{:S(2)}) collective-permute-start(f32[1,128,1024]{2,1,0:T(8,128)S(1)} %get-tuple-element.122), channel_id=1, source_target_pairs={{2,1},{3,2},{6,5},{7,6},{10,9},{11,10},{14,13},{15,14},{18,17},{19... | collective-permute-start | bytes 1572872 | tf_op jit(solution)/shard_map/ppermute | solution.py:693
  73.8 24.6 %collective-permute-start.18 = (f32[1,128,1024]{2,1,0:T(8,128)S(1)}, f32[1,128,1024]{2,1,0:T(8,128)S(1)}, u32[]{:S(2)}, u32[]{:S(2)}) collective-permute-start(f32[1,128,1024]{2,1,0:T(8,128)S(1)} %get-tuple-element.125), channel_id=1, source_target_pairs={{0,1},{1,2},{4,5},{5,6},{8,9},{9,10},{12,13},{13,14},{16,17},{17,1... | collective-permute-start | bytes 1572872 | tf_op jit(solution)/shard_map/ppermute | solution.py:692
  79.3 28.2 %collective-permute-start.19 = (f32[1,128,1024]{2,1,0:T(8,128)S(1)}, f32[1,128,1024]{2,1,0:T(8,128)S(1)}, u32[]{:S(2)}, u32[]{:S(2)}) collective-permute-start(f32[1,128,1024]{2,1,0:T(8,128)S(1)} %get-tuple-element.126), channel_id=1, source_target_pairs={{2,1},{3,2},{6,5},{7,6},{10,9},{11,10},{14,13},{15,14},{18,17},{19... | collective-permute-start | bytes 1572872 | tf_op jit(solution)/shard_map/ppermute | solution.py:693
  89.9 20.2 %collective-permute-start.20 = (f32[1,128,1024]{2,1,0:T(8,128)S(1)}, f32[1,128,1024]{2,1,0:T(8,128)S(1)}, u32[]{:S(2)}, u32[]{:S(2)}) collective-permute-start(f32[1,128,1024]{2,1,0:T(8,128)S(1)} %get-tuple-element.130), channel_id=1, source_target_pairs={{0,1},{1,2},{4,5},{5,6},{8,9},{9,10},{12,13},{13,14},{16,17},{17,1... | collective-permute-start | bytes 1572872 | tf_op jit(solution)/shard_map/ppermute | solution.py:692
  91.9 26.9 %collective-permute-start.21 = (f32[1,128,1024]{2,1,0:T(8,128)S(1)}, f32[1,128,1024]{2,1,0:T(8,128)S(1)}, u32[]{:S(2)}, u32[]{:S(2)}) collective-permute-start(f32[1,128,1024]{2,1,0:T(8,128)S(1)} %get-tuple-element.131), channel_id=1, source_target_pairs={{2,1},{3,2},{6,5},{7,6},{10,9},{11,10},{14,13},{15,14},{18,17},{19... | collective-permute-start | bytes 1572872 | tf_op jit(solution)/shard_map/ppermute | solution.py:693
  96.4 24.9 %collective-permute-start.22 = (f32[1,128,1024]{2,1,0:T(8,128)S(1)}, f32[1,128,1024]{2,1,0:T(8,128)S(1)}, u32[]{:S(2)}, u32[]{:S(2)}) collective-permute-start(f32[1,128,1024]{2,1,0:T(8,128)S(1)} %get-tuple-element.135), channel_id=1, source_target_pairs={{0,1},{1,2},{4,5},{5,6},{8,9},{9,10},{12,13},{13,14},{16,17},{17,1... | collective-permute-start | bytes 1572872 | tf_op jit(solution)/shard_map/ppermute | solution.py:692
  98.4 31.6 %collective-permute-start.23 = (f32[1,128,1024]{2,1,0:T(8,128)S(1)}, f32[1,128,1024]{2,1,0:T(8,128)S(1)}, u32[]{:S(2)}, u32[]{:S(2)}) collective-permute-start(f32[1,128,1024]{2,1,0:T(8,128)S(1)} %get-tuple-element.136), channel_id=1, source_target_pairs={{2,1},{3,2},{6,5},{7,6},{10,9},{11,10},{14,13},{15,14},{18,17},{19... | collective-permute-start | bytes 1572872 | tf_op jit(solution)/shard_map/ppermute | solution.py:693
  108.2 24.4 %collective-permute-start.28 = (f32[1,128,1024]{2,1,0:T(8,128)S(1)}, f32[1,128,1024]{2,1,0:T(8,128)S(1)}, u32[]{:S(2)}, u32[]{:S(2)}) collective-permute-start(f32[1,128,1024]{2,1,0:T(8,128)S(1)} %get-tuple-element.141), channel_id=1, source_target_pairs={{0,1},{1,2},{2,3},{4,5},{5,6},{6,7},{8,9},{9,10},{10,11},{12,13},{... | collective-permute-start | bytes 1572872 | tf_op jit(solution)/shard_map/ppermute | solution.py:692
  110.1 45.2 %collective-permute-start.29 = (f32[1,128,1024]{2,1,0:T(8,128)S(1)}, f32[1,128,1024]{2,1,0:T(8,128)S(1)}, u32[]{:S(2)}, u32[]{:S(2)}) collective-permute-start(f32[1,128,1024]{2,1,0:T(8,128)S(1)} %get-tuple-element.142), channel_id=1, source_target_pairs={{1,0},{2,1},{3,2},{5,4},{6,5},{7,6},{9,8},{10,9},{11,10},{13,12},{... | collective-permute-start | bytes 1572872 | tf_op jit(solution)/shard_map/ppermute | solution.py:693
  118.7 22.5 %collective-permute-start.30 = (f32[1,128,1024]{2,1,0:T(8,128)S(1)}, f32[1,128,1024]{2,1,0:T(8,128)S(1)}, u32[]{:S(2)}, u32[]{:S(2)}) collective-permute-start(f32[1,128,1024]{2,1,0:T(8,128)S(1)} %get-tuple-element.138), channel_id=1, source_target_pairs={{0,1},{1,2},{2,3},{4,5},{5,6},{6,7},{8,9},{9,10},{10,11},{12,13},{... | collective-permute-start | bytes 1572872 | tf_op jit(solution)/shard_map/ppermute | solution.py:692
  121.4 29.4 %collective-permute-start.31 = (f32[1,128,1024]{2,1,0:T(8,128)S(1)}, f32[1,128,1024]{2,1,0:T(8,128)S(1)}, u32[]{:S(2)}, u32[]{:S(2)}) collective-permute-start(f32[1,128,1024]{2,1,0:T(8,128)S(1)} %get-tuple-element.139), channel_id=1, source_target_pairs={{1,0},{2,1},{3,2},{5,4},{6,5},{7,6},{9,8},{10,9},{11,10},{13,12},{... | collective-permute-start | bytes 1572872 | tf_op jit(solution)/shard_map/ppermute | solution.py:693
  130.0 26.2 %collective-permute-start.26 = (f32[1,128,1024]{2,1,0:T(8,128)S(1)}, f32[1,128,1024]{2,1,0:T(8,128)S(1)}, u32[]{:S(2)}, u32[]{:S(2)}) collective-permute-start(f32[1,128,1024]{2,1,0:T(8,128)S(1)} %get-tuple-element.144), channel_id=1, source_target_pairs={{0,1},{1,2},{2,3},{4,5},{5,6},{6,7},{8,9},{9,10},{10,11},{12,13},{... | collective-permute-start | bytes 1572872 | tf_op jit(solution)/shard_map/ppermute | solution.py:692
  132.6 29.4 %collective-permute-start.27 = (f32[1,128,1024]{2,1,0:T(8,128)S(1)}, f32[1,128,1024]{2,1,0:T(8,128)S(1)}, u32[]{:S(2)}, u32[]{:S(2)}) collective-permute-start(f32[1,128,1024]{2,1,0:T(8,128)S(1)} %get-tuple-element.145), channel_id=1, source_target_pairs={{1,0},{2,1},{3,2},{5,4},{6,5},{7,6},{9,8},{10,9},{11,10},{13,12},{... | collective-permute-start | bytes 1572872 | tf_op jit(solution)/shard_map/ppermute | solution.py:693
  141.2 22.6 %collective-permute-start.24 = (f32[1,128,1024]{2,1,0:T(8,128)S(1)}, f32[1,128,1024]{2,1,0:T(8,128)S(1)}, u32[]{:S(2)}, u32[]{:S(2)}) collective-permute-start(f32[1,128,1024]{2,1,0:T(8,128)S(1)} %get-tuple-element.147), channel_id=1, source_target_pairs={{0,1},{1,2},{2,3},{4,5},{5,6},{6,7},{8,9},{9,10},{10,11},{12,13},{... | collective-permute-start | bytes 1572872 | tf_op jit(solution)/shard_map/ppermute | solution.py:692
  150.8 22.0 %collective-permute-start.25 = (f32[1,128,1024]{2,1,0:T(8,128)S(1)}, f32[1,128,1024]{2,1,0:T(8,128)S(1)}, u32[]{:S(2)}, u32[]{:S(2)}) collective-permute-start(f32[1,128,1024]{2,1,0:T(8,128)S(1)} %get-tuple-element.148), channel_id=1, source_target_pairs={{1,0},{2,1},{3,2},{5,4},{6,5},{7,6},{9,8},{10,9},{11,10},{13,12},{... | collective-permute-start | bytes 1572872 | tf_op jit(solution)/shard_map/ppermute | solution.py:693

commit v5 on v4

--- a/solution.py
+++ b/solution.py
@@ -165,7 +165,10 @@
     )(features, write_proj, step_size, log_decay, starts.reshape(1, tokens), after)
 
 
-def intra_call(scal, side, features, write_proj, read_proj, step_size, log_decay, starts, skip_weight, after):
+def intra_call(
+    scal, side, features, write_proj, read_proj, step_size, log_decay, starts, skip_weight, out_weight,
+    columns, after,
+):
     tokens, channels = features.shape
     heads = step_size.shape[0]
     groups = write_proj.shape[1] // NSTATE
@@ -176,7 +179,17 @@
     def group(s):
         return s[0] ^ side if groups > 1 else 0
 
-    def kernel(scal, feat, write, read, step, decay, starts, skip, after, out, reach):
+    def kernel(
+        scal, feat, write, read, step, decay, starts, skip, w_hbm, after, out, reach, weight, sem
+    ):
+        copy = pltpu.make_async_copy(
+            w_hbm.at[cut(group(scal) * gch, gch), pl.ds(0, columns)], weight, sem
+        )
+
+        @pl.when(pl.program_id(0) == 0)
+        def _():
+            copy.start()
+
         cum, seg = block_sums(decay[...], starts[...])
         cum_log2 = cum * LOG2E
         vrow = cum_log2 - jnp.log2(step[...])
@@ -215,6 +228,10 @@
             out[:half, part] = top
             out[half:, part] = low
 
+        @pl.when(pl.program_id(0) == blocks - 1)
+        def _():
+            copy.wait()
+
     return pl.pallas_call(
         kernel,
         grid_spec=pltpu.PrefetchScalarGridSpec(
@@ -228,18 +245,22 @@
                 pl.BlockSpec((per_group, SPAN), lambda b, s: (group(s), b)),
                 pl.BlockSpec((1, SPAN), lambda b, s: (0, b)),
                 pl.BlockSpec((1, heads), lambda b, s: (0, 0)),
+                pl.BlockSpec(memory_space=pltpu.HBM),
                 pl.BlockSpec(memory_space=pl.ANY),
             ],
             out_specs=[
                 pl.BlockSpec((SPAN, gch), lambda b, s: (b, 0)),
                 pl.BlockSpec((SPAN, 128), lambda b, s: (b, 0)),
+                pl.BlockSpec(memory_space=pl.ANY),
             ],
+            scratch_shapes=[pltpu.SemaphoreType.DMA(())],
         ),
         out_shape=[
             jax.ShapeDtypeStruct((tokens, gch), F32),
             jax.ShapeDtypeStruct((tokens, 128), F32),
+            jax.ShapeDtypeStruct((gch, columns), BF16),
         ],
-        compiler_params=params(12),
+        compiler_params=params(40),
         cost_estimate=pl.CostEstimate(flops=10**9, bytes_accessed=10**6, transcendentals=0),
         name="intra",
     )(
@@ -251,6 +272,7 @@
         log_decay,
         starts.reshape(1, tokens),
         skip_weight.reshape(1, heads),
+        out_weight,
         after,
     )
 
@@ -406,12 +428,12 @@
     return (gated * lax.rsqrt(mean_square + eps) * gain).astype(BF16)
 
 
-def first_call(scal, sides, entries, fold, inner, reach, gate, read, gain, out_weight, rows, columns, early, before):
+def first_call(scal, sides, entries, fold, inner, reach, gate, read, gain, weight, rows, columns, before):
     tokens, channels = gate.shape
     gch = inner.shape[1]
     groups = channels // gch
     parts, width = entries[0].shape[1], entries[0].shape[3]
-    wide = early * columns
+    wide = weight.shape[1]
     tile = min(512, columns)
     last = groups == 1 or bool(before)
 
@@ -421,21 +443,14 @@
     def kernel(scal, *refs):
         entry_refs, refs = refs[: len(sides)], refs[len(sides) :]
         folds, refs = refs[: len(sides)], refs[len(sides) :]
-        inner, reach, read, gain, gate_hbm, w_hbm = refs[:6]
+        inner, reach, read, gain, gate_hbm, weight = refs[:6]
         earlier, refs = refs[6 : 6 + len(before)], refs[6 + len(before) :]
-        out, *firsts, weight, gate, held, sems, gate_sem = refs
+        out, *firsts, gate, held, gate_sem = refs
         lanes = cut(group(scal) * gch, gch)
         gate_copy = pltpu.make_async_copy(
             gate_hbm.at[cut(scal[2] * rows, rows, rows), lanes], gate, gate_sem
         )
         gate_copy.start()
-        copies = []
-        for t in range(wide // tile):
-            copy = pltpu.make_async_copy(
-                w_hbm.at[cut(group(scal) * gch, gch), pl.ds(t * tile, tile)], weight.at[t], sems.at[t]
-            )
-            copy.start()
-            copies.append(copy)
         for k in range(len(sides)):
             hold_entries(scal[1], entry_refs[k], folds[k].at[0], held.at[k])
         gate_copy.wait()
@@ -448,9 +463,8 @@
         else:
             out[...] = normed
         for t in range(wide // tile):
-            copies[t].wait()
-            product = dot(normed, weight[t])
             here = slice(t * tile, (t + 1) * tile)
+            product = dot(normed, weight[:, here])
             if not last:
                 firsts[0][:, here] = product
                 continue
@@ -483,24 +497,22 @@
                 pl.BlockSpec((rows, NSTATE), lambda j, s: (s[2], group(s))),
                 pl.BlockSpec((1, gch), lambda j, s: (0, group(s))),
                 pl.BlockSpec(memory_space=pltpu.HBM),
-                pl.BlockSpec(memory_space=pltpu.HBM),
+                pl.BlockSpec(memory_space=pltpu.VMEM),
             ]
             + [whole(v) for v in before],
             out_specs=[
                 pl.BlockSpec(shape, lambda j, s, zeros=(0,) * len(shape): zeros) for shape, _ in shapes
             ],
             scratch_shapes=[
-                pltpu.VMEM((wide // tile, gch, tile), BF16),
                 pltpu.VMEM((rows, gch), BF16),
                 pltpu.VMEM((len(sides), parts, NSTATE, width), BF16),
-                pltpu.SemaphoreType.DMA((wide // tile,)),
                 pltpu.SemaphoreType.DMA(()),
             ],
         ),
         out_shape=[jax.ShapeDtypeStruct(shape, kind) for shape, kind in shapes],
-        compiler_params=params(40),
+        compiler_params=params(16),
         name="first",
-    )(scal, *entries, *fold, inner, reach, read, gain, gate, out_weight, *before)
+    )(scal, *entries, *fold, inner, reach, read, gain, gate, weight, *before)
 
 
 def rest_call(scal, entries, fold, inner, reach, gate, read, gain, rows):
@@ -726,9 +738,15 @@
     other, pre_other = states_call(1, direct, *inputs, chunks, starts)
     mine, pre_mine = states_call(0, direct, *inputs, chunks, other)
 
+    wide = out_weight.shape[1]
+    pieces = 4
+    size = wide // pieces
+    early = 2
+
     def intra(side, after):
         return intra_call(
-            scal, side, features, write_proj, read_proj, step_size, log_decay, starts, skip_weight, after
+            scal, side, features, write_proj, read_proj, step_size, log_decay, starts, skip_weight,
+            out_weight, early * size, after,
         )
 
     if direct:
@@ -751,18 +769,14 @@
         entries = [chain(mine, "ctx")[None], chain(other, "ctx")[None]]
         local = [intra(g, mine) for g in range(groups)]
         fold = [fold_call([], pre, tokens) for pre in (pre_mine, pre_other)]
-    inner, reach = zip(*local)
+    inner, reach, weights = zip(*local)
     gain = norm_gain.reshape(1, channels)
-    wide = out_weight.shape[1]
-    pieces = 4
-    size = wide // pieces
-    early = 2
     firsts = []
     for sides in [[0], [1]] if groups > 1 else [[0, 1]]:
         at = sides[0]
         firsts = first_call(
             scal, sides, [entries[k] for k in sides], [fold[k] for k in sides], inner[at], reach[at], gate_values, read_proj,
-            gain, out_weight, rows, size, early, firsts,
+            gain, weights[at], rows, size, firsts,
         )
     normed, *firsts = firsts
     moving = [send(f, f, 1, "head") for f in firsts]
@@ -777,8 +791,12 @@
     sums = None
     for s in range(2, line):
         for p in range(pieces):
+            turn = (s - 1) * pieces + p
             if sums is not None:
                 mine[p], sums = lax.optimization_barrier((mine[p], sums))
+            if turn >= 6:
+                back = (turn - 2) % pieces
+                mine[p], moving[back] = lax.optimization_barrier((mine[p], moving[back]))
             sums = sum_call(scal, mine[p], *moving[p], s)
             moving[p] = send(*sums, s, "head")
     result = None

time: 174 us -> 173 us (level); the launches traced: 174 us -> 171 us
  waiting for transfers between devices: 31.4 us -> 56.6 us
  starting transfers between devices: 87.9 us -> 63 us
  Pallas kernels: 51.8 us -> 48.8 us
    ppermute x12, starting transfers between devices: 65 us -> 40 us  [send(): lax.ppermute(to_down, axis, [(i, i - 1) for i in range(1, count) if step...]
    ppermute x12, waiting for transfers between devices: 26.3 us -> 48.6 us  [send(): lax.ppermute(to_down, axis, [(i, i - 1) for i in range(1, count) if step...]
    pallas_call x2, Pallas kernels: 6.28 us -> 3.73 us  [first_call(): pl.pallas_call(kernel, grid_spec=pltpu.PrefetchScalarGridSpec(num_scalar_...]
    ppermute x12, waiting for transfers between devices: 0.89 us -> 2.82 us  [send(): lax.ppermute(to_up, axis, [(i, i + 1) for i in range(count - 1) if step >...]
  transfers between devices with their start and end apart: 32 -> 32, of which waited for: 8 -> 15; matrix products, arithmetic and copies ran while one was open for 0% -> 0% of each run, Pallas kernels for 25% -> 25%
where the time goes in v5:
time: 173 us; the launch traced here: 171 us
  starting transfers between devices  63 us (36%)
  waiting for transfers between devices  56.6 us (33%)
  Pallas kernels  48.8 us (28%)
  local copies, waits for them, and re-layouts  1.81 us (1%)
    ppermute x12, waiting for transfers between devices, send(): lax.ppermute(to_down, axis, [(i, i - 1) for i in range(1, count) if step...  48.6 us
    ppermute x12, starting transfers between devices, send(): lax.ppermute(to_down, axis, [(i, i - 1) for i in range(1, count) if step...  40 us
    pallas_call x5, Pallas kernels, project_call(): pl.pallas_call(kernel, in_specs=[vmem] * len(parts) + [pl.BlockSpec(memor...  20.5 us
    ppermute x12, starting transfers between devices, send(): lax.ppermute(to_up, axis, [(i, i + 1) for i in range(count - 1) if step >...  15.8 us
    ppermute x6, starting transfers between devices, exchange(): lax.ppermute(parts[k], axis, [(i, i ^ 2 * k) for i in range(count)])  7.11 us
    pallas_call x2, Pallas kernels, intra_call(): pl.pallas_call(kernel, grid_spec=pltpu.PrefetchScalarGridSpec(num_scalar_...  6.82 us
    pallas_call x8, Pallas kernels, sum_call(): pl.pallas_call(kernel, grid_spec=pltpu.PrefetchScalarGridSpec(num_scalar_...  5.22 us
    pallas_call x2, Pallas kernels, states_call(): pl.pallas_call(kernel, in_specs=[pl.BlockSpec(memory_space=pltpu.HBM)] *...  4.97 us
  transfers between devices with their start and end apart: 32, of which 15 were waited for; matrix products, arithmetic and copies ran while one was open for 0% of the time, Pallas kernels for 25%

profile of v5, /device:TPU:16, one launch (start us, length us, event | category | flops | bytes accessed | tf_op | source)
XLA Modules:
  0.0 170.9 jit_solution(10398728564113507366)
XLA Ops:
  0.0 3.3 %states.2 = (f32[4,136,256]{2,1,0:T(8,128)}, f32[1,136,1024]{2,1,0:T(8,128)}) custom-call(bf16[512,2048]{1,0:T(8,128)(2,1)} %feat.3, bf16[512,256]{1,0:T(8,128)(2,1)} %write.3, f32[32,512]{1,0:T(8,128)} %step.3, f32[32,512]{1,0:T(8,128)} %decay.3, s32[1,512]{1,0:T(1,128)} %bitcast.10, s32[512]{0:T(512)} %after.1), custom_call_target="tpu_custom_call" | custom-call | flops 100000000 | bytes 1000000 | tf_op jit(solution)/shard_map/states/pallas_call | solution.py:143
  4.6 1.6 states.3
  6.4 1.6 collective-permute-start.1
  7.9 1.5 collective-permute-start.2
  10.7 3.4 %intra.2 = (f32[512,1024]{1,0:T(8,128)S(1)}, f32[512,128]{1,0:T(8,128)S(1)}, bf16[1024,2048]{1,0:T(8,128)(2,1)S(1)}) custom-call(s32[14]{0:T(128)S(1)} %pad_add_fusion.scal, bf16[512,2048]{1,0:T(8,128)(2,1)S(1)} %copy-done, bf16[512,256]{1,0:T(8,128)(2,1)S(1)} %copy-done.3, bf16[512,256]{1,0:T(8,128)(2,1)S(1)} %copy-done.2, f32[32,512]{1,0:T(8,128)S(1)} %copy-done.4, ...), custom_call_target="tpu_custom_call" | custom-call | flops 1000000000 | bytes 1000000 | tf_op jit(solution)/shard_map/intra/pallas_call | solution.py:235
  14.1 2.5 %collective-permute-done.2.refs_2_ = f32[136,256]{1,0:T(8,128)S(1)} collective-permute-done((f32[136,256]{1,0:T(8,128)S(1)}, f32[136,256]{1,0:T(8,128)S(1)}, u32[]{:S(2)}, u32[]{:S(2)}) %collective-permute-start.2) | collective-permute-done | bytes 139296 | tf_op jit(solution)/shard_map/ppermute | solution.py:390
  16.8 1.3 collective-permute-start.4
  18.9 1.4 collective-permute-start.6
  20.5 3.4 %intra.3 = (f32[512,1024]{1,0:T(8,128)S(1)}, f32[512,128]{1,0:T(8,128)S(1)}, bf16[1024,2048]{1,0:T(8,128)(2,1)S(1)}) custom-call(s32[14]{0:T(128)S(1)} %pad_add_fusion.scal, bf16[512,2048]{1,0:T(8,128)(2,1)S(1)} %copy-done, bf16[512,256]{1,0:T(8,128)(2,1)S(1)} %copy-done.3, bf16[512,256]{1,0:T(8,128)(2,1)S(1)} %copy-done.2, f32[32,512]{1,0:T(8,128)S(1)} %copy-done.4, ...), custom_call_target="tpu_custom_call" | custom-call | flops 1000000000 | bytes 1000000 | tf_op jit(solution)/shard_map/intra/pallas_call | solution.py:235
  23.9 1.8 %collective-permute-done.5.refs_2_ = f32[128,256]{1,0:T(8,128)S(1)} collective-permute-done((f32[128,256]{1,0:T(8,128)S(1)}, f32[128,256]{1,0:T(8,128)S(1)}, u32[]{:S(2)}, u32[]{:S(2)}) %collective-permute-start.5) | collective-permute-done | bytes 131104 | tf_op jit(solution)/shard_map/ppermute | solution.py:390
  25.9 1.9 %first.2 = (bf16[128,1024]{1,0:T(8,128)(2,1)S(1)}, f32[128,2048]{1,0:T(8,128)S(1)}) custom-call(s32[14]{0:T(128)S(1)} %pad_add_fusion.scal, f32[2,4,136,256]{3,2,1,0:T(8,128)S(1)} %pack.1.refs_0_, f32[2,136,1024]{2,1,0:T(8,128)S(1)} %fold.2.refs_1_.refs_6_, f32[512,1024]{1,0:T(8,128)S(1)} %get-tuple-element.131.refs_2_, ...), custom_call_target="tpu_custom_call" | custom-call | tf_op jit(solution)/shard_map/first/pallas_call | solution.py:487
  28.7 1.9 %first.3 = (bf16[1,128,2048]{2,1,0:T(8,128)(2,1)S(1)}, f32[1,128,1024]{2,1,0:T(8,128)S(1)}, f32[1,128,1024]{2,1,0:T(8,128)S(1)}) custom-call(s32[14]{0:T(128)S(1)} %pad_add_fusion.scal, f32[2,4,136,256]{3,2,1,0:T(8,128)S(1)} %collective-permute-done.7.refs_0_.refs_1_, f32[2,136,1024]{2,1,0:T(8,128)S(1)} %fold.3.refs_1_.refs_7_, ...), custom_call_target="tpu_custom_call" | custom-call | tf_op jit(solution)/shard_map/first/pallas_call | solution.py:487
  30.6 1.3 collective-permute-start.9
  32.6 1.3 collective-permute-start.15
  34.8 3.5 %rest.1.refs_1_ = bf16[3,128,2048]{2,1,0:T(8,128)(2,1)S(1)} custom-call(s32[14]{0:T(128)S(1)} %pad_add_fusion.scal, f32[2,4,136,256]{3,2,1,0:T(8,128)S(1)} %pack.1.refs_0_, f32[2,4,136,256]{3,2,1,0:T(8,128)S(1)} %collective-permute-done.7.refs_0_.refs_1_, f32[512,1024]{1,0:T(8,128)S(1)} %get-tuple-element.131.refs_2_, ...), custom_call_target="tpu_custom_call" | custom-call | flops 1000000000 | bytes 1000000 | tf_op jit(solution)/shard_map/rest/pallas_call | solution.py:562
  38.3 4.1 %project.6.a.b = f32[4,128,1024]{2,1,0:T(8,128)S(1)} custom-call(bf16[1,128,2048]{2,1,0:T(8,128)(2,1)S(1)} %get-tuple-element.138.refs_0_, bf16[3,128,2048]{2,1,0:T(8,128)(2,1)S(1)} %rest.1.refs_1_, bf16[2048,4096]{1,0:T(8,128)(2,1)} %refs_2_.7), custom_call_target="tpu_custom_call" | custom-call | flops 2147483648 | bytes 6291456 | tf_op jit(solution)/shard_map/project/pallas_call | solution.py:613
  42.4 4.1 %project.5.a.b = f32[4,128,1024]{2,1,0:T(8,128)S(1)} custom-call(bf16[1,128,2048]{2,1,0:T(8,128)(2,1)S(1)} %get-tuple-element.138.refs_0_, bf16[3,128,2048]{2,1,0:T(8,128)(2,1)S(1)} %rest.1.refs_1_, bf16[2048,4096]{1,0:T(8,128)(2,1)} %refs_2_.7), custom_call_target="tpu_custom_call" | custom-call | flops 2147483648 | bytes 6291456 | tf_op jit(solution)/shard_map/project/pallas_call | solution.py:613
  47.3 4.0 %project.7 = (f32[1,128,1024]{2,1,0:T(8,128)S(1)}, f32[1,128,1024]{2,1,0:T(8,128)S(1)}) custom-call(bf16[1,128,2048]{2,1,0:T(8,128)(2,1)S(1)} %get-tuple-element.138.refs_0_, bf16[2048,4096]{1,0:T(8,128)(2,1)} %refs_2_.7), custom_call_target="tpu_custom_call" | custom-call | flops 1073741824 | bytes 9437184 | tf_op jit(solution)/shard_map/project/pallas_call | solution.py:613
  51.3 1.3 collective-permute-start.13
  53.9 1.3 collective-permute-start.16
  55.2 3.3 %collective-permute-done.15.d = f32[1,128,1024]{2,1,0:T(8,128)S(1)} collective-permute-done((f32[1,128,1024]{2,1,0:T(8,128)S(1)}, f32[1,128,1024]{2,1,0:T(8,128)S(1)}, u32[]{:S(2)}, u32[]{:S(2)}) %collective-permute-start.15) | collective-permute-done | bytes 524320 | tf_op jit(solution)/shard_map/ppermute | solution.py:705
  58.5 1.9 %collective-permute-start.17 = (f32[1,128,1024]{2,1,0:T(8,128)S(1)}, f32[1,128,1024]{2,1,0:T(8,128)S(1)}, u32[]{:S(2)}, u32[]{:S(2)}) collective-permute-start(f32[1,128,1024]{2,1,0:T(8,128)S(1)} %get-tuple-element.148), channel_id=1, source_target_pairs={{2,1},{3,2},{6,5},{7,6},{10,9},{11,10},{14,13},{15,14},{18,17},{19... | collective-permute-start | bytes 1572872 | tf_op jit(solution)/shard_map/ppermute | solution.py:705
  60.4 1.3 collective-permute-start.11
  62.4 7.3 %collective-permute-done.13.d = f32[1,128,1024]{2,1,0:T(8,128)S(1)} collective-permute-done((f32[1,128,1024]{2,1,0:T(8,128)S(1)}, f32[1,128,1024]{2,1,0:T(8,128)S(1)}, u32[]{:S(2)}, u32[]{:S(2)}) %collective-permute-start.13) | collective-permute-done | bytes 524320 | tf_op jit(solution)/shard_map/ppermute | solution.py:705
  70.4 1.3 collective-permute-start.18
  71.7 4.1 %project.9.a.b = f32[4,128,1024]{2,1,0:T(8,128)S(1)} custom-call(bf16[1,128,2048]{2,1,0:T(8,128)(2,1)S(1)} %get-tuple-element.138.refs_0_, bf16[3,128,2048]{2,1,0:T(8,128)(2,1)S(1)} %rest.1.refs_1_, bf16[2048,4096]{1,0:T(8,128)(2,1)} %refs_2_.7), custom_call_target="tpu_custom_call" | custom-call | flops 2147483648 | bytes 6291456 | tf_op jit(solution)/shard_map/project/pallas_call | solution.py:613
  75.9 8.1 %collective-permute-start.19 = (f32[1,128,1024]{2,1,0:T(8,128)S(1)}, f32[1,128,1024]{2,1,0:T(8,128)S(1)}, u32[]{:S(2)}, u32[]{:S(2)}) collective-permute-start(f32[1,128,1024]{2,1,0:T(8,128)S(1)} %get-tuple-element.152), channel_id=1, source_target_pairs={{2,1},{3,2},{6,5},{7,6},{10,9},{11,10},{14,13},{15,14},{18,17},{19... | collective-permute-start | bytes 1572872 | tf_op jit(solution)/shard_map/ppermute | solution.py:705
  84.7 7.5 %collective-permute-done.11.d = f32[1,128,1024]{2,1,0:T(8,128)S(1)} collective-permute-done((f32[1,128,1024]{2,1,0:T(8,128)S(1)}, f32[1,128,1024]{2,1,0:T(8,128)S(1)}, u32[]{:S(2)}, u32[]{:S(2)}) %collective-permute-start.11) | collective-permute-done | bytes 524320 | tf_op jit(solution)/shard_map/ppermute | solution.py:705
  92.2 1.3 collective-permute-start.20
  93.5 4.6 %collective-permute-start.21 = (f32[1,128,1024]{2,1,0:T(8,128)S(1)}, f32[1,128,1024]{2,1,0:T(8,128)S(1)}, u32[]{:S(2)}, u32[]{:S(2)}) collective-permute-start(f32[1,128,1024]{2,1,0:T(8,128)S(1)} %get-tuple-element.158), channel_id=1, source_target_pairs={{2,1},{3,2},{6,5},{7,6},{10,9},{11,10},{14,13},{15,14},{18,17},{19... | collective-permute-start | bytes 1572872 | tf_op jit(solution)/shard_map/ppermute | solution.py:705
  98.1 4.1 %project.8.a.b = f32[4,128,1024]{2,1,0:T(8,128)S(1)} custom-call(bf16[1,128,2048]{2,1,0:T(8,128)(2,1)S(1)} %get-tuple-element.138.refs_0_, bf16[3,128,2048]{2,1,0:T(8,128)(2,1)S(1)} %rest.1.refs_1_, bf16[2048,4096]{1,0:T(8,128)(2,1)} %refs_2_.7), custom_call_target="tpu_custom_call" | custom-call | flops 2147483648 | bytes 6291456 | tf_op jit(solution)/shard_map/project/pallas_call | solution.py:613
  104.1 1.3 collective-permute-start.22
  105.4 4.6 %collective-permute-start.23 = (f32[1,128,1024]{2,1,0:T(8,128)S(1)}, f32[1,128,1024]{2,1,0:T(8,128)S(1)}, u32[]{:S(2)}, u32[]{:S(2)}) collective-permute-start(f32[1,128,1024]{2,1,0:T(8,128)S(1)} %get-tuple-element.164), channel_id=1, source_target_pairs={{2,1},{3,2},{6,5},{7,6},{10,9},{11,10},{14,13},{15,14},{18,17},{19... | collective-permute-start | bytes 1572872 | tf_op jit(solution)/shard_map/ppermute | solution.py:705
  110.0 4.7 %collective-permute-done.21.d = f32[1,128,1024]{2,1,0:T(8,128)S(1)} collective-permute-done((f32[1,128,1024]{2,1,0:T(8,128)S(1)}, f32[1,128,1024]{2,1,0:T(8,128)S(1)}, u32[]{:S(2)}, u32[]{:S(2)}) %collective-permute-start.21) | collective-permute-done | bytes 524320 | tf_op jit(solution)/shard_map/ppermute | solution.py:705
  115.3 1.9 %collective-permute-start.24 = (f32[1,128,1024]{2,1,0:T(8,128)S(1)}, f32[1,128,1024]{2,1,0:T(8,128)S(1)}, u32[]{:S(2)}, u32[]{:S(2)}) collective-permute-start(f32[1,128,1024]{2,1,0:T(8,128)S(1)} %get-tuple-element.169), channel_id=1, source_target_pairs={{0,1},{1,2},{2,3},{4,5},{5,6},{6,7},{8,9},{9,10},{10,11},{12,13},{... | collective-permute-start | bytes 1572872 | tf_op jit(solution)/shard_map/ppermute | solution.py:704
  117.3 3.9 %collective-permute-start.25 = (f32[1,128,1024]{2,1,0:T(8,128)S(1)}, f32[1,128,1024]{2,1,0:T(8,128)S(1)}, u32[]{:S(2)}, u32[]{:S(2)}) collective-permute-start(f32[1,128,1024]{2,1,0:T(8,128)S(1)} %get-tuple-element.170), channel_id=1, source_target_pairs={{1,0},{2,1},{3,2},{5,4},{6,5},{7,6},{9,8},{10,9},{11,10},{13,12},{... | collective-permute-start | bytes 1572872 | tf_op jit(solution)/shard_map/ppermute | solution.py:705
  121.2 4.7 %collective-permute-done.23.d = f32[1,128,1024]{2,1,0:T(8,128)S(1)} collective-permute-done((f32[1,128,1024]{2,1,0:T(8,128)S(1)}, f32[1,128,1024]{2,1,0:T(8,128)S(1)}, u32[]{:S(2)}, u32[]{:S(2)}) %collective-permute-start.23) | collective-permute-done | bytes 524320 | tf_op jit(solution)/shard_map/ppermute | solution.py:705
  126.6 1.9 %collective-permute-start.26 = (f32[1,128,1024]{2,1,0:T(8,128)S(1)}, f32[1,128,1024]{2,1,0:T(8,128)S(1)}, u32[]{:S(2)}, u32[]{:S(2)}) collective-permute-start(f32[1,128,1024]{2,1,0:T(8,128)S(1)} %get-tuple-element.175), channel_id=1, source_target_pairs={{0,1},{1,2},{2,3},{4,5},{5,6},{6,7},{8,9},{9,10},{10,11},{12,13},{... | collective-permute-start | bytes 1572872 | tf_op jit(solution)/shard_map/ppermute | solution.py:704
  128.5 3.9 %collective-permute-start.27 = (f32[1,128,1024]{2,1,0:T(8,128)S(1)}, f32[1,128,1024]{2,1,0:T(8,128)S(1)}, u32[]{:S(2)}, u32[]{:S(2)}) collective-permute-start(f32[1,128,1024]{2,1,0:T(8,128)S(1)} %get-tuple-element.176), channel_id=1, source_target_pairs={{1,0},{2,1},{3,2},{5,4},{6,5},{7,6},{9,8},{10,9},{11,10},{13,12},{... | collective-permute-start | bytes 1572872 | tf_op jit(solution)/shard_map/ppermute | solution.py:705
  132.4 4.7 %collective-permute-done.25.d = f32[1,128,1024]{2,1,0:T(8,128)S(1)} collective-permute-done((f32[1,128,1024]{2,1,0:T(8,128)S(1)}, f32[1,128,1024]{2,1,0:T(8,128)S(1)}, u32[]{:S(2)}, u32[]{:S(2)}) %collective-permute-start.25) | collective-permute-done | bytes 524320 | tf_op jit(solution)/shard_map/ppermute | solution.py:705
  137.8 1.9 %collective-permute-start.30 = (f32[1,128,1024]{2,1,0:T(8,128)S(1)}, f32[1,128,1024]{2,1,0:T(8,128)S(1)}, u32[]{:S(2)}, u32[]{:S(2)}) collective-permute-start(f32[1,128,1024]{2,1,0:T(8,128)S(1)} %get-tuple-element.181), channel_id=1, source_target_pairs={{0,1},{1,2},{2,3},{4,5},{5,6},{6,7},{8,9},{9,10},{10,11},{12,13},{... | collective-permute-start | bytes 1572872 | tf_op jit(solution)/shard_map/ppermute | solution.py:704
  139.7 3.9 %collective-permute-start.31 = (f32[1,128,1024]{2,1,0:T(8,128)S(1)}, f32[1,128,1024]{2,1,0:T(8,128)S(1)}, u32[]{:S(2)}, u32[]{:S(2)}) collective-permute-start(f32[1,128,1024]{2,1,0:T(8,128)S(1)} %get-tuple-element.182), channel_id=1, source_target_pairs={{1,0},{2,1},{3,2},{5,4},{6,5},{7,6},{9,8},{10,9},{11,10},{13,12},{... | collective-permute-start | bytes 1572872 | tf_op jit(solution)/shard_map/ppermute | solution.py:705
  143.7 4.7 %collective-permute-done.27.d = f32[1,128,1024]{2,1,0:T(8,128)S(1)} collective-permute-done((f32[1,128,1024]{2,1,0:T(8,128)S(1)}, f32[1,128,1024]{2,1,0:T(8,128)S(1)}, u32[]{:S(2)}, u32[]{:S(2)}) %collective-permute-start.27) | collective-permute-done | bytes 524320 | tf_op jit(solution)/shard_map/ppermute | solution.py:705
  149.1 1.9 %collective-permute-start.28 = (f32[1,128,1024]{2,1,0:T(8,128)S(1)}, f32[1,128,1024]{2,1,0:T(8,128)S(1)}, u32[]{:S(2)}, u32[]{:S(2)}) collective-permute-start(f32[1,128,1024]{2,1,0:T(8,128)S(1)} %get-tuple-element.187), channel_id=1, source_target_pairs={{0,1},{1,2},{2,3},{4,5},{5,6},{6,7},{8,9},{9,10},{10,11},{12,13},{... | collective-permute-start | bytes 1572872 | tf_op jit(solution)/shard_map/ppermute | solution.py:704
  151.0 3.9 %collective-permute-start.29 = (f32[1,128,1024]{2,1,0:T(8,128)S(1)}, f32[1,128,1024]{2,1,0:T(8,128)S(1)}, u32[]{:S(2)}, u32[]{:S(2)}) collective-permute-start(f32[1,128,1024]{2,1,0:T(8,128)S(1)} %get-tuple-element.188), channel_id=1, source_target_pairs={{1,0},{2,1},{3,2},{5,4},{6,5},{7,6},{9,8},{10,9},{11,10},{13,12},{... | collective-permute-start | bytes 1572872 | tf_op jit(solution)/shard_map/ppermute | solution.py:705
  156.7 2.9 %collective-permute-done.31.d = f32[1,128,1024]{2,1,0:T(8,128)S(1)} collective-permute-done((f32[1,128,1024]{2,1,0:T(8,128)S(1)}, f32[1,128,1024]{2,1,0:T(8,128)S(1)}, u32[]{:S(2)}, u32[]{:S(2)}) %collective-permute-start.31) | collective-permute-done | bytes 524320 | tf_op jit(solution)/shard_map/ppermute | solution.py:705
  160.5 2.8 %collective-permute-done.28.c = f32[1,128,1024]{2,1,0:T(8,128)S(1)} collective-permute-done((f32[1,128,1024]{2,1,0:T(8,128)S(1)}, f32[1,128,1024]{2,1,0:T(8,128)S(1)}, u32[]{:S(2)}, u32[]{:S(2)}) %collective-permute-start.28) | collective-permute-done | bytes 524320 | tf_op jit(solution)/shard_map/ppermute | solution.py:704
  163.3 6.8 %collective-permute-done.29.d = f32[1,128,1024]{2,1,0:T(8,128)S(1)} collective-permute-done((f32[1,128,1024]{2,1,0:T(8,128)S(1)}, f32[1,128,1024]{2,1,0:T(8,128)S(1)}, u32[]{:S(2)}, u32[]{:S(2)}) %collective-permute-start.29) | collective-permute-done | bytes 524320 | tf_op jit(solution)/shard_map/ppermute | solution.py:705
  (69 shorter events, 18.3 us)
Async XLA Ops:
  0.0 3.5 %copy-start.5 = (f32[32,512]{1,0:T(8,128)S(1)}, f32[32,512]{1,0:T(8,128)}, u32[]{:S(2)}) copy-start(f32[32,512]{1,0:T(8,128)} %decay.3) | copy-start | bytes 196612
  0.0 3.5 %copy-start.4 = (f32[32,512]{1,0:T(8,128)S(1)}, f32[32,512]{1,0:T(8,128)}, u32[]{:S(2)}) copy-start(f32[32,512]{1,0:T(8,128)} %step.3) | copy-start | bytes 196612
  0.0 3.5 %copy-start.3 = (bf16[512,256]{1,0:T(8,128)(2,1)S(1)}, bf16[512,256]{1,0:T(8,128)(2,1)}, u32[]{:S(2)}) copy-start(bf16[512,256]{1,0:T(8,128)(2,1)} %write.3) | copy-start | bytes 786436
  0.0 3.5 %copy-start = (bf16[512,2048]{1,0:T(8,128)(2,1)S(1)}, bf16[512,2048]{1,0:T(8,128)(2,1)}, u32[]{:S(2)}) copy-start(bf16[512,2048]{1,0:T(8,128)(2,1)} %feat.3) | copy-start | bytes 6291460
  0.0 3.5 %copy-start.9 = (s32[512]{0:T(512)S(1)}, s32[512]{0:T(512)}, u32[]{:S(2)}) copy-start(s32[512]{0:T(512)} %after.1) | copy-start | bytes 6148
  3.4 2.9 %collective-permute-start = (f32[4,136,256]{2,1,0:T(8,128)}, f32[4,136,256]{2,1,0:T(8,128)S(1)}, u32[]{:S(2)}, u32[]{:S(2)}) collective-permute-start(f32[4,136,256]{2,1,0:T(8,128)} %get-tuple-element.99.after), channel_id=1, source_target_pairs={{0,4},{4,0},{8,12},{12,8},{16,20},{20,16},{24,28},{28,24},{1,5},{5... | collective-permute-start | bytes 1671176 | tf_op jit(solution)/shard_map/ppermute | solution.py:396
  3.5 7.2 %copy-start.10 = (f32[32]{0:T(128)S(1)}, f32[32]{0:T(128)}, u32[]{:S(2)}) copy-start(f32[32]{0:T(128)} %param.18) | copy-start | bytes 388
  3.5 7.2 %copy-start.2 = (bf16[512,256]{1,0:T(8,128)(2,1)S(1)}, bf16[512,256]{1,0:T(8,128)(2,1)}, u32[]{:S(2)}) copy-start(bf16[512,256]{1,0:T(8,128)(2,1)} %refs_9_.1) | copy-start | bytes 786436
  3.6 1.1 copy-start.7
  6.4 7.7 %collective-permute-start.1 = (f32[136,256]{1,0:T(8,128)S(1)}, f32[136,256]{1,0:T(8,128)S(1)}, u32[]{:S(2)}, u32[]{:S(2)}) collective-permute-start(f32[136,256]{1,0:T(8,128)S(1)} %get-tuple-element.107), channel_id=1, source_target_pairs={{0,8},{4,12},{8,0},{12,4},{16,24},{20,28},{24,16},{28,20},{1,9},{5... | collective-permute-start | bytes 417800 | tf_op jit(solution)/shard_map/ppermute | solution.py:390
  7.9 8.7 %collective-permute-start.2 = (f32[136,256]{1,0:T(8,128)S(1)}, f32[136,256]{1,0:T(8,128)S(1)}, u32[]{:S(2)}, u32[]{:S(2)}) collective-permute-start(f32[136,256]{1,0:T(8,128)S(1)} %get-tuple-element.108), channel_id=1, source_target_pairs={{0,16},{4,20},{8,24},{12,28},{16,0},{20,4},{24,8},{28,12},{1,17},{... | collective-permute-start | bytes 417800 | tf_op jit(solution)/shard_map/ppermute | solution.py:390
  9.5 7.2 %collective-permute-start.3 = (f32[136,256]{1,0:T(8,128)S(1)}, f32[136,256]{1,0:T(8,128)S(1)}, u32[]{:S(2)}, u32[]{:S(2)}) collective-permute-start(f32[136,256]{1,0:T(8,128)S(1)} %get-tuple-element.109), channel_id=1, source_target_pairs={{0,24},{4,28},{8,16},{12,20},{16,8},{20,12},{24,0},{28,4},{1,25},{... | collective-permute-start | bytes 417800 | tf_op jit(solution)/shard_map/ppermute | solution.py:390
  16.8 7.1 %collective-permute-start.4 = (f32[128,256]{1,0:T(8,128)S(1)}, f32[128,256]{1,0:T(8,128)S(1)}, u32[]{:S(2)}, u32[]{:S(2)}) collective-permute-start(f32[128,256]{1,0:T(8,128)S(1)} %get-tuple-element.112), channel_id=1, source_target_pairs={{0,8},{4,12},{8,0},{12,4},{16,24},{20,28},{24,16},{28,20},{1,9},{5... | collective-permute-start | bytes 393224 | tf_op jit(solution)/shard_map/ppermute | solution.py:390
  18.1 7.6 %collective-permute-start.5 = (f32[128,256]{1,0:T(8,128)S(1)}, f32[128,256]{1,0:T(8,128)S(1)}, u32[]{:S(2)}, u32[]{:S(2)}) collective-permute-start(f32[128,256]{1,0:T(8,128)S(1)} %get-tuple-element.113), channel_id=1, source_target_pairs={{0,16},{4,20},{8,24},{12,28},{16,0},{20,4},{24,8},{28,12},{1,17},{... | collective-permute-start | bytes 393224 | tf_op jit(solution)/shard_map/ppermute | solution.py:390
  18.9 6.8 %collective-permute-start.6 = (f32[128,256]{1,0:T(8,128)S(1)}, f32[128,256]{1,0:T(8,128)S(1)}, u32[]{:S(2)}, u32[]{:S(2)}) collective-permute-start(f32[128,256]{1,0:T(8,128)S(1)} %get-tuple-element.114), channel_id=1, source_target_pairs={{0,24},{4,28},{8,16},{12,20},{16,8},{20,12},{24,0},{28,4},{1,25},{... | collective-permute-start | bytes 393224 | tf_op jit(solution)/shard_map/ppermute | solution.py:390
  23.9 2.0 %copy-start.1 = (bf16[512,2048]{1,0:T(8,128)(2,1)S(1)}, bf16[512,2048]{1,0:T(8,128)(2,1)}, u32[]{:S(2)}) copy-start(bf16[512,2048]{1,0:T(8,128)(2,1)} %refs_8_.1) | copy-start | bytes 6291460
  23.9 2.0 %copy-start.8 = (f32[2048]{0:T(1024)S(1)}, f32[2048]{0:T(1024)}, u32[]{:S(2)}) copy-start(f32[2048]{0:T(1024)} %param.19) | copy-start | bytes 24580
  25.8 2.8 %collective-permute-start.7 = (f32[2,4,136,256]{3,2,1,0:T(8,128)S(1)}, f32[2,4,136,256]{3,2,1,0:T(8,128)S(1)}, u32[]{:S(2)}, u32[]{:S(2)}) collective-permute-start(f32[2,4,136,256]{3,2,1,0:T(8,128)S(1)} %pack.1.refs_0_), channel_id=1, source_target_pairs={{0,4},{4,0},{8,12},{12,8},{16,20},{20,16},{24,28},{28,24},{1,5},{5... | collective-permute-start | bytes 3342344 | tf_op jit(solution)/shard_map/ppermute | solution.py:396
  25.9 2.7 %copy-start.6 = (f32[1,136,1024]{2,1,0:T(8,128)S(1)}, f32[1,136,1024]{2,1,0:T(8,128)}, u32[]{:S(2)}) copy-start(f32[1,136,1024]{2,1,0:T(8,128)} %get-tuple-element.126.refs_1_) | copy-start | bytes 1671172
  30.6 16.7 %collective-permute-start.9 = (f32[1,128,1024]{2,1,0:T(8,128)S(1)}, f32[1,128,1024]{2,1,0:T(8,128)S(1)}, u32[]{:S(2)}, u32[]{:S(2)}) collective-permute-start(f32[1,128,1024]{2,1,0:T(8,128)S(1)} %get-tuple-element.137), channel_id=1, source_target_pairs={{3,2},{7,6},{11,10},{15,14},{19,18},{23,22},{27,26},{31,30}} | collective-permute-start | bytes 1572872 | tf_op jit(solution)/shard_map/ppermute | solution.py:705
  31.9 15.4 %collective-permute-start.8 = (f32[1,128,1024]{2,1,0:T(8,128)S(1)}, f32[1,128,1024]{2,1,0:T(8,128)S(1)}, u32[]{:S(2)}, u32[]{:S(2)}) collective-permute-start(f32[1,128,1024]{2,1,0:T(8,128)S(1)} %get-tuple-element.137), channel_id=1, source_target_pairs={{0,1},{4,5},{8,9},{12,13},{16,17},{20,21},{24,25},{28,29}} | collective-permute-start | bytes 1572872 | tf_op jit(solution)/shard_map/ppermute | solution.py:704
  32.6 25.9 %collective-permute-start.15 = (f32[1,128,1024]{2,1,0:T(8,128)S(1)}, f32[1,128,1024]{2,1,0:T(8,128)S(1)}, u32[]{:S(2)}, u32[]{:S(2)}) collective-permute-start(f32[1,128,1024]{2,1,0:T(8,128)S(1)} %get-tuple-element.150), channel_id=1, source_target_pairs={{3,2},{7,6},{11,10},{15,14},{19,18},{23,22},{27,26},{31,30}} | collective-permute-start | bytes 1572872 | tf_op jit(solution)/shard_map/ppermute | solution.py:705
  33.9 26.5 %collective-permute-start.14 = (f32[1,128,1024]{2,1,0:T(8,128)S(1)}, f32[1,128,1024]{2,1,0:T(8,128)S(1)}, u32[]{:S(2)}, u32[]{:S(2)}) collective-permute-start(f32[1,128,1024]{2,1,0:T(8,128)S(1)} %get-tuple-element.150), channel_id=1, source_target_pairs={{0,1},{4,5},{8,9},{12,13},{16,17},{20,21},{24,25},{28,29}} | collective-permute-start | bytes 1572872 | tf_op jit(solution)/shard_map/ppermute | solution.py:704
  51.3 18.5 %collective-permute-start.13 = (f32[1,128,1024]{2,1,0:T(8,128)S(1)}, f32[1,128,1024]{2,1,0:T(8,128)S(1)}, u32[]{:S(2)}, u32[]{:S(2)}) collective-permute-start(f32[1,128,1024]{2,1,0:T(8,128)S(1)} %get-tuple-element.141), channel_id=1, source_target_pairs={{3,2},{7,6},{11,10},{15,14},{19,18},{23,22},{27,26},{31,30}} | collective-permute-start | bytes 1572872 | tf_op jit(solution)/shard_map/ppermute | solution.py:705
  52.6 17.9 %collective-permute-start.12 = (f32[1,128,1024]{2,1,0:T(8,128)S(1)}, f32[1,128,1024]{2,1,0:T(8,128)S(1)}, u32[]{:S(2)}, u32[]{:S(2)}) collective-permute-start(f32[1,128,1024]{2,1,0:T(8,128)S(1)} %get-tuple-element.141), channel_id=1, source_target_pairs={{0,1},{4,5},{8,9},{12,13},{16,17},{20,21},{24,25},{28,29}} | collective-permute-start | bytes 1572872 | tf_op jit(solution)/shard_map/ppermute | solution.py:704
  53.9 21.9 %collective-permute-start.16 = (f32[1,128,1024]{2,1,0:T(8,128)S(1)}, f32[1,128,1024]{2,1,0:T(8,128)S(1)}, u32[]{:S(2)}, u32[]{:S(2)}) collective-permute-start(f32[1,128,1024]{2,1,0:T(8,128)S(1)} %get-tuple-element.147), channel_id=1, source_target_pairs={{0,1},{1,2},{4,5},{5,6},{8,9},{9,10},{12,13},{13,14},{16,17},{17,1... | collective-permute-start | bytes 1572872 | tf_op jit(solution)/shard_map/ppermute | solution.py:704
  58.5 25.5 %collective-permute-start.17 = (f32[1,128,1024]{2,1,0:T(8,128)S(1)}, f32[1,128,1024]{2,1,0:T(8,128)S(1)}, u32[]{:S(2)}, u32[]{:S(2)}) collective-permute-start(f32[1,128,1024]{2,1,0:T(8,128)S(1)} %get-tuple-element.148), channel_id=1, source_target_pairs={{2,1},{3,2},{6,5},{7,6},{10,9},{11,10},{14,13},{15,14},{18,17},{19... | collective-permute-start | bytes 1572872 | tf_op jit(solution)/shard_map/ppermute | solution.py:705
  60.4 31.8 %collective-permute-start.11 = (f32[1,128,1024]{2,1,0:T(8,128)S(1)}, f32[1,128,1024]{2,1,0:T(8,128)S(1)}, u32[]{:S(2)}, u32[]{:S(2)}) collective-permute-start(f32[1,128,1024]{2,1,0:T(8,128)S(1)} %get-tuple-element.139), channel_id=1, source_target_pairs={{3,2},{7,6},{11,10},{15,14},{19,18},{23,22},{27,26},{31,30}} | collective-permute-start | bytes 1572872 | tf_op jit(solution)/shard_map/ppermute | solution.py:705
  69.7 22.5 %collective-permute-start.10 = (f32[1,128,1024]{2,1,0:T(8,128)S(1)}, f32[1,128,1024]{2,1,0:T(8,128)S(1)}, u32[]{:S(2)}, u32[]{:S(2)}) collective-permute-start(f32[1,128,1024]{2,1,0:T(8,128)S(1)} %get-tuple-element.139), channel_id=1, source_target_pairs={{0,1},{4,5},{8,9},{12,13},{16,17},{20,21},{24,25},{28,29}} | collective-permute-start | bytes 1572872 | tf_op jit(solution)/shard_map/ppermute | solution.py:704
  70.4 31.8 %collective-permute-start.18 = (f32[1,128,1024]{2,1,0:T(8,128)S(1)}, f32[1,128,1024]{2,1,0:T(8,128)S(1)}, u32[]{:S(2)}, u32[]{:S(2)}) collective-permute-start(f32[1,128,1024]{2,1,0:T(8,128)S(1)} %get-tuple-element.151), channel_id=1, source_target_pairs={{0,1},{1,2},{4,5},{5,6},{8,9},{9,10},{12,13},{13,14},{16,17},{17,1... | collective-permute-start | bytes 1572872 | tf_op jit(solution)/shard_map/ppermute | solution.py:704
  75.9 27.6 %collective-permute-start.19 = (f32[1,128,1024]{2,1,0:T(8,128)S(1)}, f32[1,128,1024]{2,1,0:T(8,128)S(1)}, u32[]{:S(2)}, u32[]{:S(2)}) collective-permute-start(f32[1,128,1024]{2,1,0:T(8,128)S(1)} %get-tuple-element.152), channel_id=1, source_target_pairs={{2,1},{3,2},{6,5},{7,6},{10,9},{11,10},{14,13},{15,14},{18,17},{19... | collective-permute-start | bytes 1572872 | tf_op jit(solution)/shard_map/ppermute | solution.py:705
  92.2 17.7 %collective-permute-start.20 = (f32[1,128,1024]{2,1,0:T(8,128)S(1)}, f32[1,128,1024]{2,1,0:T(8,128)S(1)}, u32[]{:S(2)}, u32[]{:S(2)}) collective-permute-start(f32[1,128,1024]{2,1,0:T(8,128)S(1)} %get-tuple-element.157), channel_id=1, source_target_pairs={{0,1},{1,2},{4,5},{5,6},{8,9},{9,10},{12,13},{13,14},{16,17},{17,1... | collective-permute-start | bytes 1572872 | tf_op jit(solution)/shard_map/ppermute | solution.py:704
  93.5 21.2 %collective-permute-start.21 = (f32[1,128,1024]{2,1,0:T(8,128)S(1)}, f32[1,128,1024]{2,1,0:T(8,128)S(1)}, u32[]{:S(2)}, u32[]{:S(2)}) collective-permute-start(f32[1,128,1024]{2,1,0:T(8,128)S(1)} %get-tuple-element.158), channel_id=1, source_target_pairs={{2,1},{3,2},{6,5},{7,6},{10,9},{11,10},{14,13},{15,14},{18,17},{19... | collective-permute-start | bytes 1572872 | tf_op jit(solution)/shard_map/ppermute | solution.py:705
  104.1 17.1 %collective-permute-start.22 = (f32[1,128,1024]{2,1,0:T(8,128)S(1)}, f32[1,128,1024]{2,1,0:T(8,128)S(1)}, u32[]{:S(2)}, u32[]{:S(2)}) collective-permute-start(f32[1,128,1024]{2,1,0:T(8,128)S(1)} %get-tuple-element.163), channel_id=1, source_target_pairs={{0,1},{1,2},{4,5},{5,6},{8,9},{9,10},{12,13},{13,14},{16,17},{17,1... | collective-permute-start | bytes 1572872 | tf_op jit(solution)/shard_map/ppermute | solution.py:704
  105.4 20.5 %collective-permute-start.23 = (f32[1,128,1024]{2,1,0:T(8,128)S(1)}, f32[1,128,1024]{2,1,0:T(8,128)S(1)}, u32[]{:S(2)}, u32[]{:S(2)}) collective-permute-start(f32[1,128,1024]{2,1,0:T(8,128)S(1)} %get-tuple-element.164), channel_id=1, source_target_pairs={{2,1},{3,2},{6,5},{7,6},{10,9},{11,10},{14,13},{15,14},{18,17},{19... | collective-permute-start | bytes 1572872 | tf_op jit(solution)/shard_map/ppermute | solution.py:705
  115.3 17.1 %collective-permute-start.24 = (f32[1,128,1024]{2,1,0:T(8,128)S(1)}, f32[1,128,1024]{2,1,0:T(8,128)S(1)}, u32[]{:S(2)}, u32[]{:S(2)}) collective-permute-start(f32[1,128,1024]{2,1,0:T(8,128)S(1)} %get-tuple-element.169), channel_id=1, source_target_pairs={{0,1},{1,2},{2,3},{4,5},{5,6},{6,7},{8,9},{9,10},{10,11},{12,13},{... | collective-permute-start | bytes 1572872 | tf_op jit(solution)/shard_map/ppermute | solution.py:704
  117.3 19.9 %collective-permute-start.25 = (f32[1,128,1024]{2,1,0:T(8,128)S(1)}, f32[1,128,1024]{2,1,0:T(8,128)S(1)}, u32[]{:S(2)}, u32[]{:S(2)}) collective-permute-start(f32[1,128,1024]{2,1,0:T(8,128)S(1)} %get-tuple-element.170), channel_id=1, source_target_pairs={{1,0},{2,1},{3,2},{5,4},{6,5},{7,6},{9,8},{10,9},{11,10},{13,12},{... | collective-permute-start | bytes 1572872 | tf_op jit(solution)/shard_map/ppermute | solution.py:705
  126.6 17.1 %collective-permute-start.26 = (f32[1,128,1024]{2,1,0:T(8,128)S(1)}, f32[1,128,1024]{2,1,0:T(8,128)S(1)}, u32[]{:S(2)}, u32[]{:S(2)}) collective-permute-start(f32[1,128,1024]{2,1,0:T(8,128)S(1)} %get-tuple-element.175), channel_id=1, source_target_pairs={{0,1},{1,2},{2,3},{4,5},{5,6},{6,7},{8,9},{9,10},{10,11},{12,13},{... | collective-permute-start | bytes 1572872 | tf_op jit(solution)/shard_map/ppermute | solution.py:704
  128.5 19.9 %collective-permute-start.27 = (f32[1,128,1024]{2,1,0:T(8,128)S(1)}, f32[1,128,1024]{2,1,0:T(8,128)S(1)}, u32[]{:S(2)}, u32[]{:S(2)}) collective-permute-start(f32[1,128,1024]{2,1,0:T(8,128)S(1)} %get-tuple-element.176), channel_id=1, source_target_pairs={{1,0},{2,1},{3,2},{5,4},{6,5},{7,6},{9,8},{10,9},{11,10},{13,12},{... | collective-permute-start | bytes 1572872 | tf_op jit(solution)/shard_map/ppermute | solution.py:705
  137.8 18.9 %collective-permute-start.30 = (f32[1,128,1024]{2,1,0:T(8,128)S(1)}, f32[1,128,1024]{2,1,0:T(8,128)S(1)}, u32[]{:S(2)}, u32[]{:S(2)}) collective-permute-start(f32[1,128,1024]{2,1,0:T(8,128)S(1)} %get-tuple-element.181), channel_id=1, source_target_pairs={{0,1},{1,2},{2,3},{4,5},{5,6},{6,7},{8,9},{9,10},{10,11},{12,13},{... | collective-permute-start | bytes 1572872 | tf_op jit(solution)/shard_map/ppermute | solution.py:704
  139.7 19.9 %collective-permute-start.31 = (f32[1,128,1024]{2,1,0:T(8,128)S(1)}, f32[1,128,1024]{2,1,0:T(8,128)S(1)}, u32[]{:S(2)}, u32[]{:S(2)}) collective-permute-start(f32[1,128,1024]{2,1,0:T(8,128)S(1)} %get-tuple-element.182), channel_id=1, source_target_pairs={{1,0},{2,1},{3,2},{5,4},{6,5},{7,6},{9,8},{10,9},{11,10},{13,12},{... | collective-permute-start | bytes 1572872 | tf_op jit(solution)/shard_map/ppermute | solution.py:705
  149.1 14.2 %collective-permute-start.28 = (f32[1,128,1024]{2,1,0:T(8,128)S(1)}, f32[1,128,1024]{2,1,0:T(8,128)S(1)}, u32[]{:S(2)}, u32[]{:S(2)}) collective-permute-start(f32[1,128,1024]{2,1,0:T(8,128)S(1)} %get-tuple-element.187), channel_id=1, source_target_pairs={{0,1},{1,2},{2,3},{4,5},{5,6},{6,7},{8,9},{9,10},{10,11},{12,13},{... | collective-permute-start | bytes 1572872 | tf_op jit(solution)/shard_map/ppermute | solution.py:704
  151.0 19.0 %collective-permute-start.29 = (f32[1,128,1024]{2,1,0:T(8,128)S(1)}, f32[1,128,1024]{2,1,0:T(8,128)S(1)}, u32[]{:S(2)}, u32[]{:S(2)}) collective-permute-start(f32[1,128,1024]{2,1,0:T(8,128)S(1)} %get-tuple-element.188), channel_id=1, source_target_pairs={{1,0},{2,1},{3,2},{5,4},{6,5},{7,6},{9,8},{10,9},{11,10},{13,12},{... | collective-permute-start | bytes 1572872 | tf_op jit(solution)/shard_map/ppermute | solution.py:705

commit v6 on v5

--- a/solution.py
+++ b/solution.py
@@ -107,13 +107,15 @@
                 copy.start()
                 copies.append(copy)
         spread = head_spread(per_part, gch)
-        for copy in small:
+        for copy in small[:2]:
             copy.wait()
         scales = []
         for block in range(blocks):
             span = slice(block * SPAN, (block + 1) * SPAN)
             cum, seg = block_sums(decay[:, span], starts[:, span])
             seg_last, last = seg[0:1, SPAN - 1 :], cum[:, SPAN - 1 :]
+            if block == 0:
+                small[2].wait()
             tail = jnp.where(seg[0:1] == seg_last, jnp.exp(last - cum), 0.0) * step[:, span]
             keep = jnp.where(seg_last == 0.0, jnp.exp(last), 0.0)
             scales.append((tail, jnp.broadcast_to(keep, (heads, 128))))
@@ -678,7 +680,7 @@
 
 def last_call(so_far, mine, up, down, first, wide):
     count, rows, width = mine.shape
-    tile = min(512, width)
+    tile = min(1024, width)
     moving = pl.BlockSpec((1, rows, tile), lambda j: (0, 0, j))
 
     def kernel(a, c, d, *refs):

time: 173 us -> 173 us (level)
  no operation moved by 1% of the time
where the time goes in v6:
time: 173 us; the launch traced here: 171 us
  starting transfers between devices  63 us (36%)
  waiting for transfers between devices  56.8 us (33%)
  Pallas kernels  48.6 us (28%)
  local copies, waits for them, and re-layouts  1.81 us (1%)
    ppermute x12, waiting for transfers between devices, send(): lax.ppermute(to_down, axis, [(i, i - 1) for i in range(1, count) if step...  48.7 us
    ppermute x12, starting transfers between devices, send(): lax.ppermute(to_down, axis, [(i, i - 1) for i in range(1, count) if step...  40 us
    pallas_call x5, Pallas kernels, project_call(): pl.pallas_call(kernel, in_specs=[vmem] * len(parts) + [pl.BlockSpec(memor...  20.5 us
    ppermute x12, starting transfers between devices, send(): lax.ppermute(to_up, axis, [(i, i + 1) for i in range(count - 1) if step >...  15.8 us
    ppermute x6, starting transfers between devices, exchange(): lax.ppermute(parts[k], axis, [(i, i ^ 2 * k) for i in range(count)])  7.11 us
    pallas_call x2, Pallas kernels, intra_call(): pl.pallas_call(kernel, grid_spec=pltpu.PrefetchScalarGridSpec(num_scalar_...  6.83 us
    pallas_call x8, Pallas kernels, sum_call(): pl.pallas_call(kernel, grid_spec=pltpu.PrefetchScalarGridSpec(num_scalar_...  5.22 us
    pallas_call x2, Pallas kernels, states_call(): pl.pallas_call(kernel, in_specs=[pl.BlockSpec(memory_space=pltpu.HBM)] *...  5.11 us
  transfers between devices with their start and end apart: 32, of which 15 were waited for; matrix products, arithmetic and copies ran while one was open for 0% of the time, Pallas kernels for 25%

profile of v6, /device:TPU:16, one launch (start us, length us, event | category | flops | bytes accessed | tf_op | source)
XLA Modules:
  0.0 171.0 jit_solution(4791884722544266333)
XLA Ops:
  0.0 3.3 %states.2 = (f32[4,136,256]{2,1,0:T(8,128)}, f32[1,136,1024]{2,1,0:T(8,128)}) custom-call(bf16[512,2048]{1,0:T(8,128)(2,1)} %feat.3, bf16[512,256]{1,0:T(8,128)(2,1)} %write.3, f32[32,512]{1,0:T(8,128)} %step.3, f32[32,512]{1,0:T(8,128)} %decay.3, s32[1,512]{1,0:T(1,128)} %bitcast.10, s32[512]{0:T(512)} %after.1), custom_call_target="tpu_custom_call" | custom-call | flops 100000000 | bytes 1000000 | tf_op jit(solution)/shard_map/states/pallas_call | solution.py:145
  4.6 1.8 %states.3 = (f32[4,136,256]{2,1,0:T(8,128)S(1)}, f32[1,136,1024]{2,1,0:T(8,128)S(1)}) custom-call(bf16[512,2048]{1,0:T(8,128)(2,1)S(1)} %copy-done, bf16[512,256]{1,0:T(8,128)(2,1)S(1)} %copy-done.3, f32[32,512]{1,0:T(8,128)S(1)} %copy-done.4, f32[32,512]{1,0:T(8,128)S(1)} %copy-done.5, s32[1,512]{1,0:T(1,128)S(1)} %bitcast.11, f32[4,136,256]{2,1,0:T(8,128)S(1)} %copy-done.7), custom_call_target="tpu_custom_call" | custom-call | flops 100000000 | bytes 1000000 | tf_op jit(solution)/shard_map/states/pallas_call | solution.py:145
  6.5 1.6 collective-permute-start.1
  8.1 1.5 collective-permute-start.2
  10.8 3.4 %intra.2 = (f32[512,1024]{1,0:T(8,128)S(1)}, f32[512,128]{1,0:T(8,128)S(1)}, bf16[1024,2048]{1,0:T(8,128)(2,1)S(1)}) custom-call(s32[14]{0:T(128)S(1)} %pad_add_fusion.scal, bf16[512,2048]{1,0:T(8,128)(2,1)S(1)} %copy-done, bf16[512,256]{1,0:T(8,128)(2,1)S(1)} %copy-done.3, bf16[512,256]{1,0:T(8,128)(2,1)S(1)} %copy-done.2, f32[32,512]{1,0:T(8,128)S(1)} %copy-done.4, ...), custom_call_target="tpu_custom_call" | custom-call | flops 1000000000 | bytes 1000000 | tf_op jit(solution)/shard_map/intra/pallas_call | solution.py:237
  14.3 2.6 %collective-permute-done.2.refs_2_ = f32[136,256]{1,0:T(8,128)S(1)} collective-permute-done((f32[136,256]{1,0:T(8,128)S(1)}, f32[136,256]{1,0:T(8,128)S(1)}, u32[]{:S(2)}, u32[]{:S(2)}) %collective-permute-start.2) | collective-permute-done | bytes 139296 | tf_op jit(solution)/shard_map/ppermute | solution.py:392
  17.0 1.3 collective-permute-start.4
  19.1 1.4 collective-permute-start.6
  20.6 3.4 %intra.3 = (f32[512,1024]{1,0:T(8,128)S(1)}, f32[512,128]{1,0:T(8,128)S(1)}, bf16[1024,2048]{1,0:T(8,128)(2,1)S(1)}) custom-call(s32[14]{0:T(128)S(1)} %pad_add_fusion.scal, bf16[512,2048]{1,0:T(8,128)(2,1)S(1)} %copy-done, bf16[512,256]{1,0:T(8,128)(2,1)S(1)} %copy-done.3, bf16[512,256]{1,0:T(8,128)(2,1)S(1)} %copy-done.2, f32[32,512]{1,0:T(8,128)S(1)} %copy-done.4, ...), custom_call_target="tpu_custom_call" | custom-call | flops 1000000000 | bytes 1000000 | tf_op jit(solution)/shard_map/intra/pallas_call | solution.py:237
  24.1 1.8 %collective-permute-done.5.refs_2_ = f32[128,256]{1,0:T(8,128)S(1)} collective-permute-done((f32[128,256]{1,0:T(8,128)S(1)}, f32[128,256]{1,0:T(8,128)S(1)}, u32[]{:S(2)}, u32[]{:S(2)}) %collective-permute-start.5) | collective-permute-done | bytes 131104 | tf_op jit(solution)/shard_map/ppermute | solution.py:392
  26.1 1.9 %first.2 = (bf16[128,1024]{1,0:T(8,128)(2,1)S(1)}, f32[128,2048]{1,0:T(8,128)S(1)}) custom-call(s32[14]{0:T(128)S(1)} %pad_add_fusion.scal, f32[2,4,136,256]{3,2,1,0:T(8,128)S(1)} %pack.1.refs_0_, f32[2,136,1024]{2,1,0:T(8,128)S(1)} %fold.2.refs_1_.refs_6_, f32[512,1024]{1,0:T(8,128)S(1)} %get-tuple-element.131.refs_2_, ...), custom_call_target="tpu_custom_call" | custom-call | tf_op jit(solution)/shard_map/first/pallas_call | solution.py:489
  28.9 1.9 %first.3 = (bf16[1,128,2048]{2,1,0:T(8,128)(2,1)S(1)}, f32[1,128,1024]{2,1,0:T(8,128)S(1)}, f32[1,128,1024]{2,1,0:T(8,128)S(1)}) custom-call(s32[14]{0:T(128)S(1)} %pad_add_fusion.scal, f32[2,4,136,256]{3,2,1,0:T(8,128)S(1)} %collective-permute-done.7.refs_0_.refs_1_, f32[2,136,1024]{2,1,0:T(8,128)S(1)} %fold.3.refs_1_.refs_7_, ...), custom_call_target="tpu_custom_call" | custom-call | tf_op jit(solution)/shard_map/first/pallas_call | solution.py:489
  30.8 1.3 collective-permute-start.9
  32.8 1.3 collective-permute-start.15
  34.9 3.5 %rest.1.refs_1_ = bf16[3,128,2048]{2,1,0:T(8,128)(2,1)S(1)} custom-call(s32[14]{0:T(128)S(1)} %pad_add_fusion.scal, f32[2,4,136,256]{3,2,1,0:T(8,128)S(1)} %pack.1.refs_0_, f32[2,4,136,256]{3,2,1,0:T(8,128)S(1)} %collective-permute-done.7.refs_0_.refs_1_, f32[512,1024]{1,0:T(8,128)S(1)} %get-tuple-element.131.refs_2_, ...), custom_call_target="tpu_custom_call" | custom-call | flops 1000000000 | bytes 1000000 | tf_op jit(solution)/shard_map/rest/pallas_call | solution.py:564
  38.4 4.1 %project.6.a.b = f32[4,128,1024]{2,1,0:T(8,128)S(1)} custom-call(bf16[1,128,2048]{2,1,0:T(8,128)(2,1)S(1)} %get-tuple-element.138.refs_0_, bf16[3,128,2048]{2,1,0:T(8,128)(2,1)S(1)} %rest.1.refs_1_, bf16[2048,4096]{1,0:T(8,128)(2,1)} %refs_2_.7), custom_call_target="tpu_custom_call" | custom-call | flops 2147483648 | bytes 6291456 | tf_op jit(solution)/shard_map/project/pallas_call | solution.py:615
  42.6 4.1 %project.5.a.b = f32[4,128,1024]{2,1,0:T(8,128)S(1)} custom-call(bf16[1,128,2048]{2,1,0:T(8,128)(2,1)S(1)} %get-tuple-element.138.refs_0_, bf16[3,128,2048]{2,1,0:T(8,128)(2,1)S(1)} %rest.1.refs_1_, bf16[2048,4096]{1,0:T(8,128)(2,1)} %refs_2_.7), custom_call_target="tpu_custom_call" | custom-call | flops 2147483648 | bytes 6291456 | tf_op jit(solution)/shard_map/project/pallas_call | solution.py:615
  47.4 4.0 %project.7 = (f32[1,128,1024]{2,1,0:T(8,128)S(1)}, f32[1,128,1024]{2,1,0:T(8,128)S(1)}) custom-call(bf16[1,128,2048]{2,1,0:T(8,128)(2,1)S(1)} %get-tuple-element.138.refs_0_, bf16[2048,4096]{1,0:T(8,128)(2,1)} %refs_2_.7), custom_call_target="tpu_custom_call" | custom-call | flops 1073741824 | bytes 9437184 | tf_op jit(solution)/shard_map/project/pallas_call | solution.py:615
  51.4 1.3 collective-permute-start.13
  54.1 1.3 collective-permute-start.16
  55.4 3.3 %collective-permute-done.15.d = f32[1,128,1024]{2,1,0:T(8,128)S(1)} collective-permute-done((f32[1,128,1024]{2,1,0:T(8,128)S(1)}, f32[1,128,1024]{2,1,0:T(8,128)S(1)}, u32[]{:S(2)}, u32[]{:S(2)}) %collective-permute-start.15) | collective-permute-done | bytes 524320 | tf_op jit(solution)/shard_map/ppermute | solution.py:707
  58.6 1.9 %collective-permute-start.17 = (f32[1,128,1024]{2,1,0:T(8,128)S(1)}, f32[1,128,1024]{2,1,0:T(8,128)S(1)}, u32[]{:S(2)}, u32[]{:S(2)}) collective-permute-start(f32[1,128,1024]{2,1,0:T(8,128)S(1)} %get-tuple-element.148), channel_id=1, source_target_pairs={{2,1},{3,2},{6,5},{7,6},{10,9},{11,10},{14,13},{15,14},{18,17},{19... | collective-permute-start | bytes 1572872 | tf_op jit(solution)/shard_map/ppermute | solution.py:707
  60.6 1.3 collective-permute-start.11
  62.5 7.3 %collective-permute-done.13.d = f32[1,128,1024]{2,1,0:T(8,128)S(1)} collective-permute-done((f32[1,128,1024]{2,1,0:T(8,128)S(1)}, f32[1,128,1024]{2,1,0:T(8,128)S(1)}, u32[]{:S(2)}, u32[]{:S(2)}) %collective-permute-start.13) | collective-permute-done | bytes 524320 | tf_op jit(solution)/shard_map/ppermute | solution.py:707
  70.6 1.3 collective-permute-start.18
  71.9 4.1 %project.9.a.b = f32[4,128,1024]{2,1,0:T(8,128)S(1)} custom-call(bf16[1,128,2048]{2,1,0:T(8,128)(2,1)S(1)} %get-tuple-element.138.refs_0_, bf16[3,128,2048]{2,1,0:T(8,128)(2,1)S(1)} %rest.1.refs_1_, bf16[2048,4096]{1,0:T(8,128)(2,1)} %refs_2_.7), custom_call_target="tpu_custom_call" | custom-call | flops 2147483648 | bytes 6291456 | tf_op jit(solution)/shard_map/project/pallas_call | solution.py:615
  76.0 8.1 %collective-permute-start.19 = (f32[1,128,1024]{2,1,0:T(8,128)S(1)}, f32[1,128,1024]{2,1,0:T(8,128)S(1)}, u32[]{:S(2)}, u32[]{:S(2)}) collective-permute-start(f32[1,128,1024]{2,1,0:T(8,128)S(1)} %get-tuple-element.152), channel_id=1, source_target_pairs={{2,1},{3,2},{6,5},{7,6},{10,9},{11,10},{14,13},{15,14},{18,17},{19... | collective-permute-start | bytes 1572872 | tf_op jit(solution)/shard_map/ppermute | solution.py:707
  84.9 7.5 %collective-permute-done.11.d = f32[1,128,1024]{2,1,0:T(8,128)S(1)} collective-permute-done((f32[1,128,1024]{2,1,0:T(8,128)S(1)}, f32[1,128,1024]{2,1,0:T(8,128)S(1)}, u32[]{:S(2)}, u32[]{:S(2)}) %collective-permute-start.11) | collective-permute-done | bytes 524320 | tf_op jit(solution)/shard_map/ppermute | solution.py:707
  92.4 1.3 collective-permute-start.20
  93.6 4.6 %collective-permute-start.21 = (f32[1,128,1024]{2,1,0:T(8,128)S(1)}, f32[1,128,1024]{2,1,0:T(8,128)S(1)}, u32[]{:S(2)}, u32[]{:S(2)}) collective-permute-start(f32[1,128,1024]{2,1,0:T(8,128)S(1)} %get-tuple-element.158), channel_id=1, source_target_pairs={{2,1},{3,2},{6,5},{7,6},{10,9},{11,10},{14,13},{15,14},{18,17},{19... | collective-permute-start | bytes 1572872 | tf_op jit(solution)/shard_map/ppermute | solution.py:707
  98.2 4.1 %project.8.a.b = f32[4,128,1024]{2,1,0:T(8,128)S(1)} custom-call(bf16[1,128,2048]{2,1,0:T(8,128)(2,1)S(1)} %get-tuple-element.138.refs_0_, bf16[3,128,2048]{2,1,0:T(8,128)(2,1)S(1)} %rest.1.refs_1_, bf16[2048,4096]{1,0:T(8,128)(2,1)} %refs_2_.7), custom_call_target="tpu_custom_call" | custom-call | flops 2147483648 | bytes 6291456 | tf_op jit(solution)/shard_map/project/pallas_call | solution.py:615
  104.2 1.3 collective-permute-start.22
  105.5 4.6 %collective-permute-start.23 = (f32[1,128,1024]{2,1,0:T(8,128)S(1)}, f32[1,128,1024]{2,1,0:T(8,128)S(1)}, u32[]{:S(2)}, u32[]{:S(2)}) collective-permute-start(f32[1,128,1024]{2,1,0:T(8,128)S(1)} %get-tuple-element.164), channel_id=1, source_target_pairs={{2,1},{3,2},{6,5},{7,6},{10,9},{11,10},{14,13},{15,14},{18,17},{19... | collective-permute-start | bytes 1572872 | tf_op jit(solution)/shard_map/ppermute | solution.py:707
  110.1 4.7 %collective-permute-done.21.d = f32[1,128,1024]{2,1,0:T(8,128)S(1)} collective-permute-done((f32[1,128,1024]{2,1,0:T(8,128)S(1)}, f32[1,128,1024]{2,1,0:T(8,128)S(1)}, u32[]{:S(2)}, u32[]{:S(2)}) %collective-permute-start.21) | collective-permute-done | bytes 524320 | tf_op jit(solution)/shard_map/ppermute | solution.py:707
  115.5 1.9 %collective-permute-start.24 = (f32[1,128,1024]{2,1,0:T(8,128)S(1)}, f32[1,128,1024]{2,1,0:T(8,128)S(1)}, u32[]{:S(2)}, u32[]{:S(2)}) collective-permute-start(f32[1,128,1024]{2,1,0:T(8,128)S(1)} %get-tuple-element.169), channel_id=1, source_target_pairs={{0,1},{1,2},{2,3},{4,5},{5,6},{6,7},{8,9},{9,10},{10,11},{12,13},{... | collective-permute-start | bytes 1572872 | tf_op jit(solution)/shard_map/ppermute | solution.py:706
  117.4 3.9 %collective-permute-start.25 = (f32[1,128,1024]{2,1,0:T(8,128)S(1)}, f32[1,128,1024]{2,1,0:T(8,128)S(1)}, u32[]{:S(2)}, u32[]{:S(2)}) collective-permute-start(f32[1,128,1024]{2,1,0:T(8,128)S(1)} %get-tuple-element.170), channel_id=1, source_target_pairs={{1,0},{2,1},{3,2},{5,4},{6,5},{7,6},{9,8},{10,9},{11,10},{13,12},{... | collective-permute-start | bytes 1572872 | tf_op jit(solution)/shard_map/ppermute | solution.py:707
  121.3 4.7 %collective-permute-done.23.d = f32[1,128,1024]{2,1,0:T(8,128)S(1)} collective-permute-done((f32[1,128,1024]{2,1,0:T(8,128)S(1)}, f32[1,128,1024]{2,1,0:T(8,128)S(1)}, u32[]{:S(2)}, u32[]{:S(2)}) %collective-permute-start.23) | collective-permute-done | bytes 524320 | tf_op jit(solution)/shard_map/ppermute | solution.py:707
  126.7 1.9 %collective-permute-start.26 = (f32[1,128,1024]{2,1,0:T(8,128)S(1)}, f32[1,128,1024]{2,1,0:T(8,128)S(1)}, u32[]{:S(2)}, u32[]{:S(2)}) collective-permute-start(f32[1,128,1024]{2,1,0:T(8,128)S(1)} %get-tuple-element.175), channel_id=1, source_target_pairs={{0,1},{1,2},{2,3},{4,5},{5,6},{6,7},{8,9},{9,10},{10,11},{12,13},{... | collective-permute-start | bytes 1572872 | tf_op jit(solution)/shard_map/ppermute | solution.py:706
  128.6 3.9 %collective-permute-start.27 = (f32[1,128,1024]{2,1,0:T(8,128)S(1)}, f32[1,128,1024]{2,1,0:T(8,128)S(1)}, u32[]{:S(2)}, u32[]{:S(2)}) collective-permute-start(f32[1,128,1024]{2,1,0:T(8,128)S(1)} %get-tuple-element.176), channel_id=1, source_target_pairs={{1,0},{2,1},{3,2},{5,4},{6,5},{7,6},{9,8},{10,9},{11,10},{13,12},{... | collective-permute-start | bytes 1572872 | tf_op jit(solution)/shard_map/ppermute | solution.py:707
  132.6 4.7 %collective-permute-done.25.d = f32[1,128,1024]{2,1,0:T(8,128)S(1)} collective-permute-done((f32[1,128,1024]{2,1,0:T(8,128)S(1)}, f32[1,128,1024]{2,1,0:T(8,128)S(1)}, u32[]{:S(2)}, u32[]{:S(2)}) %collective-permute-start.25) | collective-permute-done | bytes 524320 | tf_op jit(solution)/shard_map/ppermute | solution.py:707
  137.9 1.9 %collective-permute-start.30 = (f32[1,128,1024]{2,1,0:T(8,128)S(1)}, f32[1,128,1024]{2,1,0:T(8,128)S(1)}, u32[]{:S(2)}, u32[]{:S(2)}) collective-permute-start(f32[1,128,1024]{2,1,0:T(8,128)S(1)} %get-tuple-element.181), channel_id=1, source_target_pairs={{0,1},{1,2},{2,3},{4,5},{5,6},{6,7},{8,9},{9,10},{10,11},{12,13},{... | collective-permute-start | bytes 1572872 | tf_op jit(solution)/shard_map/ppermute | solution.py:706
  139.9 3.9 %collective-permute-start.31 = (f32[1,128,1024]{2,1,0:T(8,128)S(1)}, f32[1,128,1024]{2,1,0:T(8,128)S(1)}, u32[]{:S(2)}, u32[]{:S(2)}) collective-permute-start(f32[1,128,1024]{2,1,0:T(8,128)S(1)} %get-tuple-element.182), channel_id=1, source_target_pairs={{1,0},{2,1},{3,2},{5,4},{6,5},{7,6},{9,8},{10,9},{11,10},{13,12},{... | collective-permute-start | bytes 1572872 | tf_op jit(solution)/shard_map/ppermute | solution.py:707
  143.8 4.7 %collective-permute-done.27.d = f32[1,128,1024]{2,1,0:T(8,128)S(1)} collective-permute-done((f32[1,128,1024]{2,1,0:T(8,128)S(1)}, f32[1,128,1024]{2,1,0:T(8,128)S(1)}, u32[]{:S(2)}, u32[]{:S(2)}) %collective-permute-start.27) | collective-permute-done | bytes 524320 | tf_op jit(solution)/shard_map/ppermute | solution.py:707
  149.2 1.9 %collective-permute-start.28 = (f32[1,128,1024]{2,1,0:T(8,128)S(1)}, f32[1,128,1024]{2,1,0:T(8,128)S(1)}, u32[]{:S(2)}, u32[]{:S(2)}) collective-permute-start(f32[1,128,1024]{2,1,0:T(8,128)S(1)} %get-tuple-element.187), channel_id=1, source_target_pairs={{0,1},{1,2},{2,3},{4,5},{5,6},{6,7},{8,9},{9,10},{10,11},{12,13},{... | collective-permute-start | bytes 1572872 | tf_op jit(solution)/shard_map/ppermute | solution.py:706
  151.1 3.9 %collective-permute-start.29 = (f32[1,128,1024]{2,1,0:T(8,128)S(1)}, f32[1,128,1024]{2,1,0:T(8,128)S(1)}, u32[]{:S(2)}, u32[]{:S(2)}) collective-permute-start(f32[1,128,1024]{2,1,0:T(8,128)S(1)} %get-tuple-element.188), channel_id=1, source_target_pairs={{1,0},{2,1},{3,2},{5,4},{6,5},{7,6},{9,8},{10,9},{11,10},{13,12},{... | collective-permute-start | bytes 1572872 | tf_op jit(solution)/shard_map/ppermute | solution.py:707
  156.7 3.1 %collective-permute-done.31.d = f32[1,128,1024]{2,1,0:T(8,128)S(1)} collective-permute-done((f32[1,128,1024]{2,1,0:T(8,128)S(1)}, f32[1,128,1024]{2,1,0:T(8,128)S(1)}, u32[]{:S(2)}, u32[]{:S(2)}) %collective-permute-start.31) | collective-permute-done | bytes 524320 | tf_op jit(solution)/shard_map/ppermute | solution.py:707
  160.6 2.8 %collective-permute-done.28.c = f32[1,128,1024]{2,1,0:T(8,128)S(1)} collective-permute-done((f32[1,128,1024]{2,1,0:T(8,128)S(1)}, f32[1,128,1024]{2,1,0:T(8,128)S(1)}, u32[]{:S(2)}, u32[]{:S(2)}) %collective-permute-start.28) | collective-permute-done | bytes 524320 | tf_op jit(solution)/shard_map/ppermute | solution.py:706
  163.4 6.8 %collective-permute-done.29.d = f32[1,128,1024]{2,1,0:T(8,128)S(1)} collective-permute-done((f32[1,128,1024]{2,1,0:T(8,128)S(1)}, f32[1,128,1024]{2,1,0:T(8,128)S(1)}, u32[]{:S(2)}, u32[]{:S(2)}) %collective-permute-start.29) | collective-permute-done | bytes 524320 | tf_op jit(solution)/shard_map/ppermute | solution.py:707
  (69 shorter events, 18.0 us)
Async XLA Ops:
  0.0 3.5 %copy-start.5 = (f32[32,512]{1,0:T(8,128)S(1)}, f32[32,512]{1,0:T(8,128)}, u32[]{:S(2)}) copy-start(f32[32,512]{1,0:T(8,128)} %decay.3) | copy-start | bytes 196612
  0.0 3.5 %copy-start.4 = (f32[32,512]{1,0:T(8,128)S(1)}, f32[32,512]{1,0:T(8,128)}, u32[]{:S(2)}) copy-start(f32[32,512]{1,0:T(8,128)} %step.3) | copy-start | bytes 196612
  0.0 3.5 %copy-start.3 = (bf16[512,256]{1,0:T(8,128)(2,1)S(1)}, bf16[512,256]{1,0:T(8,128)(2,1)}, u32[]{:S(2)}) copy-start(bf16[512,256]{1,0:T(8,128)(2,1)} %write.3) | copy-start | bytes 786436
  0.0 3.5 %copy-start = (bf16[512,2048]{1,0:T(8,128)(2,1)S(1)}, bf16[512,2048]{1,0:T(8,128)(2,1)}, u32[]{:S(2)}) copy-start(bf16[512,2048]{1,0:T(8,128)(2,1)} %feat.3) | copy-start | bytes 6291460
  0.0 3.5 %copy-start.9 = (s32[512]{0:T(512)S(1)}, s32[512]{0:T(512)}, u32[]{:S(2)}) copy-start(s32[512]{0:T(512)} %after.1) | copy-start | bytes 6148
  3.4 3.0 %collective-permute-start = (f32[4,136,256]{2,1,0:T(8,128)}, f32[4,136,256]{2,1,0:T(8,128)S(1)}, u32[]{:S(2)}, u32[]{:S(2)}) collective-permute-start(f32[4,136,256]{2,1,0:T(8,128)} %get-tuple-element.99.after), channel_id=1, source_target_pairs={{0,4},{4,0},{8,12},{12,8},{16,20},{20,16},{24,28},{28,24},{1,5},{5... | collective-permute-start | bytes 1671176 | tf_op jit(solution)/shard_map/ppermute | solution.py:398
  3.5 7.4 %copy-start.10 = (f32[32]{0:T(128)S(1)}, f32[32]{0:T(128)}, u32[]{:S(2)}) copy-start(f32[32]{0:T(128)} %param.18) | copy-start | bytes 388
  3.5 7.4 %copy-start.2 = (bf16[512,256]{1,0:T(8,128)(2,1)S(1)}, bf16[512,256]{1,0:T(8,128)(2,1)}, u32[]{:S(2)}) copy-start(bf16[512,256]{1,0:T(8,128)(2,1)} %refs_9_.1) | copy-start | bytes 786436
  3.5 1.1 copy-start.7
  6.5 7.7 %collective-permute-start.1 = (f32[136,256]{1,0:T(8,128)S(1)}, f32[136,256]{1,0:T(8,128)S(1)}, u32[]{:S(2)}, u32[]{:S(2)}) collective-permute-start(f32[136,256]{1,0:T(8,128)S(1)} %get-tuple-element.107), channel_id=1, source_target_pairs={{0,8},{4,12},{8,0},{12,4},{16,24},{20,28},{24,16},{28,20},{1,9},{5... | collective-permute-start | bytes 417800 | tf_op jit(solution)/shard_map/ppermute | solution.py:392
  8.1 8.7 %collective-permute-start.2 = (f32[136,256]{1,0:T(8,128)S(1)}, f32[136,256]{1,0:T(8,128)S(1)}, u32[]{:S(2)}, u32[]{:S(2)}) collective-permute-start(f32[136,256]{1,0:T(8,128)S(1)} %get-tuple-element.108), channel_id=1, source_target_pairs={{0,16},{4,20},{8,24},{12,28},{16,0},{20,4},{24,8},{28,12},{1,17},{... | collective-permute-start | bytes 417800 | tf_op jit(solution)/shard_map/ppermute | solution.py:392
  9.6 7.2 %collective-permute-start.3 = (f32[136,256]{1,0:T(8,128)S(1)}, f32[136,256]{1,0:T(8,128)S(1)}, u32[]{:S(2)}, u32[]{:S(2)}) collective-permute-start(f32[136,256]{1,0:T(8,128)S(1)} %get-tuple-element.109), channel_id=1, source_target_pairs={{0,24},{4,28},{8,16},{12,20},{16,8},{20,12},{24,0},{28,4},{1,25},{... | collective-permute-start | bytes 417800 | tf_op jit(solution)/shard_map/ppermute | solution.py:392
  17.0 7.1 %collective-permute-start.4 = (f32[128,256]{1,0:T(8,128)S(1)}, f32[128,256]{1,0:T(8,128)S(1)}, u32[]{:S(2)}, u32[]{:S(2)}) collective-permute-start(f32[128,256]{1,0:T(8,128)S(1)} %get-tuple-element.112), channel_id=1, source_target_pairs={{0,8},{4,12},{8,0},{12,4},{16,24},{20,28},{24,16},{28,20},{1,9},{5... | collective-permute-start | bytes 393224 | tf_op jit(solution)/shard_map/ppermute | solution.py:392
  18.3 7.6 %collective-permute-start.5 = (f32[128,256]{1,0:T(8,128)S(1)}, f32[128,256]{1,0:T(8,128)S(1)}, u32[]{:S(2)}, u32[]{:S(2)}) collective-permute-start(f32[128,256]{1,0:T(8,128)S(1)} %get-tuple-element.113), channel_id=1, source_target_pairs={{0,16},{4,20},{8,24},{12,28},{16,0},{20,4},{24,8},{28,12},{1,17},{... | collective-permute-start | bytes 393224 | tf_op jit(solution)/shard_map/ppermute | solution.py:392
  19.1 6.8 %collective-permute-start.6 = (f32[128,256]{1,0:T(8,128)S(1)}, f32[128,256]{1,0:T(8,128)S(1)}, u32[]{:S(2)}, u32[]{:S(2)}) collective-permute-start(f32[128,256]{1,0:T(8,128)S(1)} %get-tuple-element.114), channel_id=1, source_target_pairs={{0,24},{4,28},{8,16},{12,20},{16,8},{20,12},{24,0},{28,4},{1,25},{... | collective-permute-start | bytes 393224 | tf_op jit(solution)/shard_map/ppermute | solution.py:392
  24.1 2.0 %copy-start.1 = (bf16[512,2048]{1,0:T(8,128)(2,1)S(1)}, bf16[512,2048]{1,0:T(8,128)(2,1)}, u32[]{:S(2)}) copy-start(bf16[512,2048]{1,0:T(8,128)(2,1)} %refs_8_.1) | copy-start | bytes 6291460
  24.1 2.0 %copy-start.8 = (f32[2048]{0:T(1024)S(1)}, f32[2048]{0:T(1024)}, u32[]{:S(2)}) copy-start(f32[2048]{0:T(1024)} %param.19) | copy-start | bytes 24580
  25.9 2.8 %collective-permute-start.7 = (f32[2,4,136,256]{3,2,1,0:T(8,128)S(1)}, f32[2,4,136,256]{3,2,1,0:T(8,128)S(1)}, u32[]{:S(2)}, u32[]{:S(2)}) collective-permute-start(f32[2,4,136,256]{3,2,1,0:T(8,128)S(1)} %pack.1.refs_0_), channel_id=1, source_target_pairs={{0,4},{4,0},{8,12},{12,8},{16,20},{20,16},{24,28},{28,24},{1,5},{5... | collective-permute-start | bytes 3342344 | tf_op jit(solution)/shard_map/ppermute | solution.py:398
  26.0 2.7 %copy-start.6 = (f32[1,136,1024]{2,1,0:T(8,128)S(1)}, f32[1,136,1024]{2,1,0:T(8,128)}, u32[]{:S(2)}) copy-start(f32[1,136,1024]{2,1,0:T(8,128)} %get-tuple-element.126.refs_1_) | copy-start | bytes 1671172
  30.8 16.7 %collective-permute-start.9 = (f32[1,128,1024]{2,1,0:T(8,128)S(1)}, f32[1,128,1024]{2,1,0:T(8,128)S(1)}, u32[]{:S(2)}, u32[]{:S(2)}) collective-permute-start(f32[1,128,1024]{2,1,0:T(8,128)S(1)} %get-tuple-element.137), channel_id=1, source_target_pairs={{3,2},{7,6},{11,10},{15,14},{19,18},{23,22},{27,26},{31,30}} | collective-permute-start | bytes 1572872 | tf_op jit(solution)/shard_map/ppermute | solution.py:707
  32.0 15.4 %collective-permute-start.8 = (f32[1,128,1024]{2,1,0:T(8,128)S(1)}, f32[1,128,1024]{2,1,0:T(8,128)S(1)}, u32[]{:S(2)}, u32[]{:S(2)}) collective-permute-start(f32[1,128,1024]{2,1,0:T(8,128)S(1)} %get-tuple-element.137), channel_id=1, source_target_pairs={{0,1},{4,5},{8,9},{12,13},{16,17},{20,21},{24,25},{28,29}} | collective-permute-start | bytes 1572872 | tf_op jit(solution)/shard_map/ppermute | solution.py:706
  32.8 25.9 %collective-permute-start.15 = (f32[1,128,1024]{2,1,0:T(8,128)S(1)}, f32[1,128,1024]{2,1,0:T(8,128)S(1)}, u32[]{:S(2)}, u32[]{:S(2)}) collective-permute-start(f32[1,128,1024]{2,1,0:T(8,128)S(1)} %get-tuple-element.150), channel_id=1, source_target_pairs={{3,2},{7,6},{11,10},{15,14},{19,18},{23,22},{27,26},{31,30}} | collective-permute-start | bytes 1572872 | tf_op jit(solution)/shard_map/ppermute | solution.py:707
  34.1 26.5 %collective-permute-start.14 = (f32[1,128,1024]{2,1,0:T(8,128)S(1)}, f32[1,128,1024]{2,1,0:T(8,128)S(1)}, u32[]{:S(2)}, u32[]{:S(2)}) collective-permute-start(f32[1,128,1024]{2,1,0:T(8,128)S(1)} %get-tuple-element.150), channel_id=1, source_target_pairs={{0,1},{4,5},{8,9},{12,13},{16,17},{20,21},{24,25},{28,29}} | collective-permute-start | bytes 1572872 | tf_op jit(solution)/shard_map/ppermute | solution.py:706
  51.4 18.5 %collective-permute-start.13 = (f32[1,128,1024]{2,1,0:T(8,128)S(1)}, f32[1,128,1024]{2,1,0:T(8,128)S(1)}, u32[]{:S(2)}, u32[]{:S(2)}) collective-permute-start(f32[1,128,1024]{2,1,0:T(8,128)S(1)} %get-tuple-element.141), channel_id=1, source_target_pairs={{3,2},{7,6},{11,10},{15,14},{19,18},{23,22},{27,26},{31,30}} | collective-permute-start | bytes 1572872 | tf_op jit(solution)/shard_map/ppermute | solution.py:707
  52.7 17.9 %collective-permute-start.12 = (f32[1,128,1024]{2,1,0:T(8,128)S(1)}, f32[1,128,1024]{2,1,0:T(8,128)S(1)}, u32[]{:S(2)}, u32[]{:S(2)}) collective-permute-start(f32[1,128,1024]{2,1,0:T(8,128)S(1)} %get-tuple-element.141), channel_id=1, source_target_pairs={{0,1},{4,5},{8,9},{12,13},{16,17},{20,21},{24,25},{28,29}} | collective-permute-start | bytes 1572872 | tf_op jit(solution)/shard_map/ppermute | solution.py:706
  54.1 21.9 %collective-permute-start.16 = (f32[1,128,1024]{2,1,0:T(8,128)S(1)}, f32[1,128,1024]{2,1,0:T(8,128)S(1)}, u32[]{:S(2)}, u32[]{:S(2)}) collective-permute-start(f32[1,128,1024]{2,1,0:T(8,128)S(1)} %get-tuple-element.147), channel_id=1, source_target_pairs={{0,1},{1,2},{4,5},{5,6},{8,9},{9,10},{12,13},{13,14},{16,17},{17,1... | collective-permute-start | bytes 1572872 | tf_op jit(solution)/shard_map/ppermute | solution.py:706
  58.6 25.5 %collective-permute-start.17 = (f32[1,128,1024]{2,1,0:T(8,128)S(1)}, f32[1,128,1024]{2,1,0:T(8,128)S(1)}, u32[]{:S(2)}, u32[]{:S(2)}) collective-permute-start(f32[1,128,1024]{2,1,0:T(8,128)S(1)} %get-tuple-element.148), channel_id=1, source_target_pairs={{2,1},{3,2},{6,5},{7,6},{10,9},{11,10},{14,13},{15,14},{18,17},{19... | collective-permute-start | bytes 1572872 | tf_op jit(solution)/shard_map/ppermute | solution.py:707
  60.6 31.8 %collective-permute-start.11 = (f32[1,128,1024]{2,1,0:T(8,128)S(1)}, f32[1,128,1024]{2,1,0:T(8,128)S(1)}, u32[]{:S(2)}, u32[]{:S(2)}) collective-permute-start(f32[1,128,1024]{2,1,0:T(8,128)S(1)} %get-tuple-element.139), channel_id=1, source_target_pairs={{3,2},{7,6},{11,10},{15,14},{19,18},{23,22},{27,26},{31,30}} | collective-permute-start | bytes 1572872 | tf_op jit(solution)/shard_map/ppermute | solution.py:707
  69.9 22.5 %collective-permute-start.10 = (f32[1,128,1024]{2,1,0:T(8,128)S(1)}, f32[1,128,1024]{2,1,0:T(8,128)S(1)}, u32[]{:S(2)}, u32[]{:S(2)}) collective-permute-start(f32[1,128,1024]{2,1,0:T(8,128)S(1)} %get-tuple-element.139), channel_id=1, source_target_pairs={{0,1},{4,5},{8,9},{12,13},{16,17},{20,21},{24,25},{28,29}} | collective-permute-start | bytes 1572872 | tf_op jit(solution)/shard_map/ppermute | solution.py:706
  70.6 31.8 %collective-permute-start.18 = (f32[1,128,1024]{2,1,0:T(8,128)S(1)}, f32[1,128,1024]{2,1,0:T(8,128)S(1)}, u32[]{:S(2)}, u32[]{:S(2)}) collective-permute-start(f32[1,128,1024]{2,1,0:T(8,128)S(1)} %get-tuple-element.151), channel_id=1, source_target_pairs={{0,1},{1,2},{4,5},{5,6},{8,9},{9,10},{12,13},{13,14},{16,17},{17,1... | collective-permute-start | bytes 1572872 | tf_op jit(solution)/shard_map/ppermute | solution.py:706
  76.0 27.6 %collective-permute-start.19 = (f32[1,128,1024]{2,1,0:T(8,128)S(1)}, f32[1,128,1024]{2,1,0:T(8,128)S(1)}, u32[]{:S(2)}, u32[]{:S(2)}) collective-permute-start(f32[1,128,1024]{2,1,0:T(8,128)S(1)} %get-tuple-element.152), channel_id=1, source_target_pairs={{2,1},{3,2},{6,5},{7,6},{10,9},{11,10},{14,13},{15,14},{18,17},{19... | collective-permute-start | bytes 1572872 | tf_op jit(solution)/shard_map/ppermute | solution.py:707
  92.4 17.7 %collective-permute-start.20 = (f32[1,128,1024]{2,1,0:T(8,128)S(1)}, f32[1,128,1024]{2,1,0:T(8,128)S(1)}, u32[]{:S(2)}, u32[]{:S(2)}) collective-permute-start(f32[1,128,1024]{2,1,0:T(8,128)S(1)} %get-tuple-element.157), channel_id=1, source_target_pairs={{0,1},{1,2},{4,5},{5,6},{8,9},{9,10},{12,13},{13,14},{16,17},{17,1... | collective-permute-start | bytes 1572872 | tf_op jit(solution)/shard_map/ppermute | solution.py:706
  93.6 21.2 %collective-permute-start.21 = (f32[1,128,1024]{2,1,0:T(8,128)S(1)}, f32[1,128,1024]{2,1,0:T(8,128)S(1)}, u32[]{:S(2)}, u32[]{:S(2)}) collective-permute-start(f32[1,128,1024]{2,1,0:T(8,128)S(1)} %get-tuple-element.158), channel_id=1, source_target_pairs={{2,1},{3,2},{6,5},{7,6},{10,9},{11,10},{14,13},{15,14},{18,17},{19... | collective-permute-start | bytes 1572872 | tf_op jit(solution)/shard_map/ppermute | solution.py:707
  104.2 17.1 %collective-permute-start.22 = (f32[1,128,1024]{2,1,0:T(8,128)S(1)}, f32[1,128,1024]{2,1,0:T(8,128)S(1)}, u32[]{:S(2)}, u32[]{:S(2)}) collective-permute-start(f32[1,128,1024]{2,1,0:T(8,128)S(1)} %get-tuple-element.163), channel_id=1, source_target_pairs={{0,1},{1,2},{4,5},{5,6},{8,9},{9,10},{12,13},{13,14},{16,17},{17,1... | collective-permute-start | bytes 1572872 | tf_op jit(solution)/shard_map/ppermute | solution.py:706
  105.5 20.5 %collective-permute-start.23 = (f32[1,128,1024]{2,1,0:T(8,128)S(1)}, f32[1,128,1024]{2,1,0:T(8,128)S(1)}, u32[]{:S(2)}, u32[]{:S(2)}) collective-permute-start(f32[1,128,1024]{2,1,0:T(8,128)S(1)} %get-tuple-element.164), channel_id=1, source_target_pairs={{2,1},{3,2},{6,5},{7,6},{10,9},{11,10},{14,13},{15,14},{18,17},{19... | collective-permute-start | bytes 1572872 | tf_op jit(solution)/shard_map/ppermute | solution.py:707
  115.5 17.1 %collective-permute-start.24 = (f32[1,128,1024]{2,1,0:T(8,128)S(1)}, f32[1,128,1024]{2,1,0:T(8,128)S(1)}, u32[]{:S(2)}, u32[]{:S(2)}) collective-permute-start(f32[1,128,1024]{2,1,0:T(8,128)S(1)} %get-tuple-element.169), channel_id=1, source_target_pairs={{0,1},{1,2},{2,3},{4,5},{5,6},{6,7},{8,9},{9,10},{10,11},{12,13},{... | collective-permute-start | bytes 1572872 | tf_op jit(solution)/shard_map/ppermute | solution.py:706
  117.4 19.9 %collective-permute-start.25 = (f32[1,128,1024]{2,1,0:T(8,128)S(1)}, f32[1,128,1024]{2,1,0:T(8,128)S(1)}, u32[]{:S(2)}, u32[]{:S(2)}) collective-permute-start(f32[1,128,1024]{2,1,0:T(8,128)S(1)} %get-tuple-element.170), channel_id=1, source_target_pairs={{1,0},{2,1},{3,2},{5,4},{6,5},{7,6},{9,8},{10,9},{11,10},{13,12},{... | collective-permute-start | bytes 1572872 | tf_op jit(solution)/shard_map/ppermute | solution.py:707
  126.7 17.1 %collective-permute-start.26 = (f32[1,128,1024]{2,1,0:T(8,128)S(1)}, f32[1,128,1024]{2,1,0:T(8,128)S(1)}, u32[]{:S(2)}, u32[]{:S(2)}) collective-permute-start(f32[1,128,1024]{2,1,0:T(8,128)S(1)} %get-tuple-element.175), channel_id=1, source_target_pairs={{0,1},{1,2},{2,3},{4,5},{5,6},{6,7},{8,9},{9,10},{10,11},{12,13},{... | collective-permute-start | bytes 1572872 | tf_op jit(solution)/shard_map/ppermute | solution.py:706
  128.6 19.9 %collective-permute-start.27 = (f32[1,128,1024]{2,1,0:T(8,128)S(1)}, f32[1,128,1024]{2,1,0:T(8,128)S(1)}, u32[]{:S(2)}, u32[]{:S(2)}) collective-permute-start(f32[1,128,1024]{2,1,0:T(8,128)S(1)} %get-tuple-element.176), channel_id=1, source_target_pairs={{1,0},{2,1},{3,2},{5,4},{6,5},{7,6},{9,8},{10,9},{11,10},{13,12},{... | collective-permute-start | bytes 1572872 | tf_op jit(solution)/shard_map/ppermute | solution.py:707
  137.9 18.7 %collective-permute-start.30 = (f32[1,128,1024]{2,1,0:T(8,128)S(1)}, f32[1,128,1024]{2,1,0:T(8,128)S(1)}, u32[]{:S(2)}, u32[]{:S(2)}) collective-permute-start(f32[1,128,1024]{2,1,0:T(8,128)S(1)} %get-tuple-element.181), channel_id=1, source_target_pairs={{0,1},{1,2},{2,3},{4,5},{5,6},{6,7},{8,9},{9,10},{10,11},{12,13},{... | collective-permute-start | bytes 1572872 | tf_op jit(solution)/shard_map/ppermute | solution.py:706
  139.9 19.9 %collective-permute-start.31 = (f32[1,128,1024]{2,1,0:T(8,128)S(1)}, f32[1,128,1024]{2,1,0:T(8,128)S(1)}, u32[]{:S(2)}, u32[]{:S(2)}) collective-permute-start(f32[1,128,1024]{2,1,0:T(8,128)S(1)} %get-tuple-element.182), channel_id=1, source_target_pairs={{1,0},{2,1},{3,2},{5,4},{6,5},{7,6},{9,8},{10,9},{11,10},{13,12},{... | collective-permute-start | bytes 1572872 | tf_op jit(solution)/shard_map/ppermute | solution.py:707
  149.2 14.2 %collective-permute-start.28 = (f32[1,128,1024]{2,1,0:T(8,128)S(1)}, f32[1,128,1024]{2,1,0:T(8,128)S(1)}, u32[]{:S(2)}, u32[]{:S(2)}) collective-permute-start(f32[1,128,1024]{2,1,0:T(8,128)S(1)} %get-tuple-element.187), channel_id=1, source_target_pairs={{0,1},{1,2},{2,3},{4,5},{5,6},{6,7},{8,9},{9,10},{10,11},{12,13},{... | collective-permute-start | bytes 1572872 | tf_op jit(solution)/shard_map/ppermute | solution.py:706
  151.1 19.0 %collective-permute-start.29 = (f32[1,128,1024]{2,1,0:T(8,128)S(1)}, f32[1,128,1024]{2,1,0:T(8,128)S(1)}, u32[]{:S(2)}, u32[]{:S(2)}) collective-permute-start(f32[1,128,1024]{2,1,0:T(8,128)S(1)} %get-tuple-element.188), channel_id=1, source_target_pairs={{1,0},{2,1},{3,2},{5,4},{6,5},{7,6},{9,8},{10,9},{11,10},{13,12},{... | collective-permute-start | bytes 1572872 | tf_op jit(solution)/shard_map/ppermute | solution.py:707
